TPU v7x, 32 devices: a whole 2x2x4 slice. The times are simulated.
32 devices in a mesh: resp: 2 (over x), fsdp: 4 (over y, core), head: 4 (over z).
Axes of the slice: x: 2, y: 2, z: 4, core: 2. Of those that a mesh axis runs over, the one named last changes fastest.
Arguments:
- queries: bfloat16 [2048, 4096], P(('resp', 'fsdp'), 'head'), may hold values from -12 to 12
- self_keys: bfloat16 [2048, 512], P(('resp', 'fsdp'), 'head'), may hold values from -12 to 12
- self_values: bfloat16 [2048, 512], P(('resp', 'fsdp'), 'head'), may hold values from -6 to 6
- d_out: bfloat16 [2048, 4096], P(('resp', 'fsdp'), 'head'), may hold values from -12 to 12
- prompt_keys: bfloat16 [4, 256, 512], P('resp', 'fsdp', 'head'), may hold values from -6 to 6
- prompt_values: bfloat16 [4, 256, 512], P('resp', 'fsdp', 'head'), may hold values from -6 to 6
- counts: int32 [4], replicated, may hold values from 1 to 4, 8 in all
- owner_slot: int32 [4], replicated, may hold values from 0 to 3, each once
- prompt_blocks: int32 [4], replicated, may hold values from 1 to 2
- resp_blocks: int32 [8], P(('resp', 'fsdp')), may hold values from 1 to 2
- grad_q: bfloat16 [8192, 4096], P('fsdp', ('resp', 'head')), may hold values from -4 to 4
- momentum: float32 [8192, 4096], P('fsdp', ('resp', 'head')), may hold values from -30 to 30
- basis: float32 [4096, 256], P(('resp', 'head')), may hold values from -0.09375 to 0.09375
Outputs:
- dq: bfloat16 [2048, 4096], P(('resp', 'fsdp'), 'head')
- resp_kv_grad: bfloat16 [2, 2048, 512], P(None, ('resp', 'fsdp'), 'head')
- prompt_kv_grad: float32 [2, 4, 256, 512], P(None, 'resp', 'fsdp', 'head')
- update: bfloat16 [8192, 4096], P('fsdp', ('resp', 'head'))
- momentum_out: float32 [8192, 4096], P('fsdp', ('resp', 'head'))
- basis_out: float32 [4096, 256], P(('resp', 'head'))
Inputs may be any that keep to these rules, and one draw needn't show every extreme that they name: `counts`: responses are stored group by group in the order of the groups. `owner_slot`: each row of prompt_keys holds the prompt of exactly one group.
All inputs are finite; a program needn't handle non-finite values.
Results may differ from a plain program's by a relative error of at most 0.0087.
Values may be sent and summed in bfloat16 or wider, within the bound.
No kernel may reach another device: no remote copies, remote signals or barrier semaphores. Data moves between devices by JAX's collectives and lax.ppermute only.
A program may use at most 64 MiB of HBM per device.

v0:
```python
import math

import jax
import jax.numpy as jnp
from jax import lax
from jax.sharding import PartitionSpec as P

D = 8192
HD = 128
QCOLS = 4096
RANK = 256


momentum_keep = 0.95
norm_eps = 1e-06


def combined_all(value, axis, combine):
    everything = lax.all_gather(value, axis)
    initial = everything[0]

    def step(k, so_far):
        return combine(so_far, everything[k])

    return lax.fori_loop(1, lax.axis_size(axis), step, initial)


def group_index(counts, order):
    ends = jnp.cumsum(counts)
    return jnp.sum((ends[None, :] <= order[:, None]).astype(jnp.int32), axis=1)


def key_mask(height, width, prompt_len, prompt_cap, resp_len):
    place = jnp.arange(width, dtype=jnp.int32)[None, :]
    position = jnp.arange(height, dtype=jnp.int32)[:, None]
    inner = place - prompt_cap
    return jnp.where(
        place < prompt_cap, place < prompt_len, (inner <= position) & (inner < resp_len)
    )


def attend_group(q_part, o_grad, keys, values, prompt_len, prompt_cap, resp_len):
    height = q_part.shape[0]
    depth = q_part.shape[2]
    scale = depth ** (-0.5)
    raw = jnp.einsum("thd,kd->htk", q_part, keys, preferred_element_type=jnp.float32) * scale
    visible = key_mask(height, keys.shape[0], prompt_len, prompt_cap, resp_len)
    logits = jnp.where(visible[None], raw, -jnp.inf)
    peak = jnp.max(logits, axis=2, keepdims=True)
    lse = peak + jnp.log(jnp.sum(jnp.exp(logits - peak), axis=2, keepdims=True))
    weight = jnp.exp(logits - lse).astype(jnp.bfloat16)
    output = jnp.einsum("htk,kd->htd", weight, values, preferred_element_type=jnp.float32)
    diag = jnp.sum(jnp.swapaxes(o_grad.astype(jnp.float32), 0, 1) * output, axis=2)
    p_grad = jnp.einsum("thd,kd->htk", o_grad, values, preferred_element_type=jnp.float32)
    s_grad = (weight.astype(jnp.float32) * (p_grad - diag[..., None])).astype(jnp.bfloat16)
    q_grad = jnp.einsum("htk,kd->thd", s_grad, keys, preferred_element_type=jnp.float32)
    k_grads = jnp.einsum("htk,thd->kd", s_grad, q_part, preferred_element_type=jnp.float32) * scale
    v_grads = jnp.einsum("htk,thd->kd", weight, o_grad, preferred_element_type=jnp.float32)
    return (q_grad * scale, k_grads, v_grads)


def on_device(
    queries,
    self_keys,
    self_values,
    d_out,
    prompt_keys,
    prompt_values,
    counts,
    owner_slot,
    prompt_blocks,
    resp_blocks,
    grad_q,
    momentum,
    basis,
):
    highest = lax.Precision.HIGHEST
    fsdp_count = lax.axis_size("fsdp")
    row_index = lax.axis_index("resp")
    col_index = lax.axis_index("fsdp")
    piece = prompt_keys.shape[1]
    kv_cols = prompt_keys.shape[2]
    prompt_cap = piece * fsdp_count
    height = queries.shape[0]
    my_group = group_index(counts, jnp.reshape(row_index * fsdp_count + col_index, (1,)))[0]
    prompt_len = prompt_blocks[my_group] * 128
    resp_len = resp_blocks[0] * 128
    stacked = jnp.stack([prompt_keys, prompt_values], 0)
    everyone = lax.all_gather(stacked, "resp", axis=1, tiled=True)
    row_slots = owner_slot[
        group_index(counts, row_index * fsdp_count + jnp.arange(fsdp_count, dtype=jnp.int32))
    ]
    outgoing = jnp.take(everyone, row_slots, axis=1)
    arrived = lax.all_to_all(outgoing, "fsdp", split_axis=1, concat_axis=2, tiled=True)
    prompt_kv = arrived.reshape(2, prompt_cap, kv_cols)
    live = jnp.arange(height, dtype=jnp.int32) < resp_len
    masked_grad = jnp.where(live[:, None], d_out, jnp.zeros((), jnp.bfloat16))
    keys_all = jnp.concatenate([prompt_kv[0], self_keys], 0)
    values_all = jnp.concatenate([prompt_kv[1], self_values], 0)
    per_group = queries.shape[1] // self_keys.shape[1]
    q_part = queries.reshape(height, per_group, HD)
    o_part = masked_grad.reshape(height, per_group, HD)
    q_grad, k_grad, v_grad = attend_group(
        q_part, o_part, keys_all, values_all, prompt_len, prompt_cap, resp_len
    )
    q_parts = q_grad.reshape(height, per_group * HD)
    k_parts = k_grad
    v_parts = v_grad
    dq = q_parts.astype(jnp.bfloat16)
    k_grad = k_parts
    v_grad = v_parts
    resp_grad = jnp.stack([k_grad[prompt_cap:], v_grad[prompt_cap:]], 0).astype(jnp.bfloat16)
    partial_value = jnp.stack([k_grad[:prompt_cap], v_grad[:prompt_cap]], 0).reshape(
        2, fsdp_count, piece, kv_cols
    )
    returned = lax.all_to_all(partial_value, "fsdp", split_axis=1, concat_axis=1, tiled=True)
    chooser = (row_slots[None, :] == jnp.arange(counts.shape[0], dtype=jnp.int32)[:, None]).astype(
        jnp.float32
    )
    by_slot = jnp.einsum("sf,afpc->aspc", chooser, returned, precision=highest)
    prompt_grad = lax.psum_scatter(by_slot, "resp", scatter_dimension=1, tiled=True)
    total = momentum + grad_q.astype(jnp.float32)
    projected = lax.psum(jnp.dot(total, basis, precision=highest), ("resp", "head"))
    gram = jnp.dot(projected.T, projected, precision=highest)

    def join(former, latter):
        summed = jnp.dot(former.T, former, precision=highest) + jnp.dot(
            latter.T, latter, precision=highest
        )
        return jnp.linalg.cholesky(summed).T

    upper = combined_all(jnp.linalg.cholesky(gram).T, "fsdp", join)
    lower = upper.T
    ortho = jax.scipy.linalg.solve_triangular(lower, projected.T, lower=True).T
    back = lax.psum(jnp.dot(total.T, ortho, precision=highest), "fsdp")
    momentum_out = total - (1.0 - momentum_keep) * jnp.dot(ortho, back.T, precision=highest)
    squares = lax.psum(jnp.sum(back * back, axis=0), ("resp", "head"))
    basis_out = back * lax.rsqrt(squares + norm_eps)
    update = (math.sqrt(D * QCOLS / RANK) * jnp.dot(ortho, basis_out.T, precision=highest)).astype(
        jnp.bfloat16
    )
    return (dq, resp_grad, prompt_grad, update, momentum_out, basis_out)


def solution(mesh):
    placed = (
        P(("resp", "fsdp"), "head"),
        P(("resp", "fsdp"), "head"),
        P(("resp", "fsdp"), "head"),
        P(("resp", "fsdp"), "head"),
        P("resp", "fsdp", "head"),
        P("resp", "fsdp", "head"),
        P(),
        P(),
        P(),
        P(("resp", "fsdp")),
        P("fsdp", ("resp", "head")),
        P("fsdp", ("resp", "head")),
        P(("resp", "head"), None),
    )
    return jax.shard_map(
        on_device,
        mesh=mesh,
        in_specs=placed,
        out_specs=(
            P(("resp", "fsdp"), "head"),
            P(None, ("resp", "fsdp"), "head"),
            P(None, "resp", "fsdp", "head"),
            P("fsdp", ("resp", "head")),
            P("fsdp", ("resp", "head")),
            P(("resp", "head"), None),
        ),
        check_vma=False,
    )
```

profile of v0, /device:TPU:0, one launch (start us, length us, event | category | flops | bytes accessed | tf_op | source)
XLA Modules:
  0.0 444.4 jit_solution(17533267559150992061)
XLA Ops:
  11.2 5.8 %all_gather.9 = bf16[2,4,64,128]{3,2,1,0:T(8,128)(2,1)S(1)} all-gather(bf16[2,2,64,128]{3,2,1,0:T(8,128)(2,1)S(1)} %pad_maximum_fusion.6), channel_id=1, replica_groups=mesh['resp'=2,'fsdp'=4,'head'=4] {'resp'}, dimensions={1}, use_global_device_ids=true | all-gather | bytes 196608 | tf_op jit(solution)/shard_map/all_gather | solution.py:89
  21.8 7.7 %fusion.11 = f32[2048,256]{1,0:T(8,128)} fusion(f32[512,256]{1,0:T(8,128)} %param.28, f32[2048,512]{1,0:T(8,128)} %param.27, bf16[2048,512]{1,0:T(8,128)(2,1)} %param.26), kind=kOutput, calls=%fused_computation.38 | convolution fusion | flops 3223322624 | bytes 8912896 | tf_op jit(solution)/shard_map/dot_general | solution.py:123
  38.6 95.1 %all-reduce.4.cloned.1.call-done = f32[2048,256]{1,0:T(8,128)} async-done(((f32[2048,256]{1,0:T(8,128)}), f32[2048,256]{1,0:T(8,128)}) %all-reduce.4.cloned.1.call-update) | async-done | bytes 2097168 | tf_op jit(solution)/shard_map/psum | solution.py:123
  133.7 5.7 %fusion.49 = f32[256,256]{1,0:T(8,128)S(1)} fusion(f32[2048,256]{1,0:T(8,128)} %all-reduce.4.cloned.1.call-done), kind=kOutput, calls=%fused_computation.126 | convolution fusion | flops 1610612736 | bytes 2359296 | tf_op jit(solution)/shard_map/dot_general | solution.py:124
  141.9 11.7 %cholesky.164 = f32[128,128]{1,0:T(8,128)S(1)} custom-call(f32[128,128]{1,0:T(8,128)S(1)} %cholesky.197), custom_call_target="Cholesky" | custom-call | tf_op jit(solution)/shard_map/jit(cholesky)/cholesky | solution.py:132
  155.7 11.5 %custom-call.15 = f32[1,128,128]{1,2,0:T(8,128)} custom-call(f32[1,128,128]{2,1,0:T(8,128)} %get-tuple-element.169), custom_call_target="InvertDiagBlocksLowerTriangular" | custom-call | tf_op jit(solution)/shard_map/jit(cholesky)/cholesky | solution.py:132
  170.0 13.2 %cholesky.181 = f32[128,128]{1,0:T(8,128)} custom-call(f32[128,128]{1,0:T(8,128)} %convolution_subtract_fusion.2), custom_call_target="Cholesky" | custom-call | tf_op jit(solution)/shard_map/jit(cholesky)/cholesky | solution.py:132
  200.3 5.9 %all-to-all-done.1 = f32[2,4,64,128]{3,2,0,1:T(8,128)S(1)} async-done(((f32[2,4,64,128]{3,2,0,1:T(8,128)}), f32[2,4,64,128]{3,2,0,1:T(8,128)S(1)}, u32[]{:S(2)}, u32[]{:S(2)}) %all-to-all-start.1) | async-done | bytes 262176 | tf_op jit(solution)/shard_map/all_to_all | solution.py:116
  210.5 111.1 %while.16 = (s32[]{:T(128)}, f32[256,256]{0,1:T(8,128)S(1)}, f32[4,256,256]{2,1,0:T(8,128)S(1)}, s32[]{:T(128)}, s32[]{:T(128)}, /*index=5*/s32[]{:T(128)}, f32[]{:T(128)}) while((s32[]{:T(128)}, f32[256,256]{0,1:T(8,128)S(1)}, f32[4,256,256]{2,1,0:T(8,128)S(1)}, s32[]{:T(128)}, s32[]{:T(128)}, /*index=5*/s32[]{:T(128)}, f32[]{:T(128)}) %tuple.96), condition=%wide.region_13.15_spmd, body=%wide.region_12.14_spmd.sunk | while | flops 453525760 | bytes 4393093 | solution.py:25
  211.8 11.7 %cholesky.347 = f32[128,128]{1,0:T(8,128)S(1)} custom-call(f32[128,128]{1,0:T(8,128)S(1)} %cholesky.346), custom_call_target="Cholesky" | custom-call | tf_op jit(solution)/shard_map/while/body/eval_jaxpr/jit(cholesky)/cholesky | solution.py:130
  223.5 9.8 %custom-call.22 = f32[1,128,128]{1,2,0:T(8,128)S(1)} custom-call(f32[1,128,128]{2,1,0:T(8,128)S(1)} %get-tuple-element.228), custom_call_target="InvertDiagBlocksLowerTriangular" | custom-call | tf_op jit(solution)/shard_map/while/body/eval_jaxpr/jit(cholesky)/cholesky | solution.py:130
  233.8 11.7 %cholesky.349 = f32[128,128]{1,0:T(8,128)S(1)} custom-call(f32[128,128]{1,0:T(8,128)S(1)} %convolution_subtract_fusion.4), custom_call_target="Cholesky" | custom-call | tf_op jit(solution)/shard_map/while/body/eval_jaxpr/jit(cholesky)/cholesky | solution.py:130
  248.8 11.7 %cholesky.347 = f32[128,128]{1,0:T(8,128)S(1)} custom-call(f32[128,128]{1,0:T(8,128)S(1)} %cholesky.346), custom_call_target="Cholesky" | custom-call | tf_op jit(solution)/shard_map/while/body/eval_jaxpr/jit(cholesky)/cholesky | solution.py:130
  260.6 9.8 %custom-call.22 = f32[1,128,128]{1,2,0:T(8,128)S(1)} custom-call(f32[1,128,128]{2,1,0:T(8,128)S(1)} %get-tuple-element.228), custom_call_target="InvertDiagBlocksLowerTriangular" | custom-call | tf_op jit(solution)/shard_map/while/body/eval_jaxpr/jit(cholesky)/cholesky | solution.py:130
  270.9 11.7 %cholesky.349 = f32[128,128]{1,0:T(8,128)S(1)} custom-call(f32[128,128]{1,0:T(8,128)S(1)} %convolution_subtract_fusion.4), custom_call_target="Cholesky" | custom-call | tf_op jit(solution)/shard_map/while/body/eval_jaxpr/jit(cholesky)/cholesky | solution.py:130
  285.9 11.7 %cholesky.347 = f32[128,128]{1,0:T(8,128)S(1)} custom-call(f32[128,128]{1,0:T(8,128)S(1)} %cholesky.346), custom_call_target="Cholesky" | custom-call | tf_op jit(solution)/shard_map/while/body/eval_jaxpr/jit(cholesky)/cholesky | solution.py:130
  297.6 9.8 %custom-call.22 = f32[1,128,128]{1,2,0:T(8,128)S(1)} custom-call(f32[1,128,128]{2,1,0:T(8,128)S(1)} %get-tuple-element.228), custom_call_target="InvertDiagBlocksLowerTriangular" | custom-call | tf_op jit(solution)/shard_map/while/body/eval_jaxpr/jit(cholesky)/cholesky | solution.py:130
  307.9 11.7 %cholesky.349 = f32[128,128]{1,0:T(8,128)S(1)} custom-call(f32[128,128]{1,0:T(8,128)S(1)} %convolution_subtract_fusion.4), custom_call_target="Cholesky" | custom-call | tf_op jit(solution)/shard_map/while/body/eval_jaxpr/jit(cholesky)/cholesky | solution.py:130
  327.0 20.6 %custom-call.12 = f32[2,128,128]{1,2,0:T(8,128)S(1)} custom-call(f32[2,128,128]{2,1,0:T(8,128)} %get-tuple-element.103), custom_call_target="InvertDiagBlocksLowerTriangular" | custom-call | tf_op jit(solution)/shard_map/jit(_solve_triangular)/triangular_solve | solution.py:134
  354.2 9.1 %fusion.10 = f32[512,256]{1,0:T(8,128)} fusion(f32[2048,512]{1,0:T(8,128)S(1)} %copy-done.1, bf16[2048,512]{1,0:T(8,128)(2,1)} %param.26, f32[128,2048]{1,0:T(8,128)S(1)} %fusion.29, f32[128,2048]{1,0:T(8,128)S(1)} %fusion.15), kind=kOutput, calls=%fused_computation.37 | convolution fusion | flops 3223846912 | bytes 8912896 | tf_op jit(solution)/shard_map/dot_general | solution.py:135
  365.6 30.0 %all-reduce.6.cloned.1.call-done = f32[512,256]{1,0:T(8,128)} async-done(((f32[512,256]{1,0:T(8,128)}), f32[512,256]{1,0:T(8,128)}) %all-reduce.6.cloned.1.call-update) | async-done | bytes 524304 | tf_op jit(solution)/shard_map/psum | solution.py:135
  396.8 21.6 %psum.23 = f32[256]{0:T(256)S(1)} all-reduce(f32[256]{0:T(256)S(1)} %multiply_reduce_fusion), channel_id=1, replica_groups=mesh['resp'=2,'fsdp'=4,'head'=4] {'resp','head'}, use_global_device_ids=true, to_apply=%region_16.18 | all-reduce | flops 256 | bytes 2048 | tf_op jit(solution)/shard_map/psum | solution.py:137
  419.7 7.9 %multiply_convert_fusion = bf16[2048,512]{1,0:T(8,128)(2,1)} fusion(f32[512,256]{1,0:T(8,128)S(1)} %broadcast_multiply_fusion, f32[128,2048]{1,0:T(8,128)S(1)} %fusion.29, f32[128,2048]{1,0:T(8,128)S(1)} %fusion.15), kind=kOutput, calls=%fused_computation.30 | convolution fusion | flops 3223846912 | bytes 4718592 | tf_op jit(solution)/shard_map/dot_general | solution.py:139
  427.5 9.5 %multiply_subtract_fusion = f32[2048,512]{1,0:T(8,128)} fusion(f32[512,256]{1,0:T(8,128)S(1)} %copy-done.4, f32[2048,512]{1,0:T(8,128)S(1)} %copy-done.2, bf16[2048,512]{1,0:T(8,128)(2,1)} %param.26, f32[128,2048]{1,0:T(8,128)S(1)} %fusion.29, f32[128,2048]{1,0:T(8,128)S(1)} %fusion.15), kind=kOutput, calls=%fused_computation.29 | convolution fusion | flops 3225944064 | bytes 13107200 | tf_op jit(solution)/shard_map/dot_general | solution.py:136
  (147 shorter events, 70.0 us)
Async XLA Ops:
  8.0 27.5 %copy-start = (bf16[256,1024]{1,0:T(8,128)(2,1)S(1)}, bf16[256,1024]{1,0:T(8,128)(2,1)}, u32[]{:S(2)}) copy-start(bf16[256,1024]{1,0:T(8,128)(2,1)} %param.16) | copy-start | bytes 1572868
  18.4 17.2 %all-to-all-start = ((bf16[2,4,64,128]{3,2,0,1:T(8,128)(2,1)}), bf16[2,4,64,128]{3,2,0,1:T(8,128)(2,1)S(1)}, u32[]{:S(2)}, u32[]{:S(2)}) async-start(bf16[2,4,64,128]{3,2,0,1:T(8,128)(2,1)} %select_bitcast_fusion.3), calls=%async_computation | async-start | bytes 262144 | tf_op jit(solution)/shard_map/all_to_all | solution.py:94
  21.7 11.3 %copy-start.12 = (s32[4]{0:T(128)S(1)}, s32[4]{0:T(128)}, u32[]{:S(2)}) copy-start(s32[4]{0:T(128)} %param.24) | copy-start | bytes 52
  21.7 12.6 %copy-start.7 = (bf16[256,1024]{1,0:T(8,128)(2,1)S(1)}, bf16[256,1024]{1,0:T(8,128)(2,1)}, u32[]{:S(2)}) copy-start(bf16[256,1024]{1,0:T(8,128)(2,1)} %param.19) | copy-start | bytes 1572868
  21.7 111.9 %all-reduce.4.cloned.1.call-start = ((), (), s32[]{:S(2)}) async-start(), calls=%async_computation.4 | async-start | bytes 4194304 | tf_op jit(solution)/shard_map/psum | solution.py:123
  29.5 6.0 %copy-start.8 = (bf16[256,128]{1,0:T(8,128)(2,1)S(1)}, bf16[256,128]{1,0:T(8,128)(2,1)}, u32[]{:S(2)}) copy-start(bf16[256,128]{1,0:T(8,128)(2,1)} %param.17) | copy-start | bytes 196612
  29.5 178.4 %all-gather.3.cloned.1.call-start = ((), (), s32[]{:S(2)}) async-start(), calls=%async_computation.6 | async-start | bytes 1310720 | tf_op jit(solution)/shard_map/all_gather | solution.py:19
  35.5 2.5 copy-start.9
  37.2 0.9 copy-start.11
  141.2 0.7 copy-start.6
  153.6 0.6 copy-start.10
  188.4 1.3 copy-start.3
  196.8 9.4 %all-to-all-start.1 = ((f32[2,4,64,128]{3,2,0,1:T(8,128)}), f32[2,4,64,128]{3,2,0,1:T(8,128)S(1)}, u32[]{:S(2)}, u32[]{:S(2)}) async-start(f32[2,4,64,128]{3,2,0,1:T(8,128)} %pad_maximum_fusion.4), calls=%async_computation.1 | async-start | bytes 524288 | tf_op jit(solution)/shard_map/all_to_all | solution.py:116
  200.2 163.8 %reduce-scatter.2.cloned.1.call-start = ((), (), s32[]{:S(2)}) async-start(), calls=%async_computation.3 | async-start | bytes 393216 | tf_op jit(solution)/shard_map/reduce_scatter | solution.py:121
  207.5 188.1 %all-reduce.6.cloned.1.call-start = ((), (), s32[]{:S(2)}) async-start(), calls=%async_computation.5 | async-start | bytes 1048576 | tf_op jit(solution)/shard_map/psum | solution.py:135
  210.5 111.2 %copy-start.13 = (s32[2]{0:T(128)S(1)}, s32[2]{0:T(128)}, u32[]{:S(2)}) copy-start(s32[2]{0:T(128)} %iota_multiply_fusion) | copy-start | bytes 28
  347.6 6.6 %copy-start.1 = (f32[2048,512]{1,0:T(8,128)S(1)}, f32[2048,512]{1,0:T(8,128)}, u32[]{:S(2)}) copy-start(f32[2048,512]{1,0:T(8,128)} %param.27) | copy-start | bytes 12582916
  395.6 32.0 %copy-start.4 = (f32[512,256]{1,0:T(8,128)S(1)}, f32[512,256]{1,0:T(8,128)}, u32[]{:S(2)}) copy-start(f32[512,256]{1,0:T(8,128)} %all-reduce.6.cloned.1.call-done) | copy-start | bytes 1572868
  418.4 9.1 %copy-start.2 = (f32[2048,512]{1,0:T(8,128)S(1)}, f32[2048,512]{1,0:T(8,128)}, u32[]{:S(2)}) copy-start(f32[2048,512]{1,0:T(8,128)} %param.27) | copy-start | bytes 12582916
  419.6 17.4 %copy-start.5 = (f32[512,256]{1,0:T(8,128)}, f32[512,256]{1,0:T(8,128)S(1)}, u32[]{:S(2)}) copy-start(f32[512,256]{1,0:T(8,128)S(1)} %broadcast_multiply_fusion) | copy-start | bytes 1572868
Sparse Core Ops, SparseCore 0:
  29.7 103.9 all-reduce.3
  186.9 16.4 all-gather.2
  363.4 32.0 all-reduce.5
Sparse Core Ops, SparseCore 1:
  207.6 10.6 reduce-scatter.1
where the time goes:
time: 449 us; the launch traced here: 444 us
  other arithmetic  173 us (39%)
  waiting for transfers between devices  131 us (29%)
  matrix products  61.4 us (14%)
  blocking collectives  27.5 us (6%)
  between operations  20.4 us (5%)
  local copies, waits for them, and re-layouts  19.7 us (4%)
  starting transfers between devices  7.49 us (2%)
    another operation x18, other arithmetic, join(): return jnp.linalg.cholesky(summed).T  102 us
    psum x1, waiting for transfers between devices, on_device(): lax.psum(jnp.dot(total, basis, precision=highest), ('resp', 'head'))  95.1 us
    another operation x6, other arithmetic, on_device(): upper = combined_all(jnp.linalg.cholesky(gram).T, 'fsdp', join)  38.5 us
    psum x1, waiting for transfers between devices, on_device(): back = lax.psum(jnp.dot(total.T, ortho, precision=highest), 'fsdp')  30 us
    psum x1, blocking collectives, on_device(): squares = lax.psum(jnp.sum(back * back, axis=0), ('resp', 'head'))  21.6 us
    another operation x3, other arithmetic, on_device(): ortho = jax.scipy.linalg.solve_triangular(lower, projected.T, lower=True).T  21.2 us
    dot_general x1, matrix products, on_device(): jnp.dot(ortho, back.T, precision=highest)  9.55 us
    dot_general x1, matrix products, on_device(): back = lax.psum(jnp.dot(total.T, ortho, precision=highest), 'fsdp')  9.07 us
  transfers between devices with their start and end apart: 6, of which 3 were waited for; matrix products, arithmetic and copies ran while one was open for 40% of the time, Pallas kernels for 0%

commit v1 on v0

v1 whole, which is shorter than its diff:
```python
import functools
import math

import jax
import jax.numpy as jnp
from jax import lax
from jax.experimental import pallas as pl
from jax.experimental.pallas import tpu as pltpu
from jax.sharding import PartitionSpec as P

HD = 128
PANEL = 8
OUTER = 32
MIB = 1 << 20

momentum_keep = 0.95
norm_eps = 1e-06

F32 = jnp.float32
BF16 = jnp.bfloat16
HIGHEST = lax.Precision.HIGHEST

SMEM = pl.BlockSpec(memory_space=pltpu.SMEM)
VMEM = pl.BlockSpec(memory_space=pltpu.VMEM)


def swap(value, axes, k):
    axes = (axes,) if isinstance(axes, str) else axes
    n = math.prod(lax.axis_size(a) for a in axes)
    return lax.ppermute(value, axes, [(i, i ^ k) for i in range(n)])


def params(mib=24):
    return pltpu.CompilerParams(vmem_limit_bytes=mib * MIB)


def cost(flops, nbytes):
    return pl.CostEstimate(flops=int(flops), bytes_accessed=int(nbytes), transcendentals=0)


def halves(x):
    hi = x.astype(BF16)
    return hi, (x - hi.astype(F32)).astype(BF16)


def mm(a, b):
    return jnp.dot(a, b, preferred_element_type=F32)


def mm_full(a, b):
    return jnp.dot(a, b, precision=HIGHEST, preferred_element_type=F32)


def project_kernel(ranks, mom, grad, basis, out, b_hi, b_lo):
    @pl.when(pl.program_id(0) == 0)
    def _():
        hi, lo = halves(basis[...])
        b_hi[...] = hi
        b_lo[...] = lo

    t_hi, t_lo = halves(mom[...] + grad[...].astype(F32))
    acc = mm(t_hi, b_hi[...]) + (mm(t_hi, b_lo[...]) + mm(t_lo, b_hi[...]))
    out[...] = acc.astype(out.dtype)


def project(ranks, momentum, grad_q, basis, k, segments, dtype):
    rows, cols = momentum.shape
    rank = basis.shape[1]
    seg = rows // segments
    tile = min(seg, 256)
    nb = seg // tile

    def rows_at(i, ranks):
        return ((ranks[0] ^ k) * nb + i, 0)

    return pl.pallas_call(
        project_kernel,
        grid_spec=pltpu.PrefetchScalarGridSpec(
            num_scalar_prefetch=1,
            grid=(nb,),
            in_specs=[
                pl.BlockSpec((tile, cols), rows_at),
                pl.BlockSpec((tile, cols), rows_at),
                pl.BlockSpec((cols, rank), lambda i, ranks: (0, 0)),
            ],
            out_specs=pl.BlockSpec((tile, rank), lambda i, ranks: (i, 0)),
            scratch_shapes=[pltpu.VMEM((cols, rank), BF16)] * 2,
        ),
        out_shape=jax.ShapeDtypeStruct((seg, rank), dtype),
        compiler_params=params(),
        cost_estimate=cost(6 * seg * cols * rank, seg * cols * 6),
    )(ranks, momentum, grad_q, basis)


def split_kernel(n_recv, n_head, ranks, *refs):
    own, recvs, outs = refs[0], refs[1 : 1 + n_recv], refs[1 + n_recv :]
    chunk = outs[0].shape[0]
    for k in range(n_head):
        rows = pl.ds(pl.multiple_of((ranks[2] ^ k) * chunk, chunk), chunk)
        acc = own[rows, :]
        for r in recvs:
            acc = acc + r[rows, :].astype(F32)
        outs[k][...] = acc.astype(outs[k].dtype)


def split_sum(ranks, own, recvs, n_head):
    rows, rank = own.shape
    chunk = rows // n_head
    return pl.pallas_call(
        functools.partial(split_kernel, len(recvs), n_head),
        in_specs=[SMEM] + [VMEM] * (1 + len(recvs)),
        out_specs=[VMEM] * n_head,
        out_shape=[
            jax.ShapeDtypeStruct((chunk, rank), BF16 if k else F32) for k in range(n_head)
        ],
        compiler_params=params(),
        cost_estimate=cost(rows * rank, rows * rank * 8),
    )(ranks, own, *recvs)


def gram_kernel(n_resp, n_head, ranks, *refs):
    chunks, (pcat, gram) = refs[: n_resp * n_head], refs[n_resp * n_head :]
    size = chunks[0].shape[0]
    for j in range(n_resp):
        for k in range(n_head):
            at = (ranks[0] ^ j) * n_head + (ranks[2] ^ k)
            pcat[pl.ds(pl.multiple_of(at * size, size), size), :] = chunks[j * n_head + k][...]
    p = pcat[...]
    gram[...] = mm(p.T, p)


def gather_gram(ranks, chunks, n_resp, n_head):
    size, rank = chunks[0].shape
    rows = size * n_resp * n_head
    return pl.pallas_call(
        functools.partial(gram_kernel, n_resp, n_head),
        in_specs=[SMEM] + [VMEM] * len(chunks),
        out_specs=[VMEM] * 2,
        out_shape=[
            jax.ShapeDtypeStruct((rows, rank), BF16),
            jax.ShapeDtypeStruct((rank, rank), F32),
        ],
        compiler_params=params(),
        cost_estimate=cost(2 * rows * rank * rank, rows * rank * 4),
    )(ranks, *chunks)


def back_part_kernel(pcat, mom, grad, out, acc):
    i = pl.program_id(0)
    t_hi, t_lo = halves(mom[...] + grad[...].astype(F32))
    pt = pcat[...].T
    part = mm(pt, t_hi) + mm(pt, t_lo)

    @pl.when(i == 0)
    def _():
        acc[...] = part

    @pl.when(i > 0)
    def _():
        acc[...] += part

    @pl.when(i == pl.num_programs(0) - 1)
    def _():
        out[...] = acc[...].astype(BF16)


def back_part(pcat, momentum, grad_q):
    rows, cols = momentum.shape
    rank = pcat.shape[1]
    tile = min(rows, 512)
    return pl.pallas_call(
        back_part_kernel,
        grid=(rows // tile,),
        in_specs=[
            pl.BlockSpec((tile, rank), lambda i: (i, 0)),
            pl.BlockSpec((tile, cols), lambda i: (i, 0)),
            pl.BlockSpec((tile, cols), lambda i: (i, 0)),
        ],
        out_specs=pl.BlockSpec((rank, cols), lambda i: (0, 0)),
        scratch_shapes=[pltpu.VMEM((rank, cols), F32)],
        out_shape=jax.ShapeDtypeStruct((rank, cols), BF16),
        compiler_params=params(),
        cost_estimate=cost(4 * rows * cols * rank, rows * cols * 6),
    )(pcat, momentum, grad_q)


def factor_panel(panel, off):
    shape = (PANEL, 128)
    d = {}
    for j in range(PANEL):
        col = jnp.broadcast_to(panel[:, off + j : off + j + 1], shape)
        for i in range(j, PANEL):
            d[i, j] = jnp.broadcast_to(col[i : i + 1, :], shape)
    low, inv = {}, {}
    for j in range(PANEL):
        r = lax.rsqrt(d[j, j])
        inv[j, j] = r
        for i in range(j + 1, PANEL):
            low[i, j] = d[i, j] * r
        for k in range(j + 1, PANEL):
            for i in range(k, PANEL):
                d[i, k] = d[i, k] - low[i, j] * low[k, j]
    for j in range(PANEL):
        for i in range(j + 1, PANEL):
            acc = low[i, j] * inv[j, j]
            for k in range(j + 1, i):
                acc = acc + low[i, k] * inv[k, j]
            inv[i, j] = -(acc * inv[i, i])
    return inv


def three_parts(x):
    a = x.astype(BF16)
    rest = x - a.astype(F32)
    b = rest.astype(BF16)
    return a, b, (rest - b.astype(F32)).astype(BF16)


def cholesky_kernel(n_parts, *refs):
    parts, out, work = refs[:n_parts], refs[n_parts], refs[n_parts + 1]
    n = out.shape[0]
    wide = 2 * n
    tiles = wide // 128
    total = parts[0][...]
    for part in parts[1:]:
        total = total + part[...]
    work[:, :n] = total
    rows = lax.broadcasted_iota(jnp.int32, (n, n), 0)
    cols = lax.broadcasted_iota(jnp.int32, (n, n), 1)
    work[:, n:] = jnp.where(rows == cols, 1.0, 0.0).astype(F32)
    sub = lax.broadcasted_iota(jnp.int32, (PANEL, 128), 0)
    n_panels = OUTER // PANEL

    def step(o, carry):
        blk = [
            [work[p * PANEL : (p + 1) * PANEL, t * 128 : (t + 1) * 128] for t in range(tiles)]
            for p in range(n_panels)
        ]
        for p in range(n_panels):
            off = p * PANEL
            inv = factor_panel(blk[p][0], off)
            rows_of = [
                [jnp.broadcast_to(blk[p][t][j : j + 1, :], (PANEL, 128)) for t in range(tiles)]
                for j in range(PANEL)
            ]
            new = [None] * tiles
            for j in range(PANEL):
                col = inv[PANEL - 1, j]
                for i in range(PANEL - 2, j - 1, -1):
                    col = jnp.where(sub == i, inv[i, j], col)
                if j:
                    col = jnp.where(sub < j, 0.0, col)
                for t in range(tiles):
                    term = col * rows_of[j][t]
                    new[t] = term if new[t] is None else new[t] + term
            blk[p] = new
            if p + 1 < n_panels:
                u_rows = [
                    [jnp.broadcast_to(new[t][j : j + 1, :], (PANEL, 128)) for t in range(tiles)]
                    for j in range(PANEL)
                ]
                for b in range(p + 1, n_panels):
                    lanes = [
                        jnp.broadcast_to(blk[b][0][:, off + m : off + m + 1], (PANEL, 128))
                        for m in range(PANEL)
                    ]
                    upd = list(blk[b])
                    for k in range(PANEL):
                        v = lanes[0] * inv[k, 0]
                        for m in range(1, k + 1):
                            v = v + lanes[m] * inv[k, m]
                        for t in range(tiles):
                            upd[t] = upd[t] - v * u_rows[k][t]
                    blk[b] = upd
        u = jnp.concatenate([jnp.concatenate(row, axis=1) for row in blk], axis=0)
        lane = lax.broadcasted_iota(jnp.int32, (OUTER, n), 1)
        left = jnp.where(lane < n - OUTER * o, u[:, :n], 0.0)
        la, lb, lc = three_parts(left)
        ua, ub, uc = three_parts(u)
        lhs = jnp.concatenate([la, la, lb, la, lc, lb], axis=0)
        rhs = jnp.concatenate([ua, ub, ua, uc, ua, ub], axis=0)
        upd = mm(lhs.T, rhs)
        rest = work[OUTER:, :] - upd[OUTER:, :]
        work[: n - OUTER, :] = pltpu.roll(rest, wide - OUTER, 1)
        work[n - OUTER :, :] = pltpu.roll(u, wide - OUTER, 1)
        return carry

    lax.fori_loop(0, n // OUTER, step, 0)
    out[...] = work[:, :n]


def inverse_factor(*parts):
    n = parts[0].shape[0]
    return pl.pallas_call(
        functools.partial(cholesky_kernel, len(parts)),
        in_specs=[VMEM] * len(parts),
        out_specs=VMEM,
        scratch_shapes=[pltpu.VMEM((n, 2 * n), F32)],
        out_shape=jax.ShapeDtypeStruct((n, n), F32),
        compiler_params=params(),
        cost_estimate=cost(10_000_000_000, 4 * n * n * 4),
    )(*parts)


def back_kernel(x, wa, wb, bt_out, y_out, s_out):
    w = wa[...].astype(F32) + wb[...].astype(F32)
    bt = mm_full(x[...], w)
    bt_out[...] = bt
    y_out[...] = ((1.0 - momentum_keep) * mm_full(x[...].T, bt)).astype(BF16)
    ones = jnp.ones((8, bt.shape[1]), F32)
    s_out[...] = lax.dot_general(
        ones, bt * bt, (((1,), (1,)), ((), ())), precision=HIGHEST, preferred_element_type=F32
    )


def back_full(x, wa, wb):
    rank, cols = wa.shape
    return pl.pallas_call(
        back_kernel,
        in_specs=[VMEM] * 3,
        out_specs=[VMEM] * 3,
        out_shape=[
            jax.ShapeDtypeStruct((rank, cols), F32),
            jax.ShapeDtypeStruct((rank, cols), BF16),
            jax.ShapeDtypeStruct((8, rank), F32),
        ],
        compiler_params=params(),
        cost_estimate=cost(24 * rank * rank * cols, rank * cols * 12),
    )(x, wa, wb)


def momentum_kernel(pcat, mom, grad, y, out):
    out[...] = mom[...] + grad[...].astype(F32) - mm(pcat[...], y[...])


def new_momentum(pcat, momentum, grad_q, y):
    rows, cols = momentum.shape
    rank = pcat.shape[1]
    tile = min(rows, 256)
    return pl.pallas_call(
        momentum_kernel,
        grid=(rows // tile,),
        in_specs=[
            pl.BlockSpec((tile, rank), lambda i: (i, 0)),
            pl.BlockSpec((tile, cols), lambda i: (i, 0)),
            pl.BlockSpec((tile, cols), lambda i: (i, 0)),
            pl.BlockSpec((rank, cols), lambda i: (0, 0)),
        ],
        out_specs=pl.BlockSpec((tile, cols), lambda i: (i, 0)),
        out_shape=jax.ShapeDtypeStruct((rows, cols), F32),
        compiler_params=params(),
        cost_estimate=cost(2 * rows * cols * rank, rows * cols * 10),
    )(pcat, momentum, grad_q, y)


def update_kernel(n_sums, gain, pcat, x, bt, *refs):
    sums, (upd, basis_out, z_hi, z_lo) = refs[:n_sums], refs[n_sums:]

    @pl.when(pl.program_id(0) == 0)
    def _():
        total = sums[0][...]
        for s in sums[1:]:
            total = total + s[...]
        scale = lax.rsqrt(total + norm_eps).T[:, :1]
        scaled = bt[...] * scale
        basis_out[...] = scaled.T
        hi, lo = halves(gain * mm_full(x[...].T, scaled))
        z_hi[...] = hi
        z_lo[...] = lo

    p = pcat[...]
    upd[...] = (mm(p, z_hi[...]) + mm(p, z_lo[...])).astype(BF16)


def final_update(pcat, x, bt, sums, gain):
    rows, rank = pcat.shape
    cols = bt.shape[1]
    tile = min(rows, 512)
    whole = lambda i: (0, 0)
    return pl.pallas_call(
        functools.partial(update_kernel, len(sums), gain),
        grid=(rows // tile,),
        in_specs=[
            pl.BlockSpec((tile, rank), lambda i: (i, 0)),
            pl.BlockSpec((rank, rank), whole),
            pl.BlockSpec((rank, cols), whole),
        ]
        + [pl.BlockSpec((8, rank), whole)] * len(sums),
        out_specs=[
            pl.BlockSpec((tile, cols), lambda i: (i, 0)),
            pl.BlockSpec((cols, rank), whole),
        ],
        scratch_shapes=[pltpu.VMEM((rank, cols), BF16)] * 2,
        out_shape=[
            jax.ShapeDtypeStruct((rows, cols), BF16),
            jax.ShapeDtypeStruct((cols, rank), F32),
        ],
        compiler_params=params(),
        cost_estimate=cost(4 * rows * cols * rank, rows * cols * 3),
    )(pcat, x, bt, *sums)


def group_of(counts, response):
    group = jnp.int32(0)
    end = jnp.int32(0)
    for g in range(counts.shape[0]):
        end = end + counts[g]
        group = group + (end <= response).astype(jnp.int32)
    return group


def select_kernel(n_resp, n_fsdp, ranks, counts, slots, *refs):
    keys, values, outs = refs[:n_resp], refs[n_resp : 2 * n_resp], refs[2 * n_resp :]
    held = keys[0].shape[0]
    for k in range(n_fsdp):
        slot = slots[group_of(counts, ranks[0] * n_fsdp + (ranks[1] ^ k))]
        owner, local = slot // held, slot % held
        for a, arrays in enumerate((keys, values)):
            for j in range(n_resp):

                @pl.when(owner == (ranks[0] ^ j))
                def _():
                    outs[k][a] = arrays[j][local]


def select_prompts(ranks, counts, slots, keys, values, n_fsdp):
    _, piece, width = keys[0].shape
    return pl.pallas_call(
        functools.partial(select_kernel, len(keys), n_fsdp),
        in_specs=[SMEM] * 3 + [VMEM] * (2 * len(keys)),
        out_specs=[VMEM] * n_fsdp,
        out_shape=[jax.ShapeDtypeStruct((2, piece, width), BF16)] * n_fsdp,
        compiler_params=params(),
        cost_estimate=cost(1000, 8 * n_fsdp * piece * width),
    )(ranks, counts, slots, *keys, *values)


def attention_kernel(n_fsdp, ranks, counts, prompt_blocks, resp_blocks, q, sk, sv, go, *refs):
    pieces, refs = refs[:n_fsdp], refs[n_fsdp:]
    dq, own, refs = refs[0], refs[1], refs[2:]
    sends, (keys, values, dk, dv) = refs[:n_fsdp], refs[n_fsdp:]
    piece = pieces[0].shape[1]
    cap = piece * n_fsdp
    length = q.shape[0]
    scale = HD ** (-0.5)
    for k in range(n_fsdp):
        rows = pl.ds(pl.multiple_of((ranks[1] ^ k) * piece, piece), piece)
        keys[rows, :] = pieces[k][0]
        values[rows, :] = pieces[k][1]
    keys[cap:, :] = sk[...]
    values[cap:, :] = sv[...]
    prompt_len = prompt_blocks[group_of(counts, ranks[0] * n_fsdp + ranks[1])] * 128
    resp_len = resp_blocks[0] * 128
    width = keys.shape[0]
    place = lax.broadcasted_iota(jnp.int32, (width, length), 0)
    pos = lax.broadcasted_iota(jnp.int32, (width, length), 1)
    inner = place - cap
    seen = ((place < cap) & (place < prompt_len)) | (
        (place >= cap) & (inner <= pos) & (inner < resp_len)
    )
    bias = jnp.where(seen, 0.0, -jnp.inf).astype(F32)
    live = lax.broadcasted_iota(jnp.int32, (length, HD), 0) < resp_len
    nt = (((1,), (1,)), ((), ()))
    kall = keys[...]
    vall = values[...]
    kt = kall.T
    dk[...] = jnp.zeros_like(dk)
    dv[...] = jnp.zeros_like(dv)
    for h in range(q.shape[1] // HD):
        cols = slice(h * HD, (h + 1) * HD)
        qh = q[:, cols]
        gh = jnp.where(live, go[:, cols], jnp.zeros((), BF16))
        logits = lax.dot_general(kall, qh, nt, preferred_element_type=F32) * scale + bias
        peak = jnp.max(logits, axis=0, keepdims=True)
        e = jnp.exp(logits - peak)
        w = (e * (1.0 / jnp.sum(e, axis=0, keepdims=True))).astype(BF16)
        dp = lax.dot_general(vall, gh, nt, preferred_element_type=F32)
        wf = w.astype(F32)
        diag = jnp.sum(wf * dp, axis=0, keepdims=True)
        ds = (wf * (dp - diag)).astype(BF16)
        dk[...] += mm(ds, qh)
        dv[...] += mm(w, gh)
        dq[:, cols] = (mm(kt, ds) * scale).T.astype(BF16)
    own[0] = (dk[cap:, :] * scale).astype(BF16)
    own[1] = dv[cap:, :].astype(BF16)
    for k in range(n_fsdp):
        rows = pl.ds(pl.multiple_of((ranks[1] ^ k) * piece, piece), piece)
        sends[k][0] = dk[rows, :] * scale
        sends[k][1] = dv[rows, :]


def attention(ranks, counts, prompt_blocks, resp_blocks, q, sk, sv, go, pieces):
    n_fsdp = len(pieces)
    piece = pieces[0].shape[1]
    length, width = q.shape
    total = piece * n_fsdp + length
    return pl.pallas_call(
        functools.partial(attention_kernel, n_fsdp),
        in_specs=[SMEM] * 4 + [VMEM] * (4 + n_fsdp),
        out_specs=[VMEM] * (2 + n_fsdp),
        out_shape=[
            jax.ShapeDtypeStruct((length, width), BF16),
            jax.ShapeDtypeStruct((2, length, HD), BF16),
        ]
        + [jax.ShapeDtypeStruct((2, piece, HD), F32)] * n_fsdp,
        scratch_shapes=[pltpu.VMEM((total, HD), BF16)] * 2 + [pltpu.VMEM((total, HD), F32)] * 2,
        compiler_params=params(32),
        cost_estimate=cost(6_000_000_000, length * width * 8),
    )(ranks, counts, prompt_blocks, resp_blocks, q, sk, sv, go, *pieces)


def by_slot_kernel(n_resp, n_fsdp, ranks, counts, slots, *refs):
    parts, outs = refs[:n_fsdp], refs[n_fsdp:]
    held = outs[0].shape[1]
    slot_of = [
        slots[group_of(counts, ranks[0] * n_fsdp + (ranks[1] ^ k))] for k in range(n_fsdp)
    ]
    for j in range(n_resp):
        for local in range(held):
            slot = (ranks[0] ^ j) * held + local
            acc = jnp.zeros(parts[0].shape, F32)
            for k in range(n_fsdp):
                acc = acc + jnp.where(slot_of[k] == slot, parts[k][...], 0.0)
            outs[j][:, local] = acc


def sum_by_slot(ranks, counts, slots, parts, n_resp):
    held = counts.shape[0] // n_resp
    _, piece, width = parts[0].shape
    return pl.pallas_call(
        functools.partial(by_slot_kernel, n_resp, len(parts)),
        in_specs=[SMEM] * 3 + [VMEM] * len(parts),
        out_specs=[VMEM] * n_resp,
        out_shape=[jax.ShapeDtypeStruct((2, held, piece, width), F32)] * n_resp,
        compiler_params=params(),
        cost_estimate=cost(1000, 8 * len(parts) * piece * width * 4),
    )(ranks, counts, slots, *parts)


def on_device(
    queries,
    self_keys,
    self_values,
    d_out,
    prompt_keys,
    prompt_values,
    counts,
    owner_slot,
    prompt_blocks,
    resp_blocks,
    grad_q,
    momentum,
    basis,
):
    n_resp, n_fsdp, n_head = (lax.axis_size(a) for a in ("resp", "fsdp", "head"))
    ranks = jnp.stack([lax.axis_index(a) for a in ("resp", "fsdp", "head")]).astype(jnp.int32)
    gain = math.sqrt(
        momentum.shape[0] * n_fsdp * momentum.shape[1] * n_resp * n_head / basis.shape[1]
    )

    keys = [prompt_keys] + [swap(prompt_keys, "resp", j) for j in range(1, n_resp)]
    values = [prompt_values] + [swap(prompt_values, "resp", j) for j in range(1, n_resp)]

    sent = [project(ranks, momentum, grad_q, basis, j, n_resp, BF16) for j in range(1, n_resp)]
    recvs = [swap(s, "resp", j + 1) for j, s in enumerate(sent)]
    mine = project(ranks, momentum, grad_q, basis, 0, n_resp, F32)

    chosen = select_prompts(ranks, counts, owner_slot, keys, values, n_fsdp)
    pieces = [chosen[0]] + [swap(chosen[k], "fsdp", k) for k in range(1, n_fsdp)]

    split = split_sum(ranks, mine, recvs, n_head)
    acc = split[0]
    for part in [swap(split[k], "head", k) for k in range(1, n_head)]:
        acc = acc + part.astype(F32)
    piece0 = acc.astype(BF16)

    attended = attention(
        ranks, counts, prompt_blocks, resp_blocks, queries, self_keys, self_values, d_out, pieces
    )
    dq, resp_grad, parts = attended[0], attended[1], attended[2:]

    along = [piece0] + [swap(piece0, "head", k) for k in range(1, n_head)]
    chunks = list(along)
    for j in range(1, n_resp):
        chunks += [swap(c, "resp", j) for c in along]
    pcat, gram = gather_gram(ranks, chunks, n_resp, n_head)

    returned = [parts[0]] + [swap(parts[k], "fsdp", k) for k in range(1, n_fsdp)]
    slots = sum_by_slot(ranks, counts, owner_slot, returned, n_resp)
    prompt_grad = slots[0]
    for j in range(1, n_resp):
        prompt_grad = prompt_grad + swap(slots[j], "resp", j)

    bits = [1 << b for b in range(n_fsdp.bit_length() - 1)]
    for bit in bits[:-1]:
        gram = gram + swap(gram, "fsdp", bit)
    gram_parts = (gram, swap(gram, "fsdp", bits[-1]))
    w = back_part(pcat, momentum, grad_q)
    for bit in bits[:-1]:
        w = (w.astype(F32) + swap(w, "fsdp", bit).astype(F32)).astype(BF16)
    w_other = swap(w, "fsdp", bits[-1])

    x = inverse_factor(*gram_parts)
    bt, y, squares = back_full(x, w, w_other)
    sums = [squares] + [
        swap(squares, ("resp", "head"), k) for k in range(1, n_resp * n_head)
    ]
    momentum_out = new_momentum(pcat, momentum, grad_q, y)
    update, basis_out = final_update(pcat, x, bt, sums, gain)
    return (dq, resp_grad, prompt_grad, update, momentum_out, basis_out)


def solution(mesh):
    placed = (
        P(("resp", "fsdp"), "head"),
        P(("resp", "fsdp"), "head"),
        P(("resp", "fsdp"), "head"),
        P(("resp", "fsdp"), "head"),
        P("resp", "fsdp", "head"),
        P("resp", "fsdp", "head"),
        P(),
        P(),
        P(),
        P(("resp", "fsdp")),
        P("fsdp", ("resp", "head")),
        P("fsdp", ("resp", "head")),
        P(("resp", "head"), None),
    )
    return jax.shard_map(
        on_device,
        mesh=mesh,
        in_specs=placed,
        out_specs=(
            P(("resp", "fsdp"), "head"),
            P(None, ("resp", "fsdp"), "head"),
            P(None, "resp", "fsdp", "head"),
            P("fsdp", ("resp", "head")),
            P("fsdp", ("resp", "head")),
            P(("resp", "head"), None),
        ),
        check_vma=False,
    )
```

time: 449 us -> 120 us (0.27); the launches traced: 444 us -> 120 us
  other arithmetic: 173 us -> 0.92 us
  waiting for transfers between devices: 131 us -> 36.3 us
  matrix products: 61.4 us -> 0 us
  Pallas kernels: 0 us -> 37.2 us
  starting transfers between devices: 7.49 us -> 39.2 us
  blocking collectives: 27.5 us -> 0 us
  between operations: 20.4 us -> 1.56 us
  local copies, waits for them, and re-layouts: 19.7 us -> 4.88 us
    another operation x31 -> x1, other arithmetic: 165 us -> 0.08 us  [on_device(): jnp.stack([lax.axis_index(a) for a in ('resp', 'fsdp', 'head')])]
    psum x2 -> x0, waiting for transfers between devices: 125 us -> none  [the longest x1 95.1 us: on_device(): lax.psum(jnp.dot(total, basis, precision=highest), ('resp', 'head'))]
    dot_general x18 -> x0, matrix products: 50.6 us -> none  [the longest x1 9.55 us: on_device(): jnp.dot(ortho, back.T, precision=highest)]
    ppermute x0 -> x31, starting transfers between devices: none -> 39.2 us  [swap(): return lax.ppermute(value, axes, [(i, i ^ k) for i in range(n)])]
    pallas_call x0 -> x12, Pallas kernels: none -> 37.2 us  [the longest x1 10.8 us: inverse_factor(): pl.pallas_call(functools.partial(cholesky_kernel, len(parts)), in_specs=[...]
    ppermute x0 -> x31, waiting for transfers between devices: none -> 36.3 us  [swap(): return lax.ppermute(value, axes, [(i, i ^ k) for i in range(n)])]
    psum x1 -> x0, blocking collectives: 21.6 us -> none  [on_device(): squares = lax.psum(jnp.sum(back * back, axis=0), ('resp', 'head'))]
    another operation x11 -> x0, matrix products: 10.8 us -> none  [the longest x3 6.54 us: on_device(): ortho = jax.scipy.linalg.solve_triangular(lower, projected.T, lower=True).T]
  transfers between devices with their start and end apart: 6 -> 31, of which waited for: 3 -> 11; matrix products, arithmetic and copies ran while one was open for 40% -> 1% of each run, Pallas kernels for 0% -> 25%
where the time goes in v1:
time: 120 us
  starting transfers between devices  39.2 us (33%)
  Pallas kernels  37.2 us (31%)
  waiting for transfers between devices  36.3 us (30%)
  local copies, waits for them, and re-layouts  4.88 us (4%)
  between operations  1.56 us (1%)
    ppermute x31, starting transfers between devices, swap(): return lax.ppermute(value, axes, [(i, i ^ k) for i in range(n)])  39.2 us
    ppermute x31, waiting for transfers between devices, swap(): return lax.ppermute(value, axes, [(i, i ^ k) for i in range(n)])  36.3 us
    pallas_call x1, Pallas kernels, inverse_factor(): pl.pallas_call(functools.partial(cholesky_kernel, len(parts)), in_specs=[...  10.8 us
    pallas_call x1, Pallas kernels, attention(): pl.pallas_call(functools.partial(attention_kernel, n_fsdp), in_specs=[SME...  6.5 us
    unnamed x28, local copies, waits for them, and re-layouts  4.88 us
    pallas_call x2, Pallas kernels, project(): pl.pallas_call(project_kernel, grid_spec=pltpu.PrefetchScalarGridSpec(num...  4.51 us
    pallas_call x1, Pallas kernels, new_momentum(): pl.pallas_call(momentum_kernel, grid=(rows // tile,), in_specs=[pl.BlockS...  4.32 us
    pallas_call x1, Pallas kernels, final_update(): pl.pallas_call(functools.partial(update_kernel, len(sums), gain), grid=(r...  3.81 us
  transfers between devices with their start and end apart: 31, of which 11 were waited for; matrix products, arithmetic and copies ran while one was open for 1% of the time, Pallas kernels for 25%

profile of v1, /device:TPU:0, one launch (start us, length us, event | category | flops | bytes accessed | tf_op | source)
XLA Modules:
  0.0 120.1 jit_solution(5196625980281813752)
XLA Ops:
  0.7 2.2 %copy-done = f32[2048,512]{1,0:T(8,128)S(1)} copy-done((f32[2048,512]{1,0:T(8,128)S(1)}, f32[2048,512]{1,0:T(8,128)}, u32[]{:S(2)}) %copy-start) | copy-done | bytes 4194328
  5.5 2.3 %shard_map.176 = bf16[1024,256]{1,0:T(8,128)(2,1)S(1)} custom-call(s32[3]{0:T(128)S(1)} %pad_add_fusion.ranks, f32[2048,512]{1,0:T(8,128)S(1)} %copy-done, bf16[2048,512]{1,0:T(8,128)(2,1)S(1)} %copy-done.2, f32[512,256]{1,0:T(8,128)S(1)} %copy-done.4), custom_call_target="tpu_custom_call" | custom-call | flops 805306368 | bytes 3145728 | tf_op jit(solution)/shard_map/pallas_call | solution.py:76
  7.9 3.0 %collective-permute-start.9 = (bf16[1024,256]{1,0:T(8,128)(2,1)S(1)}, bf16[1024,256]{1,0:T(8,128)(2,1)S(1)}, u32[]{:S(2)}, u32[]{:S(2)}) collective-permute-start(bf16[1024,256]{1,0:T(8,128)(2,1)S(1)} %shard_map.176), channel_id=1, source_target_pairs={{0,16},{16,0},{1,17},{17,1},{2,18},{18,2},{3,19},{19,3},{4,20},{20... | collective-permute-start | bytes 1572872 | tf_op jit(solution)/shard_map/ppermute | solution.py:30
  10.9 2.3 %shard_map.175.refs_0_ = f32[1024,256]{1,0:T(8,128)S(1)} custom-call(s32[3]{0:T(128)S(1)} %pad_add_fusion.ranks, f32[2048,512]{1,0:T(8,128)S(1)} %copy-done, bf16[2048,512]{1,0:T(8,128)(2,1)S(1)} %copy-done.2, f32[512,256]{1,0:T(8,128)S(1)} %copy-done.4), custom_call_target="tpu_custom_call" | custom-call | flops 805306368 | bytes 3145728 | tf_op jit(solution)/shard_map/pallas_call | solution.py:76
  13.1 9.7 %collective-permute-done.9.refs_1_ = bf16[1024,256]{1,0:T(8,128)(2,1)S(1)} collective-permute-done((bf16[1024,256]{1,0:T(8,128)(2,1)S(1)}, bf16[1024,256]{1,0:T(8,128)(2,1)S(1)}, u32[]{:S(2)}, u32[]{:S(2)}) %collective-permute-start.9) | collective-permute-done | bytes 524320 | tf_op jit(solution)/shard_map/ppermute | solution.py:30
  23.4 1.9 %collective-permute-start.10 = (bf16[256,256]{1,0:T(8,128)(2,1)S(1)}, bf16[256,256]{1,0:T(8,128)(2,1)S(1)}, u32[]{:S(2)}, u32[]{:S(2)}) collective-permute-start(bf16[256,256]{1,0:T(8,128)(2,1)S(1)} %get-tuple-element.42), channel_id=1, source_target_pairs={{0,1},{1,0},{2,3},{3,2},{4,5},{5,4},{6,7},{7,6},{8,9},{9,8},{10,11... | collective-permute-start | bytes 393224 | tf_op jit(solution)/shard_map/ppermute | solution.py:30
  25.3 2.6 %collective-permute-start.11 = (bf16[256,256]{1,0:T(8,128)(2,1)S(1)}, bf16[256,256]{1,0:T(8,128)(2,1)S(1)}, u32[]{:S(2)}, u32[]{:S(2)}) collective-permute-start(bf16[256,256]{1,0:T(8,128)(2,1)S(1)} %get-tuple-element.43), channel_id=1, source_target_pairs={{0,2},{1,3},{2,0},{3,1},{4,6},{5,7},{6,4},{7,5},{8,10},{9,11},{10,... | collective-permute-start | bytes 393224 | tf_op jit(solution)/shard_map/ppermute | solution.py:30
  27.9 1.9 %collective-permute-done.10 = bf16[256,256]{1,0:T(8,128)(2,1)S(1)} collective-permute-done((bf16[256,256]{1,0:T(8,128)(2,1)S(1)}, bf16[256,256]{1,0:T(8,128)(2,1)S(1)}, u32[]{:S(2)}, u32[]{:S(2)}) %collective-permute-start.10) | collective-permute-done | bytes 131104 | tf_op jit(solution)/shard_map/ppermute | solution.py:30
  29.9 7.5 %collective-permute-done.11 = bf16[256,256]{1,0:T(8,128)(2,1)S(1)} collective-permute-done((bf16[256,256]{1,0:T(8,128)(2,1)S(1)}, bf16[256,256]{1,0:T(8,128)(2,1)S(1)}, u32[]{:S(2)}, u32[]{:S(2)}) %collective-permute-start.11) | collective-permute-done | bytes 131104 | tf_op jit(solution)/shard_map/ppermute | solution.py:30
  37.5 2.0 %collective-permute-start.13 = (bf16[256,256]{1,0:T(8,128)(2,1)S(1)}, bf16[256,256]{1,0:T(8,128)(2,1)S(1)}, u32[]{:S(2)}, u32[]{:S(2)}) collective-permute-start(bf16[256,256]{1,0:T(8,128)(2,1)S(1)} %add_convert_fusion.1.refs_0_), channel_id=1, source_target_pairs={{0,1},{1,0},{2,3},{3,2},{4,5},{5,4},{6,7},{7,6},{8,9},{9,8},{10,11... | collective-permute-start | bytes 393224 | tf_op jit(solution)/shard_map/ppermute | solution.py:30
  45.1 5.7 %collective-permute-done.14.refs_2_ = bf16[256,256]{1,0:T(8,128)(2,1)S(1)} collective-permute-done((bf16[256,256]{1,0:T(8,128)(2,1)S(1)}, bf16[256,256]{1,0:T(8,128)(2,1)S(1)}, u32[]{:S(2)}, u32[]{:S(2)}) %collective-permute-start.14) | collective-permute-done | bytes 131104 | tf_op jit(solution)/shard_map/ppermute | solution.py:30
  54.3 3.3 %collective-permute-done.refs_1_ = bf16[2,64,128]{2,1,0:T(8,128)(2,1)S(1)} collective-permute-done((bf16[2,64,128]{2,1,0:T(8,128)(2,1)S(1)}, bf16[2,64,128]{2,1,0:T(8,128)(2,1)S(1)}, u32[]{:S(2)}, u32[]{:S(2)}) %collective-permute-start) | collective-permute-done | bytes 32800 | tf_op jit(solution)/shard_map/ppermute | solution.py:30
  59.7 1.9 %collective-permute-done.1.refs_3_ = bf16[2,64,128]{2,1,0:T(8,128)(2,1)S(1)} collective-permute-done((bf16[2,64,128]{2,1,0:T(8,128)(2,1)S(1)}, bf16[2,64,128]{2,1,0:T(8,128)(2,1)S(1)}, u32[]{:S(2)}, u32[]{:S(2)}) %collective-permute-start.1) | collective-permute-done | bytes 32800 | tf_op jit(solution)/shard_map/ppermute | solution.py:30
  62.4 1.6 %collective-permute-start.3 = (bf16[2,64,128]{2,1,0:T(8,128)(2,1)S(1)}, bf16[2,64,128]{2,1,0:T(8,128)(2,1)S(1)}, u32[]{:S(2)}, u32[]{:S(2)}) collective-permute-start(bf16[2,64,128]{2,1,0:T(8,128)(2,1)S(1)} %get-tuple-element.31), channel_id=1, source_target_pairs={{0,8},{4,12},{8,0},{12,4},{1,9},{5,13},{9,1},{13,5},{2,10},{6,14},... | collective-permute-start | bytes 98312 | tf_op jit(solution)/shard_map/ppermute | solution.py:30
  65.5 2.4 %shard_map.180 = bf16[256,512]{1,0:T(8,128)(2,1)S(1)} custom-call(bf16[2048,256]{1,0:T(8,128)(2,1)S(1)} %get-tuple-element.45.pcat, f32[2048,512]{1,0:T(8,128)S(1)} %copy-done.1, bf16[2048,512]{1,0:T(8,128)(2,1)S(1)} %copy-done.3), custom_call_target="tpu_custom_call" | custom-call | flops 1073741824 | bytes 6291456 | tf_op jit(solution)/shard_map/pallas_call | solution.py:171
  68.5 6.5 %shard_map.173 = (bf16[256,1024]{1,0:T(8,128)(2,1)}, bf16[2,256,128]{2,1,0:T(8,128)(2,1)}, f32[2,64,128]{2,1,0:T(8,128)S(1)}, f32[2,64,128]{2,1,0:T(8,128)S(1)},...) custom-call(s32[3]{0:T(128)S(1)} %pad_add_fusion.ranks, s32[4]{0:T(128)S(1)} %copy-done.7, s32[4]{0:T(128)S(1)} %copy-done.13, ...), custom_call_target="tpu_custom_call" | custom-call | flops 6000000000 | bytes 2097152 | tf_op jit(solution)/shard_map/pallas_call | solution.py:497
  79.7 1.6 %collective-permute-done.7.refs_3_ = f32[2,64,128]{2,1,0:T(8,128)S(1)} collective-permute-done((f32[2,64,128]{2,1,0:T(8,128)S(1)}, f32[2,64,128]{2,1,0:T(8,128)S(1)}, u32[]{:S(2)}, u32[]{:S(2)}) %collective-permute-start.7) | collective-permute-done | bytes 65568 | tf_op jit(solution)/shard_map/ppermute | solution.py:30
  84.1 2.9 %collective-permute-done.21.refs_1_ = f32[256,256]{1,0:T(8,128)S(1)} collective-permute-done((f32[256,256]{1,0:T(8,128)S(1)}, f32[256,256]{1,0:T(8,128)S(1)}, u32[]{:S(2)}, u32[]{:S(2)}) %collective-permute-start.21) | collective-permute-done | bytes 262176 | tf_op jit(solution)/shard_map/ppermute | solution.py:30
  87.0 10.8 %shard_map.179.x = f32[256,256]{1,0:T(8,128)S(1)} custom-call(f32[256,256]{1,0:T(8,128)S(1)} %add.22.refs_0_, f32[256,256]{1,0:T(8,128)S(1)} %collective-permute-done.21.refs_1_), custom_call_target="tpu_custom_call" | custom-call | flops 10000000000 | bytes 1048576 | tf_op jit(solution)/shard_map/pallas_call | solution.py:294
  97.8 1.8 %shard_map.181 = (f32[256,512]{1,0:T(8,128)S(1)}, bf16[256,512]{1,0:T(8,128)(2,1)S(1)}, f32[8,256]{1,0:T(8,128)S(1)}) custom-call(f32[256,256]{1,0:T(8,128)S(1)} %shard_map.179.x, bf16[256,512]{1,0:T(8,128)(2,1)S(1)} %add_convert_fusion.wa, bf16[256,512]{1,0:T(8,128)(2,1)S(1)} %collective-permute-done.23.wb), custom_call_target="tpu_custom_call" | custom-call | flops 805306368 | bytes 1572864 | tf_op jit(solution)/shard_map/pallas_call | solution.py:318
  100.6 1.9 %collective-permute-start.25 = (f32[8,256]{1,0:T(8,128)S(1)}, f32[8,256]{1,0:T(8,128)S(1)}, u32[]{:S(2)}, u32[]{:S(2)}) collective-permute-start(f32[8,256]{1,0:T(8,128)S(1)} %get-tuple-element.48.refs_0_), channel_id=1, source_target_pairs={{0,2},{1,3},{2,0},{3,1},{16,18},{17,19},{18,16},{19,17},{4,6},{5,7... | collective-permute-start | bytes 24584 | tf_op jit(solution)/shard_map/ppermute | solution.py:30
  106.2 3.7 %collective-permute-start.29 = (f32[8,256]{1,0:T(8,128)S(1)}, f32[8,256]{1,0:T(8,128)S(1)}, u32[]{:S(2)}, u32[]{:S(2)}) collective-permute-start(f32[8,256]{1,0:T(8,128)S(1)} %get-tuple-element.48.refs_0_), channel_id=1, source_target_pairs={{0,18},{1,19},{2,16},{3,17},{16,2},{17,3},{18,0},{19,1},{4,22},{5,... | collective-permute-start | bytes 24584 | tf_op jit(solution)/shard_map/ppermute | solution.py:30
  111.5 4.3 %shard_map.183 = f32[2048,512]{1,0:T(8,128)} custom-call(bf16[2048,256]{1,0:T(8,128)(2,1)S(1)} %get-tuple-element.45.pcat, f32[2048,512]{1,0:T(8,128)S(1)} %copy-done.1, bf16[2048,512]{1,0:T(8,128)(2,1)S(1)} %copy-done.3, bf16[256,512]{1,0:T(8,128)(2,1)S(1)} %get-tuple-element.50.y), custom_call_target="tpu_custom_call" | custom-call | flops 536870912 | bytes 10485760 | tf_op jit(solution)/shard_map/pallas_call | solution.py:340
  116.3 3.8 %shard_map.182 = (bf16[2048,512]{1,0:T(8,128)(2,1)}, f32[512,256]{1,0:T(8,128)}) custom-call(bf16[2048,256]{1,0:T(8,128)(2,1)S(1)} %get-tuple-element.45.pcat, f32[256,256]{1,0:T(8,128)S(1)} %shard_map.179.x, f32[256,512]{1,0:T(8,128)S(1)} %get-tuple-element.47.bt, f32[8,256]{1,0:T(8,128)S(1)} %get-tuple-element.48.refs_0_, ...), custom_call_target="tpu_custom_call" | custom-call | flops 1073741824 | bytes 3145728 | tf_op jit(solution)/shard_map/pallas_call | solution.py:380
  (83 shorter events, 31.0 us)
Async XLA Ops:
  7.9 14.9 %collective-permute-start.9 = (bf16[1024,256]{1,0:T(8,128)(2,1)S(1)}, bf16[1024,256]{1,0:T(8,128)(2,1)S(1)}, u32[]{:S(2)}, u32[]{:S(2)}) collective-permute-start(bf16[1024,256]{1,0:T(8,128)(2,1)S(1)} %shard_map.176), channel_id=1, source_target_pairs={{0,16},{16,0},{1,17},{17,1},{2,18},{18,2},{3,19},{19,3},{4,20},{20... | collective-permute-start | bytes 1572872 | tf_op jit(solution)/shard_map/ppermute | solution.py:30
  23.4 6.4 %collective-permute-start.10 = (bf16[256,256]{1,0:T(8,128)(2,1)S(1)}, bf16[256,256]{1,0:T(8,128)(2,1)S(1)}, u32[]{:S(2)}, u32[]{:S(2)}) collective-permute-start(bf16[256,256]{1,0:T(8,128)(2,1)S(1)} %get-tuple-element.42), channel_id=1, source_target_pairs={{0,1},{1,0},{2,3},{3,2},{4,5},{5,4},{6,7},{7,6},{8,9},{9,8},{10,11... | collective-permute-start | bytes 393224 | tf_op jit(solution)/shard_map/ppermute | solution.py:30
  25.3 12.1 %collective-permute-start.11 = (bf16[256,256]{1,0:T(8,128)(2,1)S(1)}, bf16[256,256]{1,0:T(8,128)(2,1)S(1)}, u32[]{:S(2)}, u32[]{:S(2)}) collective-permute-start(bf16[256,256]{1,0:T(8,128)(2,1)S(1)} %get-tuple-element.43), channel_id=1, source_target_pairs={{0,2},{1,3},{2,0},{3,1},{4,6},{5,7},{6,4},{7,5},{8,10},{9,11},{10,... | collective-permute-start | bytes 393224 | tf_op jit(solution)/shard_map/ppermute | solution.py:30
  27.9 9.5 %collective-permute-start.12 = (bf16[256,256]{1,0:T(8,128)(2,1)S(1)}, bf16[256,256]{1,0:T(8,128)(2,1)S(1)}, u32[]{:S(2)}, u32[]{:S(2)}) collective-permute-start(bf16[256,256]{1,0:T(8,128)(2,1)S(1)} %get-tuple-element.44), channel_id=1, source_target_pairs={{0,3},{1,2},{2,1},{3,0},{4,7},{5,6},{6,5},{7,4},{8,11},{9,10},{10,... | collective-permute-start | bytes 393224 | tf_op jit(solution)/shard_map/ppermute | solution.py:30
  37.5 6.1 %collective-permute-start.13 = (bf16[256,256]{1,0:T(8,128)(2,1)S(1)}, bf16[256,256]{1,0:T(8,128)(2,1)S(1)}, u32[]{:S(2)}, u32[]{:S(2)}) collective-permute-start(bf16[256,256]{1,0:T(8,128)(2,1)S(1)} %add_convert_fusion.1.refs_0_), channel_id=1, source_target_pairs={{0,1},{1,0},{2,3},{3,2},{4,5},{5,4},{6,7},{7,6},{8,9},{9,8},{10,11... | collective-permute-start | bytes 393224 | tf_op jit(solution)/shard_map/ppermute | solution.py:30
  39.5 11.3 %collective-permute-start.14 = (bf16[256,256]{1,0:T(8,128)(2,1)S(1)}, bf16[256,256]{1,0:T(8,128)(2,1)S(1)}, u32[]{:S(2)}, u32[]{:S(2)}) collective-permute-start(bf16[256,256]{1,0:T(8,128)(2,1)S(1)} %add_convert_fusion.1.refs_0_), channel_id=1, source_target_pairs={{0,2},{1,3},{2,0},{3,1},{4,6},{5,7},{6,4},{7,5},{8,10},{9,11},{10,... | collective-permute-start | bytes 393224 | tf_op jit(solution)/shard_map/ppermute | solution.py:30
  40.6 11.7 %collective-permute-start.15 = (bf16[256,256]{1,0:T(8,128)(2,1)S(1)}, bf16[256,256]{1,0:T(8,128)(2,1)S(1)}, u32[]{:S(2)}, u32[]{:S(2)}) collective-permute-start(bf16[256,256]{1,0:T(8,128)(2,1)S(1)} %add_convert_fusion.1.refs_0_), channel_id=1, source_target_pairs={{0,3},{1,2},{2,1},{3,0},{4,7},{5,6},{6,5},{7,4},{8,11},{9,10},{10,... | collective-permute-start | bytes 393224 | tf_op jit(solution)/shard_map/ppermute | solution.py:30
  42.0 20.4 %collective-permute-start.16 = (bf16[256,256]{1,0:T(8,128)(2,1)S(1)}, bf16[256,256]{1,0:T(8,128)(2,1)S(1)}, u32[]{:S(2)}, u32[]{:S(2)}) collective-permute-start(bf16[256,256]{1,0:T(8,128)(2,1)S(1)} %add_convert_fusion.1.refs_0_), channel_id=1, source_target_pairs={{0,16},{16,0},{1,17},{17,1},{2,18},{18,2},{3,19},{19,3},{4,20},{20... | collective-permute-start | bytes 393224 | tf_op jit(solution)/shard_map/ppermute | solution.py:30
  43.6 20.4 %collective-permute-start.17 = (bf16[256,256]{1,0:T(8,128)(2,1)S(1)}, bf16[256,256]{1,0:T(8,128)(2,1)S(1)}, u32[]{:S(2)}, u32[]{:S(2)}) collective-permute-start(bf16[256,256]{1,0:T(8,128)(2,1)S(1)} %collective-permute-done.13.refs_1_), channel_id=1, source_target_pairs={{0,16},{16,0},{1,17},{17,1},{2,18},{18,2},{3,19},{19,3},{4,20},{20... | collective-permute-start | bytes 393224 | tf_op jit(solution)/shard_map/ppermute | solution.py:30
  50.8 13.6 %collective-permute-start.18 = (bf16[256,256]{1,0:T(8,128)(2,1)S(1)}, bf16[256,256]{1,0:T(8,128)(2,1)S(1)}, u32[]{:S(2)}, u32[]{:S(2)}) collective-permute-start(bf16[256,256]{1,0:T(8,128)(2,1)S(1)} %collective-permute-done.14.refs_2_), channel_id=1, source_target_pairs={{0,16},{16,0},{1,17},{17,1},{2,18},{18,2},{3,19},{19,3},{4,20},{20... | collective-permute-start | bytes 393224 | tf_op jit(solution)/shard_map/ppermute | solution.py:30
  52.3 12.1 %collective-permute-start.19 = (bf16[256,256]{1,0:T(8,128)(2,1)S(1)}, bf16[256,256]{1,0:T(8,128)(2,1)S(1)}, u32[]{:S(2)}, u32[]{:S(2)}) collective-permute-start(bf16[256,256]{1,0:T(8,128)(2,1)S(1)} %collective-permute-done.15.refs_3_), channel_id=1, source_target_pairs={{0,16},{16,0},{1,17},{17,1},{2,18},{18,2},{3,19},{19,3},{4,20},{20... | collective-permute-start | bytes 393224 | tf_op jit(solution)/shard_map/ppermute | solution.py:30
  62.3 6.2 %collective-permute-start.2 = (bf16[2,64,128]{2,1,0:T(8,128)(2,1)S(1)}, bf16[2,64,128]{2,1,0:T(8,128)(2,1)S(1)}, u32[]{:S(2)}, u32[]{:S(2)}) collective-permute-start(bf16[2,64,128]{2,1,0:T(8,128)(2,1)S(1)} %get-tuple-element.30), channel_id=1, source_target_pairs={{0,4},{4,0},{8,12},{12,8},{1,5},{5,1},{9,13},{13,9},{2,6},{6,2},{1... | collective-permute-start | bytes 98312 | tf_op jit(solution)/shard_map/ppermute | solution.py:30
  67.9 15.5 %collective-permute-start.22 = (bf16[256,512]{1,0:T(8,128)(2,1)S(1)}, bf16[256,512]{1,0:T(8,128)(2,1)S(1)}, u32[]{:S(2)}, u32[]{:S(2)}) collective-permute-start(bf16[256,512]{1,0:T(8,128)(2,1)S(1)} %shard_map.180), channel_id=1, source_target_pairs={{0,4},{4,0},{8,12},{12,8},{1,5},{5,1},{9,13},{13,9},{2,6},{6,2},{1... | collective-permute-start | bytes 786440 | tf_op jit(solution)/shard_map/ppermute | solution.py:30
  68.3 8.6 %collective-permute-start.20 = (f32[256,256]{1,0:T(8,128)S(1)}, f32[256,256]{1,0:T(8,128)S(1)}, u32[]{:S(2)}, u32[]{:S(2)}) collective-permute-start(f32[256,256]{1,0:T(8,128)S(1)} %get-tuple-element.46), channel_id=1, source_target_pairs={{0,4},{4,0},{8,12},{12,8},{1,5},{5,1},{9,13},{13,9},{2,6},{6,2},{1... | collective-permute-start | bytes 786440 | tf_op jit(solution)/shard_map/ppermute | solution.py:30
  77.0 10.0 %collective-permute-start.21 = (f32[256,256]{1,0:T(8,128)S(1)}, f32[256,256]{1,0:T(8,128)S(1)}, u32[]{:S(2)}, u32[]{:S(2)}) collective-permute-start(f32[256,256]{1,0:T(8,128)S(1)} %add.22.refs_0_), channel_id=1, source_target_pairs={{0,8},{4,12},{8,0},{12,4},{1,9},{5,13},{9,1},{13,5},{2,10},{6,14},... | collective-permute-start | bytes 786440 | tf_op jit(solution)/shard_map/ppermute | solution.py:30
  81.9 20.6 %collective-permute-start.8 = (f32[2,2,64,128]{3,2,1,0:T(8,128)S(1)}, f32[2,2,64,128]{3,2,1,0:T(8,128)S(1)}, u32[]{:S(2)}, u32[]{:S(2)}) collective-permute-start(f32[2,2,64,128]{3,2,1,0:T(8,128)S(1)} %get-tuple-element.40), channel_id=1, source_target_pairs={{0,16},{16,0},{1,17},{17,1},{2,18},{18,2},{3,19},{19,3},{4,20},{20... | collective-permute-start | bytes 393224 | tf_op jit(solution)/shard_map/ppermute | solution.py:30
  83.5 14.3 %collective-permute-start.23 = (bf16[256,512]{1,0:T(8,128)(2,1)S(1)}, bf16[256,512]{1,0:T(8,128)(2,1)S(1)}, u32[]{:S(2)}, u32[]{:S(2)}) collective-permute-start(bf16[256,512]{1,0:T(8,128)(2,1)S(1)} %add_convert_fusion.wa), channel_id=1, source_target_pairs={{0,8},{4,12},{8,0},{12,4},{1,9},{5,13},{9,1},{13,5},{2,10},{6,14},... | collective-permute-start | bytes 786440 | tf_op jit(solution)/shard_map/ppermute | solution.py:30
  99.6 6.6 %collective-permute-start.24 = (f32[8,256]{1,0:T(8,128)S(1)}, f32[8,256]{1,0:T(8,128)S(1)}, u32[]{:S(2)}, u32[]{:S(2)}) collective-permute-start(f32[8,256]{1,0:T(8,128)S(1)} %get-tuple-element.48.refs_0_), channel_id=1, source_target_pairs={{0,1},{1,0},{2,3},{3,2},{16,17},{17,16},{18,19},{19,18},{4,5},{5,4... | collective-permute-start | bytes 24584 | tf_op jit(solution)/shard_map/ppermute | solution.py:30
  100.6 9.4 %collective-permute-start.25 = (f32[8,256]{1,0:T(8,128)S(1)}, f32[8,256]{1,0:T(8,128)S(1)}, u32[]{:S(2)}, u32[]{:S(2)}) collective-permute-start(f32[8,256]{1,0:T(8,128)S(1)} %get-tuple-element.48.refs_0_), channel_id=1, source_target_pairs={{0,2},{1,3},{2,0},{3,1},{16,18},{17,19},{18,16},{19,17},{4,6},{5,7... | collective-permute-start | bytes 24584 | tf_op jit(solution)/shard_map/ppermute | solution.py:30
  103.2 12.6 %collective-permute-start.26 = (f32[8,256]{1,0:T(8,128)S(1)}, f32[8,256]{1,0:T(8,128)S(1)}, u32[]{:S(2)}, u32[]{:S(2)}) collective-permute-start(f32[8,256]{1,0:T(8,128)S(1)} %get-tuple-element.48.refs_0_), channel_id=1, source_target_pairs={{0,3},{1,2},{2,1},{3,0},{16,19},{17,18},{18,17},{19,16},{4,7},{5,6... | collective-permute-start | bytes 24584 | tf_op jit(solution)/shard_map/ppermute | solution.py:30
  104.7 11.1 %collective-permute-start.27 = (f32[8,256]{1,0:T(8,128)S(1)}, f32[8,256]{1,0:T(8,128)S(1)}, u32[]{:S(2)}, u32[]{:S(2)}) collective-permute-start(f32[8,256]{1,0:T(8,128)S(1)} %get-tuple-element.48.refs_0_), channel_id=1, source_target_pairs={{0,16},{1,17},{2,18},{3,19},{16,0},{17,1},{18,2},{19,3},{4,20},{5,... | collective-permute-start | bytes 24584 | tf_op jit(solution)/shard_map/ppermute | solution.py:30
  106.1 9.6 %collective-permute-start.28 = (f32[8,256]{1,0:T(8,128)S(1)}, f32[8,256]{1,0:T(8,128)S(1)}, u32[]{:S(2)}, u32[]{:S(2)}) collective-permute-start(f32[8,256]{1,0:T(8,128)S(1)} %get-tuple-element.48.refs_0_), channel_id=1, source_target_pairs={{0,17},{1,16},{2,19},{3,18},{16,1},{17,0},{18,3},{19,2},{4,21},{5,... | collective-permute-start | bytes 24584 | tf_op jit(solution)/shard_map/ppermute | solution.py:30
  106.2 9.5 %collective-permute-start.29 = (f32[8,256]{1,0:T(8,128)S(1)}, f32[8,256]{1,0:T(8,128)S(1)}, u32[]{:S(2)}, u32[]{:S(2)}) collective-permute-start(f32[8,256]{1,0:T(8,128)S(1)} %get-tuple-element.48.refs_0_), channel_id=1, source_target_pairs={{0,18},{1,19},{2,16},{3,17},{16,2},{17,3},{18,0},{19,1},{4,22},{5,... | collective-permute-start | bytes 24584 | tf_op jit(solution)/shard_map/ppermute | solution.py:30
  110.0 6.3 %collective-permute-start.30 = (f32[8,256]{1,0:T(8,128)S(1)}, f32[8,256]{1,0:T(8,128)S(1)}, u32[]{:S(2)}, u32[]{:S(2)}) collective-permute-start(f32[8,256]{1,0:T(8,128)S(1)} %get-tuple-element.48.refs_0_), channel_id=1, source_target_pairs={{0,19},{1,18},{2,17},{3,16},{16,3},{17,2},{18,1},{19,0},{4,23},{5,... | collective-permute-start | bytes 24584 | tf_op jit(solution)/shard_map/ppermute | solution.py:30
  (21 other events, 376.3 us)

commit v2 on v1

--- a/solution.py
+++ b/solution.py
@@ -22,6 +22,7 @@
 
 SMEM = pl.BlockSpec(memory_space=pltpu.SMEM)
 VMEM = pl.BlockSpec(memory_space=pltpu.VMEM)
+ANY = pl.BlockSpec(memory_space=pl.ANY)
 
 
 def swap(value, axes, k):
@@ -51,7 +52,9 @@
     return jnp.dot(a, b, precision=HIGHEST, preferred_element_type=F32)
 
 
-def project_kernel(ranks, mom, grad, basis, out, b_hi, b_lo):
+def project_kernel(ranks, mom, grad, basis, *refs):
+    out, b_hi, b_lo = refs[-3:]
+
     @pl.when(pl.program_id(0) == 0)
     def _():
         hi, lo = halves(basis[...])
@@ -63,63 +66,81 @@
     out[...] = acc.astype(out.dtype)
 
 
-def project(ranks, momentum, grad_q, basis, k, segments, dtype):
+def project(ranks, momentum, grad_q, basis, j, first, number, n_resp, n_head, dtype, after):
     rows, cols = momentum.shape
     rank = basis.shape[1]
-    seg = rows // segments
-    tile = min(seg, 256)
-    nb = seg // tile
+    chunk = rows // (n_resp * n_head)
 
     def rows_at(i, ranks):
-        return ((ranks[0] ^ k) * nb + i, 0)
+        return ((ranks[0] ^ j) * n_head + (ranks[2] ^ (first + i)), 0)
 
     return pl.pallas_call(
         project_kernel,
         grid_spec=pltpu.PrefetchScalarGridSpec(
             num_scalar_prefetch=1,
-            grid=(nb,),
+            grid=(number,),
             in_specs=[
-                pl.BlockSpec((tile, cols), rows_at),
-                pl.BlockSpec((tile, cols), rows_at),
+                pl.BlockSpec((chunk, cols), rows_at),
+                pl.BlockSpec((chunk, cols), rows_at),
                 pl.BlockSpec((cols, rank), lambda i, ranks: (0, 0)),
-            ],
-            out_specs=pl.BlockSpec((tile, rank), lambda i, ranks: (i, 0)),
+            ]
+            + [ANY] * len(after),
+            out_specs=pl.BlockSpec((chunk, rank), lambda i, ranks: (i, 0)),
             scratch_shapes=[pltpu.VMEM((cols, rank), BF16)] * 2,
         ),
-        out_shape=jax.ShapeDtypeStruct((seg, rank), dtype),
-        compiler_params=params(),
-        cost_estimate=cost(6 * seg * cols * rank, seg * cols * 6),
-    )(ranks, momentum, grad_q, basis)
-
-
-def split_kernel(n_recv, n_head, ranks, *refs):
-    own, recvs, outs = refs[0], refs[1 : 1 + n_recv], refs[1 + n_recv :]
+        out_shape=jax.ShapeDtypeStruct((number * chunk, rank), dtype),
+        compiler_params=params(60),
+        cost_estimate=cost(6 * number * chunk * cols * rank, number * chunk * cols * 6),
+    )(ranks, momentum, grad_q, basis, *after)
+
+
+def split_kernel(n_recv, first, number, own, *refs):
+    recvs, outs = refs[:n_recv], refs[-number:]
     chunk = outs[0].shape[0]
-    for k in range(n_head):
-        rows = pl.ds(pl.multiple_of((ranks[2] ^ k) * chunk, chunk), chunk)
-        acc = own[rows, :]
+    for i in range(number):
+        acc = own[(first + i) * chunk : (first + i + 1) * chunk, :]
         for r in recvs:
-            acc = acc + r[rows, :].astype(F32)
-        outs[k][...] = acc.astype(outs[k].dtype)
-
-
-def split_sum(ranks, own, recvs, n_head):
+            acc = acc + r[i * chunk : (i + 1) * chunk, :].astype(F32)
+        outs[i][...] = acc.astype(outs[i].dtype)
+
+
+def split_sum(own, recvs, first, number, n_head, after):
     rows, rank = own.shape
     chunk = rows // n_head
     return pl.pallas_call(
-        functools.partial(split_kernel, len(recvs), n_head),
-        in_specs=[SMEM] + [VMEM] * (1 + len(recvs)),
-        out_specs=[VMEM] * n_head,
+        functools.partial(split_kernel, len(recvs), first, number),
+        in_specs=[VMEM] * (1 + len(recvs)) + [ANY] * len(after),
+        out_specs=[VMEM] * number,
         out_shape=[
-            jax.ShapeDtypeStruct((chunk, rank), BF16 if k else F32) for k in range(n_head)
+            jax.ShapeDtypeStruct((chunk, rank), BF16 if first + i else F32)
+            for i in range(number)
         ],
         compiler_params=params(),
         cost_estimate=cost(rows * rank, rows * rank * 8),
-    )(ranks, own, *recvs)
+    )(own, *recvs, *after)
+
+
+def sum_kernel(n_parts, *refs):
+    acc = refs[0][...].astype(F32)
+    for r in refs[1:n_parts]:
+        acc = acc + r[...].astype(F32)
+    refs[-1][...] = acc.astype(refs[-1].dtype)
+
+
+def sum_parts(parts, dtype, after=()):
+    shape = parts[0].shape
+    return pl.pallas_call(
+        functools.partial(sum_kernel, len(parts)),
+        in_specs=[VMEM] * len(parts) + [ANY] * len(after),
+        out_specs=VMEM,
+        out_shape=jax.ShapeDtypeStruct(shape, dtype),
+        compiler_params=params(),
+        cost_estimate=cost(1000, 12 * math.prod(shape)),
+    )(*parts, *after)
 
 
 def gram_kernel(n_resp, n_head, ranks, *refs):
-    chunks, (pcat, gram) = refs[: n_resp * n_head], refs[n_resp * n_head :]
+    chunks, (pcat, gram) = refs[: n_resp * n_head], refs[-2:]
     size = chunks[0].shape[0]
     for j in range(n_resp):
         for k in range(n_head):
@@ -129,12 +150,12 @@
     gram[...] = mm(p.T, p)
 
 
-def gather_gram(ranks, chunks, n_resp, n_head):
+def gather_gram(ranks, chunks, n_resp, n_head, after):
     size, rank = chunks[0].shape
     rows = size * n_resp * n_head
     return pl.pallas_call(
         functools.partial(gram_kernel, n_resp, n_head),
-        in_specs=[SMEM] + [VMEM] * len(chunks),
+        in_specs=[SMEM] + [VMEM] * len(chunks) + [ANY] * len(after),
         out_specs=[VMEM] * 2,
         out_shape=[
             jax.ShapeDtypeStruct((rows, rank), BF16),
@@ -142,7 +163,7 @@
         ],
         compiler_params=params(),
         cost_estimate=cost(2 * rows * rank * rank, rows * rank * 4),
-    )(ranks, *chunks)
+    )(ranks, *chunks, *after)
 
 
 def back_part_kernel(pcat, mom, grad, out, acc):
@@ -308,12 +329,14 @@
     bt_out[...] = bt
     y_out[...] = ((1.0 - momentum_keep) * mm_full(x[...].T, bt)).astype(BF16)
     ones = jnp.ones((8, bt.shape[1]), F32)
-    s_out[...] = lax.dot_general(
+    squares = lax.dot_general(
         ones, bt * bt, (((1,), (1,)), ((), ())), precision=HIGHEST, preferred_element_type=F32
     )
-
-
-def back_full(x, wa, wb):
+    for i in range(s_out.shape[0]):
+        s_out[i] = squares
+
+
+def back_full(x, wa, wb, copies):
     rank, cols = wa.shape
     return pl.pallas_call(
         back_kernel,
@@ -322,7 +345,7 @@
         out_shape=[
             jax.ShapeDtypeStruct((rank, cols), F32),
             jax.ShapeDtypeStruct((rank, cols), BF16),
-            jax.ShapeDtypeStruct((8, rank), F32),
+            jax.ShapeDtypeStruct((copies, 8, rank), F32),
         ],
         compiler_params=params(),
         cost_estimate=cost(24 * rank * rank * cols, rank * cols * 12),
@@ -353,14 +376,12 @@
     )(pcat, momentum, grad_q, y)
 
 
-def update_kernel(n_sums, gain, pcat, x, bt, *refs):
-    sums, (upd, basis_out, z_hi, z_lo) = refs[:n_sums], refs[n_sums:]
-
+def update_kernel(gain, pcat, x, bt, sums, upd, basis_out, z_hi, z_lo):
     @pl.when(pl.program_id(0) == 0)
     def _():
-        total = sums[0][...]
-        for s in sums[1:]:
-            total = total + s[...]
+        total = sums[0]
+        for i in range(1, sums.shape[0]):
+            total = total + sums[i]
         scale = lax.rsqrt(total + norm_eps).T[:, :1]
         scaled = bt[...] * scale
         basis_out[...] = scaled.T
@@ -378,14 +399,14 @@
     tile = min(rows, 512)
     whole = lambda i: (0, 0)
     return pl.pallas_call(
-        functools.partial(update_kernel, len(sums), gain),
+        functools.partial(update_kernel, gain),
         grid=(rows // tile,),
         in_specs=[
             pl.BlockSpec((tile, rank), lambda i: (i, 0)),
             pl.BlockSpec((rank, rank), whole),
             pl.BlockSpec((rank, cols), whole),
-        ]
-        + [pl.BlockSpec((8, rank), whole)] * len(sums),
+            pl.BlockSpec(sums.shape, lambda i: (0, 0, 0)),
+        ],
         out_specs=[
             pl.BlockSpec((tile, cols), lambda i: (i, 0)),
             pl.BlockSpec((cols, rank), whole),
@@ -397,7 +418,7 @@
         ],
         compiler_params=params(),
         cost_estimate=cost(4 * rows * cols * rank, rows * cols * 3),
-    )(pcat, x, bt, *sums)
+    )(pcat, x, bt, sums)
 
 
 def group_of(counts, response):
@@ -409,44 +430,58 @@
     return group
 
 
+def pack_kernel(*refs):
+    keys, values, out = refs[0], refs[1], refs[-1]
+    out[0] = keys[...]
+    out[1] = values[...]
+
+
+def pack_prompts(keys, values, after):
+    return pl.pallas_call(
+        pack_kernel,
+        in_specs=[VMEM] * 2 + [ANY] * len(after),
+        out_specs=VMEM,
+        out_shape=jax.ShapeDtypeStruct((2,) + keys.shape, BF16),
+        compiler_params=params(),
+        cost_estimate=cost(1000, 8 * math.prod(keys.shape)),
+    )(keys, values, *after)
+
+
 def select_kernel(n_resp, n_fsdp, ranks, counts, slots, *refs):
-    keys, values, outs = refs[:n_resp], refs[n_resp : 2 * n_resp], refs[2 * n_resp :]
-    held = keys[0].shape[0]
-    for k in range(n_fsdp):
-        slot = slots[group_of(counts, ranks[0] * n_fsdp + (ranks[1] ^ k))]
+    stored, out = refs[:n_resp], refs[-1]
+    held = stored[0].shape[1]
+    for f in range(n_fsdp):
+        slot = slots[group_of(counts, ranks[0] * n_fsdp + f)]
         owner, local = slot // held, slot % held
-        for a, arrays in enumerate((keys, values)):
-            for j in range(n_resp):
-
-                @pl.when(owner == (ranks[0] ^ j))
-                def _():
-                    outs[k][a] = arrays[j][local]
-
-
-def select_prompts(ranks, counts, slots, keys, values, n_fsdp):
-    _, piece, width = keys[0].shape
-    return pl.pallas_call(
-        functools.partial(select_kernel, len(keys), n_fsdp),
-        in_specs=[SMEM] * 3 + [VMEM] * (2 * len(keys)),
-        out_specs=[VMEM] * n_fsdp,
-        out_shape=[jax.ShapeDtypeStruct((2, piece, width), BF16)] * n_fsdp,
+        for j in range(n_resp):
+
+            @pl.when(owner == (ranks[0] ^ j))
+            def _():
+                out[f, 0] = stored[j][0, local]
+                out[f, 1] = stored[j][1, local]
+
+
+def select_prompts(ranks, counts, slots, stored, n_fsdp, after):
+    _, _, piece, width = stored[0].shape
+    return pl.pallas_call(
+        functools.partial(select_kernel, len(stored), n_fsdp),
+        in_specs=[SMEM] * 3 + [VMEM] * len(stored) + [ANY] * len(after),
+        out_specs=VMEM,
+        out_shape=jax.ShapeDtypeStruct((n_fsdp, 2, piece, width), BF16),
         compiler_params=params(),
         cost_estimate=cost(1000, 8 * n_fsdp * piece * width),
-    )(ranks, counts, slots, *keys, *values)
-
-
-def attention_kernel(n_fsdp, ranks, counts, prompt_blocks, resp_blocks, q, sk, sv, go, *refs):
-    pieces, refs = refs[:n_fsdp], refs[n_fsdp:]
-    dq, own, refs = refs[0], refs[1], refs[2:]
-    sends, (keys, values, dk, dv) = refs[:n_fsdp], refs[n_fsdp:]
-    piece = pieces[0].shape[1]
+    )(ranks, counts, slots, *stored, *after)
+
+
+def attention_kernel(ranks, counts, prompt_blocks, resp_blocks, q, sk, sv, go, pieces, *refs):
+    dq, own, part, keys, values, dk, dv = refs[-7:]
+    n_fsdp, _, piece, _ = pieces.shape
     cap = piece * n_fsdp
     length = q.shape[0]
     scale = HD ** (-0.5)
-    for k in range(n_fsdp):
-        rows = pl.ds(pl.multiple_of((ranks[1] ^ k) * piece, piece), piece)
-        keys[rows, :] = pieces[k][0]
-        values[rows, :] = pieces[k][1]
+    for f in range(n_fsdp):
+        keys[f * piece : (f + 1) * piece, :] = pieces[f, 0]
+        values[f * piece : (f + 1) * piece, :] = pieces[f, 1]
     keys[cap:, :] = sk[...]
     values[cap:, :] = sv[...]
     prompt_len = prompt_blocks[group_of(counts, ranks[0] * n_fsdp + ranks[1])] * 128
@@ -483,58 +518,77 @@
         dq[:, cols] = (mm(kt, ds) * scale).T.astype(BF16)
     own[0] = (dk[cap:, :] * scale).astype(BF16)
     own[1] = dv[cap:, :].astype(BF16)
-    for k in range(n_fsdp):
-        rows = pl.ds(pl.multiple_of((ranks[1] ^ k) * piece, piece), piece)
-        sends[k][0] = dk[rows, :] * scale
-        sends[k][1] = dv[rows, :]
-
-
-def attention(ranks, counts, prompt_blocks, resp_blocks, q, sk, sv, go, pieces):
-    n_fsdp = len(pieces)
-    piece = pieces[0].shape[1]
+    part[0] = dk[:cap, :] * scale
+    part[1] = dv[:cap, :]
+
+
+def attention(ranks, counts, prompt_blocks, resp_blocks, q, sk, sv, go, pieces, after):
+    n_fsdp, _, piece, _ = pieces.shape
     length, width = q.shape
-    total = piece * n_fsdp + length
-    return pl.pallas_call(
-        functools.partial(attention_kernel, n_fsdp),
-        in_specs=[SMEM] * 4 + [VMEM] * (4 + n_fsdp),
-        out_specs=[VMEM] * (2 + n_fsdp),
+    cap = piece * n_fsdp
+    total = cap + length
+    return pl.pallas_call(
+        attention_kernel,
+        in_specs=[SMEM] * 4 + [VMEM] * 5 + [ANY] * len(after),
+        out_specs=[VMEM] * 3,
         out_shape=[
             jax.ShapeDtypeStruct((length, width), BF16),
             jax.ShapeDtypeStruct((2, length, HD), BF16),
-        ]
-        + [jax.ShapeDtypeStruct((2, piece, HD), F32)] * n_fsdp,
+            jax.ShapeDtypeStruct((2, cap, HD), F32),
+        ],
         scratch_shapes=[pltpu.VMEM((total, HD), BF16)] * 2 + [pltpu.VMEM((total, HD), F32)] * 2,
         compiler_params=params(32),
         cost_estimate=cost(6_000_000_000, length * width * 8),
-    )(ranks, counts, prompt_blocks, resp_blocks, q, sk, sv, go, *pieces)
-
-
-def by_slot_kernel(n_resp, n_fsdp, ranks, counts, slots, *refs):
-    parts, outs = refs[:n_fsdp], refs[n_fsdp:]
-    held = outs[0].shape[1]
-    slot_of = [
-        slots[group_of(counts, ranks[0] * n_fsdp + (ranks[1] ^ k))] for k in range(n_fsdp)
-    ]
-    for j in range(n_resp):
-        for local in range(held):
-            slot = (ranks[0] ^ j) * held + local
-            acc = jnp.zeros(parts[0].shape, F32)
-            for k in range(n_fsdp):
-                acc = acc + jnp.where(slot_of[k] == slot, parts[k][...], 0.0)
-            outs[j][:, local] = acc
-
-
-def sum_by_slot(ranks, counts, slots, parts, n_resp):
+    )(ranks, counts, prompt_blocks, resp_blocks, q, sk, sv, go, pieces, *after)
+
+
+def address_kernel(n_resp, n_fsdp, ranks, counts, slots, part, *refs):
+    out = refs[-1]
+    piece = out.shape[2]
     held = counts.shape[0] // n_resp
-    _, piece, width = parts[0].shape
-    return pl.pallas_call(
-        functools.partial(by_slot_kernel, n_resp, len(parts)),
-        in_specs=[SMEM] * 3 + [VMEM] * len(parts),
-        out_specs=[VMEM] * n_resp,
-        out_shape=[jax.ShapeDtypeStruct((2, held, piece, width), F32)] * n_resp,
-        compiler_params=params(),
-        cost_estimate=cost(1000, 8 * len(parts) * piece * width * 4),
-    )(ranks, counts, slots, *parts)
+    owner = slots[group_of(counts, ranks[0] * n_fsdp + ranks[1])] // held
+    for r in range(n_resp):
+        for f in range(n_fsdp):
+            out[r * n_fsdp + f] = jnp.where(
+                owner == r, part[:, f * piece : (f + 1) * piece, :], 0.0
+            )
+
+
+def address_parts(ranks, counts, slots, part, n_resp, n_fsdp, after):
+    piece = part.shape[1] // n_fsdp
+    shape = (n_resp * n_fsdp, 2, piece, part.shape[2])
+    return pl.pallas_call(
+        functools.partial(address_kernel, n_resp, n_fsdp),
+        in_specs=[SMEM] * 3 + [VMEM] + [ANY] * len(after),
+        out_specs=VMEM,
+        out_shape=jax.ShapeDtypeStruct(shape, F32),
+        compiler_params=params(),
+        cost_estimate=cost(1000, 8 * math.prod(shape)),
+    )(ranks, counts, slots, part, *after)
+
+
+def collect_kernel(ranks, counts, slots, arrived, out):
+    held = out.shape[1]
+    sources = arrived.shape[0]
+    slot_of = [slots[group_of(counts, jnp.int32(i))] for i in range(sources)]
+    for local in range(held):
+        slot = ranks[0] * held + local
+        acc = jnp.where(slot_of[0] == slot, arrived[0], 0.0)
+        for i in range(1, sources):
+            acc = acc + jnp.where(slot_of[i] == slot, arrived[i], 0.0)
+        out[:, local] = acc
+
+
+def collect(ranks, counts, slots, arrived, held):
+    _, two, piece, width = arrived.shape
+    return pl.pallas_call(
+        collect_kernel,
+        in_specs=[SMEM] * 3 + [VMEM],
+        out_specs=VMEM,
+        out_shape=jax.ShapeDtypeStruct((two, held, piece, width), F32),
+        compiler_params=params(),
+        cost_estimate=cost(1000, 4 * math.prod(arrived.shape)),
+    )(ranks, counts, slots, arrived)
 
 
 def on_device(
@@ -558,54 +612,67 @@
         momentum.shape[0] * n_fsdp * momentum.shape[1] * n_resp * n_head / basis.shape[1]
     )
 
-    keys = [prompt_keys] + [swap(prompt_keys, "resp", j) for j in range(1, n_resp)]
-    values = [prompt_values] + [swap(prompt_values, "resp", j) for j in range(1, n_resp)]
-
-    sent = [project(ranks, momentum, grad_q, basis, j, n_resp, BF16) for j in range(1, n_resp)]
-    recvs = [swap(s, "resp", j + 1) for j, s in enumerate(sent)]
-    mine = project(ranks, momentum, grad_q, basis, 0, n_resp, F32)
-
-    chosen = select_prompts(ranks, counts, owner_slot, keys, values, n_fsdp)
-    pieces = [chosen[0]] + [swap(chosen[k], "fsdp", k) for k in range(1, n_fsdp)]
-
-    split = split_sum(ranks, mine, recvs, n_head)
-    acc = split[0]
-    for part in [swap(split[k], "head", k) for k in range(1, n_head)]:
-        acc = acc + part.astype(F32)
-    piece0 = acc.astype(BF16)
-
-    attended = attention(
-        ranks, counts, prompt_blocks, resp_blocks, queries, self_keys, self_values, d_out, pieces
+    half = n_head // 2
+    groups = [(half, half), (0, half)] if half else [(0, n_head)]
+
+    sent, after = [], ()
+    for first, number in groups:
+        row = []
+        for j in range(1, n_resp):
+            row.append(
+                project(
+                    ranks, momentum, grad_q, basis, j, first, number, n_resp, n_head, BF16, after
+                )
+            )
+            after = (row[-1],)
+        sent.append(row)
+    arrived = [[swap(s, "resp", j + 1) for j, s in enumerate(row)] for row in sent]
+    mine = project(
+        ranks, momentum, grad_q, basis, 0, 0, n_head, n_resp, n_head, F32, after
     )
-    dq, resp_grad, parts = attended[0], attended[1], attended[2:]
-
-    along = [piece0] + [swap(piece0, "head", k) for k in range(1, n_head)]
-    chunks = list(along)
+    packed = pack_prompts(prompt_keys, prompt_values, after)
+    stored = [packed] + [swap(packed, "resp", j) for j in range(1, n_resp)]
+
+    split, after = {}, ()
+    for (first, number), recvs in zip(groups, arrived):
+        outs = split_sum(mine, recvs, first, number, n_head, after)
+        after = (outs[0],)
+        for i in range(number):
+            split[first + i] = outs[i]
+    chosen = select_prompts(ranks, counts, owner_slot, stored, n_fsdp, after)
+    pieces = lax.all_to_all(chosen, "fsdp", 0, 0, tiled=True)
+    far_first = [k for first, number in groups for k in range(first, first + number) if k]
+    summands = {k: swap(split[k], "head", k) for k in far_first}
+    piece0 = sum_parts([split[0]] + [summands[k] for k in range(1, n_head)], BF16, (chosen,))
+
+    along = {0: piece0}
+    for k in far_first:
+        along[k] = swap(piece0, "head", k)
+    chunks = [along[k] for k in range(n_head)]
     for j in range(1, n_resp):
-        chunks += [swap(c, "resp", j) for c in along]
-    pcat, gram = gather_gram(ranks, chunks, n_resp, n_head)
-
-    returned = [parts[0]] + [swap(parts[k], "fsdp", k) for k in range(1, n_fsdp)]
-    slots = sum_by_slot(ranks, counts, owner_slot, returned, n_resp)
-    prompt_grad = slots[0]
-    for j in range(1, n_resp):
-        prompt_grad = prompt_grad + swap(slots[j], "resp", j)
+        chunks += [swap(along[k], "resp", j) for k in range(n_head)]
+
+    dq, resp_grad, part = attention(
+        ranks, counts, prompt_blocks, resp_blocks, queries, self_keys, self_values, d_out, pieces,
+        (along[n_head - 1],),
+    )
+    pcat, gram = gather_gram(ranks, chunks, n_resp, n_head, (part,))
 
     bits = [1 << b for b in range(n_fsdp.bit_length() - 1)]
+    w = back_part(pcat, momentum, grad_q)
+    addressed = address_parts(ranks, counts, owner_slot, part, n_resp, n_fsdp, (w,))
     for bit in bits[:-1]:
-        gram = gram + swap(gram, "fsdp", bit)
+        gram = sum_parts([gram, swap(gram, "fsdp", bit)], F32)
+        w = sum_parts([w, swap(w, "fsdp", bit)], BF16, (gram,))
     gram_parts = (gram, swap(gram, "fsdp", bits[-1]))
-    w = back_part(pcat, momentum, grad_q)
-    for bit in bits[:-1]:
-        w = (w.astype(F32) + swap(w, "fsdp", bit).astype(F32)).astype(BF16)
     w_other = swap(w, "fsdp", bits[-1])
+    returned = lax.all_to_all(addressed, ("resp", "fsdp"), 0, 0, tiled=True)
 
     x = inverse_factor(*gram_parts)
-    bt, y, squares = back_full(x, w, w_other)
-    sums = [squares] + [
-        swap(squares, ("resp", "head"), k) for k in range(1, n_resp * n_head)
-    ]
+    bt, y, squares = back_full(x, w, w_other, n_resp * n_head)
+    sums = lax.all_to_all(squares, ("resp", "head"), 0, 0, tiled=True)
     momentum_out = new_momentum(pcat, momentum, grad_q, y)
+    prompt_grad = collect(ranks, counts, owner_slot, returned, prompt_keys.shape[0])
     update, basis_out = final_update(pcat, x, bt, sums, gain)
     return (dq, resp_grad, prompt_grad, update, momentum_out, basis_out)
 

time: 120 us -> 116 us (0.967); the launches traced: 120 us -> 115 us
  waiting for transfers between devices: 36.3 us -> 11.9 us
  Pallas kernels: 37.2 us -> 50.6 us
  local copies, waits for them, and re-layouts: 4.88 us -> 17 us
  starting transfers between devices: 39.2 us -> 33.2 us
    ppermute x31 -> x17, waiting for transfers between devices: 36.3 us -> 11.9 us  [swap(): return lax.ppermute(value, axes, [(i, i ^ k) for i in range(n)])]
    ppermute x31 -> x17, starting transfers between devices: 39.2 us -> 21.7 us  [swap(): return lax.ppermute(value, axes, [(i, i ^ k) for i in range(n)])]
    unnamed x28 -> x60, local copies, waits for them, and re-layouts: 4.88 us -> 17 us
    all_to_all x0 -> x3, starting transfers between devices: none -> 11.5 us  [the longest x1 4.16 us: on_device(): returned = lax.all_to_all(addressed, ('resp', 'fsdp'), 0, 0, tiled=True)]
    pallas_call x2 -> x3, Pallas kernels: 4.51 us -> 12.5 us  [project(): pl.pallas_call(project_kernel, grid_spec=pltpu.PrefetchScalarGridSpec(num...]
    pallas_call x5 -> x11, Pallas kernels: 12.3 us -> 16 us  [the longest x1 6.47 us: attention(): pl.pallas_call(attention_kernel, in_specs=[SMEM] * 4 + [VMEM] * 5 + [ANY]...]
  transfers between devices with their start and end apart: 31 -> 20, of which waited for: 11 -> 5; matrix products, arithmetic and copies ran while one was open for 1% -> 0% of each run, Pallas kernels for 25% -> 37%
where the time goes in v2:
time: 116 us; the launch traced here: 115 us
  Pallas kernels  50.6 us (44%)
  starting transfers between devices  33.2 us (29%)
  local copies, waits for them, and re-layouts  17 us (15%)
  waiting for transfers between devices  11.9 us (10%)
  between operations  1.52 us (1%)
    ppermute x17, starting transfers between devices, swap(): return lax.ppermute(value, axes, [(i, i ^ k) for i in range(n)])  21.7 us
    unnamed x60, local copies, waits for them, and re-layouts  17 us
    pallas_call x3, Pallas kernels, project(): pl.pallas_call(project_kernel, grid_spec=pltpu.PrefetchScalarGridSpec(num...  12.5 us
    ppermute x17, waiting for transfers between devices, swap(): return lax.ppermute(value, axes, [(i, i ^ k) for i in range(n)])  11.9 us
    pallas_call x1, Pallas kernels, inverse_factor(): pl.pallas_call(functools.partial(cholesky_kernel, len(parts)), in_specs=[...  11.9 us
    pallas_call x1, Pallas kernels, attention(): pl.pallas_call(attention_kernel, in_specs=[SMEM] * 4 + [VMEM] * 5 + [ANY]...  6.47 us
    pallas_call x1, Pallas kernels, new_momentum(): pl.pallas_call(momentum_kernel, grid=(rows // tile,), in_specs=[pl.BlockS...  4.32 us
    all_to_all x1, starting transfers between devices, on_device(): returned = lax.all_to_all(addressed, ('resp', 'fsdp'), 0, 0, tiled=True)  4.16 us
  transfers between devices with their start and end apart: 20, of which 5 were waited for; matrix products, arithmetic and copies ran while one was open for 0% of the time, Pallas kernels for 37%

profile of v2, /device:TPU:0, one launch (start us, length us, event | category | flops | bytes accessed | tf_op | source)
XLA Modules:
  0.0 114.9 jit_solution(7896078911043522554)
XLA Ops:
  1.2 3.5 %shard_map.172.refs_0_ = bf16[512,256]{1,0:T(8,128)(2,1)} custom-call(s32[3]{0:T(128)} %pad_add_fusion.ranks, f32[2048,512]{1,0:T(8,128)} %mom.9, bf16[2048,512]{1,0:T(8,128)(2,1)} %grad.9, f32[512,256]{1,0:T(8,128)} %basis.5), custom_call_target="tpu_custom_call" | custom-call | flops 402653184 | bytes 1572864 | tf_op jit(solution)/shard_map/pallas_call | solution.py:77
  4.7 2.9 %collective-permute-start.2 = (bf16[512,256]{1,0:T(8,128)(2,1)}, bf16[512,256]{1,0:T(8,128)(2,1)S(1)}, u32[]{:S(2)}, u32[]{:S(2)}) collective-permute-start(bf16[512,256]{1,0:T(8,128)(2,1)} %shard_map.172.refs_0_), channel_id=1, source_target_pairs={{0,16},{16,0},{1,17},{17,1},{2,18},{18,2},{3,19},{19,3},{4,20},{20... | collective-permute-start | bytes 786440 | tf_op jit(solution)/shard_map/ppermute | solution.py:31
  7.7 3.5 %shard_map.173.refs_2_.refs_0_ = bf16[512,256]{1,0:T(8,128)(2,1)} custom-call(s32[3]{0:T(128)} %pad_add_fusion.ranks, f32[2048,512]{1,0:T(8,128)} %mom.9, bf16[2048,512]{1,0:T(8,128)(2,1)} %grad.9, f32[512,256]{1,0:T(8,128)} %basis.5, bf16[512,256]{1,0:T(8,128)(2,1)} %shard_map.172.refs_0_), custom_call_target="tpu_custom_call" | custom-call | flops 402653184 | bytes 1572864 | tf_op jit(solution)/shard_map/pallas_call | solution.py:77
  11.3 5.5 %shard_map.175.own = f32[1024,256]{1,0:T(8,128)} custom-call(s32[3]{0:T(128)} %pad_add_fusion.ranks, f32[2048,512]{1,0:T(8,128)} %mom.9, bf16[2048,512]{1,0:T(8,128)(2,1)} %grad.9, f32[512,256]{1,0:T(8,128)} %basis.5, bf16[512,256]{1,0:T(8,128)(2,1)} %shard_map.173.refs_2_.refs_0_), custom_call_target="tpu_custom_call" | custom-call | flops 805306368 | bytes 3145728 | tf_op jit(solution)/shard_map/pallas_call | solution.py:77
  18.1 1.7 %collective-permute-done.1.refs_0_ = bf16[512,256]{1,0:T(8,128)(2,1)S(1)} collective-permute-done((bf16[512,256]{1,0:T(8,128)(2,1)}, bf16[512,256]{1,0:T(8,128)(2,1)S(1)}, u32[]{:S(2)}, u32[]{:S(2)}) %collective-permute-start.1) | collective-permute-done | bytes 262176 | tf_op jit(solution)/shard_map/ppermute | solution.py:31
  19.9 1.9 %collective-permute-start.3 = (bf16[256,256]{1,0:T(8,128)(2,1)S(1)}, bf16[256,256]{1,0:T(8,128)(2,1)S(1)}, u32[]{:S(2)}, u32[]{:S(2)}) collective-permute-start(bf16[256,256]{1,0:T(8,128)(2,1)S(1)} %get-tuple-element.22), channel_id=1, source_target_pairs={{0,1},{1,0},{2,3},{3,2},{4,5},{5,4},{6,7},{7,6},{8,9},{9,8},{10,11... | collective-permute-start | bytes 393224 | tf_op jit(solution)/shard_map/ppermute | solution.py:31
  21.8 2.5 %collective-permute-start.5 = (bf16[256,256]{1,0:T(8,128)(2,1)S(1)}, bf16[256,256]{1,0:T(8,128)(2,1)S(1)}, u32[]{:S(2)}, u32[]{:S(2)}) collective-permute-start(bf16[256,256]{1,0:T(8,128)(2,1)S(1)} %get-tuple-element.23), channel_id=1, source_target_pairs={{0,3},{1,2},{2,1},{3,0},{4,7},{5,6},{6,5},{7,4},{8,11},{9,10},{10,... | collective-permute-start | bytes 393224 | tf_op jit(solution)/shard_map/ppermute | solution.py:31
  24.4 1.6 %collective-permute-start = (bf16[2,2,64,128]{3,2,1,0:T(8,128)(2,1)S(1)}, bf16[2,2,64,128]{3,2,1,0:T(8,128)(2,1)S(1)}, u32[]{:S(2)}, u32[]{:S(2)}) collective-permute-start(bf16[2,2,64,128]{3,2,1,0:T(8,128)(2,1)S(1)} %shard_map.174.refs_0_), channel_id=1, source_target_pairs={{0,16},{16,0},{1,17},{17,1},{2,18},{18,2},{3,19},{19,3},{4,20},{20... | collective-permute-start | bytes 196616 | tf_op jit(solution)/shard_map/ppermute | solution.py:31
  25.9 2.8 %collective-permute-done.refs_1_ = bf16[2,2,64,128]{3,2,1,0:T(8,128)(2,1)S(1)} collective-permute-done((bf16[2,2,64,128]{3,2,1,0:T(8,128)(2,1)S(1)}, bf16[2,2,64,128]{3,2,1,0:T(8,128)(2,1)S(1)}, u32[]{:S(2)}, u32[]{:S(2)}) %collective-permute-start) | collective-permute-done | bytes 65568 | tf_op jit(solution)/shard_map/ppermute | solution.py:31
  31.2 4.3 %collective-permute-done.4.refs_2_ = bf16[256,256]{1,0:T(8,128)(2,1)S(1)} collective-permute-done((bf16[256,256]{1,0:T(8,128)(2,1)S(1)}, bf16[256,256]{1,0:T(8,128)(2,1)S(1)}, u32[]{:S(2)}, u32[]{:S(2)}) %collective-permute-start.4) | collective-permute-done | bytes 131104 | tf_op jit(solution)/shard_map/ppermute | solution.py:31
  36.0 2.9 %collective-permute-start.7 = (bf16[256,256]{1,0:T(8,128)(2,1)S(1)}, bf16[256,256]{1,0:T(8,128)(2,1)S(1)}, u32[]{:S(2)}, u32[]{:S(2)}) collective-permute-start(bf16[256,256]{1,0:T(8,128)(2,1)S(1)} %shard_map.179.refs_0_), channel_id=1, source_target_pairs={{0,1},{1,0},{2,3},{3,2},{4,5},{5,4},{6,7},{7,6},{8,9},{9,8},{10,11... | collective-permute-start | bytes 393224 | tf_op jit(solution)/shard_map/ppermute | solution.py:31
  40.1 3.3 %all-to-all-start = ((bf16[4,2,64,128]{3,2,1,0:T(8,128)(2,1)}), bf16[4,2,64,128]{3,2,1,0:T(8,128)(2,1)S(1)}, u32[]{:S(2)}, u32[]{:S(2)}) async-start(bf16[4,2,64,128]{3,2,1,0:T(8,128)(2,1)} %shard_map.178.refs_4_), calls=%async_computation | async-start | bytes 262144 | tf_op jit(solution)/shard_map/all_to_all | solution.py:643
  45.2 1.9 %collective-permute-done.8.refs_2_ = bf16[256,256]{1,0:T(8,128)(2,1)S(1)} collective-permute-done((bf16[256,256]{1,0:T(8,128)(2,1)S(1)}, bf16[256,256]{1,0:T(8,128)(2,1)S(1)}, u32[]{:S(2)}, u32[]{:S(2)}) %collective-permute-start.8) | collective-permute-done | bytes 131104 | tf_op jit(solution)/shard_map/ppermute | solution.py:31
  52.3 6.5 %shard_map.180 = (bf16[256,1024]{1,0:T(8,128)(2,1)}, bf16[2,256,128]{2,1,0:T(8,128)(2,1)}, f32[2,256,128]{2,1,0:T(8,128)S(1)}) custom-call(s32[3]{0:T(128)S(1)} %copy-done.18, s32[4]{0:T(128)S(1)} %copy-done.19, s32[4]{0:T(128)S(1)} %copy-done.25, s32[1]{0:T(128)S(6)} %copy.19.resp_blocks, bf16[256,1024]{1,0:T(8,128)(2,1)S(1)} %copy-done.21, ...), custom_call_target="tpu_custom_call" | custom-call | flops 6000000000 | bytes 2097152 | tf_op jit(solution)/shard_map/pallas_call | solution.py:530
  67.1 2.4 %shard_map.182.refs_0_ = bf16[256,512]{1,0:T(8,128)(2,1)S(1)} custom-call(bf16[2048,256]{1,0:T(8,128)(2,1)S(1)} %get-tuple-element.27.pcat, f32[2048,512]{1,0:T(8,128)S(1)} %copy-done, bf16[2048,512]{1,0:T(8,128)(2,1)S(1)} %copy-done.2), custom_call_target="tpu_custom_call" | custom-call | flops 1073741824 | bytes 6291456 | tf_op jit(solution)/shard_map/pallas_call | solution.py:192
  73.7 4.2 %all-to-all-start.1 = ((f32[8,2,64,128]{3,2,1,0:T(8,128)}), f32[8,2,64,128]{3,2,1,0:T(8,128)}, u32[]{:S(2)}, u32[]{:S(2)}) async-start(f32[8,2,64,128]{3,2,1,0:T(8,128)} %copy-done.5), calls=%async_computation.1 | async-start | bytes 1048576 | tf_op jit(solution)/shard_map/all_to_all | solution.py:669
  78.9 2.0 %collective-permute-start.16 = (bf16[256,512]{1,0:T(8,128)(2,1)S(1)}, bf16[256,512]{1,0:T(8,128)(2,1)S(1)}, u32[]{:S(2)}, u32[]{:S(2)}) collective-permute-start(bf16[256,512]{1,0:T(8,128)(2,1)S(1)} %shard_map.187.wa), channel_id=1, source_target_pairs={{0,8},{4,12},{8,0},{12,4},{1,9},{5,13},{9,1},{13,5},{2,10},{6,14},... | collective-permute-start | bytes 786440 | tf_op jit(solution)/shard_map/ppermute | solution.py:31
  80.9 11.9 %shard_map.186.x = f32[256,256]{1,0:T(8,128)S(1)} custom-call(f32[256,256]{1,0:T(8,128)} %shard_map.185.refs_0_.refs_2_, f32[256,256]{1,0:T(8,128)} %collective-permute-done.14.refs_1_), custom_call_target="tpu_custom_call" | custom-call | flops 10000000000 | bytes 1048576 | tf_op jit(solution)/shard_map/pallas_call | solution.py:315
  92.8 2.4 %shard_map.188 = (f32[256,512]{1,0:T(8,128)S(1)}, bf16[256,512]{1,0:T(8,128)(2,1)S(1)}, f32[8,8,256]{2,1,0:T(8,128)}) custom-call(f32[256,256]{1,0:T(8,128)S(1)} %shard_map.186.x, bf16[256,512]{1,0:T(8,128)(2,1)S(1)} %shard_map.187.wa, bf16[256,512]{1,0:T(8,128)(2,1)S(1)} %collective-permute-done.16.wb), custom_call_target="tpu_custom_call" | custom-call | flops 805306368 | bytes 1572864 | tf_op jit(solution)/shard_map/pallas_call | solution.py:341
  96.7 4.0 %all-to-all-start.2 = ((f32[8,8,256]{2,1,0:T(8,128)}), f32[8,8,256]{2,1,0:T(8,128)S(1)}, u32[]{:S(2)}, u32[]{:S(2)}) async-start(f32[8,8,256]{2,1,0:T(8,128)} %get-tuple-element.30), calls=%async_computation.2 | async-start | bytes 131072 | tf_op jit(solution)/shard_map/all_to_all | solution.py:673
  100.7 1.8 %shard_map.184 = f32[2,2,64,128]{3,2,1,0:T(8,128)} custom-call(s32[3]{0:T(128)S(1)} %copy-done.18, s32[4]{0:T(128)S(1)} %copy-done.19, s32[4]{0:T(128)S(1)} %copy-done.20, f32[8,2,64,128]{3,2,1,0:T(8,128)} %all-to-all-done.1.arrived), custom_call_target="tpu_custom_call" | custom-call | flops 1000 | bytes 524288 | tf_op jit(solution)/shard_map/pallas_call | solution.py:584
  102.6 2.2 %copy-done.1 = f32[2048,512]{1,0:T(8,128)S(1)} copy-done((f32[2048,512]{1,0:T(8,128)S(1)}, f32[2048,512]{1,0:T(8,128)}, u32[]{:S(2)}) %copy-start.1) | copy-done | bytes 4194328
  104.8 4.3 %shard_map.190 = f32[2048,512]{1,0:T(8,128)} custom-call(bf16[2048,256]{1,0:T(8,128)(2,1)S(1)} %get-tuple-element.27.pcat, f32[2048,512]{1,0:T(8,128)S(1)} %copy-done.1, bf16[2048,512]{1,0:T(8,128)(2,1)S(1)} %copy-done.2, bf16[256,512]{1,0:T(8,128)(2,1)S(1)} %get-tuple-element.32.y), custom_call_target="tpu_custom_call" | custom-call | flops 536870912 | bytes 10485760 | tf_op jit(solution)/shard_map/pallas_call | solution.py:363
  111.1 3.8 %shard_map.189 = (bf16[2048,512]{1,0:T(8,128)(2,1)}, f32[512,256]{1,0:T(8,128)}) custom-call(bf16[2048,256]{1,0:T(8,128)(2,1)S(1)} %get-tuple-element.27.pcat, f32[256,256]{1,0:T(8,128)S(1)} %copy-done.29, f32[256,512]{1,0:T(8,128)S(1)} %copy-done.27, f32[8,8,256]{2,1,0:T(8,128)S(1)} %all-to-all-done.2.sums), custom_call_target="tpu_custom_call" | custom-call | flops 1073741824 | bytes 3145728 | tf_op jit(solution)/shard_map/pallas_call | solution.py:401
  (96 shorter events, 29.5 us)
Async XLA Ops:
  4.7 12.1 %collective-permute-start.2 = (bf16[512,256]{1,0:T(8,128)(2,1)}, bf16[512,256]{1,0:T(8,128)(2,1)S(1)}, u32[]{:S(2)}, u32[]{:S(2)}) collective-permute-start(bf16[512,256]{1,0:T(8,128)(2,1)} %shard_map.172.refs_0_), channel_id=1, source_target_pairs={{0,16},{16,0},{1,17},{17,1},{2,18},{18,2},{3,19},{19,3},{4,20},{20... | collective-permute-start | bytes 786440 | tf_op jit(solution)/shard_map/ppermute | solution.py:31
  11.2 8.6 %collective-permute-start.1 = (bf16[512,256]{1,0:T(8,128)(2,1)}, bf16[512,256]{1,0:T(8,128)(2,1)S(1)}, u32[]{:S(2)}, u32[]{:S(2)}) collective-permute-start(bf16[512,256]{1,0:T(8,128)(2,1)} %shard_map.173.refs_2_.refs_0_), channel_id=1, source_target_pairs={{0,16},{16,0},{1,17},{17,1},{2,18},{18,2},{3,19},{19,3},{4,20},{20... | collective-permute-start | bytes 786440 | tf_op jit(solution)/shard_map/ppermute | solution.py:31
  18.1 32.1 %copy-start.23 = (bf16[256,128]{1,0:T(8,128)(2,1)S(1)}, bf16[256,128]{1,0:T(8,128)(2,1)}, u32[]{:S(2)}) copy-start(bf16[256,128]{1,0:T(8,128)(2,1)} %sk.1) | copy-start | bytes 196612
  18.1 32.1 %copy-start.24 = (bf16[256,128]{1,0:T(8,128)(2,1)S(1)}, bf16[256,128]{1,0:T(8,128)(2,1)}, u32[]{:S(2)}) copy-start(bf16[256,128]{1,0:T(8,128)(2,1)} %sv.1) | copy-start | bytes 196612
  18.1 32.1 %copy-start.25 = (s32[4]{0:T(128)S(1)}, s32[4]{0:T(128)}, u32[]{:S(2)}) copy-start(s32[4]{0:T(128)} %prompt_blocks.1) | copy-start | bytes 52
  19.9 10.2 %collective-permute-start.3 = (bf16[256,256]{1,0:T(8,128)(2,1)S(1)}, bf16[256,256]{1,0:T(8,128)(2,1)S(1)}, u32[]{:S(2)}, u32[]{:S(2)}) collective-permute-start(bf16[256,256]{1,0:T(8,128)(2,1)S(1)} %get-tuple-element.22), channel_id=1, source_target_pairs={{0,1},{1,0},{2,3},{3,2},{4,5},{5,4},{6,7},{7,6},{8,9},{9,8},{10,11... | collective-permute-start | bytes 393224 | tf_op jit(solution)/shard_map/ppermute | solution.py:31
  21.8 9.5 %collective-permute-start.5 = (bf16[256,256]{1,0:T(8,128)(2,1)S(1)}, bf16[256,256]{1,0:T(8,128)(2,1)S(1)}, u32[]{:S(2)}, u32[]{:S(2)}) collective-permute-start(bf16[256,256]{1,0:T(8,128)(2,1)S(1)} %get-tuple-element.23), channel_id=1, source_target_pairs={{0,3},{1,2},{2,1},{3,0},{4,7},{5,6},{6,5},{7,4},{8,11},{9,10},{10,... | collective-permute-start | bytes 393224 | tf_op jit(solution)/shard_map/ppermute | solution.py:31
  24.2 11.3 %collective-permute-start.4 = (bf16[256,256]{1,0:T(8,128)(2,1)S(1)}, bf16[256,256]{1,0:T(8,128)(2,1)S(1)}, u32[]{:S(2)}, u32[]{:S(2)}) collective-permute-start(bf16[256,256]{1,0:T(8,128)(2,1)S(1)} %get-tuple-element.20.refs_1_), channel_id=1, source_target_pairs={{0,2},{1,3},{2,0},{3,1},{4,6},{5,7},{6,4},{7,5},{8,10},{9,11},{10,... | collective-permute-start | bytes 393224 | tf_op jit(solution)/shard_map/ppermute | solution.py:31
  24.4 4.3 %collective-permute-start = (bf16[2,2,64,128]{3,2,1,0:T(8,128)(2,1)S(1)}, bf16[2,2,64,128]{3,2,1,0:T(8,128)(2,1)S(1)}, u32[]{:S(2)}, u32[]{:S(2)}) collective-permute-start(bf16[2,2,64,128]{3,2,1,0:T(8,128)(2,1)S(1)} %shard_map.174.refs_0_), channel_id=1, source_target_pairs={{0,16},{16,0},{1,17},{17,1},{2,18},{18,2},{3,19},{19,3},{4,20},{20... | collective-permute-start | bytes 196616 | tf_op jit(solution)/shard_map/ppermute | solution.py:31
  35.6 11.5 %collective-permute-start.8 = (bf16[256,256]{1,0:T(8,128)(2,1)S(1)}, bf16[256,256]{1,0:T(8,128)(2,1)S(1)}, u32[]{:S(2)}, u32[]{:S(2)}) collective-permute-start(bf16[256,256]{1,0:T(8,128)(2,1)S(1)} %shard_map.179.refs_0_), channel_id=1, source_target_pairs={{0,2},{1,3},{2,0},{3,1},{4,6},{5,7},{6,4},{7,5},{8,10},{9,11},{10,... | collective-permute-start | bytes 393224 | tf_op jit(solution)/shard_map/ppermute | solution.py:31
  36.0 12.2 %collective-permute-start.7 = (bf16[256,256]{1,0:T(8,128)(2,1)S(1)}, bf16[256,256]{1,0:T(8,128)(2,1)S(1)}, u32[]{:S(2)}, u32[]{:S(2)}) collective-permute-start(bf16[256,256]{1,0:T(8,128)(2,1)S(1)} %shard_map.179.refs_0_), channel_id=1, source_target_pairs={{0,1},{1,0},{2,3},{3,2},{4,5},{5,4},{6,7},{7,6},{8,9},{9,8},{10,11... | collective-permute-start | bytes 393224 | tf_op jit(solution)/shard_map/ppermute | solution.py:31
  38.9 10.3 %collective-permute-start.6 = (bf16[256,256]{1,0:T(8,128)(2,1)S(1)}, bf16[256,256]{1,0:T(8,128)(2,1)S(1)}, u32[]{:S(2)}, u32[]{:S(2)}) collective-permute-start(bf16[256,256]{1,0:T(8,128)(2,1)S(1)} %shard_map.179.refs_0_), channel_id=1, source_target_pairs={{0,3},{1,2},{2,1},{3,0},{4,7},{5,6},{6,5},{7,4},{8,11},{9,10},{10,... | collective-permute-start | bytes 393224 | tf_op jit(solution)/shard_map/ppermute | solution.py:31
  40.1 10.1 %all-to-all-start = ((bf16[4,2,64,128]{3,2,1,0:T(8,128)(2,1)}), bf16[4,2,64,128]{3,2,1,0:T(8,128)(2,1)S(1)}, u32[]{:S(2)}, u32[]{:S(2)}) async-start(bf16[4,2,64,128]{3,2,1,0:T(8,128)(2,1)} %shard_map.178.refs_4_), calls=%async_computation | async-start | bytes 262144 | tf_op jit(solution)/shard_map/all_to_all | solution.py:643
  44.0 23.1 %copy-start.2 = (bf16[2048,512]{1,0:T(8,128)(2,1)S(1)}, bf16[2048,512]{1,0:T(8,128)(2,1)}, u32[]{:S(2)}) copy-start(bf16[2048,512]{1,0:T(8,128)(2,1)} %grad.9) | copy-start | bytes 6291460
  44.1 14.7 %collective-permute-start.9 = (bf16[256,256]{1,0:T(8,128)(2,1)S(1)}, bf16[256,256]{1,0:T(8,128)(2,1)S(1)}, u32[]{:S(2)}, u32[]{:S(2)}) collective-permute-start(bf16[256,256]{1,0:T(8,128)(2,1)S(1)} %shard_map.179.refs_0_), channel_id=1, source_target_pairs={{0,16},{16,0},{1,17},{17,1},{2,18},{18,2},{3,19},{19,3},{4,20},{20... | collective-permute-start | bytes 393224 | tf_op jit(solution)/shard_map/ppermute | solution.py:31
  47.1 12.3 %collective-permute-start.11 = (bf16[256,256]{1,0:T(8,128)(2,1)S(1)}, bf16[256,256]{1,0:T(8,128)(2,1)S(1)}, u32[]{:S(2)}, u32[]{:S(2)}) collective-permute-start(bf16[256,256]{1,0:T(8,128)(2,1)S(1)} %collective-permute-done.8.refs_2_), channel_id=1, source_target_pairs={{0,16},{16,0},{1,17},{17,1},{2,18},{18,2},{3,19},{19,3},{4,20},{20... | collective-permute-start | bytes 393224 | tf_op jit(solution)/shard_map/ppermute | solution.py:31
  48.1 11.9 %collective-permute-start.10 = (bf16[256,256]{1,0:T(8,128)(2,1)S(1)}, bf16[256,256]{1,0:T(8,128)(2,1)S(1)}, u32[]{:S(2)}, u32[]{:S(2)}) collective-permute-start(bf16[256,256]{1,0:T(8,128)(2,1)S(1)} %collective-permute-done.7.refs_1_), channel_id=1, source_target_pairs={{0,16},{16,0},{1,17},{17,1},{2,18},{18,2},{3,19},{19,3},{4,20},{20... | collective-permute-start | bytes 393224 | tf_op jit(solution)/shard_map/ppermute | solution.py:31
  49.1 11.6 %collective-permute-start.12 = (bf16[256,256]{1,0:T(8,128)(2,1)S(1)}, bf16[256,256]{1,0:T(8,128)(2,1)S(1)}, u32[]{:S(2)}, u32[]{:S(2)}) collective-permute-start(bf16[256,256]{1,0:T(8,128)(2,1)S(1)} %collective-permute-done.6.refs_0_.refs_3_), channel_id=1, source_target_pairs={{0,16},{16,0},{1,17},{17,1},{2,18},{18,2},{3,19},{19,3},{4,20},{20... | collective-permute-start | bytes 393224 | tf_op jit(solution)/shard_map/ppermute | solution.py:31
  67.0 3.0 %collective-permute-start.13 = (f32[256,256]{1,0:T(8,128)S(1)}, f32[256,256]{1,0:T(8,128)S(1)}, u32[]{:S(2)}, u32[]{:S(2)}) collective-permute-start(f32[256,256]{1,0:T(8,128)S(1)} %get-tuple-element.28.refs_0_), channel_id=1, source_target_pairs={{0,4},{4,0},{8,12},{12,8},{1,5},{5,1},{9,13},{13,9},{2,6},{6,2},{1... | collective-permute-start | bytes 786440 | tf_op jit(solution)/shard_map/ppermute | solution.py:31
  69.5 8.4 %collective-permute-start.15 = (bf16[256,512]{1,0:T(8,128)(2,1)S(1)}, bf16[256,512]{1,0:T(8,128)(2,1)}, u32[]{:S(2)}, u32[]{:S(2)}) collective-permute-start(bf16[256,512]{1,0:T(8,128)(2,1)S(1)} %shard_map.182.refs_0_), channel_id=1, source_target_pairs={{0,4},{4,0},{8,12},{12,8},{1,5},{5,1},{9,13},{13,9},{2,6},{6,2},{1... | collective-permute-start | bytes 786440 | tf_op jit(solution)/shard_map/ppermute | solution.py:31
  70.8 10.1 %collective-permute-start.14 = (f32[256,256]{1,0:T(8,128)}, f32[256,256]{1,0:T(8,128)}, u32[]{:S(2)}, u32[]{:S(2)}) collective-permute-start(f32[256,256]{1,0:T(8,128)} %shard_map.185.refs_0_.refs_2_), channel_id=1, source_target_pairs={{0,8},{4,12},{8,0},{12,4},{1,9},{5,13},{9,1},{13,5},{2,10},{6,14},... | collective-permute-start | bytes 786440 | tf_op jit(solution)/shard_map/ppermute | solution.py:31
  73.7 23.0 %all-to-all-start.1 = ((f32[8,2,64,128]{3,2,1,0:T(8,128)}), f32[8,2,64,128]{3,2,1,0:T(8,128)}, u32[]{:S(2)}, u32[]{:S(2)}) async-start(f32[8,2,64,128]{3,2,1,0:T(8,128)} %copy-done.5), calls=%async_computation.1 | async-start | bytes 1048576 | tf_op jit(solution)/shard_map/all_to_all | solution.py:669
  78.9 13.8 %collective-permute-start.16 = (bf16[256,512]{1,0:T(8,128)(2,1)S(1)}, bf16[256,512]{1,0:T(8,128)(2,1)S(1)}, u32[]{:S(2)}, u32[]{:S(2)}) collective-permute-start(bf16[256,512]{1,0:T(8,128)(2,1)S(1)} %shard_map.187.wa), channel_id=1, source_target_pairs={{0,8},{4,12},{8,0},{12,4},{1,9},{5,13},{9,1},{13,5},{2,10},{6,14},... | collective-permute-start | bytes 786440 | tf_op jit(solution)/shard_map/ppermute | solution.py:31
  96.7 12.4 %all-to-all-start.2 = ((f32[8,8,256]{2,1,0:T(8,128)}), f32[8,8,256]{2,1,0:T(8,128)S(1)}, u32[]{:S(2)}, u32[]{:S(2)}) async-start(f32[8,8,256]{2,1,0:T(8,128)} %get-tuple-element.30), calls=%async_computation.2 | async-start | bytes 131072 | tf_op jit(solution)/shard_map/all_to_all | solution.py:673
  (26 other events, 133.4 us)

commit v3 on v2

--- a/solution.py
+++ b/solution.py
@@ -23,6 +23,7 @@
 SMEM = pl.BlockSpec(memory_space=pltpu.SMEM)
 VMEM = pl.BlockSpec(memory_space=pltpu.VMEM)
 ANY = pl.BlockSpec(memory_space=pl.ANY)
+HBM = pl.BlockSpec(memory_space=pltpu.HBM)
 
 
 def swap(value, axes, k):
@@ -31,7 +32,7 @@
     return lax.ppermute(value, axes, [(i, i ^ k) for i in range(n)])
 
 
-def params(mib=24):
+def params(mib=6):
     return pltpu.CompilerParams(vmem_limit_bytes=mib * MIB)
 
 
@@ -52,45 +53,65 @@
     return jnp.dot(a, b, precision=HIGHEST, preferred_element_type=F32)
 
 
-def project_kernel(ranks, mom, grad, basis, *refs):
-    out, b_hi, b_lo = refs[-3:]
-
-    @pl.when(pl.program_id(0) == 0)
-    def _():
-        hi, lo = halves(basis[...])
-        b_hi[...] = hi
-        b_lo[...] = lo
-
-    t_hi, t_lo = halves(mom[...] + grad[...].astype(F32))
-    acc = mm(t_hi, b_hi[...]) + (mm(t_hi, b_lo[...]) + mm(t_lo, b_hi[...]))
-    out[...] = acc.astype(out.dtype)
-
-
-def project(ranks, momentum, grad_q, basis, j, first, number, n_resp, n_head, dtype, after):
+def project_kernel(j, n_head, groups, ranks, mom, grad, basis, *refs):
+    n_out = len(groups)
+    total, outs = refs[-5], refs[-5 - n_out : -5]
+    grads, right, sems, right_sem = refs[-4:]
+    chunk = total.shape[0] // n_head
+    pieces = 2 if chunk % 32 == 0 else 1
+    size = chunk // pieces
+    copies = {}
+    order = [k for first, number in groups for k in range(first, first + number)]
+    fetch = pltpu.make_async_copy(basis, right, right_sem)
+    fetch.start()
+    for k in order:
+        at = ((ranks[0] ^ j) * n_head + (ranks[2] ^ k)) * chunk
+        copies[k] = []
+        for i in range(pieces):
+            src = pl.ds(pl.multiple_of(at + i * size, size), size)
+            dst = pl.ds(k * chunk + i * size, size)
+            n = k * pieces + i
+            copies[k].append(
+                pltpu.make_async_copy(mom.at[src, :], total.at[dst, :], sems.at[0, n])
+            )
+            copies[k].append(
+                pltpu.make_async_copy(grad.at[src, :], grads.at[dst, :], sems.at[1, n])
+            )
+        for c in copies[k]:
+            c.start()
+    fetch.wait()
+    b_hi, b_lo = halves(right[...])
+    for (first, number), out in zip(groups, outs):
+        for k in range(first, first + number):
+            for c in copies[k]:
+                c.wait()
+            rows = slice(k * chunk, (k + 1) * chunk)
+            t = total[rows, :] + grads[rows, :].astype(F32)
+            total[rows, :] = t
+            t_hi, t_lo = halves(t)
+            acc = mm(t_hi, b_hi) + (mm(t_hi, b_lo) + mm(t_lo, b_hi))
+            out[(k - first) * chunk : (k - first + 1) * chunk, :] = acc.astype(out.dtype)
+
+
+def project(ranks, momentum, grad_q, basis, j, groups, n_resp, n_head, dtype, after):
     rows, cols = momentum.shape
     rank = basis.shape[1]
     chunk = rows // (n_resp * n_head)
-
-    def rows_at(i, ranks):
-        return ((ranks[0] ^ j) * n_head + (ranks[2] ^ (first + i)), 0)
-
-    return pl.pallas_call(
-        project_kernel,
-        grid_spec=pltpu.PrefetchScalarGridSpec(
-            num_scalar_prefetch=1,
-            grid=(number,),
-            in_specs=[
-                pl.BlockSpec((chunk, cols), rows_at),
-                pl.BlockSpec((chunk, cols), rows_at),
-                pl.BlockSpec((cols, rank), lambda i, ranks: (0, 0)),
-            ]
-            + [ANY] * len(after),
-            out_specs=pl.BlockSpec((chunk, rank), lambda i, ranks: (i, 0)),
-            scratch_shapes=[pltpu.VMEM((cols, rank), BF16)] * 2,
-        ),
-        out_shape=jax.ShapeDtypeStruct((number * chunk, rank), dtype),
-        compiler_params=params(60),
-        cost_estimate=cost(6 * number * chunk * cols * rank, number * chunk * cols * 6),
+    seg = chunk * n_head
+    return pl.pallas_call(
+        functools.partial(project_kernel, j, n_head, groups),
+        in_specs=[SMEM] + [HBM] * 3 + [ANY] * len(after),
+        out_specs=[VMEM] * (len(groups) + 1),
+        scratch_shapes=[
+            pltpu.VMEM((seg, cols), BF16),
+            pltpu.VMEM((cols, rank), F32),
+            pltpu.SemaphoreType.DMA((2, 2 * n_head)),
+            pltpu.SemaphoreType.DMA,
+        ],
+        out_shape=[jax.ShapeDtypeStruct((n * chunk, rank), dtype) for _, n in groups]
+        + [jax.ShapeDtypeStruct((seg, cols), F32)],
+        compiler_params=params(14),
+        cost_estimate=cost(6 * seg * cols * rank, seg * cols * 6),
     )(ranks, momentum, grad_q, basis, *after)
 
 
@@ -139,70 +160,60 @@
     )(*parts, *after)
 
 
-def gram_kernel(n_resp, n_head, ranks, *refs):
-    chunks, (pcat, gram) = refs[: n_resp * n_head], refs[-2:]
+def gram_kernel(n_chunks, *refs):
+    chunks, (pcat, pcat_t, gram) = refs[:n_chunks], refs[-3:]
     size = chunks[0].shape[0]
-    for j in range(n_resp):
-        for k in range(n_head):
-            at = (ranks[0] ^ j) * n_head + (ranks[2] ^ k)
-            pcat[pl.ds(pl.multiple_of(at * size, size), size), :] = chunks[j * n_head + k][...]
+    for i in range(n_chunks):
+        pcat[i * size : (i + 1) * size, :] = chunks[i][...]
     p = pcat[...]
-    gram[...] = mm(p.T, p)
-
-
-def gather_gram(ranks, chunks, n_resp, n_head, after):
+    pt = p.T
+    pcat_t[...] = pt
+    gram[...] = mm(pt, p)
+
+
+def gather_gram(chunks, after):
     size, rank = chunks[0].shape
-    rows = size * n_resp * n_head
-    return pl.pallas_call(
-        functools.partial(gram_kernel, n_resp, n_head),
-        in_specs=[SMEM] + [VMEM] * len(chunks) + [ANY] * len(after),
-        out_specs=[VMEM] * 2,
+    rows = size * len(chunks)
+    return pl.pallas_call(
+        functools.partial(gram_kernel, len(chunks)),
+        in_specs=[VMEM] * len(chunks) + [ANY] * len(after),
+        out_specs=[VMEM] * 3,
         out_shape=[
             jax.ShapeDtypeStruct((rows, rank), BF16),
+            jax.ShapeDtypeStruct((rank, rows), BF16),
             jax.ShapeDtypeStruct((rank, rank), F32),
         ],
-        compiler_params=params(),
-        cost_estimate=cost(2 * rows * rank * rank, rows * rank * 4),
-    )(ranks, *chunks, *after)
-
-
-def back_part_kernel(pcat, mom, grad, out, acc):
-    i = pl.program_id(0)
-    t_hi, t_lo = halves(mom[...] + grad[...].astype(F32))
-    pt = pcat[...].T
-    part = mm(pt, t_hi) + mm(pt, t_lo)
-
-    @pl.when(i == 0)
-    def _():
-        acc[...] = part
-
-    @pl.when(i > 0)
-    def _():
-        acc[...] += part
-
-    @pl.when(i == pl.num_programs(0) - 1)
-    def _():
-        out[...] = acc[...].astype(BF16)
-
-
-def back_part(pcat, momentum, grad_q):
-    rows, cols = momentum.shape
-    rank = pcat.shape[1]
-    tile = min(rows, 512)
+        compiler_params=params(8),
+        cost_estimate=cost(2 * rows * rank * rank, rows * rank * 6),
+    )(*chunks, *after)
+
+
+def back_part_kernel(pcat_t, *refs):
+    totals, out = refs[:-1], refs[-1]
+    seg = totals[0].shape[0]
+    step = min(seg, 512)
+    acc = None
+    for j, total in enumerate(totals):
+        for i in range(0, seg, step):
+            t_hi, t_lo = halves(total[i : i + step, :])
+            pt = pcat_t[:, j * seg + i : j * seg + i + step]
+            part = mm(pt, t_hi) + mm(pt, t_lo)
+            acc = part if acc is None else acc + part
+    out[...] = acc.astype(BF16)
+
+
+def back_part(pcat_t, totals):
+    rank = pcat_t.shape[0]
+    seg, cols = totals[0].shape
+    rows = seg * len(totals)
     return pl.pallas_call(
         back_part_kernel,
-        grid=(rows // tile,),
-        in_specs=[
-            pl.BlockSpec((tile, rank), lambda i: (i, 0)),
-            pl.BlockSpec((tile, cols), lambda i: (i, 0)),
-            pl.BlockSpec((tile, cols), lambda i: (i, 0)),
-        ],
-        out_specs=pl.BlockSpec((rank, cols), lambda i: (0, 0)),
-        scratch_shapes=[pltpu.VMEM((rank, cols), F32)],
+        in_specs=[VMEM] * (1 + len(totals)),
+        out_specs=VMEM,
         out_shape=jax.ShapeDtypeStruct((rank, cols), BF16),
-        compiler_params=params(),
-        cost_estimate=cost(4 * rows * cols * rank, rows * cols * 6),
-    )(pcat, momentum, grad_q)
+        compiler_params=params(14),
+        cost_estimate=cost(4 * rows * cols * rank, rows * cols * 4),
+    )(pcat_t, *totals)
 
 
 def factor_panel(panel, off):
@@ -352,73 +363,89 @@
     )(x, wa, wb)
 
 
-def momentum_kernel(pcat, mom, grad, y, out):
-    out[...] = mom[...] + grad[...].astype(F32) - mm(pcat[...], y[...])
-
-
-def new_momentum(pcat, momentum, grad_q, y):
-    rows, cols = momentum.shape
-    rank = pcat.shape[1]
-    tile = min(rows, 256)
-    return pl.pallas_call(
-        momentum_kernel,
-        grid=(rows // tile,),
-        in_specs=[
-            pl.BlockSpec((tile, rank), lambda i: (i, 0)),
-            pl.BlockSpec((tile, cols), lambda i: (i, 0)),
-            pl.BlockSpec((tile, cols), lambda i: (i, 0)),
-            pl.BlockSpec((rank, cols), lambda i: (0, 0)),
+def row_blocks(ranks, n_resp, n_head, chunk):
+    return [
+        pl.multiple_of(((ranks[0] ^ j) * n_head + (ranks[2] ^ k)) * chunk, chunk)
+        for j in range(n_resp)
+        for k in range(n_head)
+    ]
+
+
+def momentum_kernel(n_resp, n_head, ranks, pcat, y, *refs):
+    totals, (out, held, sems) = refs[:-3], refs[-3:]
+    seg = totals[0].shape[0]
+    chunk = seg // n_head
+    copies = []
+    for i, at in enumerate(row_blocks(ranks, n_resp, n_head, chunk)):
+        rows = slice(i * chunk, (i + 1) * chunk)
+        off = i % n_head * chunk
+        total = totals[i // n_head][off : off + chunk, :]
+        held[rows, :] = total - mm(pcat[rows, :], y[...])
+        copies.append(
+            pltpu.make_async_copy(held.at[rows, :], out.at[pl.ds(at, chunk), :], sems.at[i])
+        )
+        copies[-1].start()
+    for c in copies:
+        c.wait()
+
+
+def new_momentum(ranks, pcat, totals, y, n_resp, n_head):
+    rows, rank = pcat.shape
+    cols = totals[0].shape[1]
+    return pl.pallas_call(
+        functools.partial(momentum_kernel, n_resp, n_head),
+        in_specs=[SMEM] + [VMEM] * (2 + len(totals)),
+        out_specs=HBM,
+        scratch_shapes=[
+            pltpu.VMEM((rows, cols), F32),
+            pltpu.SemaphoreType.DMA((n_resp * n_head,)),
         ],
-        out_specs=pl.BlockSpec((tile, cols), lambda i: (i, 0)),
         out_shape=jax.ShapeDtypeStruct((rows, cols), F32),
-        compiler_params=params(),
-        cost_estimate=cost(2 * rows * cols * rank, rows * cols * 10),
-    )(pcat, momentum, grad_q, y)
-
-
-def update_kernel(gain, pcat, x, bt, sums, upd, basis_out, z_hi, z_lo):
-    @pl.when(pl.program_id(0) == 0)
-    def _():
-        total = sums[0]
-        for i in range(1, sums.shape[0]):
-            total = total + sums[i]
-        scale = lax.rsqrt(total + norm_eps).T[:, :1]
-        scaled = bt[...] * scale
-        basis_out[...] = scaled.T
-        hi, lo = halves(gain * mm_full(x[...].T, scaled))
-        z_hi[...] = hi
-        z_lo[...] = lo
-
-    p = pcat[...]
-    upd[...] = (mm(p, z_hi[...]) + mm(p, z_lo[...])).astype(BF16)
-
-
-def final_update(pcat, x, bt, sums, gain):
+        compiler_params=params(14),
+        cost_estimate=cost(2 * rows * cols * rank, rows * cols * 8),
+    )(ranks, pcat, y, *totals)
+
+
+def update_kernel(gain, n_resp, n_head, ranks, pcat, x, bt, sums, upd, basis_out, held, sems):
+    total = sums[0]
+    for i in range(1, sums.shape[0]):
+        total = total + sums[i]
+    scale = lax.rsqrt(total + norm_eps).T[:, :1]
+    scaled = bt[...] * scale
+    z_hi, z_lo = halves(gain * mm_full(x[...].T, scaled))
+    basis_out[...] = scaled.T
+    chunk = pcat.shape[0] // (n_resp * n_head)
+    copies = []
+    for i, at in enumerate(row_blocks(ranks, n_resp, n_head, chunk)):
+        rows = slice(i * chunk, (i + 1) * chunk)
+        p = pcat[rows, :]
+        held[rows, :] = (mm(p, z_hi) + mm(p, z_lo)).astype(BF16)
+        copies.append(
+            pltpu.make_async_copy(held.at[rows, :], upd.at[pl.ds(at, chunk), :], sems.at[i])
+        )
+        copies[-1].start()
+    for c in copies:
+        c.wait()
+
+
+def final_update(ranks, pcat, x, bt, sums, gain, n_resp, n_head):
     rows, rank = pcat.shape
     cols = bt.shape[1]
-    tile = min(rows, 512)
-    whole = lambda i: (0, 0)
-    return pl.pallas_call(
-        functools.partial(update_kernel, gain),
-        grid=(rows // tile,),
-        in_specs=[
-            pl.BlockSpec((tile, rank), lambda i: (i, 0)),
-            pl.BlockSpec((rank, rank), whole),
-            pl.BlockSpec((rank, cols), whole),
-            pl.BlockSpec(sums.shape, lambda i: (0, 0, 0)),
+    return pl.pallas_call(
+        functools.partial(update_kernel, gain, n_resp, n_head),
+        in_specs=[SMEM] + [VMEM] * 4,
+        out_specs=[HBM, VMEM],
+        scratch_shapes=[
+            pltpu.VMEM((rows, cols), BF16),
+            pltpu.SemaphoreType.DMA((n_resp * n_head,)),
         ],
-        out_specs=[
-            pl.BlockSpec((tile, cols), lambda i: (i, 0)),
-            pl.BlockSpec((cols, rank), whole),
-        ],
-        scratch_shapes=[pltpu.VMEM((rank, cols), BF16)] * 2,
         out_shape=[
             jax.ShapeDtypeStruct((rows, cols), BF16),
             jax.ShapeDtypeStruct((cols, rank), F32),
         ],
-        compiler_params=params(),
+        compiler_params=params(10),
         cost_estimate=cost(4 * rows * cols * rank, rows * cols * 3),
-    )(pcat, x, bt, sums)
+    )(ranks, pcat, x, bt, sums)
 
 
 def group_of(counts, response):
@@ -537,7 +564,7 @@
             jax.ShapeDtypeStruct((2, cap, HD), F32),
         ],
         scratch_shapes=[pltpu.VMEM((total, HD), BF16)] * 2 + [pltpu.VMEM((total, HD), F32)] * 2,
-        compiler_params=params(32),
+        compiler_params=params(12),
         cost_estimate=cost(6_000_000_000, length * width * 8),
     )(ranks, counts, prompt_blocks, resp_blocks, q, sk, sv, go, pieces, *after)
 
@@ -612,25 +639,25 @@
         momentum.shape[0] * n_fsdp * momentum.shape[1] * n_resp * n_head / basis.shape[1]
     )
 
+    in_hbm = [pltpu.with_memory_space_constraint(a, pltpu.HBM) for a in (momentum, grad_q, basis)]
     half = n_head // 2
     groups = [(half, half), (0, half)] if half else [(0, n_head)]
 
-    sent, after = [], ()
-    for first, number in groups:
-        row = []
-        for j in range(1, n_resp):
-            row.append(
-                project(
-                    ranks, momentum, grad_q, basis, j, first, number, n_resp, n_head, BF16, after
-                )
-            )
-            after = (row[-1],)
-        sent.append(row)
-    arrived = [[swap(s, "resp", j + 1) for j, s in enumerate(row)] for row in sent]
-    mine = project(
-        ranks, momentum, grad_q, basis, 0, 0, n_head, n_resp, n_head, F32, after
+    sent, totals, after = [], {}, ()
+    for j in range(1, n_resp):
+        *outs, totals[j] = project(
+            ranks, *in_hbm, j, groups, n_resp, n_head, BF16, after
+        )
+        after = (outs[0],)
+        sent.append(outs)
+    arrived = [
+        [swap(outs[g], "resp", j + 1) for j, outs in enumerate(sent)] for g in range(len(groups))
+    ]
+    mine, totals[0] = project(
+        ranks, *in_hbm, 0, [(0, n_head)], n_resp, n_head, F32, after
     )
-    packed = pack_prompts(prompt_keys, prompt_values, after)
+    totals = [totals[j] for j in range(n_resp)]
+    packed = pack_prompts(prompt_keys, prompt_values, (mine,))
     stored = [packed] + [swap(packed, "resp", j) for j in range(1, n_resp)]
 
     split, after = {}, ()
@@ -643,7 +670,7 @@
     pieces = lax.all_to_all(chosen, "fsdp", 0, 0, tiled=True)
     far_first = [k for first, number in groups for k in range(first, first + number) if k]
     summands = {k: swap(split[k], "head", k) for k in far_first}
-    piece0 = sum_parts([split[0]] + [summands[k] for k in range(1, n_head)], BF16, (chosen,))
+    piece0 = sum_parts([split[0]] + [summands[k] for k in range(1, n_head)], BF16, (pieces,))
 
     along = {0: piece0}
     for k in far_first:
@@ -656,10 +683,10 @@
         ranks, counts, prompt_blocks, resp_blocks, queries, self_keys, self_values, d_out, pieces,
         (along[n_head - 1],),
     )
-    pcat, gram = gather_gram(ranks, chunks, n_resp, n_head, (part,))
+    pcat, pcat_t, gram = gather_gram(chunks, (part,))
 
     bits = [1 << b for b in range(n_fsdp.bit_length() - 1)]
-    w = back_part(pcat, momentum, grad_q)
+    w = back_part(pcat_t, totals)
     addressed = address_parts(ranks, counts, owner_slot, part, n_resp, n_fsdp, (w,))
     for bit in bits[:-1]:
         gram = sum_parts([gram, swap(gram, "fsdp", bit)], F32)
@@ -671,9 +698,9 @@
     x = inverse_factor(*gram_parts)
     bt, y, squares = back_full(x, w, w_other, n_resp * n_head)
     sums = lax.all_to_all(squares, ("resp", "head"), 0, 0, tiled=True)
-    momentum_out = new_momentum(pcat, momentum, grad_q, y)
+    momentum_out = new_momentum(ranks, pcat, totals, y, n_resp, n_head)
     prompt_grad = collect(ranks, counts, owner_slot, returned, prompt_keys.shape[0])
-    update, basis_out = final_update(pcat, x, bt, sums, gain)
+    update, basis_out = final_update(ranks, pcat, x, bt, sums, gain, n_resp, n_head)
     return (dq, resp_grad, prompt_grad, update, momentum_out, basis_out)
 
 

time: 116 us -> 104 us (0.90)
  local copies, waits for them, and re-layouts: 17 us -> 7.37 us
  Pallas kernels: 50.6 us -> 43.3 us
  blocking collectives: 0 us -> 7.22 us
  starting transfers between devices: 33.2 us -> 31 us
    unnamed x60 -> x36, local copies, waits for them, and re-layouts: 17 us -> 7.37 us
    all_to_all x0 -> x1, blocking collectives: none -> 7.22 us  [on_device(): pieces = lax.all_to_all(chosen, 'fsdp', 0, 0, tiled=True)]
    pallas_call x7 -> x6, Pallas kernels: 24.2 us -> 19 us  [the longest x2 10 us: project(): pl.pallas_call(functools.partial(project_kernel, j, n_head, groups), in_s...]
    all_to_all x1 -> x0, starting transfers between devices: 3.33 us -> none  [on_device(): pieces = lax.all_to_all(chosen, 'fsdp', 0, 0, tiled=True)]
    pallas_call x3, Pallas kernels: 1.83 us -> 0.15 us  [sum_parts(): pl.pallas_call(functools.partial(sum_kernel, len(parts)), in_specs=[VMEM]...]
    ppermute x17, starting transfers between devices: 21.7 us -> 23 us  [swap(): return lax.ppermute(value, axes, [(i, i ^ k) for i in range(n)])]
  transfers between devices with their start and end apart: 20 -> 19, of which waited for: 5 -> 4; matrix products, arithmetic and copies ran while one was open for 0% -> 0% of each run, Pallas kernels for 37% -> 32%
where the time goes in v3:
time: 104 us; the launch traced here: 103 us
  Pallas kernels  43.3 us (42%)
  starting transfers between devices  31 us (30%)
  waiting for transfers between devices  12.8 us (12%)
  local copies, waits for them, and re-layouts  7.37 us (7%)
  blocking collectives  7.22 us (7%)
  between operations  1.72 us (2%)
    ppermute x17, starting transfers between devices, swap(): return lax.ppermute(value, axes, [(i, i ^ k) for i in range(n)])  23 us
    ppermute x17, waiting for transfers between devices, swap(): return lax.ppermute(value, axes, [(i, i ^ k) for i in range(n)])  12.8 us
    pallas_call x1, Pallas kernels, inverse_factor(): pl.pallas_call(functools.partial(cholesky_kernel, len(parts)), in_specs=[...  11.8 us
    pallas_call x2, Pallas kernels, project(): pl.pallas_call(functools.partial(project_kernel, j, n_head, groups), in_s...  10 us
    unnamed x36, local copies, waits for them, and re-layouts  7.37 us
    all_to_all x1, blocking collectives, on_device(): pieces = lax.all_to_all(chosen, 'fsdp', 0, 0, tiled=True)  7.22 us
    pallas_call x1, Pallas kernels, attention(): pl.pallas_call(attention_kernel, in_specs=[SMEM] * 4 + [VMEM] * 5 + [ANY]...  6.47 us
    all_to_all x1, starting transfers between devices, on_device(): sums = lax.all_to_all(squares, ('resp', 'head'), 0, 0, tiled=True)  4.28 us
  transfers between devices with their start and end apart: 19, of which 4 were waited for; matrix products, arithmetic and copies ran while one was open for 0% of the time, Pallas kernels for 32%

profile of v3, /device:TPU:0, one launch (start us, length us, event | category | flops | bytes accessed | tf_op | source)
XLA Modules:
  0.0 103.5 jit_solution(14261523282889688523)
XLA Ops:
  0.7 5.0 %shard_map.172 = (bf16[512,256]{1,0:T(8,128)(2,1)S(1)}, bf16[512,256]{1,0:T(8,128)(2,1)S(1)}, f32[1024,512]{1,0:T(8,128)S(1)}) custom-call(s32[3]{0:T(128)S(1)} %pad_add_fusion.ranks, f32[2048,512]{1,0:T(8,128)} %mom.3, bf16[2048,512]{1,0:T(8,128)(2,1)} %grad.3, f32[512,256]{1,0:T(8,128)} %basis.3), custom_call_target="tpu_custom_call" | custom-call | flops 805306368 | bytes 3145728 | tf_op jit(solution)/shard_map/pallas_call | solution.py:101
  5.7 3.0 %collective-permute-start.2 = (bf16[512,256]{1,0:T(8,128)(2,1)S(1)}, bf16[512,256]{1,0:T(8,128)(2,1)S(1)}, u32[]{:S(2)}, u32[]{:S(2)}) collective-permute-start(bf16[512,256]{1,0:T(8,128)(2,1)S(1)} %get-tuple-element.26.refs_0_), channel_id=1, source_target_pairs={{0,16},{16,0},{1,17},{17,1},{2,18},{18,2},{3,19},{19,3},{4,20},{20... | collective-permute-start | bytes 786440 | tf_op jit(solution)/shard_map/ppermute | solution.py:32
  8.8 5.0 %shard_map.173 = (f32[1024,256]{1,0:T(8,128)S(1)}, f32[1024,512]{1,0:T(8,128)S(1)}) custom-call(s32[3]{0:T(128)S(1)} %pad_add_fusion.ranks, f32[2048,512]{1,0:T(8,128)} %mom.3, bf16[2048,512]{1,0:T(8,128)(2,1)} %grad.3, f32[512,256]{1,0:T(8,128)} %basis.3, bf16[512,256]{1,0:T(8,128)(2,1)S(1)} %get-tuple-element.26.refs_0_), custom_call_target="tpu_custom_call" | custom-call | flops 805306368 | bytes 3145728 | tf_op jit(solution)/shard_map/pallas_call | solution.py:101
  14.0 2.0 %collective-permute-start = (bf16[2,2,64,128]{3,2,1,0:T(8,128)(2,1)S(1)}, bf16[2,2,64,128]{3,2,1,0:T(8,128)(2,1)S(1)}, u32[]{:S(2)}, u32[]{:S(2)}) collective-permute-start(bf16[2,2,64,128]{3,2,1,0:T(8,128)(2,1)S(1)} %shard_map.174.refs_0_), channel_id=1, source_target_pairs={{0,16},{16,0},{1,17},{17,1},{2,18},{18,2},{3,19},{19,3},{4,20},{20... | collective-permute-start | bytes 196616 | tf_op jit(solution)/shard_map/ppermute | solution.py:32
  16.0 5.3 %collective-permute-done.1.refs_0_ = bf16[512,256]{1,0:T(8,128)(2,1)S(1)} collective-permute-done((bf16[512,256]{1,0:T(8,128)(2,1)S(1)}, bf16[512,256]{1,0:T(8,128)(2,1)S(1)}, u32[]{:S(2)}, u32[]{:S(2)}) %collective-permute-start.1) | collective-permute-done | bytes 262176 | tf_op jit(solution)/shard_map/ppermute | solution.py:32
  21.4 1.9 %collective-permute-start.3 = (bf16[256,256]{1,0:T(8,128)(2,1)S(1)}, bf16[256,256]{1,0:T(8,128)(2,1)S(1)}, u32[]{:S(2)}, u32[]{:S(2)}) collective-permute-start(bf16[256,256]{1,0:T(8,128)(2,1)S(1)} %get-tuple-element.31), channel_id=1, source_target_pairs={{0,1},{1,0},{2,3},{3,2},{4,5},{5,4},{6,7},{7,6},{8,9},{9,8},{10,11... | collective-permute-start | bytes 393224 | tf_op jit(solution)/shard_map/ppermute | solution.py:32
  23.3 2.5 %collective-permute-start.5 = (bf16[256,256]{1,0:T(8,128)(2,1)S(1)}, bf16[256,256]{1,0:T(8,128)(2,1)S(1)}, u32[]{:S(2)}, u32[]{:S(2)}) collective-permute-start(bf16[256,256]{1,0:T(8,128)(2,1)S(1)} %get-tuple-element.32), channel_id=1, source_target_pairs={{0,3},{1,2},{2,1},{3,0},{4,7},{5,6},{6,5},{7,4},{8,11},{9,10},{10,... | collective-permute-start | bytes 393224 | tf_op jit(solution)/shard_map/ppermute | solution.py:32
  26.6 7.2 %all_to_all.15.refs_4_.pieces = bf16[4,2,64,128]{3,2,1,0:T(8,128)(2,1)S(1)} all-to-all(bf16[4,2,64,128]{3,2,1,0:T(8,128)(2,1)S(1)} %shard_map.177), channel_id=1, replica_groups=mesh['resp'=2,'fsdp'=4,'head'=4] {'fsdp'}, dimensions={0} | all-to-all | bytes 262144 | tf_op jit(solution)/shard_map/all_to_all | solution.py:670
  33.8 2.1 %collective-permute-done.4.refs_2_ = bf16[256,256]{1,0:T(8,128)(2,1)S(1)} collective-permute-done((bf16[256,256]{1,0:T(8,128)(2,1)S(1)}, bf16[256,256]{1,0:T(8,128)(2,1)S(1)}, u32[]{:S(2)}, u32[]{:S(2)}) %collective-permute-start.4) | collective-permute-done | bytes 131104 | tf_op jit(solution)/shard_map/ppermute | solution.py:32
  36.8 2.5 %collective-permute-start.7 = (bf16[256,256]{1,0:T(8,128)(2,1)S(1)}, bf16[256,256]{1,0:T(8,128)(2,1)S(1)}, u32[]{:S(2)}, u32[]{:S(2)}) collective-permute-start(bf16[256,256]{1,0:T(8,128)(2,1)S(1)} %shard_map.178.refs_0_), channel_id=1, source_target_pairs={{0,1},{1,0},{2,3},{3,2},{4,5},{5,4},{6,7},{7,6},{8,9},{9,8},{10,11... | collective-permute-start | bytes 393224 | tf_op jit(solution)/shard_map/ppermute | solution.py:32
  41.1 1.6 %collective-permute-start.9 = (bf16[256,256]{1,0:T(8,128)(2,1)S(1)}, bf16[256,256]{1,0:T(8,128)(2,1)S(1)}, u32[]{:S(2)}, u32[]{:S(2)}) collective-permute-start(bf16[256,256]{1,0:T(8,128)(2,1)S(1)} %shard_map.178.refs_0_), channel_id=1, source_target_pairs={{0,16},{16,0},{1,17},{17,1},{2,18},{18,2},{3,19},{19,3},{4,20},{20... | collective-permute-start | bytes 393224 | tf_op jit(solution)/shard_map/ppermute | solution.py:32
  42.7 4.8 %collective-permute-done.8.refs_2_ = bf16[256,256]{1,0:T(8,128)(2,1)S(1)} collective-permute-done((bf16[256,256]{1,0:T(8,128)(2,1)S(1)}, bf16[256,256]{1,0:T(8,128)(2,1)S(1)}, u32[]{:S(2)}, u32[]{:S(2)}) %collective-permute-start.8) | collective-permute-done | bytes 131104 | tf_op jit(solution)/shard_map/ppermute | solution.py:32
  47.5 1.5 %collective-permute-start.11 = (bf16[256,256]{1,0:T(8,128)(2,1)S(1)}, bf16[256,256]{1,0:T(8,128)(2,1)S(1)}, u32[]{:S(2)}, u32[]{:S(2)}) collective-permute-start(bf16[256,256]{1,0:T(8,128)(2,1)S(1)} %collective-permute-done.8.refs_2_), channel_id=1, source_target_pairs={{0,16},{16,0},{1,17},{17,1},{2,18},{18,2},{3,19},{19,3},{4,20},{20... | collective-permute-start | bytes 393224 | tf_op jit(solution)/shard_map/ppermute | solution.py:32
  49.6 1.5 %collective-permute-start.12 = (bf16[256,256]{1,0:T(8,128)(2,1)S(1)}, bf16[256,256]{1,0:T(8,128)(2,1)S(1)}, u32[]{:S(2)}, u32[]{:S(2)}) collective-permute-start(bf16[256,256]{1,0:T(8,128)(2,1)S(1)} %collective-permute-done.6.refs_0_.refs_3_), channel_id=1, source_target_pairs={{0,16},{16,0},{1,17},{17,1},{2,18},{18,2},{3,19},{19,3},{4,20},{20... | collective-permute-start | bytes 393224 | tf_op jit(solution)/shard_map/ppermute | solution.py:32
  51.1 6.5 %shard_map.179 = (bf16[256,1024]{1,0:T(8,128)(2,1)}, bf16[2,256,128]{2,1,0:T(8,128)(2,1)}, f32[2,256,128]{2,1,0:T(8,128)S(1)}) custom-call(s32[3]{0:T(128)S(1)} %pad_add_fusion.ranks, s32[4]{0:T(128)S(1)} %copy-done.7, s32[4]{0:T(128)S(1)} %copy-done.13, s32[1]{0:T(128)S(6)} %copy.19.resp_blocks, bf16[256,1024]{1,0:T(8,128)(2,1)S(1)} %copy-done.9, ...), custom_call_target="tpu_custom_call" | custom-call | flops 6000000000 | bytes 2097152 | tf_op jit(solution)/shard_map/pallas_call | solution.py:557
  61.1 1.6 %collective-permute-start.14 = (f32[256,256]{1,0:T(8,128)S(1)}, f32[256,256]{1,0:T(8,128)}, u32[]{:S(2)}, u32[]{:S(2)}) collective-permute-start(f32[256,256]{1,0:T(8,128)S(1)} %shard_map.184.refs_0_.refs_2_), channel_id=1, source_target_pairs={{0,8},{4,12},{8,0},{12,4},{1,9},{5,13},{9,1},{13,5},{2,10},{6,14},... | collective-permute-start | bytes 786440 | tf_op jit(solution)/shard_map/ppermute | solution.py:32
  64.0 3.7 %all-to-all-start.1 = ((f32[8,2,64,128]{3,2,1,0:T(8,128)}), f32[8,2,64,128]{3,2,1,0:T(8,128)S(1)}, u32[]{:S(2)}, u32[]{:S(2)}) async-start(f32[8,2,64,128]{3,2,1,0:T(8,128)} %shard_map.182), calls=%async_computation.1 | async-start | bytes 1048576 | tf_op jit(solution)/shard_map/all_to_all | solution.py:696
  67.8 1.8 %collective-permute-start.16 = (bf16[256,512]{1,0:T(8,128)(2,1)S(1)}, bf16[256,512]{1,0:T(8,128)(2,1)S(1)}, u32[]{:S(2)}, u32[]{:S(2)}) collective-permute-start(bf16[256,512]{1,0:T(8,128)(2,1)S(1)} %shard_map.186.wa), channel_id=1, source_target_pairs={{0,8},{4,12},{8,0},{12,4},{1,9},{5,13},{9,1},{13,5},{2,10},{6,14},... | collective-permute-start | bytes 786440 | tf_op jit(solution)/shard_map/ppermute | solution.py:32
  69.6 11.8 %shard_map.185.x = f32[256,256]{1,0:T(8,128)S(1)} custom-call(f32[256,256]{1,0:T(8,128)S(1)} %shard_map.184.refs_0_.refs_2_, f32[256,256]{1,0:T(8,128)} %collective-permute-done.14.refs_1_), custom_call_target="tpu_custom_call" | custom-call | flops 10000000000 | bytes 1048576 | tf_op jit(solution)/shard_map/pallas_call | solution.py:326
  81.9 2.4 %shard_map.187 = (f32[256,512]{1,0:T(8,128)S(1)}, bf16[256,512]{1,0:T(8,128)(2,1)S(1)}, f32[8,8,256]{2,1,0:T(8,128)}) custom-call(f32[256,256]{1,0:T(8,128)S(1)} %shard_map.185.x, bf16[256,512]{1,0:T(8,128)(2,1)S(1)} %shard_map.186.wa, bf16[256,512]{1,0:T(8,128)(2,1)S(1)} %collective-permute-done.16.wb), custom_call_target="tpu_custom_call" | custom-call | flops 805306368 | bytes 1572864 | tf_op jit(solution)/shard_map/pallas_call | solution.py:352
  85.8 4.3 %all-to-all-start.2 = ((f32[8,8,256]{2,1,0:T(8,128)}), f32[8,8,256]{2,1,0:T(8,128)S(1)}, u32[]{:S(2)}, u32[]{:S(2)}) async-start(f32[8,8,256]{2,1,0:T(8,128)} %get-tuple-element.42), calls=%async_computation.2 | async-start | bytes 131072 | tf_op jit(solution)/shard_map/all_to_all | solution.py:700
  91.4 1.6 %copy-done.1 = f32[1024,512]{1,0:T(8,128)S(1)} copy-done((f32[1024,512]{1,0:T(8,128)S(1)}, f32[1024,512]{1,0:T(8,128)}, u32[]{:S(2)}) %copy-start.1) | copy-done | bytes 2097176
  94.3 2.8 %shard_map.189 = f32[2048,512]{1,0:T(8,128)} custom-call(s32[3]{0:T(128)S(1)} %pad_add_fusion.ranks, bf16[2048,256]{1,0:T(8,128)(2,1)S(1)} %copy-done.3, bf16[256,512]{1,0:T(8,128)(2,1)S(1)} %get-tuple-element.44.y, f32[1024,512]{1,0:T(8,128)S(1)} %copy-done.1, f32[1024,512]{1,0:T(8,128)S(1)} %get-tuple-element.38.refs_1_), custom_call_target="tpu_custom_call" | custom-call | flops 536870912 | bytes 8388608 | tf_op jit(solution)/shard_map/pallas_call | solution.py:395
  99.1 4.2 %shard_map.188 = (bf16[2048,512]{1,0:T(8,128)(2,1)}, f32[512,256]{1,0:T(8,128)}) custom-call(s32[3]{0:T(128)S(1)} %pad_add_fusion.ranks, bf16[2048,256]{1,0:T(8,128)(2,1)S(1)} %copy-done.4, f32[256,256]{1,0:T(8,128)S(1)} %copy-done.17, f32[256,512]{1,0:T(8,128)S(1)} %copy-done.15, f32[8,8,256]{2,1,0:T(8,128)S(1)} %all-to-all-done.2.sums), custom_call_target="tpu_custom_call" | custom-call | flops 1073741824 | bytes 3145728 | tf_op jit(solution)/shard_map/pallas_call | solution.py:434
  (70 shorter events, 15.2 us)
Async XLA Ops:
  5.7 10.3 %collective-permute-start.2 = (bf16[512,256]{1,0:T(8,128)(2,1)S(1)}, bf16[512,256]{1,0:T(8,128)(2,1)S(1)}, u32[]{:S(2)}, u32[]{:S(2)}) collective-permute-start(bf16[512,256]{1,0:T(8,128)(2,1)S(1)} %get-tuple-element.26.refs_0_), channel_id=1, source_target_pairs={{0,16},{16,0},{1,17},{17,1},{2,18},{18,2},{3,19},{19,3},{4,20},{20... | collective-permute-start | bytes 786440 | tf_op jit(solution)/shard_map/ppermute | solution.py:32
  8.7 12.6 %collective-permute-start.1 = (bf16[512,256]{1,0:T(8,128)(2,1)S(1)}, bf16[512,256]{1,0:T(8,128)(2,1)S(1)}, u32[]{:S(2)}, u32[]{:S(2)}) collective-permute-start(bf16[512,256]{1,0:T(8,128)(2,1)S(1)} %get-tuple-element.28), channel_id=1, source_target_pairs={{0,16},{16,0},{1,17},{17,1},{2,18},{18,2},{3,19},{19,3},{4,20},{20... | collective-permute-start | bytes 786440 | tf_op jit(solution)/shard_map/ppermute | solution.py:32
  13.9 45.3 %copy-start = (f32[1024,512]{1,0:T(8,128)}, f32[1024,512]{1,0:T(8,128)S(1)}, u32[]{:S(2)}) copy-start(f32[1024,512]{1,0:T(8,128)S(1)} %get-tuple-element.37.refs_0_) | copy-start | bytes 6291460
  13.9 37.1 %copy-start.9 = (bf16[256,1024]{1,0:T(8,128)(2,1)S(1)}, bf16[256,1024]{1,0:T(8,128)(2,1)}, u32[]{:S(2)}) copy-start(bf16[256,1024]{1,0:T(8,128)(2,1)} %q.1) | copy-start | bytes 1572868
  14.0 37.1 %copy-start.10 = (bf16[256,1024]{1,0:T(8,128)(2,1)S(1)}, bf16[256,1024]{1,0:T(8,128)(2,1)}, u32[]{:S(2)}) copy-start(bf16[256,1024]{1,0:T(8,128)(2,1)} %go.1) | copy-start | bytes 1572868
  14.0 37.1 %copy-start.11 = (bf16[256,128]{1,0:T(8,128)(2,1)S(1)}, bf16[256,128]{1,0:T(8,128)(2,1)}, u32[]{:S(2)}) copy-start(bf16[256,128]{1,0:T(8,128)(2,1)} %sk.1) | copy-start | bytes 196612
  14.0 37.1 %copy-start.12 = (bf16[256,128]{1,0:T(8,128)(2,1)S(1)}, bf16[256,128]{1,0:T(8,128)(2,1)}, u32[]{:S(2)}) copy-start(bf16[256,128]{1,0:T(8,128)(2,1)} %sv.1) | copy-start | bytes 196612
  14.0 11.9 %collective-permute-start = (bf16[2,2,64,128]{3,2,1,0:T(8,128)(2,1)S(1)}, bf16[2,2,64,128]{3,2,1,0:T(8,128)(2,1)S(1)}, u32[]{:S(2)}, u32[]{:S(2)}) collective-permute-start(bf16[2,2,64,128]{3,2,1,0:T(8,128)(2,1)S(1)} %shard_map.174.refs_0_), channel_id=1, source_target_pairs={{0,16},{16,0},{1,17},{17,1},{2,18},{18,2},{3,19},{19,3},{4,20},{20... | collective-permute-start | bytes 196616 | tf_op jit(solution)/shard_map/ppermute | solution.py:32
  21.4 12.4 %collective-permute-start.3 = (bf16[256,256]{1,0:T(8,128)(2,1)S(1)}, bf16[256,256]{1,0:T(8,128)(2,1)S(1)}, u32[]{:S(2)}, u32[]{:S(2)}) collective-permute-start(bf16[256,256]{1,0:T(8,128)(2,1)S(1)} %get-tuple-element.31), channel_id=1, source_target_pairs={{0,1},{1,0},{2,3},{3,2},{4,5},{5,4},{6,7},{7,6},{8,9},{9,8},{10,11... | collective-permute-start | bytes 393224 | tf_op jit(solution)/shard_map/ppermute | solution.py:32
  23.3 10.5 %collective-permute-start.5 = (bf16[256,256]{1,0:T(8,128)(2,1)S(1)}, bf16[256,256]{1,0:T(8,128)(2,1)S(1)}, u32[]{:S(2)}, u32[]{:S(2)}) collective-permute-start(bf16[256,256]{1,0:T(8,128)(2,1)S(1)} %get-tuple-element.32), channel_id=1, source_target_pairs={{0,3},{1,2},{2,1},{3,0},{4,7},{5,6},{6,5},{7,4},{8,11},{9,10},{10,... | collective-permute-start | bytes 393224 | tf_op jit(solution)/shard_map/ppermute | solution.py:32
  25.8 10.2 %collective-permute-start.4 = (bf16[256,256]{1,0:T(8,128)(2,1)S(1)}, bf16[256,256]{1,0:T(8,128)(2,1)S(1)}, u32[]{:S(2)}, u32[]{:S(2)}) collective-permute-start(bf16[256,256]{1,0:T(8,128)(2,1)S(1)} %get-tuple-element.29.refs_1_), channel_id=1, source_target_pairs={{0,2},{1,3},{2,0},{3,1},{4,6},{5,7},{6,4},{7,5},{8,10},{9,11},{10,... | collective-permute-start | bytes 393224 | tf_op jit(solution)/shard_map/ppermute | solution.py:32
  36.0 11.5 %collective-permute-start.8 = (bf16[256,256]{1,0:T(8,128)(2,1)S(1)}, bf16[256,256]{1,0:T(8,128)(2,1)S(1)}, u32[]{:S(2)}, u32[]{:S(2)}) collective-permute-start(bf16[256,256]{1,0:T(8,128)(2,1)S(1)} %shard_map.178.refs_0_), channel_id=1, source_target_pairs={{0,2},{1,3},{2,0},{3,1},{4,6},{5,7},{6,4},{7,5},{8,10},{9,11},{10,... | collective-permute-start | bytes 393224 | tf_op jit(solution)/shard_map/ppermute | solution.py:32
  36.8 12.2 %collective-permute-start.7 = (bf16[256,256]{1,0:T(8,128)(2,1)S(1)}, bf16[256,256]{1,0:T(8,128)(2,1)S(1)}, u32[]{:S(2)}, u32[]{:S(2)}) collective-permute-start(bf16[256,256]{1,0:T(8,128)(2,1)S(1)} %shard_map.178.refs_0_), channel_id=1, source_target_pairs={{0,1},{1,0},{2,3},{3,2},{4,5},{5,4},{6,7},{7,6},{8,9},{9,8},{10,11... | collective-permute-start | bytes 393224 | tf_op jit(solution)/shard_map/ppermute | solution.py:32
  39.3 10.3 %collective-permute-start.6 = (bf16[256,256]{1,0:T(8,128)(2,1)S(1)}, bf16[256,256]{1,0:T(8,128)(2,1)S(1)}, u32[]{:S(2)}, u32[]{:S(2)}) collective-permute-start(bf16[256,256]{1,0:T(8,128)(2,1)S(1)} %shard_map.178.refs_0_), channel_id=1, source_target_pairs={{0,3},{1,2},{2,1},{3,0},{4,7},{5,6},{6,5},{7,4},{8,11},{9,10},{10,... | collective-permute-start | bytes 393224 | tf_op jit(solution)/shard_map/ppermute | solution.py:32
  41.1 16.4 %collective-permute-start.9 = (bf16[256,256]{1,0:T(8,128)(2,1)S(1)}, bf16[256,256]{1,0:T(8,128)(2,1)S(1)}, u32[]{:S(2)}, u32[]{:S(2)}) collective-permute-start(bf16[256,256]{1,0:T(8,128)(2,1)S(1)} %shard_map.178.refs_0_), channel_id=1, source_target_pairs={{0,16},{16,0},{1,17},{17,1},{2,18},{18,2},{3,19},{19,3},{4,20},{20... | collective-permute-start | bytes 393224 | tf_op jit(solution)/shard_map/ppermute | solution.py:32
  47.5 10.0 %collective-permute-start.11 = (bf16[256,256]{1,0:T(8,128)(2,1)S(1)}, bf16[256,256]{1,0:T(8,128)(2,1)S(1)}, u32[]{:S(2)}, u32[]{:S(2)}) collective-permute-start(bf16[256,256]{1,0:T(8,128)(2,1)S(1)} %collective-permute-done.8.refs_2_), channel_id=1, source_target_pairs={{0,16},{16,0},{1,17},{17,1},{2,18},{18,2},{3,19},{19,3},{4,20},{20... | collective-permute-start | bytes 393224 | tf_op jit(solution)/shard_map/ppermute | solution.py:32
  49.0 8.5 %collective-permute-start.10 = (bf16[256,256]{1,0:T(8,128)(2,1)S(1)}, bf16[256,256]{1,0:T(8,128)(2,1)S(1)}, u32[]{:S(2)}, u32[]{:S(2)}) collective-permute-start(bf16[256,256]{1,0:T(8,128)(2,1)S(1)} %collective-permute-done.7.refs_1_), channel_id=1, source_target_pairs={{0,16},{16,0},{1,17},{17,1},{2,18},{18,2},{3,19},{19,3},{4,20},{20... | collective-permute-start | bytes 393224 | tf_op jit(solution)/shard_map/ppermute | solution.py:32
  49.6 8.0 %collective-permute-start.12 = (bf16[256,256]{1,0:T(8,128)(2,1)S(1)}, bf16[256,256]{1,0:T(8,128)(2,1)S(1)}, u32[]{:S(2)}, u32[]{:S(2)}) collective-permute-start(bf16[256,256]{1,0:T(8,128)(2,1)S(1)} %collective-permute-done.6.refs_0_.refs_3_), channel_id=1, source_target_pairs={{0,16},{16,0},{1,17},{17,1},{2,18},{18,2},{3,19},{19,3},{4,20},{20... | collective-permute-start | bytes 393224 | tf_op jit(solution)/shard_map/ppermute | solution.py:32
  59.2 1.9 %collective-permute-start.13 = (f32[256,256]{1,0:T(8,128)S(1)}, f32[256,256]{1,0:T(8,128)S(1)}, u32[]{:S(2)}, u32[]{:S(2)}) collective-permute-start(f32[256,256]{1,0:T(8,128)S(1)} %get-tuple-element.40.refs_0_), channel_id=1, source_target_pairs={{0,4},{4,0},{8,12},{12,8},{1,5},{5,1},{9,13},{13,9},{2,6},{6,2},{1... | collective-permute-start | bytes 786440 | tf_op jit(solution)/shard_map/ppermute | solution.py:32
  60.5 7.2 %collective-permute-start.15 = (bf16[256,512]{1,0:T(8,128)(2,1)S(1)}, bf16[256,512]{1,0:T(8,128)(2,1)S(1)}, u32[]{:S(2)}, u32[]{:S(2)}) collective-permute-start(bf16[256,512]{1,0:T(8,128)(2,1)S(1)} %shard_map.181.refs_0_), channel_id=1, source_target_pairs={{0,4},{4,0},{8,12},{12,8},{1,5},{5,1},{9,13},{13,9},{2,6},{6,2},{1... | collective-permute-start | bytes 786440 | tf_op jit(solution)/shard_map/ppermute | solution.py:32
  61.1 8.5 %collective-permute-start.14 = (f32[256,256]{1,0:T(8,128)S(1)}, f32[256,256]{1,0:T(8,128)}, u32[]{:S(2)}, u32[]{:S(2)}) collective-permute-start(f32[256,256]{1,0:T(8,128)S(1)} %shard_map.184.refs_0_.refs_2_), channel_id=1, source_target_pairs={{0,8},{4,12},{8,0},{12,4},{1,9},{5,13},{9,1},{13,5},{2,10},{6,14},... | collective-permute-start | bytes 786440 | tf_op jit(solution)/shard_map/ppermute | solution.py:32
  64.0 21.8 %all-to-all-start.1 = ((f32[8,2,64,128]{3,2,1,0:T(8,128)}), f32[8,2,64,128]{3,2,1,0:T(8,128)S(1)}, u32[]{:S(2)}, u32[]{:S(2)}) async-start(f32[8,2,64,128]{3,2,1,0:T(8,128)} %shard_map.182), calls=%async_computation.1 | async-start | bytes 1048576 | tf_op jit(solution)/shard_map/all_to_all | solution.py:696
  67.8 14.1 %collective-permute-start.16 = (bf16[256,512]{1,0:T(8,128)(2,1)S(1)}, bf16[256,512]{1,0:T(8,128)(2,1)S(1)}, u32[]{:S(2)}, u32[]{:S(2)}) collective-permute-start(bf16[256,512]{1,0:T(8,128)(2,1)S(1)} %shard_map.186.wa), channel_id=1, source_target_pairs={{0,8},{4,12},{8,0},{12,4},{1,9},{5,13},{9,1},{13,5},{2,10},{6,14},... | collective-permute-start | bytes 786440 | tf_op jit(solution)/shard_map/ppermute | solution.py:32
  85.8 11.3 %all-to-all-start.2 = ((f32[8,8,256]{2,1,0:T(8,128)}), f32[8,8,256]{2,1,0:T(8,128)S(1)}, u32[]{:S(2)}, u32[]{:S(2)}) async-start(f32[8,8,256]{2,1,0:T(8,128)} %get-tuple-element.42), calls=%async_computation.2 | async-start | bytes 131072 | tf_op jit(solution)/shard_map/all_to_all | solution.py:700
  (13 other events, 81.7 us)

commit v4 on v3

v4 whole, which is shorter than its diff:
```python
import functools
import math

import jax
import jax.numpy as jnp
from jax import lax
from jax.experimental import pallas as pl
from jax.experimental.pallas import tpu as pltpu
from jax.sharding import PartitionSpec as P

HD = 128
PANEL = 8
OUTER = 32
MIB = 1 << 20

momentum_keep = 0.95
norm_eps = 1e-06

F32 = jnp.float32
BF16 = jnp.bfloat16
HIGHEST = lax.Precision.HIGHEST

SMEM = pl.BlockSpec(memory_space=pltpu.SMEM)
VMEM = pl.BlockSpec(memory_space=pltpu.VMEM)
ANY = pl.BlockSpec(memory_space=pl.ANY)
HBM = pl.BlockSpec(memory_space=pltpu.HBM)


def swap(value, axes, k):
    axes = (axes,) if isinstance(axes, str) else axes
    n = math.prod(lax.axis_size(a) for a in axes)
    return lax.ppermute(value, axes, [(i, i ^ k) for i in range(n)])


def params(mib=6):
    return pltpu.CompilerParams(vmem_limit_bytes=mib * MIB)


def cost(flops, nbytes):
    return pl.CostEstimate(flops=int(flops), bytes_accessed=int(nbytes), transcendentals=0)


def halves(x):
    hi = x.astype(BF16)
    return hi, (x - hi.astype(F32)).astype(BF16)


def mm(a, b):
    return jnp.dot(a, b, preferred_element_type=F32)


def mm_full(a, b):
    return jnp.dot(a, b, precision=HIGHEST, preferred_element_type=F32)


def project_kernel(j, n_head, first, number, ranks, mom, grad, basis, *refs):
    out, total, grads, right, sems, right_sem = refs[-6:]
    chunk = total.shape[0] // number
    pieces = 2 if chunk % 32 == 0 else 1
    size = chunk // pieces
    fetch = pltpu.make_async_copy(basis, right, right_sem)
    copies = []
    for i in range(number):
        at = ((ranks[0] ^ j) * n_head + (ranks[2] ^ (first + i))) * chunk
        copies.append([])
        for p in range(pieces):
            src = pl.ds(pl.multiple_of(at + p * size, size), size)
            dst = pl.ds(i * chunk + p * size, size)
            n = i * pieces + p
            copies[i].append(
                pltpu.make_async_copy(mom.at[src, :], total.at[dst, :], sems.at[0, n])
            )
            copies[i].append(
                pltpu.make_async_copy(grad.at[src, :], grads.at[dst, :], sems.at[1, n])
            )
        for c in copies[i]:
            c.start()
        if i == 0:
            fetch.start()
    fetch.wait()
    b_hi, b_lo = halves(right[...])
    for i in range(number):
        for c in copies[i]:
            c.wait()
        rows = slice(i * chunk, (i + 1) * chunk)
        t = total[rows, :] + grads[rows, :].astype(F32)
        total[rows, :] = t
        t_hi, t_lo = halves(t)
        acc = mm(t_hi, b_hi) + (mm(t_hi, b_lo) + mm(t_lo, b_hi))
        out[rows, :] = acc.astype(out.dtype)


def project(ranks, momentum, grad_q, basis, j, first, number, n_resp, n_head, dtype, after):
    rows, cols = momentum.shape
    rank = basis.shape[1]
    size = rows // (n_resp * n_head) * number
    return pl.pallas_call(
        functools.partial(project_kernel, j, n_head, first, number),
        in_specs=[SMEM] + [HBM] * 3 + [ANY] * len(after),
        out_specs=[VMEM] * 2,
        scratch_shapes=[
            pltpu.VMEM((size, cols), BF16),
            pltpu.VMEM((cols, rank), F32),
            pltpu.SemaphoreType.DMA((2, 2 * number)),
            pltpu.SemaphoreType.DMA,
        ],
        out_shape=[
            jax.ShapeDtypeStruct((size, rank), dtype),
            jax.ShapeDtypeStruct((size, cols), F32),
        ],
        compiler_params=params(10),
        cost_estimate=cost(6 * size * cols * rank, size * cols * 6),
    )(ranks, momentum, grad_q, basis, *after)


def split_kernel(n_recv, number, own, *refs):
    recvs, outs = refs[:n_recv], refs[-number:]
    chunk = outs[0].shape[0]
    for i in range(number):
        rows = slice(i * chunk, (i + 1) * chunk)
        acc = own[rows, :]
        for r in recvs:
            acc = acc + r[rows, :].astype(F32)
        outs[i][...] = acc.astype(outs[i].dtype)


def split_sum(own, recvs, first, number):
    rows, rank = own.shape
    chunk = rows // number
    return pl.pallas_call(
        functools.partial(split_kernel, len(recvs), number),
        in_specs=[VMEM] * (1 + len(recvs)),
        out_specs=[VMEM] * number,
        out_shape=[
            jax.ShapeDtypeStruct((chunk, rank), BF16 if first + i else F32)
            for i in range(number)
        ],
        compiler_params=params(),
        cost_estimate=cost(rows * rank, rows * rank * 8),
    )(own, *recvs)


def sum_kernel(n_parts, *refs):
    acc = refs[0][...].astype(F32)
    for r in refs[1:n_parts]:
        acc = acc + r[...].astype(F32)
    refs[-1][...] = acc.astype(refs[-1].dtype)


def sum_parts(parts, dtype, after=()):
    shape = parts[0].shape
    return pl.pallas_call(
        functools.partial(sum_kernel, len(parts)),
        in_specs=[VMEM] * len(parts) + [ANY] * len(after),
        out_specs=VMEM,
        out_shape=jax.ShapeDtypeStruct(shape, dtype),
        compiler_params=params(),
        cost_estimate=cost(1000, 12 * math.prod(shape)),
    )(*parts, *after)


def gram_kernel(n_chunks, *refs):
    chunks, (pcat, pcat_t, gram) = refs[:n_chunks], refs[-3:]
    size = chunks[0].shape[0]
    for i in range(n_chunks):
        pcat[i * size : (i + 1) * size, :] = chunks[i][...]
    p = pcat[...]
    pt = p.T
    pcat_t[...] = pt
    half = p.shape[1] // 2
    gram[:half, :] = mm(pt[:half, :], p[:, :half])
    low = mm(pt[half:, :], p)
    gram[half : 2 * half, :] = low[:, :half]
    gram[2 * half :, :] = low[:, half:]


def gather_gram(chunks, after):
    size, rank = chunks[0].shape
    rows = size * len(chunks)
    return pl.pallas_call(
        functools.partial(gram_kernel, len(chunks)),
        in_specs=[VMEM] * len(chunks) + [ANY] * len(after),
        out_specs=[VMEM] * 3,
        out_shape=[
            jax.ShapeDtypeStruct((rows, rank), BF16),
            jax.ShapeDtypeStruct((rank, rows), BF16),
            jax.ShapeDtypeStruct((3 * rank // 2, rank // 2), F32),
        ],
        compiler_params=params(8),
        cost_estimate=cost(2 * rows * rank * rank, rows * rank * 6),
    )(*chunks, *after)


def back_part_kernel(pcat_t, *refs):
    totals, out = refs[:-1], refs[-1]
    seg = totals[0].shape[0]
    step = min(seg, 512)
    acc = None
    for j, total in enumerate(totals):
        for i in range(0, seg, step):
            t_hi, t_lo = halves(total[i : i + step, :])
            pt = pcat_t[:, j * seg + i : j * seg + i + step]
            part = mm(pt, t_hi) + mm(pt, t_lo)
            acc = part if acc is None else acc + part
    out[...] = acc.astype(BF16)


def back_part(pcat_t, totals):
    rank = pcat_t.shape[0]
    seg, cols = totals[0].shape
    rows = seg * len(totals)
    return pl.pallas_call(
        back_part_kernel,
        in_specs=[VMEM] * (1 + len(totals)),
        out_specs=VMEM,
        out_shape=jax.ShapeDtypeStruct((rank, cols), BF16),
        compiler_params=params(14),
        cost_estimate=cost(4 * rows * cols * rank, rows * cols * 4),
    )(pcat_t, *totals)


def factor_panel(panel, off):
    shape = (PANEL, 128)
    d = {}
    for j in range(PANEL):
        col = jnp.broadcast_to(panel[:, off + j : off + j + 1], shape)
        for i in range(j, PANEL):
            d[i, j] = jnp.broadcast_to(col[i : i + 1, :], shape)
    low, inv = {}, {}
    for j in range(PANEL):
        r = lax.rsqrt(d[j, j])
        inv[j, j] = r
        for i in range(j + 1, PANEL):
            low[i, j] = d[i, j] * r
        for k in range(j + 1, PANEL):
            for i in range(k, PANEL):
                d[i, k] = d[i, k] - low[i, j] * low[k, j]
    for j in range(PANEL):
        for i in range(j + 1, PANEL):
            acc = low[i, j] * inv[j, j]
            for k in range(j + 1, i):
                acc = acc + low[i, k] * inv[k, j]
            inv[i, j] = -(acc * inv[i, i])
    return inv


def three_parts(x):
    a = x.astype(BF16)
    rest = x - a.astype(F32)
    b = rest.astype(BF16)
    return a, b, (rest - b.astype(F32)).astype(BF16)


def cholesky_kernel(n_parts, *refs):
    parts, out, work = refs[:n_parts], refs[n_parts], refs[n_parts + 1]
    n = out.shape[0]
    half = n // 2
    tiles = n // 128 + 1
    total = parts[0][...]
    for part in parts[1:]:
        total = total + part[...]
    low = total[half : 2 * half, :]
    work[:half, :half] = total[:half, :]
    work[half:, :half] = low
    work[:half, half:] = low.T
    work[half:, half:] = total[2 * half :, :]
    sub = lax.broadcasted_iota(jnp.int32, (PANEL, 128), 0)
    lane = lax.broadcasted_iota(jnp.int32, (PANEL, 128), 1)
    n_panels = OUTER // PANEL

    def step(o, carry):
        blk = [
            [work[p * PANEL : (p + 1) * PANEL, t * 128 : (t + 1) * 128] for t in range(tiles - 1)]
            + [jnp.where(lane == sub + p * PANEL, 1.0, 0.0).astype(F32)]
            for p in range(n_panels)
        ]
        for p in range(n_panels):
            off = p * PANEL
            inv = factor_panel(blk[p][0], off)
            rows_of = [
                [jnp.broadcast_to(blk[p][t][j : j + 1, :], (PANEL, 128)) for t in range(tiles)]
                for j in range(PANEL)
            ]
            new = [None] * tiles
            for j in range(PANEL):
                col = inv[PANEL - 1, j]
                for i in range(PANEL - 2, j - 1, -1):
                    col = jnp.where(sub == i, inv[i, j], col)
                if j:
                    col = jnp.where(sub < j, 0.0, col)
                for t in range(tiles):
                    term = col * rows_of[j][t]
                    new[t] = term if new[t] is None else new[t] + term
            blk[p] = new
            if p + 1 < n_panels:
                u_rows = [
                    [jnp.broadcast_to(new[t][j : j + 1, :], (PANEL, 128)) for t in range(tiles)]
                    for j in range(PANEL)
                ]
                for b in range(p + 1, n_panels):
                    lanes = [
                        jnp.broadcast_to(blk[b][0][:, off + m : off + m + 1], (PANEL, 128))
                        for m in range(PANEL)
                    ]
                    upd = list(blk[b])
                    for k in range(PANEL):
                        v = lanes[0] * inv[k, 0]
                        for m in range(1, k + 1):
                            v = v + lanes[m] * inv[k, m]
                        for t in range(tiles):
                            upd[t] = upd[t] - v * u_rows[k][t]
                    blk[b] = upd
        u = jnp.concatenate([jnp.concatenate(row, axis=1) for row in blk], axis=0)
        u = pltpu.roll(u, tiles * 128 - OUTER, 1)[:, :n]
        at = lax.broadcasted_iota(jnp.int32, (OUTER, n), 1)
        left = jnp.where(at < n - OUTER * (o + 1), u, 0.0)
        la, lb, lc = three_parts(left)
        ua, ub, uc = three_parts(u)
        lhs = jnp.concatenate([la, la, lb, la, lc, lb], axis=0)
        rhs = jnp.concatenate([ua, ub, ua, uc, ua, ub], axis=0)
        upd = mm(lhs.T, rhs)
        rest = work[OUTER:, :]
        lanes_at = lax.broadcasted_iota(jnp.int32, rest.shape, 1)
        rest = pltpu.roll(jnp.where(lanes_at < OUTER, 0.0, rest), n - OUTER, 1)
        work[: n - OUTER, :] = rest - upd[: n - OUTER, :]
        work[n - OUTER :, :] = u
        return carry

    lax.fori_loop(0, n // OUTER, step, 0)
    out[...] = work[...]


def inverse_factor(*parts):
    n = 2 * parts[0].shape[1]
    return pl.pallas_call(
        functools.partial(cholesky_kernel, len(parts)),
        in_specs=[VMEM] * len(parts),
        out_specs=VMEM,
        scratch_shapes=[pltpu.VMEM((n, n), F32)],
        out_shape=jax.ShapeDtypeStruct((n, n), F32),
        compiler_params=params(),
        cost_estimate=cost(10_000_000_000, 4 * n * n * 4),
    )(*parts)


def mm_three(a, b):
    a_hi, a_lo = halves(a)
    b_hi, b_lo = halves(b)
    return mm(a_hi, b_hi) + (mm(a_hi, b_lo) + mm(a_lo, b_hi))


def back_kernel(x, wa, wb, bt_out, y_out, s_out):
    w = wa[...].astype(F32) + wb[...].astype(F32)
    bt = mm_three(x[...], w)
    bt_out[...] = bt
    s = jnp.sum(bt * bt, axis=1, keepdims=True)
    s_out[...] = jnp.broadcast_to(s, (s.shape[0], 128)).T[:8, :]
    y_out[...] = ((1.0 - momentum_keep) * mm(x[...].T.astype(BF16), bt.astype(BF16))).astype(BF16)


def back_full(x, wa, wb):
    rank, cols = wa.shape
    return pl.pallas_call(
        back_kernel,
        in_specs=[VMEM] * 3,
        out_specs=[VMEM] * 3,
        out_shape=[
            jax.ShapeDtypeStruct((rank, cols), F32),
            jax.ShapeDtypeStruct((rank, cols), BF16),
            jax.ShapeDtypeStruct((8, rank), F32),
        ],
        compiler_params=params(),
        cost_estimate=cost(8 * rank * rank * cols, rank * cols * 12),
    )(x, wa, wb)


def row_blocks(ranks, n_resp, n_head, chunk):
    return [
        pl.multiple_of(((ranks[0] ^ j) * n_head + (ranks[2] ^ k)) * chunk, chunk)
        for j in range(n_resp)
        for k in range(n_head)
    ]


def momentum_kernel(n_resp, n_head, ranks, pcat, y, *refs):
    totals, (out, held, sems) = refs[:-3], refs[-3:]
    seg = totals[0].shape[0]
    chunk = pcat.shape[0] // (n_resp * n_head)
    copies = []
    for i, at in enumerate(row_blocks(ranks, n_resp, n_head, chunk)):
        rows = slice(i * chunk, (i + 1) * chunk)
        off = i * chunk % seg
        total = totals[i * chunk // seg][off : off + chunk, :]
        held[rows, :] = total - mm(pcat[rows, :], y[...])
        copies.append(
            pltpu.make_async_copy(held.at[rows, :], out.at[pl.ds(at, chunk), :], sems.at[i])
        )
        copies[-1].start()
    for c in copies:
        c.wait()


def new_momentum(ranks, pcat, totals, y, n_resp, n_head):
    rows, rank = pcat.shape
    cols = totals[0].shape[1]
    return pl.pallas_call(
        functools.partial(momentum_kernel, n_resp, n_head),
        in_specs=[SMEM] + [VMEM] * (2 + len(totals)),
        out_specs=HBM,
        scratch_shapes=[
            pltpu.VMEM((rows, cols), F32),
            pltpu.SemaphoreType.DMA((n_resp * n_head,)),
        ],
        out_shape=jax.ShapeDtypeStruct((rows, cols), F32),
        compiler_params=params(14),
        cost_estimate=cost(2 * rows * cols * rank, rows * cols * 8),
    )(ranks, pcat, y, *totals)


def update_kernel(gain, n_resp, n_head, n_sums, ranks, pcat, x, bt, *refs):
    sums, (upd, basis_out, held, held_basis, sems, basis_sem) = refs[:n_sums], refs[n_sums:]
    total = sums[0][...]
    for s in sums[1:]:
        total = total + s[...]
    scale = lax.rsqrt(total + norm_eps).T[:, :1]
    scaled = bt[...] * scale
    held_basis[...] = scaled.T
    basis_copy = pltpu.make_async_copy(held_basis, basis_out, basis_sem)
    basis_copy.start()
    z_hi, z_lo = halves(gain * mm_three(x[...].T, scaled))
    chunk = pcat.shape[0] // (n_resp * n_head)
    copies = []
    for i, at in enumerate(row_blocks(ranks, n_resp, n_head, chunk)):
        rows = slice(i * chunk, (i + 1) * chunk)
        p = pcat[rows, :]
        held[rows, :] = (mm(p, z_hi) + mm(p, z_lo)).astype(BF16)
        copies.append(
            pltpu.make_async_copy(held.at[rows, :], upd.at[pl.ds(at, chunk), :], sems.at[i])
        )
        copies[-1].start()
    for c in copies:
        c.wait()
    basis_copy.wait()


def final_update(ranks, pcat, x, bt, sums, gain, n_resp, n_head):
    rows, rank = pcat.shape
    cols = bt.shape[1]
    return pl.pallas_call(
        functools.partial(update_kernel, gain, n_resp, n_head, len(sums)),
        in_specs=[SMEM] + [VMEM] * (3 + len(sums)),
        out_specs=[HBM, HBM],
        scratch_shapes=[
            pltpu.VMEM((rows, cols), BF16),
            pltpu.VMEM((cols, rank), F32),
            pltpu.SemaphoreType.DMA((n_resp * n_head,)),
            pltpu.SemaphoreType.DMA,
        ],
        out_shape=[
            jax.ShapeDtypeStruct((rows, cols), BF16),
            jax.ShapeDtypeStruct((cols, rank), F32),
        ],
        compiler_params=params(10),
        cost_estimate=cost(4 * rows * cols * rank, rows * cols * 3),
    )(ranks, pcat, x, bt, *sums)


def group_of(counts, response):
    group = jnp.int32(0)
    end = jnp.int32(0)
    for g in range(counts.shape[0]):
        end = end + counts[g]
        group = group + (end <= response).astype(jnp.int32)
    return group


def pack_kernel(*refs):
    keys, values, out = refs[0], refs[1], refs[-1]
    out[0] = keys[...]
    out[1] = values[...]


def pack_prompts(keys, values, after):
    return pl.pallas_call(
        pack_kernel,
        in_specs=[VMEM] * 2 + [ANY] * len(after),
        out_specs=VMEM,
        out_shape=jax.ShapeDtypeStruct((2,) + keys.shape, BF16),
        compiler_params=params(),
        cost_estimate=cost(1000, 8 * math.prod(keys.shape)),
    )(keys, values, *after)


def select_kernel(n_resp, n_fsdp, ranks, counts, slots, *refs):
    stored, outs = refs[:n_resp], refs[-n_fsdp:]
    held = stored[0].shape[1]
    for k in range(n_fsdp):
        slot = slots[group_of(counts, ranks[0] * n_fsdp + (ranks[1] ^ k))]
        owner, local = slot // held, slot % held
        for j in range(n_resp):

            @pl.when(owner == (ranks[0] ^ j))
            def _():
                outs[k][0] = stored[j][0, local]
                outs[k][1] = stored[j][1, local]


def select_prompts(ranks, counts, slots, stored, n_fsdp, after):
    _, _, piece, width = stored[0].shape
    return pl.pallas_call(
        functools.partial(select_kernel, len(stored), n_fsdp),
        in_specs=[SMEM] * 3 + [VMEM] * len(stored) + [ANY] * len(after),
        out_specs=[VMEM] * n_fsdp,
        out_shape=[jax.ShapeDtypeStruct((2, piece, width), BF16)] * n_fsdp,
        compiler_params=params(),
        cost_estimate=cost(1000, 8 * n_fsdp * piece * width),
    )(ranks, counts, slots, *stored, *after)


def attention_kernel(
    n_fsdp, heads, last, ranks, counts, prompt_blocks, resp_blocks, q, sk, sv, go, *refs
):
    pieces, refs = refs[:n_fsdp], refs[n_fsdp:]
    dq_held, keys, values, dk, dv, sem = refs[-6:]
    n_out = 2 + n_fsdp if last else 3
    outs = refs[-6 - n_out : -6]
    dq = outs[0]
    piece = pieces[0].shape[1]
    cap = piece * n_fsdp
    length = q.shape[0]
    scale = HD ** (-0.5)
    for k in range(n_fsdp):
        rows = pl.ds(pl.multiple_of((ranks[1] ^ k) * piece, piece), piece)
        keys[rows, :] = pieces[k][0]
        values[rows, :] = pieces[k][1]
    keys[cap:, :] = sk[...]
    values[cap:, :] = sv[...]
    prompt_len = prompt_blocks[group_of(counts, ranks[0] * n_fsdp + ranks[1])] * 128
    resp_len = resp_blocks[0] * 128
    width = keys.shape[0]
    place = lax.broadcasted_iota(jnp.int32, (width, length), 0)
    pos = lax.broadcasted_iota(jnp.int32, (width, length), 1)
    inner = place - cap
    seen = ((place < cap) & (place < prompt_len)) | (
        (place >= cap) & (inner <= pos) & (inner < resp_len)
    )
    bias = jnp.where(seen, 0.0, -jnp.inf).astype(F32)
    live = lax.broadcasted_iota(jnp.int32, (length, HD), 0) < resp_len
    nt = (((1,), (1,)), ((), ()))
    kall = keys[...]
    vall = values[...]
    kt = kall.T
    if last:
        dk[...] = refs[0][...]
        dv[...] = refs[1][...]
    else:
        dk[...] = jnp.zeros_like(dk)
        dv[...] = jnp.zeros_like(dv)
    for i, h in enumerate(heads):
        cols = slice(h * HD, (h + 1) * HD)
        qh = q[:, cols]
        gh = jnp.where(live, go[:, cols], jnp.zeros((), BF16))
        logits = lax.dot_general(kall, qh, nt, preferred_element_type=F32) * scale + bias
        peak = jnp.max(logits, axis=0, keepdims=True)
        e = jnp.exp(logits - peak)
        w = (e * (1.0 / jnp.sum(e, axis=0, keepdims=True))).astype(BF16)
        dp = lax.dot_general(vall, gh, nt, preferred_element_type=F32)
        wf = w.astype(F32)
        diag = jnp.sum(wf * dp, axis=0, keepdims=True)
        ds = (wf * (dp - diag)).astype(BF16)
        dk[...] += mm(ds, qh)
        dv[...] += mm(w, gh)
        dq_held[:, i * HD : (i + 1) * HD] = (mm(kt, ds) * scale).T.astype(BF16)
    to = dq.at[:, pl.ds(heads[0] * HD, len(heads) * HD)]
    copy = pltpu.make_async_copy(dq_held, to, sem)
    copy.start()
    if last:
        own, sends = outs[1], outs[2:]
        own[0] = (dk[cap:, :] * scale).astype(BF16)
        own[1] = dv[cap:, :].astype(BF16)
        for k in range(n_fsdp):
            rows = pl.ds(pl.multiple_of((ranks[1] ^ k) * piece, piece), piece)
            sends[k][0] = (dk[rows, :] * scale).astype(sends[k].dtype)
            sends[k][1] = dv[rows, :].astype(sends[k].dtype)
    else:
        outs[1][...] = dk[...]
        outs[2][...] = dv[...]
    copy.wait()


def attention(heads, earlier, ranks, counts, prompt_blocks, resp_blocks, q, sk, sv, go, pieces, after):
    n_fsdp = len(pieces)
    piece = pieces[0].shape[1]
    length, width = q.shape
    cap = piece * n_fsdp
    total = cap + length
    last = earlier is not None
    dq_shape = jax.ShapeDtypeStruct((length, width), BF16)
    if last:
        extra, specs = (earlier[1], earlier[2], earlier[0]), [VMEM, VMEM, HBM]
        out_shape = [dq_shape, jax.ShapeDtypeStruct((2, length, HD), BF16)] + [
            jax.ShapeDtypeStruct((2, piece, HD), BF16 if k else F32) for k in range(n_fsdp)
        ]
        aliases = {8 + n_fsdp + 2: 0}
    else:
        extra, specs = (), []
        out_shape = [dq_shape] + [jax.ShapeDtypeStruct((total, HD), F32)] * 2
        aliases = {}
    return pl.pallas_call(
        functools.partial(attention_kernel, n_fsdp, heads, last),
        in_specs=[SMEM] * 4 + [VMEM] * (4 + n_fsdp) + specs + [ANY] * len(after),
        out_specs=[HBM] + [VMEM] * (len(out_shape) - 1),
        scratch_shapes=[pltpu.VMEM((length, len(heads) * HD), BF16)]
        + [pltpu.VMEM((total, HD), BF16)] * 2
        + [pltpu.VMEM((total, HD), F32)] * 2
        + [pltpu.SemaphoreType.DMA],
        out_shape=out_shape,
        input_output_aliases=aliases,
        compiler_params=params(12),
        cost_estimate=cost(3_000_000_000, length * width * 8),
    )(ranks, counts, prompt_blocks, resp_blocks, q, sk, sv, go, *pieces, *extra, *after)


def by_slot_kernel(n_resp, n_fsdp, ranks, counts, slots, *refs):
    parts, outs = refs[:n_fsdp], refs[-n_resp:]
    held = outs[0].shape[1]
    slot_of = [
        slots[group_of(counts, ranks[0] * n_fsdp + (ranks[1] ^ k))] for k in range(n_fsdp)
    ]
    for j in range(n_resp):
        for local in range(held):
            slot = (ranks[0] ^ j) * held + local
            acc = jnp.zeros(parts[0].shape, F32)
            for k in range(n_fsdp):
                acc = acc + jnp.where(slot_of[k] == slot, parts[k][...].astype(F32), 0.0)
            outs[j][:, local] = acc.astype(outs[j].dtype)


def sum_by_slot(ranks, counts, slots, parts, n_resp, after):
    held = counts.shape[0] // n_resp
    _, piece, width = parts[0].shape
    return pl.pallas_call(
        functools.partial(by_slot_kernel, n_resp, len(parts)),
        in_specs=[SMEM] * 3 + [VMEM] * len(parts) + [ANY] * len(after),
        out_specs=[VMEM] * n_resp,
        out_shape=[
            jax.ShapeDtypeStruct((2, held, piece, width), BF16 if j else F32)
            for j in range(n_resp)
        ],
        compiler_params=params(),
        cost_estimate=cost(1000, 8 * len(parts) * piece * width * 4),
    )(ranks, counts, slots, *parts, *after)


def on_device(
    queries,
    self_keys,
    self_values,
    d_out,
    prompt_keys,
    prompt_values,
    counts,
    owner_slot,
    prompt_blocks,
    resp_blocks,
    grad_q,
    momentum,
    basis,
):
    n_resp, n_fsdp, n_head = (lax.axis_size(a) for a in ("resp", "fsdp", "head"))
    ranks = jnp.stack([lax.axis_index(a) for a in ("resp", "fsdp", "head")]).astype(jnp.int32)
    gain = math.sqrt(
        momentum.shape[0] * n_fsdp * momentum.shape[1] * n_resp * n_head / basis.shape[1]
    )

    in_hbm = [pltpu.with_memory_space_constraint(a, pltpu.HBM) for a in (momentum, grad_q, basis)]
    half = n_head // 2
    groups = [(half, half), (0, half)] if half else [(0, n_head)]

    totals, after = {}, ()
    arrived = []
    for first, number in groups:
        row = []
        for j in range(1, n_resp):
            sent, totals[j, first] = project(
                ranks, *in_hbm, j, first, number, n_resp, n_head, BF16, after
            )
            after = (sent,)
            row.append(swap(sent, "resp", j))
        arrived.append(row)
    packed = pack_prompts(prompt_keys, prompt_values, after)
    stored = [packed] + [swap(packed, "resp", j) for j in range(1, n_resp)]
    after = (packed,)
    split = {}
    for (first, number), recvs in zip(groups, arrived):
        mine, totals[0, first] = project(
            ranks, *in_hbm, 0, first, number, n_resp, n_head, F32, after
        )
        outs = split_sum(mine, recvs, first, number)
        after = (outs[0],)
        for i in range(number):
            split[first + i] = outs[i]
    totals = [totals[at] for at in sorted(totals)]
    chosen = select_prompts(ranks, counts, owner_slot, stored, n_fsdp, after)
    far_first = [k for first, number in groups for k in range(first, first + number) if k]
    summands = {k: swap(split[k], "head", k) for k in far_first}
    pieces = [chosen[0]] + [swap(chosen[k], "fsdp", k) for k in range(1, n_fsdp)]
    piece0 = sum_parts(
        [split[0]] + [summands[k] for k in range(1, n_head)], BF16, (pieces[-1],)
    )

    along = {0: piece0}
    for k in far_first:
        along[k] = swap(piece0, "head", k)
    chunks = [along[k] for k in range(n_head)]
    for j in range(1, n_resp):
        chunks += [swap(along[k], "resp", j) for k in range(n_head)]

    n_q = queries.shape[1] // HD
    heads = [list(range(n_q // 2)), list(range(n_q // 2, n_q))]
    held = (
        ranks, counts, prompt_blocks, resp_blocks, queries, self_keys, self_values, d_out, pieces
    )
    earlier = attention(heads[0], None, *held, (piece0,))
    dq, resp_grad, *parts = attention(heads[1], earlier, *held, (along[n_head - 1],))
    pcat, pcat_t, gram = gather_gram(chunks, (resp_grad,))

    bits = [1 << b for b in range(n_fsdp.bit_length() - 1)]
    w = back_part(pcat_t, totals)
    for bit in bits[:-1]:
        gram = sum_parts([gram, swap(gram, "fsdp", bit)], F32)
        w = sum_parts([w, swap(w, "fsdp", bit)], BF16, (gram,))
    gram_parts = (gram, swap(gram, "fsdp", bits[-1]))
    w_other = swap(w, "fsdp", bits[-1])
    returned = [parts[0]] + [swap(parts[k], "fsdp", k) for k in range(1, n_fsdp)]
    slots = sum_by_slot(ranks, counts, owner_slot, returned, n_resp, (w,))
    x = inverse_factor(*gram_parts)
    prompt_grad = sum_parts(
        [slots[0]] + [swap(slots[j], "resp", j) for j in range(1, n_resp)], F32
    )

    bt, y, squares = back_full(x, w, w_other)
    squares = sum_parts([squares] + [swap(squares, "head", k) for k in range(1, n_head)], F32)
    momentum_out = new_momentum(ranks, pcat, totals, y, n_resp, n_head)
    sums = [squares] + [swap(squares, "resp", j) for j in range(1, n_resp)]
    update, basis_out = final_update(ranks, pcat, x, bt, sums, gain, n_resp, n_head)
    return (dq, resp_grad, prompt_grad, update, momentum_out, basis_out)


def solution(mesh):
    placed = (
        P(("resp", "fsdp"), "head"),
        P(("resp", "fsdp"), "head"),
        P(("resp", "fsdp"), "head"),
        P(("resp", "fsdp"), "head"),
        P("resp", "fsdp", "head"),
        P("resp", "fsdp", "head"),
        P(),
        P(),
        P(),
        P(("resp", "fsdp")),
        P("fsdp", ("resp", "head")),
        P("fsdp", ("resp", "head")),
        P(("resp", "head"), None),
    )
    return jax.shard_map(
        on_device,
        mesh=mesh,
        in_specs=placed,
        out_specs=(
            P(("resp", "fsdp"), "head"),
            P(None, ("resp", "fsdp"), "head"),
            P(None, "resp", "fsdp", "head"),
            P("fsdp", ("resp", "head")),
            P("fsdp", ("resp", "head")),
            P(("resp", "head"), None),
        ),
        check_vma=False,
    )
```

time: 104 us -> 91.1 us (0.88)
  blocking collectives: 7.22 us -> 0 us
  local copies, waits for them, and re-layouts: 7.37 us -> 0.95 us
  starting transfers between devices: 31 us -> 33.6 us
  waiting for transfers between devices: 12.8 us -> 11.3 us
    ppermute x17 -> x28, starting transfers between devices: 23 us -> 33.6 us  [swap(): return lax.ppermute(value, axes, [(i, i ^ k) for i in range(n)])]
    all_to_all x2 -> x0, starting transfers between devices: 7.95 us -> none  [the longest x1 4.28 us: on_device(): sums = lax.all_to_all(squares, ('resp', 'head'), 0, 0, tiled=True)]
    all_to_all x1 -> x0, blocking collectives: 7.22 us -> none  [on_device(): pieces = lax.all_to_all(chosen, 'fsdp', 0, 0, tiled=True)]
    unnamed x36 -> x20, local copies, waits for them, and re-layouts: 7.37 us -> 0.95 us
    pallas_call x8 -> x10, Pallas kernels: 23.5 us -> 26 us  [the longest x4 13.4 us: project(): pl.pallas_call(functools.partial(project_kernel, j, n_head, first, number...]
    pallas_call x1, Pallas kernels: 2.41 us -> 0.62 us  [back_full(): pl.pallas_call(back_kernel, in_specs=[VMEM] * 3, out_specs=[VMEM] * 3, ou...]
    pallas_call x1, Pallas kernels: 11.8 us -> 10 us  [inverse_factor(): pl.pallas_call(functools.partial(cholesky_kernel, len(parts)), in_specs=[...]
    ppermute x17 -> x28, waiting for transfers between devices: 12.8 us -> 11.3 us  [swap(): return lax.ppermute(value, axes, [(i, i ^ k) for i in range(n)])]
  transfers between devices with their start and end apart: 19 -> 28, of which waited for: 4 -> 8; matrix products, arithmetic and copies ran while one was open for 0% -> 0% of each run, Pallas kernels for 32% -> 40%
where the time goes in v4:
time: 91.1 us; the launch traced here: 90.8 us
  Pallas kernels  43.1 us (47%)
  starting transfers between devices  33.6 us (37%)
  waiting for transfers between devices  11.3 us (12%)
  between operations  1.79 us (2%)
  local copies, waits for them, and re-layouts  0.95 us (1%)
    ppermute x28, starting transfers between devices, swap(): return lax.ppermute(value, axes, [(i, i ^ k) for i in range(n)])  33.6 us
    pallas_call x4, Pallas kernels, project(): pl.pallas_call(functools.partial(project_kernel, j, n_head, first, number...  13.4 us
    ppermute x28, waiting for transfers between devices, swap(): return lax.ppermute(value, axes, [(i, i ^ k) for i in range(n)])  11.3 us
    pallas_call x1, Pallas kernels, inverse_factor(): pl.pallas_call(functools.partial(cholesky_kernel, len(parts)), in_specs=[...  10 us
    pallas_call x2, Pallas kernels, attention(): pl.pallas_call(functools.partial(attention_kernel, n_fsdp, heads, last),...  8.55 us
    pallas_call x1, Pallas kernels, final_update(): pl.pallas_call(functools.partial(update_kernel, gain, n_resp, n_head, len...  3.32 us
    pallas_call x1, Pallas kernels, new_momentum(): pl.pallas_call(functools.partial(momentum_kernel, n_resp, n_head), in_spe...  2.84 us
  transfers between devices with their start and end apart: 28, of which 8 were waited for; matrix products, arithmetic and copies ran while one was open for 0% of the time, Pallas kernels for 40%

profile of v4, /device:TPU:0, one launch (start us, length us, event | category | flops | bytes accessed | tf_op | source)
XLA Modules:
  0.0 90.8 jit_solution(7220707862788734667)
XLA Ops:
  0.7 3.4 %shard_map.172 = (bf16[512,256]{1,0:T(8,128)(2,1)S(1)}, f32[512,512]{1,0:T(8,128)S(1)}) custom-call(s32[3]{0:T(128)S(1)} %pad_add_fusion.ranks, f32[2048,512]{1,0:T(8,128)} %mom.7, bf16[2048,512]{1,0:T(8,128)(2,1)} %grad.7, f32[512,256]{1,0:T(8,128)} %basis.7), custom_call_target="tpu_custom_call" | custom-call | flops 402653184 | bytes 1572864 | tf_op jit(solution)/shard_map/pallas_call | solution.py:97
  4.1 3.0 %collective-permute-start.1 = (bf16[512,256]{1,0:T(8,128)(2,1)S(1)}, bf16[512,256]{1,0:T(8,128)(2,1)S(1)}, u32[]{:S(2)}, u32[]{:S(2)}) collective-permute-start(bf16[512,256]{1,0:T(8,128)(2,1)S(1)} %get-tuple-element.41.refs_0_), channel_id=1, source_target_pairs={{0,16},{16,0},{1,17},{17,1},{2,18},{18,2},{3,19},{19,3},{4,20},{20... | collective-permute-start | bytes 786440 | tf_op jit(solution)/shard_map/ppermute | solution.py:32
  7.1 3.3 %shard_map.173 = (bf16[512,256]{1,0:T(8,128)(2,1)S(1)}, f32[512,512]{1,0:T(8,128)S(1)}) custom-call(s32[3]{0:T(128)S(1)} %pad_add_fusion.ranks, f32[2048,512]{1,0:T(8,128)} %mom.7, bf16[2048,512]{1,0:T(8,128)(2,1)} %grad.7, f32[512,256]{1,0:T(8,128)} %basis.7, bf16[512,256]{1,0:T(8,128)(2,1)S(1)} %get-tuple-element.41.refs_0_), custom_call_target="tpu_custom_call" | custom-call | flops 402653184 | bytes 1572864 | tf_op jit(solution)/shard_map/pallas_call | solution.py:97
  10.6 2.1 %collective-permute-start = (bf16[2,2,64,128]{3,2,1,0:T(8,128)(2,1)S(1)}, bf16[2,2,64,128]{3,2,1,0:T(8,128)(2,1)S(1)}, u32[]{:S(2)}, u32[]{:S(2)}) collective-permute-start(bf16[2,2,64,128]{3,2,1,0:T(8,128)(2,1)S(1)} %shard_map.174.refs_0_), channel_id=1, source_target_pairs={{0,16},{16,0},{1,17},{17,1},{2,18},{18,2},{3,19},{19,3},{4,20},{20... | collective-permute-start | bytes 196616 | tf_op jit(solution)/shard_map/ppermute | solution.py:32
  12.6 3.3 %shard_map.175 = (f32[512,256]{1,0:T(8,128)S(1)}, f32[512,512]{1,0:T(8,128)S(1)}) custom-call(s32[3]{0:T(128)S(1)} %pad_add_fusion.ranks, f32[2048,512]{1,0:T(8,128)} %mom.7, bf16[2048,512]{1,0:T(8,128)(2,1)} %grad.7, f32[512,256]{1,0:T(8,128)} %basis.7, bf16[2,2,64,128]{3,2,1,0:T(8,128)(2,1)S(1)} %shard_map.174.refs_0_), custom_call_target="tpu_custom_call" | custom-call | flops 402653184 | bytes 1572864 | tf_op jit(solution)/shard_map/pallas_call | solution.py:97
  16.1 3.7 %collective-permute-start.8 = (bf16[256,256]{1,0:T(8,128)(2,1)S(1)}, bf16[256,256]{1,0:T(8,128)(2,1)S(1)}, u32[]{:S(2)}, u32[]{:S(2)}) collective-permute-start(bf16[256,256]{1,0:T(8,128)(2,1)S(1)} %get-tuple-element.52), channel_id=1, source_target_pairs={{0,3},{1,2},{2,1},{3,0},{4,7},{5,6},{6,5},{7,4},{8,11},{9,10},{10,... | collective-permute-start | bytes 393224 | tf_op jit(solution)/shard_map/ppermute | solution.py:32
  19.9 3.4 %shard_map.177 = (f32[512,256]{1,0:T(8,128)S(1)}, f32[512,512]{1,0:T(8,128)S(1)}) custom-call(s32[3]{0:T(128)S(1)} %pad_add_fusion.ranks, f32[2048,512]{1,0:T(8,128)} %mom.7, bf16[2048,512]{1,0:T(8,128)(2,1)} %grad.7, f32[512,256]{1,0:T(8,128)} %basis.7, bf16[256,256]{1,0:T(8,128)(2,1)S(1)} %get-tuple-element.44.refs_0_), custom_call_target="tpu_custom_call" | custom-call | flops 402653184 | bytes 1572864 | tf_op jit(solution)/shard_map/pallas_call | solution.py:97
  25.1 1.6 %collective-permute-start.3 = (bf16[2,64,128]{2,1,0:T(8,128)(2,1)S(1)}, bf16[2,64,128]{2,1,0:T(8,128)(2,1)S(1)}, u32[]{:S(2)}, u32[]{:S(2)}) collective-permute-start(bf16[2,64,128]{2,1,0:T(8,128)(2,1)S(1)} %get-tuple-element.48), channel_id=1, source_target_pairs={{0,4},{4,0},{8,12},{12,8},{1,5},{5,1},{9,13},{13,9},{2,6},{6,2},{1... | collective-permute-start | bytes 98312 | tf_op jit(solution)/shard_map/ppermute | solution.py:32
  26.7 2.0 %collective-permute-done.5.refs_4_.refs_3_ = bf16[2,64,128]{2,1,0:T(8,128)(2,1)S(1)} collective-permute-done((bf16[2,64,128]{2,1,0:T(8,128)(2,1)S(1)}, bf16[2,64,128]{2,1,0:T(8,128)(2,1)S(1)}, u32[]{:S(2)}, u32[]{:S(2)}) %collective-permute-start.5) | collective-permute-done | bytes 32800 | tf_op jit(solution)/shard_map/ppermute | solution.py:32
  31.4 2.0 %collective-permute-start.14 = (bf16[256,256]{1,0:T(8,128)(2,1)S(1)}, bf16[256,256]{1,0:T(8,128)(2,1)S(1)}, u32[]{:S(2)}, u32[]{:S(2)}) collective-permute-start(bf16[256,256]{1,0:T(8,128)(2,1)S(1)} %shard_map.180.refs_4_.refs_0_), channel_id=1, source_target_pairs={{0,2},{1,3},{2,0},{3,1},{4,6},{5,7},{6,4},{7,5},{8,10},{9,11},{10,... | collective-permute-start | bytes 393224 | tf_op jit(solution)/shard_map/ppermute | solution.py:32
  33.5 2.0 %collective-permute-start.13 = (bf16[256,256]{1,0:T(8,128)(2,1)S(1)}, bf16[256,256]{1,0:T(8,128)(2,1)S(1)}, u32[]{:S(2)}, u32[]{:S(2)}) collective-permute-start(bf16[256,256]{1,0:T(8,128)(2,1)S(1)} %shard_map.180.refs_4_.refs_0_), channel_id=1, source_target_pairs={{0,1},{1,0},{2,3},{3,2},{4,5},{5,4},{6,7},{7,6},{8,9},{9,8},{10,11... | collective-permute-start | bytes 393224 | tf_op jit(solution)/shard_map/ppermute | solution.py:32
  35.8 3.9 %shard_map.181 = (bf16[256,1024]{1,0:T(8,128)(2,1)}, f32[512,128]{1,0:T(8,128)S(1)}, f32[512,128]{1,0:T(8,128)S(1)}) custom-call(s32[3]{0:T(128)S(1)} %pad_add_fusion.ranks, s32[4]{0:T(128)S(1)} %copy-done.3, s32[4]{0:T(128)S(1)} %copy-done.9, s32[1]{0:T(128)S(6)} %copy.21.resp_blocks, bf16[256,1024]{1,0:T(8,128)(2,1)S(1)} %copy-done.5, ...), custom_call_target="tpu_custom_call" | custom-call | flops 3000000000 | bytes 2097152 | tf_op jit(solution)/shard_map/pallas_call | solution.py:609
  39.8 1.8 %collective-permute-done.14.refs_2_ = bf16[256,256]{1,0:T(8,128)(2,1)S(1)} collective-permute-done((bf16[256,256]{1,0:T(8,128)(2,1)S(1)}, bf16[256,256]{1,0:T(8,128)(2,1)S(1)}, u32[]{:S(2)}, u32[]{:S(2)}) %collective-permute-start.14) | collective-permute-done | bytes 131104 | tf_op jit(solution)/shard_map/ppermute | solution.py:32
  41.6 1.5 %collective-permute-start.17 = (bf16[256,256]{1,0:T(8,128)(2,1)S(1)}, bf16[256,256]{1,0:T(8,128)(2,1)S(1)}, u32[]{:S(2)}, u32[]{:S(2)}) collective-permute-start(bf16[256,256]{1,0:T(8,128)(2,1)S(1)} %collective-permute-done.14.refs_2_), channel_id=1, source_target_pairs={{0,16},{16,0},{1,17},{17,1},{2,18},{18,2},{3,19},{19,3},{4,20},{20... | collective-permute-start | bytes 393224 | tf_op jit(solution)/shard_map/ppermute | solution.py:32
  43.6 1.5 %collective-permute-start.18 = (bf16[256,256]{1,0:T(8,128)(2,1)S(1)}, bf16[256,256]{1,0:T(8,128)(2,1)S(1)}, u32[]{:S(2)}, u32[]{:S(2)}) collective-permute-start(bf16[256,256]{1,0:T(8,128)(2,1)S(1)} %collective-permute-done.9.refs_7_.refs_3_), channel_id=1, source_target_pairs={{0,16},{16,0},{1,17},{17,1},{2,18},{18,2},{3,19},{19,3},{4,20},{20... | collective-permute-start | bytes 393224 | tf_op jit(solution)/shard_map/ppermute | solution.py:32
  45.1 4.6 %shard_map.182 = (bf16[256,1024]{1,0:T(8,128)(2,1)}, bf16[2,256,128]{2,1,0:T(8,128)(2,1)}, f32[2,64,128]{2,1,0:T(8,128)S(1)}, bf16[2,64,128]{2,1,0:T(8,128)(2,1)...) custom-call(s32[3]{0:T(128)S(1)} %pad_add_fusion.ranks, ...), custom_call_target="tpu_custom_call", output_to_operand_aliasing={{0}: (14, {})} | custom-call | flops 3000000000 | bytes 2097152 | tf_op jit(solution)/shard_map/pallas_call | solution.py:609
  53.2 3.2 %collective-permute-start.22 = (f32[384,128]{1,0:T(8,128)S(1)}, f32[384,128]{1,0:T(8,128)S(1)}, u32[]{:S(2)}, u32[]{:S(2)}) collective-permute-start(f32[384,128]{1,0:T(8,128)S(1)} %shard_map.185.refs_2_.refs_0_), channel_id=1, source_target_pairs={{0,8},{4,12},{8,0},{12,4},{1,9},{5,13},{9,1},{13,5},{2,10},{6,14},... | collective-permute-start | bytes 589832 | tf_op jit(solution)/shard_map/ppermute | solution.py:32
  56.6 1.7 %collective-permute-start.12 = (bf16[2,64,128]{2,1,0:T(8,128)(2,1)S(1)}, bf16[2,64,128]{2,1,0:T(8,128)(2,1)S(1)}, u32[]{:S(2)}, u32[]{:S(2)}) collective-permute-start(bf16[2,64,128]{2,1,0:T(8,128)(2,1)S(1)} %get-tuple-element.61), channel_id=1, source_target_pairs={{0,12},{4,8},{8,4},{12,0},{1,13},{5,9},{9,5},{13,1},{2,14},{6,10},... | collective-permute-start | bytes 98312 | tf_op jit(solution)/shard_map/ppermute | solution.py:32
  58.8 4.1 %collective-permute-done.11.refs_2_ = bf16[2,64,128]{2,1,0:T(8,128)(2,1)S(1)} collective-permute-done((bf16[2,64,128]{2,1,0:T(8,128)(2,1)S(1)}, bf16[2,64,128]{2,1,0:T(8,128)(2,1)S(1)}, u32[]{:S(2)}, u32[]{:S(2)}) %collective-permute-start.11) | collective-permute-done | bytes 32800 | tf_op jit(solution)/shard_map/ppermute | solution.py:32
  64.9 10.0 %shard_map.189.x = f32[256,256]{1,0:T(8,128)S(1)} custom-call(f32[384,128]{1,0:T(8,128)S(1)} %shard_map.185.refs_2_.refs_0_, f32[384,128]{1,0:T(8,128)S(1)} %collective-permute-done.22.refs_1_), custom_call_target="tpu_custom_call" | custom-call | flops 10000000000 | bytes 1048576 | tf_op jit(solution)/shard_map/pallas_call | solution.py:335
  75.6 3.5 %collective-permute-start.26 = (f32[8,256]{1,0:T(8,128)S(1)}, f32[8,256]{1,0:T(8,128)S(1)}, u32[]{:S(2)}, u32[]{:S(2)}) collective-permute-start(f32[8,256]{1,0:T(8,128)S(1)} %get-tuple-element.72.refs_0_), channel_id=1, source_target_pairs={{0,3},{1,2},{2,1},{3,0},{4,7},{5,6},{6,5},{7,4},{8,11},{9,10},{10,... | collective-permute-start | bytes 24584 | tf_op jit(solution)/shard_map/ppermute | solution.py:32
  81.1 2.5 %collective-permute-done.25.refs_2_ = f32[8,256]{1,0:T(8,128)S(1)} collective-permute-done((f32[8,256]{1,0:T(8,128)S(1)}, f32[8,256]{1,0:T(8,128)S(1)}, u32[]{:S(2)}, u32[]{:S(2)}) %collective-permute-start.25) | collective-permute-done | bytes 8224 | tf_op jit(solution)/shard_map/ppermute | solution.py:32
  84.4 2.8 %shard_map.193 = f32[2048,512]{1,0:T(8,128)} custom-call(s32[3]{0:T(128)S(1)} %pad_add_fusion.ranks, bf16[2048,256]{1,0:T(8,128)(2,1)S(1)} %get-tuple-element.70.pcat, bf16[256,512]{1,0:T(8,128)(2,1)S(1)} %get-tuple-element.74.y, f32[512,512]{1,0:T(8,128)S(1)} %get-tuple-element.63.refs_0_, f32[512,512]{1,0:T(8,128)S(1)} %get-tuple-element.64.refs_1_, ...), custom_call_target="tpu_custom_call" | custom-call | flops 536870912 | bytes 8388608 | tf_op jit(solution)/shard_map/pallas_call | solution.py:406
  87.3 3.3 %shard_map.192 = (bf16[2048,512]{1,0:T(8,128)(2,1)}, f32[512,256]{1,0:T(8,128)}) custom-call(s32[3]{0:T(128)S(1)} %pad_add_fusion.ranks, bf16[2048,256]{1,0:T(8,128)(2,1)S(1)} %get-tuple-element.70.pcat, f32[256,256]{1,0:T(8,128)S(1)} %shard_map.189.x, f32[256,512]{1,0:T(8,128)S(1)} %get-tuple-element.71.bt, f32[8,256]{1,0:T(8,128)S(1)} %shard_map.191.refs_0_, ...), custom_call_target="tpu_custom_call" | custom-call | flops 1073741824 | bytes 3145728 | tf_op jit(solution)/shard_map/pallas_call | solution.py:449
  (75 shorter events, 14.8 us)
Async XLA Ops:
  4.1 11.9 %collective-permute-start.1 = (bf16[512,256]{1,0:T(8,128)(2,1)S(1)}, bf16[512,256]{1,0:T(8,128)(2,1)S(1)}, u32[]{:S(2)}, u32[]{:S(2)}) collective-permute-start(bf16[512,256]{1,0:T(8,128)(2,1)S(1)} %get-tuple-element.41.refs_0_), channel_id=1, source_target_pairs={{0,16},{16,0},{1,17},{17,1},{2,18},{18,2},{3,19},{19,3},{4,20},{20... | collective-permute-start | bytes 786440 | tf_op jit(solution)/shard_map/ppermute | solution.py:32
  10.5 12.8 %collective-permute-start.2 = (bf16[512,256]{1,0:T(8,128)(2,1)S(1)}, bf16[512,256]{1,0:T(8,128)(2,1)S(1)}, u32[]{:S(2)}, u32[]{:S(2)}) collective-permute-start(bf16[512,256]{1,0:T(8,128)(2,1)S(1)} %get-tuple-element.42.refs_2_), channel_id=1, source_target_pairs={{0,16},{16,0},{1,17},{17,1},{2,18},{18,2},{3,19},{19,3},{4,20},{20... | collective-permute-start | bytes 786440 | tf_op jit(solution)/shard_map/ppermute | solution.py:32
  10.6 13.5 %collective-permute-start = (bf16[2,2,64,128]{3,2,1,0:T(8,128)(2,1)S(1)}, bf16[2,2,64,128]{3,2,1,0:T(8,128)(2,1)S(1)}, u32[]{:S(2)}, u32[]{:S(2)}) collective-permute-start(bf16[2,2,64,128]{3,2,1,0:T(8,128)(2,1)S(1)} %shard_map.174.refs_0_), channel_id=1, source_target_pairs={{0,16},{16,0},{1,17},{17,1},{2,18},{18,2},{3,19},{19,3},{4,20},{20... | collective-permute-start | bytes 196616 | tf_op jit(solution)/shard_map/ppermute | solution.py:32
  16.1 14.5 %collective-permute-start.8 = (bf16[256,256]{1,0:T(8,128)(2,1)S(1)}, bf16[256,256]{1,0:T(8,128)(2,1)S(1)}, u32[]{:S(2)}, u32[]{:S(2)}) collective-permute-start(bf16[256,256]{1,0:T(8,128)(2,1)S(1)} %get-tuple-element.52), channel_id=1, source_target_pairs={{0,3},{1,2},{2,1},{3,0},{4,7},{5,6},{6,5},{7,4},{8,11},{9,10},{10,... | collective-permute-start | bytes 393224 | tf_op jit(solution)/shard_map/ppermute | solution.py:32
  19.8 10.8 %collective-permute-start.7 = (bf16[256,256]{1,0:T(8,128)(2,1)S(1)}, bf16[256,256]{1,0:T(8,128)(2,1)S(1)}, u32[]{:S(2)}, u32[]{:S(2)}) collective-permute-start(bf16[256,256]{1,0:T(8,128)(2,1)S(1)} %get-tuple-element.44.refs_0_), channel_id=1, source_target_pairs={{0,2},{1,3},{2,0},{3,1},{4,6},{5,7},{6,4},{7,5},{8,10},{9,11},{10,... | collective-permute-start | bytes 393224 | tf_op jit(solution)/shard_map/ppermute | solution.py:32
  23.3 7.5 %collective-permute-start.6 = (bf16[256,256]{1,0:T(8,128)(2,1)S(1)}, bf16[256,256]{1,0:T(8,128)(2,1)S(1)}, u32[]{:S(2)}, u32[]{:S(2)}) collective-permute-start(bf16[256,256]{1,0:T(8,128)(2,1)S(1)} %get-tuple-element.51), channel_id=1, source_target_pairs={{0,1},{1,0},{2,3},{3,2},{4,5},{5,4},{6,7},{7,6},{8,9},{9,8},{10,11... | collective-permute-start | bytes 393224 | tf_op jit(solution)/shard_map/ppermute | solution.py:32
  25.1 10.4 %collective-permute-start.3 = (bf16[2,64,128]{2,1,0:T(8,128)(2,1)S(1)}, bf16[2,64,128]{2,1,0:T(8,128)(2,1)S(1)}, u32[]{:S(2)}, u32[]{:S(2)}) collective-permute-start(bf16[2,64,128]{2,1,0:T(8,128)(2,1)S(1)} %get-tuple-element.48), channel_id=1, source_target_pairs={{0,4},{4,0},{8,12},{12,8},{1,5},{5,1},{9,13},{13,9},{2,6},{6,2},{1... | collective-permute-start | bytes 98312 | tf_op jit(solution)/shard_map/ppermute | solution.py:32
  28.7 7.1 %collective-permute-start.4 = (bf16[2,64,128]{2,1,0:T(8,128)(2,1)S(1)}, bf16[2,64,128]{2,1,0:T(8,128)(2,1)S(1)}, u32[]{:S(2)}, u32[]{:S(2)}) collective-permute-start(bf16[2,64,128]{2,1,0:T(8,128)(2,1)S(1)} %get-tuple-element.49), channel_id=1, source_target_pairs={{0,8},{4,12},{8,0},{12,4},{1,9},{5,13},{9,1},{13,5},{2,10},{6,14},... | collective-permute-start | bytes 98312 | tf_op jit(solution)/shard_map/ppermute | solution.py:32
  30.8 18.9 %collective-permute-start.15 = (bf16[256,256]{1,0:T(8,128)(2,1)S(1)}, bf16[256,256]{1,0:T(8,128)(2,1)S(1)}, u32[]{:S(2)}, u32[]{:S(2)}) collective-permute-start(bf16[256,256]{1,0:T(8,128)(2,1)S(1)} %shard_map.180.refs_4_.refs_0_), channel_id=1, source_target_pairs={{0,16},{16,0},{1,17},{17,1},{2,18},{18,2},{3,19},{19,3},{4,20},{20... | collective-permute-start | bytes 393224 | tf_op jit(solution)/shard_map/ppermute | solution.py:32
  31.4 10.2 %collective-permute-start.14 = (bf16[256,256]{1,0:T(8,128)(2,1)S(1)}, bf16[256,256]{1,0:T(8,128)(2,1)S(1)}, u32[]{:S(2)}, u32[]{:S(2)}) collective-permute-start(bf16[256,256]{1,0:T(8,128)(2,1)S(1)} %shard_map.180.refs_4_.refs_0_), channel_id=1, source_target_pairs={{0,2},{1,3},{2,0},{3,1},{4,6},{5,7},{6,4},{7,5},{8,10},{9,11},{10,... | collective-permute-start | bytes 393224 | tf_op jit(solution)/shard_map/ppermute | solution.py:32
  33.5 9.6 %collective-permute-start.13 = (bf16[256,256]{1,0:T(8,128)(2,1)S(1)}, bf16[256,256]{1,0:T(8,128)(2,1)S(1)}, u32[]{:S(2)}, u32[]{:S(2)}) collective-permute-start(bf16[256,256]{1,0:T(8,128)(2,1)S(1)} %shard_map.180.refs_4_.refs_0_), channel_id=1, source_target_pairs={{0,1},{1,0},{2,3},{3,2},{4,5},{5,4},{6,7},{7,6},{8,9},{9,8},{10,11... | collective-permute-start | bytes 393224 | tf_op jit(solution)/shard_map/ppermute | solution.py:32
  35.4 8.2 %collective-permute-start.9 = (bf16[256,256]{1,0:T(8,128)(2,1)S(1)}, bf16[256,256]{1,0:T(8,128)(2,1)S(1)}, u32[]{:S(2)}, u32[]{:S(2)}) collective-permute-start(bf16[256,256]{1,0:T(8,128)(2,1)S(1)} %shard_map.180.refs_4_.refs_0_), channel_id=1, source_target_pairs={{0,3},{1,2},{2,1},{3,0},{4,7},{5,6},{6,5},{7,4},{8,11},{9,10},{10,... | collective-permute-start | bytes 393224 | tf_op jit(solution)/shard_map/ppermute | solution.py:32
  41.6 8.1 %collective-permute-start.17 = (bf16[256,256]{1,0:T(8,128)(2,1)S(1)}, bf16[256,256]{1,0:T(8,128)(2,1)S(1)}, u32[]{:S(2)}, u32[]{:S(2)}) collective-permute-start(bf16[256,256]{1,0:T(8,128)(2,1)S(1)} %collective-permute-done.14.refs_2_), channel_id=1, source_target_pairs={{0,16},{16,0},{1,17},{17,1},{2,18},{18,2},{3,19},{19,3},{4,20},{20... | collective-permute-start | bytes 393224 | tf_op jit(solution)/shard_map/ppermute | solution.py:32
  43.1 6.7 %collective-permute-start.16 = (bf16[256,256]{1,0:T(8,128)(2,1)S(1)}, bf16[256,256]{1,0:T(8,128)(2,1)S(1)}, u32[]{:S(2)}, u32[]{:S(2)}) collective-permute-start(bf16[256,256]{1,0:T(8,128)(2,1)S(1)} %collective-permute-done.13.refs_1_), channel_id=1, source_target_pairs={{0,16},{16,0},{1,17},{17,1},{2,18},{18,2},{3,19},{19,3},{4,20},{20... | collective-permute-start | bytes 393224 | tf_op jit(solution)/shard_map/ppermute | solution.py:32
  43.6 6.1 %collective-permute-start.18 = (bf16[256,256]{1,0:T(8,128)(2,1)S(1)}, bf16[256,256]{1,0:T(8,128)(2,1)S(1)}, u32[]{:S(2)}, u32[]{:S(2)}) collective-permute-start(bf16[256,256]{1,0:T(8,128)(2,1)S(1)} %collective-permute-done.9.refs_7_.refs_3_), channel_id=1, source_target_pairs={{0,16},{16,0},{1,17},{17,1},{2,18},{18,2},{3,19},{19,3},{4,20},{20... | collective-permute-start | bytes 393224 | tf_op jit(solution)/shard_map/ppermute | solution.py:32
  52.7 5.7 %collective-permute-start.19 = (bf16[256,512]{1,0:T(8,128)(2,1)S(1)}, bf16[256,512]{1,0:T(8,128)(2,1)S(1)}, u32[]{:S(2)}, u32[]{:S(2)}) collective-permute-start(bf16[256,512]{1,0:T(8,128)(2,1)S(1)} %shard_map.184.refs_0_), channel_id=1, source_target_pairs={{0,4},{4,0},{8,12},{12,8},{1,5},{5,1},{9,13},{13,9},{2,6},{6,2},{1... | collective-permute-start | bytes 786440 | tf_op jit(solution)/shard_map/ppermute | solution.py:32
  53.2 11.7 %collective-permute-start.22 = (f32[384,128]{1,0:T(8,128)S(1)}, f32[384,128]{1,0:T(8,128)S(1)}, u32[]{:S(2)}, u32[]{:S(2)}) collective-permute-start(f32[384,128]{1,0:T(8,128)S(1)} %shard_map.185.refs_2_.refs_0_), channel_id=1, source_target_pairs={{0,8},{4,12},{8,0},{12,4},{1,9},{5,13},{9,1},{13,5},{2,10},{6,14},... | collective-permute-start | bytes 589832 | tf_op jit(solution)/shard_map/ppermute | solution.py:32
  56.4 6.4 %collective-permute-start.11 = (bf16[2,64,128]{2,1,0:T(8,128)(2,1)S(1)}, bf16[2,64,128]{2,1,0:T(8,128)(2,1)S(1)}, u32[]{:S(2)}, u32[]{:S(2)}) collective-permute-start(bf16[2,64,128]{2,1,0:T(8,128)(2,1)S(1)} %get-tuple-element.60), channel_id=1, source_target_pairs={{0,8},{4,12},{8,0},{12,4},{1,9},{5,13},{9,1},{13,5},{2,10},{6,14},... | collective-permute-start | bytes 98312 | tf_op jit(solution)/shard_map/ppermute | solution.py:32
  56.6 6.5 %collective-permute-start.12 = (bf16[2,64,128]{2,1,0:T(8,128)(2,1)S(1)}, bf16[2,64,128]{2,1,0:T(8,128)(2,1)S(1)}, u32[]{:S(2)}, u32[]{:S(2)}) collective-permute-start(bf16[2,64,128]{2,1,0:T(8,128)(2,1)S(1)} %get-tuple-element.61), channel_id=1, source_target_pairs={{0,12},{4,8},{8,4},{12,0},{1,13},{5,9},{9,5},{13,1},{2,14},{6,10},... | collective-permute-start | bytes 98312 | tf_op jit(solution)/shard_map/ppermute | solution.py:32
  58.4 16.6 %collective-permute-start.23 = (bf16[256,512]{1,0:T(8,128)(2,1)S(1)}, bf16[256,512]{1,0:T(8,128)(2,1)S(1)}, u32[]{:S(2)}, u32[]{:S(2)}) collective-permute-start(bf16[256,512]{1,0:T(8,128)(2,1)S(1)} %shard_map.186.refs_4_.wa), channel_id=1, source_target_pairs={{0,8},{4,12},{8,0},{12,4},{1,9},{5,13},{9,1},{13,5},{2,10},{6,14},... | collective-permute-start | bytes 786440 | tf_op jit(solution)/shard_map/ppermute | solution.py:32
  63.8 16.3 %collective-permute-start.21 = (bf16[2,2,64,128]{3,2,1,0:T(8,128)(2,1)S(1)}, bf16[2,2,64,128]{3,2,1,0:T(8,128)(2,1)S(1)}, u32[]{:S(2)}, u32[]{:S(2)}) collective-permute-start(bf16[2,2,64,128]{3,2,1,0:T(8,128)(2,1)S(1)} %get-tuple-element.69), channel_id=1, source_target_pairs={{0,16},{16,0},{1,17},{17,1},{2,18},{18,2},{3,19},{19,3},{4,20},{20... | collective-permute-start | bytes 196616 | tf_op jit(solution)/shard_map/ppermute | solution.py:32
  75.6 5.5 %collective-permute-start.26 = (f32[8,256]{1,0:T(8,128)S(1)}, f32[8,256]{1,0:T(8,128)S(1)}, u32[]{:S(2)}, u32[]{:S(2)}) collective-permute-start(f32[8,256]{1,0:T(8,128)S(1)} %get-tuple-element.72.refs_0_), channel_id=1, source_target_pairs={{0,3},{1,2},{2,1},{3,0},{4,7},{5,6},{6,5},{7,4},{8,11},{9,10},{10,... | collective-permute-start | bytes 24584 | tf_op jit(solution)/shard_map/ppermute | solution.py:32
  79.1 4.5 %collective-permute-start.25 = (f32[8,256]{1,0:T(8,128)S(1)}, f32[8,256]{1,0:T(8,128)S(1)}, u32[]{:S(2)}, u32[]{:S(2)}) collective-permute-start(f32[8,256]{1,0:T(8,128)S(1)} %get-tuple-element.72.refs_0_), channel_id=1, source_target_pairs={{0,2},{1,3},{2,0},{3,1},{4,6},{5,7},{6,4},{7,5},{8,10},{9,11},{10,... | collective-permute-start | bytes 24584 | tf_op jit(solution)/shard_map/ppermute | solution.py:32
  79.1 4.5 %collective-permute-start.24 = (f32[8,256]{1,0:T(8,128)S(1)}, f32[8,256]{1,0:T(8,128)S(1)}, u32[]{:S(2)}, u32[]{:S(2)}) collective-permute-start(f32[8,256]{1,0:T(8,128)S(1)} %get-tuple-element.72.refs_0_), channel_id=1, source_target_pairs={{0,1},{1,0},{2,3},{3,2},{4,5},{5,4},{6,7},{7,6},{8,9},{9,8},{10,11... | collective-permute-start | bytes 24584 | tf_op jit(solution)/shard_map/ppermute | solution.py:32
  (14 other events, 122.1 us)

commit v5 on v4

--- a/solution.py
+++ b/solution.py
@@ -53,12 +53,11 @@
     return jnp.dot(a, b, precision=HIGHEST, preferred_element_type=F32)
 
 
-def project_kernel(j, n_head, first, number, ranks, mom, grad, basis, *refs):
-    out, total, grads, right, sems, right_sem = refs[-6:]
-    chunk = total.shape[0] // number
+def row_copies(ranks, n_head, part, mom, grad, mom_to, grad_to, sems):
+    j, first, number = part
+    chunk = mom_to.shape[0] // number
     pieces = 2 if chunk % 32 == 0 else 1
     size = chunk // pieces
-    fetch = pltpu.make_async_copy(basis, right, right_sem)
     copies = []
     for i in range(number):
         at = ((ranks[0] ^ j) * n_head + (ranks[2] ^ (first + i))) * chunk
@@ -67,50 +66,100 @@
             src = pl.ds(pl.multiple_of(at + p * size, size), size)
             dst = pl.ds(i * chunk + p * size, size)
             n = i * pieces + p
+            copies[i].append(pltpu.make_async_copy(mom.at[src, :], mom_to.at[dst, :], sems.at[0, n]))
             copies[i].append(
-                pltpu.make_async_copy(mom.at[src, :], total.at[dst, :], sems.at[0, n])
+                pltpu.make_async_copy(grad.at[src, :], grad_to.at[dst, :], sems.at[1, n])
             )
-            copies[i].append(
-                pltpu.make_async_copy(grad.at[src, :], grads.at[dst, :], sems.at[1, n])
-            )
-        for c in copies[i]:
+    return copies
+
+
+def start_all(copies):
+    for row in copies:
+        for c in row:
             c.start()
-        if i == 0:
-            fetch.start()
-    fetch.wait()
-    b_hi, b_lo = halves(right[...])
+
+
+def project_kernel(n_head, part, following, is_first, n_in, ranks, mom, grad, *refs):
+    ins, refs = refs[:n_in], list(refs)
+    number = part[2]
+    sems = refs.pop()
+    ahead = []
+    if is_first:
+        right_sem, right, grad_in = refs.pop(), refs.pop(), refs.pop()
+    if following:
+        next_grad, next_mom = refs.pop(), refs.pop()
+        ahead = row_copies(ranks, n_head, following, mom, grad, next_mom, next_grad, sems.at[1])
+    if is_first:
+        b_lo, b_hi = refs.pop(), refs.pop()
+        total, out = refs.pop(), refs.pop()
+        mom_in = total
+        copies = row_copies(ranks, n_head, part, mom, grad, mom_in, grad_in, sems.at[0])
+        fetch = pltpu.make_async_copy(ins[0], right, right_sem)
+        start_all(copies[:1])
+        fetch.start()
+        start_all(copies[1:])
+        fetch.wait()
+        hi, lo = halves(right[...])
+        b_hi[...] = hi
+        b_lo[...] = lo
+    else:
+        total, out = refs.pop(), refs.pop()
+        b_hi, b_lo, mom_in, grad_in = ins
+        copies = [[]] * number
+        start_all(ahead)
+    chunk = total.shape[0] // number
     for i in range(number):
         for c in copies[i]:
             c.wait()
+        if is_first and i == 0:
+            start_all(ahead)
         rows = slice(i * chunk, (i + 1) * chunk)
-        t = total[rows, :] + grads[rows, :].astype(F32)
+        t = mom_in[rows, :] + grad_in[rows, :].astype(F32)
         total[rows, :] = t
         t_hi, t_lo = halves(t)
-        acc = mm(t_hi, b_hi) + (mm(t_hi, b_lo) + mm(t_lo, b_hi))
+        acc = mm(t_hi, b_hi[...]) + (mm(t_hi, b_lo[...]) + mm(t_lo, b_hi[...]))
         out[rows, :] = acc.astype(out.dtype)
-
-
-def project(ranks, momentum, grad_q, basis, j, first, number, n_resp, n_head, dtype, after):
+    for row in ahead:
+        for c in row:
+            c.wait()
+
+
+def project(ranks, momentum, grad_q, ins, part, following, n_resp, n_head, dtype, after):
+    is_first = len(ins) == 1
     rows, cols = momentum.shape
-    rank = basis.shape[1]
-    size = rows // (n_resp * n_head) * number
-    return pl.pallas_call(
-        functools.partial(project_kernel, j, n_head, first, number),
-        in_specs=[SMEM] + [HBM] * 3 + [ANY] * len(after),
-        out_specs=[VMEM] * 2,
-        scratch_shapes=[
-            pltpu.VMEM((size, cols), BF16),
-            pltpu.VMEM((cols, rank), F32),
-            pltpu.SemaphoreType.DMA((2, 2 * number)),
-            pltpu.SemaphoreType.DMA,
-        ],
-        out_shape=[
-            jax.ShapeDtypeStruct((size, rank), dtype),
-            jax.ShapeDtypeStruct((size, cols), F32),
-        ],
-        compiler_params=params(10),
+    chunk = rows // (n_resp * n_head)
+    size = part[2] * chunk
+    if is_first:
+        right = ins[0]
+        rank = right.shape[1]
+        specs = [HBM]
+    else:
+        rank = ins[0].shape[1]
+        specs = [VMEM] * 4
+    out_shape = [jax.ShapeDtypeStruct((size, rank), dtype), jax.ShapeDtypeStruct((size, cols), F32)]
+    if is_first:
+        out_shape += [jax.ShapeDtypeStruct((cols, rank), BF16)] * 2
+    if following:
+        ahead = following[2] * chunk
+        out_shape += [
+            jax.ShapeDtypeStruct((ahead, cols), F32), jax.ShapeDtypeStruct((ahead, cols), BF16)
+        ]
+    scratch = [pltpu.SemaphoreType.DMA((2, 2, 2 * n_head))]
+    if is_first:
+        scratch = [
+            pltpu.VMEM((size, cols), BF16), pltpu.VMEM((cols, rank), F32), pltpu.SemaphoreType.DMA
+        ] + scratch
+    outs = pl.pallas_call(
+        functools.partial(project_kernel, n_head, part, following, is_first, len(ins)),
+        in_specs=[SMEM, HBM, HBM] + specs + [ANY] * len(after),
+        out_specs=[VMEM] * len(out_shape),
+        scratch_shapes=scratch,
+        out_shape=out_shape,
+        compiler_params=params(14),
         cost_estimate=cost(6 * size * cols * rank, size * cols * 6),
-    )(ranks, momentum, grad_q, basis, *after)
+    )(ranks, momentum, grad_q, *ins, *after)
+    right = tuple(outs[2:4]) if is_first else tuple(ins[:2])
+    return outs[0], outs[1], right + tuple(outs[-2:] if following else ())
 
 
 def split_kernel(n_recv, number, own, *refs):
@@ -227,14 +276,18 @@
         for i in range(j, PANEL):
             d[i, j] = jnp.broadcast_to(col[i : i + 1, :], shape)
     low, inv = {}, {}
-    for j in range(PANEL):
-        r = lax.rsqrt(d[j, j])
-        inv[j, j] = r
-        for i in range(j + 1, PANEL):
-            low[i, j] = d[i, j] * r
-        for k in range(j + 1, PANEL):
+    for j in range(0, PANEL, 2):
+        a, b, c = d[j, j], d[j + 1, j], d[j + 1, j + 1]
+        first = lax.rsqrt(a)
+        second = lax.rsqrt(a * c - b * b) * (a * first)
+        inv[j, j], inv[j + 1, j + 1] = first, second
+        low[j + 1, j] = b * first
+        for i in range(j + 2, PANEL):
+            low[i, j] = d[i, j] * first
+            low[i, j + 1] = (d[i, j + 1] - low[i, j] * low[j + 1, j]) * second
+        for k in range(j + 2, PANEL):
             for i in range(k, PANEL):
-                d[i, k] = d[i, k] - low[i, j] * low[k, j]
+                d[i, k] = d[i, k] - (low[i, j] * low[k, j] + low[i, j + 1] * low[k, j + 1])
     for j in range(PANEL):
         for i in range(j + 1, PANEL):
             acc = low[i, j] * inv[j, j]
@@ -264,6 +317,11 @@
     work[half:, :half] = low
     work[:half, half:] = low.T
     work[half:, half:] = total[2 * half :, :]
+    eye = lax.broadcasted_iota(jnp.int32, (n, n), 0) == lax.broadcasted_iota(jnp.int32, (n, n), 1)
+    whole = work[...]
+    diag = jnp.where(eye, whole, 0.0)
+    across = lax.rsqrt(jnp.sum(diag, axis=0, keepdims=True))
+    work[...] = whole * lax.rsqrt(jnp.sum(diag, axis=1, keepdims=True)) * across
     sub = lax.broadcasted_iota(jnp.int32, (PANEL, 128), 0)
     lane = lax.broadcasted_iota(jnp.int32, (PANEL, 128), 1)
     n_panels = OUTER // PANEL
@@ -327,7 +385,7 @@
         return carry
 
     lax.fori_loop(0, n // OUTER, step, 0)
-    out[...] = work[...]
+    out[...] = work[...] * across
 
 
 def inverse_factor(*parts):
@@ -382,39 +440,47 @@
     ]
 
 
-def momentum_kernel(n_resp, n_head, ranks, pcat, y, *refs):
-    totals, (out, held, sems) = refs[:-3], refs[-3:]
+def momentum_kernel(n_resp, n_head, begin, end, n_totals, ranks, pcat, y, *refs):
+    totals, (out, held, sems) = refs[:n_totals], refs[-3:]
     seg = totals[0].shape[0]
     chunk = pcat.shape[0] // (n_resp * n_head)
+    blocks = row_blocks(ranks, n_resp, n_head, chunk)
     copies = []
-    for i, at in enumerate(row_blocks(ranks, n_resp, n_head, chunk)):
+    for i in range(begin, end):
         rows = slice(i * chunk, (i + 1) * chunk)
+        kept = slice((i - begin) * chunk, (i - begin + 1) * chunk)
         off = i * chunk % seg
-        total = totals[i * chunk // seg][off : off + chunk, :]
-        held[rows, :] = total - mm(pcat[rows, :], y[...])
+        total = totals[(i - begin) * chunk // seg][off : off + chunk, :]
+        held[kept, :] = total - mm(pcat[rows, :], y[...])
         copies.append(
-            pltpu.make_async_copy(held.at[rows, :], out.at[pl.ds(at, chunk), :], sems.at[i])
+            pltpu.make_async_copy(
+                held.at[kept, :], out.at[pl.ds(blocks[i], chunk), :], sems.at[i - begin]
+            )
         )
         copies[-1].start()
     for c in copies:
         c.wait()
 
 
-def new_momentum(ranks, pcat, totals, y, n_resp, n_head):
+def new_momentum(ranks, pcat, totals, y, n_resp, n_head, half, earlier):
     rows, rank = pcat.shape
     cols = totals[0].shape[1]
-    return pl.pallas_call(
-        functools.partial(momentum_kernel, n_resp, n_head),
-        in_specs=[SMEM] + [VMEM] * (2 + len(totals)),
+    n_chunks = n_resp * n_head // 2
+    part = len(totals) // 2
+    totals = totals[half * part : (half + 1) * part]
+    aliases = {3 + part: 0} if earlier else {}
+    return pl.pallas_call(
+        functools.partial(
+            momentum_kernel, n_resp, n_head, half * n_chunks, (half + 1) * n_chunks, part
+        ),
+        in_specs=[SMEM] + [VMEM] * (2 + part) + [HBM] * len(earlier),
         out_specs=HBM,
-        scratch_shapes=[
-            pltpu.VMEM((rows, cols), F32),
-            pltpu.SemaphoreType.DMA((n_resp * n_head,)),
-        ],
+        scratch_shapes=[pltpu.VMEM((rows // 2, cols), F32), pltpu.SemaphoreType.DMA((n_chunks,))],
         out_shape=jax.ShapeDtypeStruct((rows, cols), F32),
-        compiler_params=params(14),
-        cost_estimate=cost(2 * rows * cols * rank, rows * cols * 8),
-    )(ranks, pcat, y, *totals)
+        input_output_aliases=aliases,
+        compiler_params=params(10),
+        cost_estimate=cost(rows * cols * rank, rows * cols * 4),
+    )(ranks, pcat, y, *totals, *earlier)
 
 
 def update_kernel(gain, n_resp, n_head, n_sums, ranks, pcat, x, bt, *refs):
@@ -521,9 +587,9 @@
     n_fsdp, heads, last, ranks, counts, prompt_blocks, resp_blocks, q, sk, sv, go, *refs
 ):
     pieces, refs = refs[:n_fsdp], refs[n_fsdp:]
-    dq_held, keys, values, dk, dv, sem = refs[-6:]
+    keys, values, dk, dv = refs[-4:]
     n_out = 2 + n_fsdp if last else 3
-    outs = refs[-6 - n_out : -6]
+    outs = refs[-4 - n_out : -4]
     dq = outs[0]
     piece = pieces[0].shape[1]
     cap = piece * n_fsdp
@@ -556,7 +622,7 @@
     else:
         dk[...] = jnp.zeros_like(dk)
         dv[...] = jnp.zeros_like(dv)
-    for i, h in enumerate(heads):
+    for h in heads:
         cols = slice(h * HD, (h + 1) * HD)
         qh = q[:, cols]
         gh = jnp.where(live, go[:, cols], jnp.zeros((), BF16))
@@ -570,11 +636,10 @@
         ds = (wf * (dp - diag)).astype(BF16)
         dk[...] += mm(ds, qh)
         dv[...] += mm(w, gh)
-        dq_held[:, i * HD : (i + 1) * HD] = (mm(kt, ds) * scale).T.astype(BF16)
-    to = dq.at[:, pl.ds(heads[0] * HD, len(heads) * HD)]
-    copy = pltpu.make_async_copy(dq_held, to, sem)
-    copy.start()
+        dq[:, cols] = (mm(kt, ds) * scale).T.astype(BF16)
     if last:
+        done = heads[0] * HD
+        dq[:, :done] = refs[2][...]
         own, sends = outs[1], outs[2:]
         own[0] = (dk[cap:, :] * scale).astype(BF16)
         own[1] = dv[cap:, :].astype(BF16)
@@ -585,7 +650,6 @@
     else:
         outs[1][...] = dk[...]
         outs[2][...] = dv[...]
-    copy.wait()
 
 
 def attention(heads, earlier, ranks, counts, prompt_blocks, resp_blocks, q, sk, sv, go, pieces, after):
@@ -595,27 +659,21 @@
     cap = piece * n_fsdp
     total = cap + length
     last = earlier is not None
-    dq_shape = jax.ShapeDtypeStruct((length, width), BF16)
     if last:
-        extra, specs = (earlier[1], earlier[2], earlier[0]), [VMEM, VMEM, HBM]
-        out_shape = [dq_shape, jax.ShapeDtypeStruct((2, length, HD), BF16)] + [
+        extra, specs = (earlier[1], earlier[2], earlier[0]), [VMEM] * 3
+        out_shape = [pltpu.VMEM((length, width), BF16), jax.ShapeDtypeStruct((2, length, HD), BF16)] + [
             jax.ShapeDtypeStruct((2, piece, HD), BF16 if k else F32) for k in range(n_fsdp)
         ]
-        aliases = {8 + n_fsdp + 2: 0}
     else:
         extra, specs = (), []
-        out_shape = [dq_shape] + [jax.ShapeDtypeStruct((total, HD), F32)] * 2
-        aliases = {}
+        out_shape = [jax.ShapeDtypeStruct((length, len(heads) * HD), BF16)]
+        out_shape += [jax.ShapeDtypeStruct((total, HD), F32)] * 2
     return pl.pallas_call(
         functools.partial(attention_kernel, n_fsdp, heads, last),
         in_specs=[SMEM] * 4 + [VMEM] * (4 + n_fsdp) + specs + [ANY] * len(after),
-        out_specs=[HBM] + [VMEM] * (len(out_shape) - 1),
-        scratch_shapes=[pltpu.VMEM((length, len(heads) * HD), BF16)]
-        + [pltpu.VMEM((total, HD), BF16)] * 2
-        + [pltpu.VMEM((total, HD), F32)] * 2
-        + [pltpu.SemaphoreType.DMA],
+        out_specs=[VMEM] * len(out_shape),
+        scratch_shapes=[pltpu.VMEM((total, HD), BF16)] * 2 + [pltpu.VMEM((total, HD), F32)] * 2,
         out_shape=out_shape,
-        input_output_aliases=aliases,
         compiler_params=params(12),
         cost_estimate=cost(3_000_000_000, length * width * 8),
     )(ranks, counts, prompt_blocks, resp_blocks, q, sk, sv, go, *pieces, *extra, *after)
@@ -677,29 +735,33 @@
     half = n_head // 2
     groups = [(half, half), (0, half)] if half else [(0, n_head)]
 
-    totals, after = {}, ()
-    arrived = []
-    for first, number in groups:
+    mom_hbm, grad_hbm, basis_hbm = in_hbm
+    order = [(j, *group) for group in groups for j in range(1, n_resp)]
+    order += [(0, *group) for group in groups]
+    nexts = dict(zip(order, order[1:] + [None]))
+    totals, arrived, ins = {}, [], (basis_hbm,)
+
+    def project_next(part, dtype, after):
+        return project(
+            ranks, mom_hbm, grad_hbm, ins, part, nexts[part], n_resp, n_head, dtype, after
+        )
+
+    for group in groups:
         row = []
         for j in range(1, n_resp):
-            sent, totals[j, first] = project(
-                ranks, *in_hbm, j, first, number, n_resp, n_head, BF16, after
-            )
-            after = (sent,)
+            sent, totals[j, group[0]], ins = project_next((j, *group), BF16, ())
             row.append(swap(sent, "resp", j))
         arrived.append(row)
-    packed = pack_prompts(prompt_keys, prompt_values, after)
+    packed = pack_prompts(prompt_keys, prompt_values, (sent,))
     stored = [packed] + [swap(packed, "resp", j) for j in range(1, n_resp)]
     after = (packed,)
     split = {}
-    for (first, number), recvs in zip(groups, arrived):
-        mine, totals[0, first] = project(
-            ranks, *in_hbm, 0, first, number, n_resp, n_head, F32, after
-        )
-        outs = split_sum(mine, recvs, first, number)
+    for group, recvs in zip(groups, arrived):
+        mine, totals[0, group[0]], ins = project_next((0, *group), F32, after)
+        outs = split_sum(mine, recvs, *group)
         after = (outs[0],)
-        for i in range(number):
-            split[first + i] = outs[i]
+        for i in range(group[1]):
+            split[group[0] + i] = outs[i]
     totals = [totals[at] for at in sorted(totals)]
     chosen = select_prompts(ranks, counts, owner_slot, stored, n_fsdp, after)
     far_first = [k for first, number in groups for k in range(first, first + number) if k]
@@ -733,16 +795,18 @@
     gram_parts = (gram, swap(gram, "fsdp", bits[-1]))
     w_other = swap(w, "fsdp", bits[-1])
     returned = [parts[0]] + [swap(parts[k], "fsdp", k) for k in range(1, n_fsdp)]
-    slots = sum_by_slot(ranks, counts, owner_slot, returned, n_resp, (w,))
     x = inverse_factor(*gram_parts)
+    slots = sum_by_slot(ranks, counts, owner_slot, returned, n_resp, (x,))
     prompt_grad = sum_parts(
         [slots[0]] + [swap(slots[j], "resp", j) for j in range(1, n_resp)], F32
     )
 
     bt, y, squares = back_full(x, w, w_other)
-    squares = sum_parts([squares] + [swap(squares, "head", k) for k in range(1, n_head)], F32)
-    momentum_out = new_momentum(ranks, pcat, totals, y, n_resp, n_head)
+    from_head = [swap(squares, "head", k) for k in range(1, n_head)]
+    momentum_out = new_momentum(ranks, pcat, totals, y, n_resp, n_head, 0, ())
+    squares = sum_parts([squares] + from_head, F32, (momentum_out,))
     sums = [squares] + [swap(squares, "resp", j) for j in range(1, n_resp)]
+    momentum_out = new_momentum(ranks, pcat, totals, y, n_resp, n_head, 1, (momentum_out,))
     update, basis_out = final_update(ranks, pcat, x, bt, sums, gain, n_resp, n_head)
     return (dq, resp_grad, prompt_grad, update, momentum_out, basis_out)
 

time: 91.1 us -> 99 us (1.087)
  waiting for transfers between devices: 11.3 us -> 21.8 us
  Pallas kernels: 43.1 us -> 39.7 us
  local copies, waits for them, and re-layouts: 0.95 us -> 3.93 us
  starting transfers between devices: 33.6 us -> 31.5 us
    ppermute x28, waiting for transfers between devices: 11.3 us -> 21.8 us  [swap(): return lax.ppermute(value, axes, [(i, i ^ k) for i in range(n)])]
    unnamed x20 -> x23, local copies, waits for them, and re-layouts: 0.95 us -> 3.93 us
    ppermute x28, starting transfers between devices: 33.6 us -> 31.5 us  [swap(): return lax.ppermute(value, axes, [(i, i ^ k) for i in range(n)])]
    pallas_call x5 -> x6, Pallas kernels: 16.2 us -> 14.7 us  [the longest x4 10.4 us: project(): pl.pallas_call(functools.partial(project_kernel, n_head, part, following,...]
    pallas_call x2, Pallas kernels: 8.55 us -> 7.09 us  [attention(): pl.pallas_call(functools.partial(attention_kernel, n_fsdp, heads, last),...]
  transfers between devices with their start and end apart: 28 -> 28, of which waited for: 8 -> 8; matrix products, arithmetic and copies ran while one was open for 0% -> 1% of each run, Pallas kernels for 40% -> 32%
where the time goes in v5:
time: 99 us; the launch traced here: 98.7 us
  Pallas kernels  39.7 us (40%)
  starting transfers between devices  31.5 us (32%)
  waiting for transfers between devices  21.8 us (22%)
  local copies, waits for them, and re-layouts  3.93 us (4%)
  between operations  1.79 us (2%)
    ppermute x28, starting transfers between devices, swap(): return lax.ppermute(value, axes, [(i, i ^ k) for i in range(n)])  31.5 us
    ppermute x28, waiting for transfers between devices, swap(): return lax.ppermute(value, axes, [(i, i ^ k) for i in range(n)])  21.8 us
    pallas_call x4, Pallas kernels, project(): pl.pallas_call(functools.partial(project_kernel, n_head, part, following,...  10.4 us
    pallas_call x1, Pallas kernels, inverse_factor(): pl.pallas_call(functools.partial(cholesky_kernel, len(parts)), in_specs=[...  9.89 us
    pallas_call x2, Pallas kernels, attention(): pl.pallas_call(functools.partial(attention_kernel, n_fsdp, heads, last),...  7.09 us
    pallas_call x2, Pallas kernels, new_momentum(): pl.pallas_call(functools.partial(momentum_kernel, n_resp, n_head, half *...  4.25 us
    unnamed x23, local copies, waits for them, and re-layouts  3.93 us
    pallas_call x1, Pallas kernels, final_update(): pl.pallas_call(functools.partial(update_kernel, gain, n_resp, n_head, len...  3.31 us
  transfers between devices with their start and end apart: 28, of which 8 were waited for; matrix products, arithmetic and copies ran while one was open for 1% of the time, Pallas kernels for 32%

profile of v5, /device:TPU:0, one launch (start us, length us, event | category | flops | bytes accessed | tf_op | source)
XLA Modules:
  0.0 98.7 jit_solution(17087090349156146532)
XLA Ops:
  0.7 3.8 %shard_map.172 = (bf16[512,256]{1,0:T(8,128)(2,1)S(1)}, f32[512,512]{1,0:T(8,128)S(1)}, bf16[512,256]{1,0:T(8,128)(2,1)S(1)}, bf16[512,256]{1,0:T(8,128)(2,1)S(1...) custom-call(s32[3]{0:T(128)S(1)} %pad_add_fusion.ranks, f32[2048,512]{1,0:T(8,128)} %mom.7, ...), custom_call_target="tpu_custom_call" | custom-call | flops 402653184 | bytes 1572864 | tf_op jit(solution)/shard_map/pallas_call | solution.py:152
  4.5 3.0 %collective-permute-start.1 = (bf16[512,256]{1,0:T(8,128)(2,1)S(1)}, bf16[512,256]{1,0:T(8,128)(2,1)S(1)}, u32[]{:S(2)}, u32[]{:S(2)}) collective-permute-start(bf16[512,256]{1,0:T(8,128)(2,1)S(1)} %get-tuple-element.59), channel_id=1, source_target_pairs={{0,16},{16,0},{1,17},{17,1},{2,18},{18,2},{3,19},{19,3},{4,20},{20... | collective-permute-start | bytes 786440 | tf_op jit(solution)/shard_map/ppermute | solution.py:32
  7.5 2.6 %shard_map.173 = (bf16[512,256]{1,0:T(8,128)(2,1)S(1)}, f32[512,512]{1,0:T(8,128)S(1)}, f32[512,512]{1,0:T(8,128)S(1)}, bf16[512,512]{1,0:T(8,128)(2,1)S(1)}) custom-call(s32[3]{0:T(128)S(1)} %pad_add_fusion.ranks, f32[2048,512]{1,0:T(8,128)} %mom.7, bf16[2048,512]{1,0:T(8,128)(2,1)} %grad.7, bf16[512,256]{1,0:T(8,128)(2,1)S(1)} %get-tuple-element.49.refs_0_, ...), custom_call_target="tpu_custom_call" | custom-call | flops 402653184 | bytes 1572864 | tf_op jit(solution)/shard_map/pallas_call | solution.py:152
  10.2 2.1 %collective-permute-start = (bf16[2,2,64,128]{3,2,1,0:T(8,128)(2,1)S(1)}, bf16[2,2,64,128]{3,2,1,0:T(8,128)(2,1)S(1)}, u32[]{:S(2)}, u32[]{:S(2)}) collective-permute-start(bf16[2,2,64,128]{3,2,1,0:T(8,128)(2,1)S(1)} %shard_map.174.refs_4_.refs_0_), channel_id=1, source_target_pairs={{0,16},{16,0},{1,17},{17,1},{2,18},{18,2},{3,19},{19,3},{4,20},{20... | collective-permute-start | bytes 196616 | tf_op jit(solution)/shard_map/ppermute | solution.py:32
  12.3 2.6 %shard_map.175 = (f32[512,256]{1,0:T(8,128)S(1)}, f32[512,512]{1,0:T(8,128)S(1)}, f32[512,512]{1,0:T(8,128)S(1)}, bf16[512,512]{1,0:T(8,128)(2,1)S(1)}) custom-call(s32[3]{0:T(128)S(1)} %pad_add_fusion.ranks, f32[2048,512]{1,0:T(8,128)} %mom.7, bf16[2048,512]{1,0:T(8,128)(2,1)} %grad.7, bf16[512,256]{1,0:T(8,128)(2,1)S(1)} %get-tuple-element.49.refs_0_, ...), custom_call_target="tpu_custom_call" | custom-call | flops 402653184 | bytes 1572864 | tf_op jit(solution)/shard_map/pallas_call | solution.py:152
  16.5 3.7 %collective-permute-done.2.refs_0_ = bf16[512,256]{1,0:T(8,128)(2,1)S(1)} collective-permute-done((bf16[512,256]{1,0:T(8,128)(2,1)S(1)}, bf16[512,256]{1,0:T(8,128)(2,1)S(1)}, u32[]{:S(2)}, u32[]{:S(2)}) %collective-permute-start.2) | collective-permute-done | bytes 262176 | tf_op jit(solution)/shard_map/ppermute | solution.py:32
  20.2 1.9 %collective-permute-start.6 = (bf16[256,256]{1,0:T(8,128)(2,1)S(1)}, bf16[256,256]{1,0:T(8,128)(2,1)S(1)}, u32[]{:S(2)}, u32[]{:S(2)}) collective-permute-start(bf16[256,256]{1,0:T(8,128)(2,1)S(1)} %get-tuple-element.67), channel_id=1, source_target_pairs={{0,1},{1,0},{2,3},{3,2},{4,5},{5,4},{6,7},{7,6},{8,9},{9,8},{10,11... | collective-permute-start | bytes 393224 | tf_op jit(solution)/shard_map/ppermute | solution.py:32
  22.1 2.5 %collective-permute-start.8 = (bf16[256,256]{1,0:T(8,128)(2,1)S(1)}, bf16[256,256]{1,0:T(8,128)(2,1)S(1)}, u32[]{:S(2)}, u32[]{:S(2)}) collective-permute-start(bf16[256,256]{1,0:T(8,128)(2,1)S(1)} %get-tuple-element.68), channel_id=1, source_target_pairs={{0,3},{1,2},{2,1},{3,0},{4,7},{5,6},{6,5},{7,4},{8,11},{9,10},{10,... | collective-permute-start | bytes 393224 | tf_op jit(solution)/shard_map/ppermute | solution.py:32
  25.5 1.6 %collective-permute-start.3 = (bf16[2,64,128]{2,1,0:T(8,128)(2,1)S(1)}, bf16[2,64,128]{2,1,0:T(8,128)(2,1)S(1)}, u32[]{:S(2)}, u32[]{:S(2)}) collective-permute-start(bf16[2,64,128]{2,1,0:T(8,128)(2,1)S(1)} %get-tuple-element.64), channel_id=1, source_target_pairs={{0,4},{4,0},{8,12},{12,8},{1,5},{5,1},{9,13},{13,9},{2,6},{6,2},{1... | collective-permute-start | bytes 98312 | tf_op jit(solution)/shard_map/ppermute | solution.py:32
  27.1 2.0 %collective-permute-done.5.refs_4_.refs_3_ = bf16[2,64,128]{2,1,0:T(8,128)(2,1)S(1)} collective-permute-done((bf16[2,64,128]{2,1,0:T(8,128)(2,1)S(1)}, bf16[2,64,128]{2,1,0:T(8,128)(2,1)S(1)}, u32[]{:S(2)}, u32[]{:S(2)}) %collective-permute-start.5) | collective-permute-done | bytes 32800 | tf_op jit(solution)/shard_map/ppermute | solution.py:32
  31.0 3.8 %collective-permute-done.7.refs_2_ = bf16[256,256]{1,0:T(8,128)(2,1)S(1)} collective-permute-done((bf16[256,256]{1,0:T(8,128)(2,1)S(1)}, bf16[256,256]{1,0:T(8,128)(2,1)S(1)}, u32[]{:S(2)}, u32[]{:S(2)}) %collective-permute-start.7) | collective-permute-done | bytes 131104 | tf_op jit(solution)/shard_map/ppermute | solution.py:32
  36.7 2.9 %collective-permute-start.13 = (bf16[256,256]{1,0:T(8,128)(2,1)S(1)}, bf16[256,256]{1,0:T(8,128)(2,1)S(1)}, u32[]{:S(2)}, u32[]{:S(2)}) collective-permute-start(bf16[256,256]{1,0:T(8,128)(2,1)S(1)} %shard_map.180.refs_4_.refs_0_), channel_id=1, source_target_pairs={{0,1},{1,0},{2,3},{3,2},{4,5},{5,4},{6,7},{7,6},{8,9},{9,8},{10,11... | collective-permute-start | bytes 393224 | tf_op jit(solution)/shard_map/ppermute | solution.py:32
  40.8 3.2 %shard_map.181 = (bf16[256,512]{1,0:T(8,128)(2,1)S(1)}, f32[512,128]{1,0:T(8,128)S(1)}, f32[512,128]{1,0:T(8,128)S(1)}) custom-call(s32[3]{0:T(128)S(1)} %pad_add_fusion.ranks, s32[4]{0:T(128)S(1)} %copy-done.4, s32[4]{0:T(128)S(1)} %copy-done.10, s32[1]{0:T(128)S(6)} %copy.22.resp_blocks, bf16[256,1024]{1,0:T(8,128)(2,1)S(1)} %copy-done.6, ...), custom_call_target="tpu_custom_call" | custom-call | flops 3000000000 | bytes 2097152 | tf_op jit(solution)/shard_map/pallas_call | solution.py:671
  44.0 3.5 %collective-permute-done.14.refs_2_ = bf16[256,256]{1,0:T(8,128)(2,1)S(1)} collective-permute-done((bf16[256,256]{1,0:T(8,128)(2,1)S(1)}, bf16[256,256]{1,0:T(8,128)(2,1)S(1)}, u32[]{:S(2)}, u32[]{:S(2)}) %collective-permute-start.14) | collective-permute-done | bytes 131104 | tf_op jit(solution)/shard_map/ppermute | solution.py:32
  50.1 3.9 %shard_map.182 = (bf16[256,1024]{1,0:T(8,128)(2,1)S(1)}, bf16[2,256,128]{2,1,0:T(8,128)(2,1)}, f32[2,64,128]{2,1,0:T(8,128)S(1)}, bf16[2,64,128]{2,1,0:T(8,128)(...) custom-call(s32[3]{0:T(128)S(1)} %pad_add_fusion.ranks, s32[4]{0:T(128)S(1)} %copy-done.4, ...), custom_call_target="tpu_custom_call" | custom-call | flops 3000000000 | bytes 2097152 | tf_op jit(solution)/shard_map/pallas_call | solution.py:671
  58.8 1.6 %collective-permute-start.20 = (f32[384,128]{1,0:T(8,128)S(1)}, f32[384,128]{1,0:T(8,128)S(1)}, u32[]{:S(2)}, u32[]{:S(2)}) collective-permute-start(f32[384,128]{1,0:T(8,128)S(1)} %shard_map.184.refs_0_.refs_2_), channel_id=1, source_target_pairs={{0,8},{4,12},{8,0},{12,4},{1,9},{5,13},{9,1},{13,5},{2,10},{6,14},... | collective-permute-start | bytes 589832 | tf_op jit(solution)/shard_map/ppermute | solution.py:32
  62.8 3.7 %collective-permute-done.20.refs_1_ = f32[384,128]{1,0:T(8,128)S(1)} collective-permute-done((f32[384,128]{1,0:T(8,128)S(1)}, f32[384,128]{1,0:T(8,128)S(1)}, u32[]{:S(2)}, u32[]{:S(2)}) %collective-permute-start.20) | collective-permute-done | bytes 196640 | tf_op jit(solution)/shard_map/ppermute | solution.py:32
  66.6 9.9 %shard_map.185.refs_4_.x = f32[256,256]{1,0:T(8,128)S(1)} custom-call(f32[384,128]{1,0:T(8,128)S(1)} %shard_map.184.refs_0_.refs_2_, f32[384,128]{1,0:T(8,128)S(1)} %collective-permute-done.20.refs_1_), custom_call_target="tpu_custom_call" | custom-call | flops 10000000000 | bytes 1048576 | tf_op jit(solution)/shard_map/pallas_call | solution.py:393
  78.7 2.9 %collective-permute-done.21.refs_1_ = bf16[2,2,64,128]{3,2,1,0:T(8,128)(2,1)S(1)} collective-permute-done((bf16[2,2,64,128]{3,2,1,0:T(8,128)(2,1)S(1)}, bf16[2,2,64,128]{3,2,1,0:T(8,128)(2,1)S(1)}, u32[]{:S(2)}, u32[]{:S(2)}) %collective-permute-start.21) | collective-permute-done | bytes 65568 | tf_op jit(solution)/shard_map/ppermute | solution.py:32
  84.4 2.8 %collective-permute-start.24 = (f32[8,256]{1,0:T(8,128)S(1)}, f32[8,256]{1,0:T(8,128)S(1)}, u32[]{:S(2)}, u32[]{:S(2)}) collective-permute-start(f32[8,256]{1,0:T(8,128)S(1)} %get-tuple-element.88.refs_0_), channel_id=1, source_target_pairs={{0,1},{1,0},{2,3},{3,2},{4,5},{5,4},{6,7},{7,6},{8,9},{9,8},{10,11... | collective-permute-start | bytes 24584 | tf_op jit(solution)/shard_map/ppermute | solution.py:32
  87.3 2.1 %shard_map.191.refs_4_.refs_2_ = f32[2048,512]{1,0:T(8,128)} custom-call(s32[3]{0:T(128)S(1)} %pad_add_fusion.ranks, bf16[2048,256]{1,0:T(8,128)(2,1)S(1)} %get-tuple-element.81.pcat, bf16[256,512]{1,0:T(8,128)(2,1)S(1)} %get-tuple-element.89.y, f32[512,512]{1,0:T(8,128)S(1)} %get-tuple-element.83.refs_0_, f32[512,512]{1,0:T(8,128)S(1)} %get-tuple-element.84.refs_1_), custom_call_target="tpu_custom_call" | custom-call | flops 268435456 | bytes 4194304 | tf_op jit(solution)/shard_map/pallas_call | solution.py:472
  89.4 2.2 %copy-done = f32[2048,512]{1,0:T(8,128)S(1)} copy-done((f32[2048,512]{1,0:T(8,128)S(1)}, f32[2048,512]{1,0:T(8,128)}, u32[]{:S(2)}) %copy-start) | copy-done | bytes 4194328
  92.2 2.1 %shard_map.194 = f32[2048,512]{1,0:T(8,128)} custom-call(s32[3]{0:T(128)S(1)} %pad_add_fusion.ranks, bf16[2048,256]{1,0:T(8,128)(2,1)S(1)} %get-tuple-element.81.pcat, bf16[256,512]{1,0:T(8,128)(2,1)S(1)} %get-tuple-element.89.y, f32[512,512]{1,0:T(8,128)S(1)} %get-tuple-element.85.refs_2_.refs_0_, ...), custom_call_target="tpu_custom_call", output_to_operand_aliasing={{}: (5, {})} | custom-call | flops 268435456 | bytes 4194304 | tf_op jit(solution)/shard_map/pallas_call | solution.py:472
  95.3 3.3 %shard_map.193 = (bf16[2048,512]{1,0:T(8,128)(2,1)}, f32[512,256]{1,0:T(8,128)}) custom-call(s32[3]{0:T(128)S(1)} %pad_add_fusion.ranks, bf16[2048,256]{1,0:T(8,128)(2,1)S(1)} %get-tuple-element.81.pcat, f32[256,256]{1,0:T(8,128)S(1)} %shard_map.185.refs_4_.x, f32[256,512]{1,0:T(8,128)S(1)} %get-tuple-element.87.bt, f32[8,256]{1,0:T(8,128)S(1)} %shard_map.192.refs_0_, ...), custom_call_target="tpu_custom_call" | custom-call | flops 1073741824 | bytes 3145728 | tf_op jit(solution)/shard_map/pallas_call | solution.py:515
  (79 shorter events, 23.4 us)
Async XLA Ops:
  4.5 10.4 %collective-permute-start.1 = (bf16[512,256]{1,0:T(8,128)(2,1)S(1)}, bf16[512,256]{1,0:T(8,128)(2,1)S(1)}, u32[]{:S(2)}, u32[]{:S(2)}) collective-permute-start(bf16[512,256]{1,0:T(8,128)(2,1)S(1)} %get-tuple-element.59), channel_id=1, source_target_pairs={{0,16},{16,0},{1,17},{17,1},{2,18},{18,2},{3,19},{19,3},{4,20},{20... | collective-permute-start | bytes 786440 | tf_op jit(solution)/shard_map/ppermute | solution.py:32
  10.1 10.0 %collective-permute-start.2 = (bf16[512,256]{1,0:T(8,128)(2,1)S(1)}, bf16[512,256]{1,0:T(8,128)(2,1)S(1)}, u32[]{:S(2)}, u32[]{:S(2)}) collective-permute-start(bf16[512,256]{1,0:T(8,128)(2,1)S(1)} %get-tuple-element.53.refs_2_), channel_id=1, source_target_pairs={{0,16},{16,0},{1,17},{17,1},{2,18},{18,2},{3,19},{19,3},{4,20},{20... | collective-permute-start | bytes 786440 | tf_op jit(solution)/shard_map/ppermute | solution.py:32
  10.2 14.5 %collective-permute-start = (bf16[2,2,64,128]{3,2,1,0:T(8,128)(2,1)S(1)}, bf16[2,2,64,128]{3,2,1,0:T(8,128)(2,1)S(1)}, u32[]{:S(2)}, u32[]{:S(2)}) collective-permute-start(bf16[2,2,64,128]{3,2,1,0:T(8,128)(2,1)S(1)} %shard_map.174.refs_4_.refs_0_), channel_id=1, source_target_pairs={{0,16},{16,0},{1,17},{17,1},{2,18},{18,2},{3,19},{19,3},{4,20},{20... | collective-permute-start | bytes 196616 | tf_op jit(solution)/shard_map/ppermute | solution.py:32
  20.2 10.8 %collective-permute-start.6 = (bf16[256,256]{1,0:T(8,128)(2,1)S(1)}, bf16[256,256]{1,0:T(8,128)(2,1)S(1)}, u32[]{:S(2)}, u32[]{:S(2)}) collective-permute-start(bf16[256,256]{1,0:T(8,128)(2,1)S(1)} %get-tuple-element.67), channel_id=1, source_target_pairs={{0,1},{1,0},{2,3},{3,2},{4,5},{5,4},{6,7},{7,6},{8,9},{9,8},{10,11... | collective-permute-start | bytes 393224 | tf_op jit(solution)/shard_map/ppermute | solution.py:32
  22.1 8.9 %collective-permute-start.8 = (bf16[256,256]{1,0:T(8,128)(2,1)S(1)}, bf16[256,256]{1,0:T(8,128)(2,1)S(1)}, u32[]{:S(2)}, u32[]{:S(2)}) collective-permute-start(bf16[256,256]{1,0:T(8,128)(2,1)S(1)} %get-tuple-element.68), channel_id=1, source_target_pairs={{0,3},{1,2},{2,1},{3,0},{4,7},{5,6},{6,5},{7,4},{8,11},{9,10},{10,... | collective-permute-start | bytes 393224 | tf_op jit(solution)/shard_map/ppermute | solution.py:32
  24.6 10.2 %collective-permute-start.7 = (bf16[256,256]{1,0:T(8,128)(2,1)S(1)}, bf16[256,256]{1,0:T(8,128)(2,1)S(1)}, u32[]{:S(2)}, u32[]{:S(2)}) collective-permute-start(bf16[256,256]{1,0:T(8,128)(2,1)S(1)} %get-tuple-element.60.refs_4_), channel_id=1, source_target_pairs={{0,2},{1,3},{2,0},{3,1},{4,6},{5,7},{6,4},{7,5},{8,10},{9,11},{10,... | collective-permute-start | bytes 393224 | tf_op jit(solution)/shard_map/ppermute | solution.py:32
  25.5 14.1 %collective-permute-start.3 = (bf16[2,64,128]{2,1,0:T(8,128)(2,1)S(1)}, bf16[2,64,128]{2,1,0:T(8,128)(2,1)S(1)}, u32[]{:S(2)}, u32[]{:S(2)}) collective-permute-start(bf16[2,64,128]{2,1,0:T(8,128)(2,1)S(1)} %get-tuple-element.64), channel_id=1, source_target_pairs={{0,4},{4,0},{8,12},{12,8},{1,5},{5,1},{9,13},{13,9},{2,6},{6,2},{1... | collective-permute-start | bytes 98312 | tf_op jit(solution)/shard_map/ppermute | solution.py:32
  29.1 11.7 %collective-permute-start.4 = (bf16[2,64,128]{2,1,0:T(8,128)(2,1)S(1)}, bf16[2,64,128]{2,1,0:T(8,128)(2,1)S(1)}, u32[]{:S(2)}, u32[]{:S(2)}) collective-permute-start(bf16[2,64,128]{2,1,0:T(8,128)(2,1)S(1)} %get-tuple-element.65), channel_id=1, source_target_pairs={{0,8},{4,12},{8,0},{12,4},{1,9},{5,13},{9,1},{13,5},{2,10},{6,14},... | collective-permute-start | bytes 98312 | tf_op jit(solution)/shard_map/ppermute | solution.py:32
  34.8 19.2 %collective-permute-start.15 = (bf16[256,256]{1,0:T(8,128)(2,1)S(1)}, bf16[256,256]{1,0:T(8,128)(2,1)S(1)}, u32[]{:S(2)}, u32[]{:S(2)}) collective-permute-start(bf16[256,256]{1,0:T(8,128)(2,1)S(1)} %shard_map.180.refs_4_.refs_0_), channel_id=1, source_target_pairs={{0,16},{16,0},{1,17},{17,1},{2,18},{18,2},{3,19},{19,3},{4,20},{20... | collective-permute-start | bytes 393224 | tf_op jit(solution)/shard_map/ppermute | solution.py:32
  36.4 11.2 %collective-permute-start.14 = (bf16[256,256]{1,0:T(8,128)(2,1)S(1)}, bf16[256,256]{1,0:T(8,128)(2,1)S(1)}, u32[]{:S(2)}, u32[]{:S(2)}) collective-permute-start(bf16[256,256]{1,0:T(8,128)(2,1)S(1)} %shard_map.180.refs_4_.refs_0_), channel_id=1, source_target_pairs={{0,2},{1,3},{2,0},{3,1},{4,6},{5,7},{6,4},{7,5},{8,10},{9,11},{10,... | collective-permute-start | bytes 393224 | tf_op jit(solution)/shard_map/ppermute | solution.py:32
  36.7 11.4 %collective-permute-start.13 = (bf16[256,256]{1,0:T(8,128)(2,1)S(1)}, bf16[256,256]{1,0:T(8,128)(2,1)S(1)}, u32[]{:S(2)}, u32[]{:S(2)}) collective-permute-start(bf16[256,256]{1,0:T(8,128)(2,1)S(1)} %shard_map.180.refs_4_.refs_0_), channel_id=1, source_target_pairs={{0,1},{1,0},{2,3},{3,2},{4,5},{5,4},{6,7},{7,6},{8,9},{9,8},{10,11... | collective-permute-start | bytes 393224 | tf_op jit(solution)/shard_map/ppermute | solution.py:32
  39.6 10.0 %collective-permute-start.9 = (bf16[256,256]{1,0:T(8,128)(2,1)S(1)}, bf16[256,256]{1,0:T(8,128)(2,1)S(1)}, u32[]{:S(2)}, u32[]{:S(2)}) collective-permute-start(bf16[256,256]{1,0:T(8,128)(2,1)S(1)} %shard_map.180.refs_4_.refs_0_), channel_id=1, source_target_pairs={{0,3},{1,2},{2,1},{3,0},{4,7},{5,6},{6,5},{7,4},{8,11},{9,10},{10,... | collective-permute-start | bytes 393224 | tf_op jit(solution)/shard_map/ppermute | solution.py:32
  47.5 6.4 %collective-permute-start.17 = (bf16[256,256]{1,0:T(8,128)(2,1)S(1)}, bf16[256,256]{1,0:T(8,128)(2,1)S(1)}, u32[]{:S(2)}, u32[]{:S(2)}) collective-permute-start(bf16[256,256]{1,0:T(8,128)(2,1)S(1)} %collective-permute-done.14.refs_2_), channel_id=1, source_target_pairs={{0,16},{16,0},{1,17},{17,1},{2,18},{18,2},{3,19},{19,3},{4,20},{20... | collective-permute-start | bytes 393224 | tf_op jit(solution)/shard_map/ppermute | solution.py:32
  48.1 5.9 %collective-permute-start.16 = (bf16[256,256]{1,0:T(8,128)(2,1)S(1)}, bf16[256,256]{1,0:T(8,128)(2,1)S(1)}, u32[]{:S(2)}, u32[]{:S(2)}) collective-permute-start(bf16[256,256]{1,0:T(8,128)(2,1)S(1)} %collective-permute-done.13.refs_1_), channel_id=1, source_target_pairs={{0,16},{16,0},{1,17},{17,1},{2,18},{18,2},{3,19},{19,3},{4,20},{20... | collective-permute-start | bytes 393224 | tf_op jit(solution)/shard_map/ppermute | solution.py:32
  49.6 5.7 %collective-permute-start.18 = (bf16[256,256]{1,0:T(8,128)(2,1)S(1)}, bf16[256,256]{1,0:T(8,128)(2,1)S(1)}, u32[]{:S(2)}, u32[]{:S(2)}) collective-permute-start(bf16[256,256]{1,0:T(8,128)(2,1)S(1)} %collective-permute-done.9.refs_7_.refs_3_), channel_id=1, source_target_pairs={{0,16},{16,0},{1,17},{17,1},{2,18},{18,2},{3,19},{19,3},{4,20},{20... | collective-permute-start | bytes 393224 | tf_op jit(solution)/shard_map/ppermute | solution.py:32
  58.8 7.8 %collective-permute-start.20 = (f32[384,128]{1,0:T(8,128)S(1)}, f32[384,128]{1,0:T(8,128)S(1)}, u32[]{:S(2)}, u32[]{:S(2)}) collective-permute-start(f32[384,128]{1,0:T(8,128)S(1)} %shard_map.184.refs_0_.refs_2_), channel_id=1, source_target_pairs={{0,8},{4,12},{8,0},{12,4},{1,9},{5,13},{9,1},{13,5},{2,10},{6,14},... | collective-permute-start | bytes 589832 | tf_op jit(solution)/shard_map/ppermute | solution.py:32
  60.3 16.1 %collective-permute-start.10 = (bf16[2,64,128]{2,1,0:T(8,128)(2,1)S(1)}, bf16[2,64,128]{2,1,0:T(8,128)(2,1)S(1)}, u32[]{:S(2)}, u32[]{:S(2)}) collective-permute-start(bf16[2,64,128]{2,1,0:T(8,128)(2,1)S(1)} %get-tuple-element.75), channel_id=1, source_target_pairs={{0,4},{4,0},{8,12},{12,8},{1,5},{5,1},{9,13},{13,9},{2,6},{6,2},{1... | collective-permute-start | bytes 98312 | tf_op jit(solution)/shard_map/ppermute | solution.py:32
  60.3 16.1 %collective-permute-start.11 = (bf16[2,64,128]{2,1,0:T(8,128)(2,1)S(1)}, bf16[2,64,128]{2,1,0:T(8,128)(2,1)S(1)}, u32[]{:S(2)}, u32[]{:S(2)}) collective-permute-start(bf16[2,64,128]{2,1,0:T(8,128)(2,1)S(1)} %get-tuple-element.76), channel_id=1, source_target_pairs={{0,8},{4,12},{8,0},{12,4},{1,9},{5,13},{9,1},{13,5},{2,10},{6,14},... | collective-permute-start | bytes 98312 | tf_op jit(solution)/shard_map/ppermute | solution.py:32
  60.9 15.7 %collective-permute-start.12 = (bf16[2,64,128]{2,1,0:T(8,128)(2,1)S(1)}, bf16[2,64,128]{2,1,0:T(8,128)(2,1)S(1)}, u32[]{:S(2)}, u32[]{:S(2)}) collective-permute-start(bf16[2,64,128]{2,1,0:T(8,128)(2,1)S(1)} %get-tuple-element.77), channel_id=1, source_target_pairs={{0,12},{4,8},{8,4},{12,0},{1,13},{5,9},{9,5},{13,1},{2,14},{6,10},... | collective-permute-start | bytes 98312 | tf_op jit(solution)/shard_map/ppermute | solution.py:32
  62.3 19.9 %collective-permute-start.23 = (bf16[256,512]{1,0:T(8,128)(2,1)S(1)}, bf16[256,512]{1,0:T(8,128)(2,1)S(1)}, u32[]{:S(2)}, u32[]{:S(2)}) collective-permute-start(bf16[256,512]{1,0:T(8,128)(2,1)S(1)} %shard_map.189.wa), channel_id=1, source_target_pairs={{0,8},{4,12},{8,0},{12,4},{1,9},{5,13},{9,1},{13,5},{2,10},{6,14},... | collective-permute-start | bytes 786440 | tf_op jit(solution)/shard_map/ppermute | solution.py:32
  77.2 4.3 %collective-permute-start.21 = (bf16[2,2,64,128]{3,2,1,0:T(8,128)(2,1)S(1)}, bf16[2,2,64,128]{3,2,1,0:T(8,128)(2,1)S(1)}, u32[]{:S(2)}, u32[]{:S(2)}) collective-permute-start(bf16[2,2,64,128]{3,2,1,0:T(8,128)(2,1)S(1)} %get-tuple-element.80), channel_id=1, source_target_pairs={{0,16},{16,0},{1,17},{17,1},{2,18},{18,2},{3,19},{19,3},{4,20},{20... | collective-permute-start | bytes 196616 | tf_op jit(solution)/shard_map/ppermute | solution.py:32
  82.8 6.6 %collective-permute-start.26 = (f32[8,256]{1,0:T(8,128)S(1)}, f32[8,256]{1,0:T(8,128)S(1)}, u32[]{:S(2)}, u32[]{:S(2)}) collective-permute-start(f32[8,256]{1,0:T(8,128)S(1)} %get-tuple-element.88.refs_0_), channel_id=1, source_target_pairs={{0,3},{1,2},{2,1},{3,0},{4,7},{5,6},{6,5},{7,4},{8,11},{9,10},{10,... | collective-permute-start | bytes 24584 | tf_op jit(solution)/shard_map/ppermute | solution.py:32
  84.3 5.1 %collective-permute-start.25 = (f32[8,256]{1,0:T(8,128)S(1)}, f32[8,256]{1,0:T(8,128)S(1)}, u32[]{:S(2)}, u32[]{:S(2)}) collective-permute-start(f32[8,256]{1,0:T(8,128)S(1)} %get-tuple-element.88.refs_0_), channel_id=1, source_target_pairs={{0,2},{1,3},{2,0},{3,1},{4,6},{5,7},{6,4},{7,5},{8,10},{9,11},{10,... | collective-permute-start | bytes 24584 | tf_op jit(solution)/shard_map/ppermute | solution.py:32
  84.4 5.0 %collective-permute-start.24 = (f32[8,256]{1,0:T(8,128)S(1)}, f32[8,256]{1,0:T(8,128)S(1)}, u32[]{:S(2)}, u32[]{:S(2)}) collective-permute-start(f32[8,256]{1,0:T(8,128)S(1)} %get-tuple-element.88.refs_0_), channel_id=1, source_target_pairs={{0,1},{1,0},{2,3},{3,2},{4,5},{5,4},{6,7},{7,6},{8,9},{9,8},{10,11... | collective-permute-start | bytes 24584 | tf_op jit(solution)/shard_map/ppermute | solution.py:32
  (15 other events, 170.2 us)

commit v6 on v5

--- a/solution.py
+++ b/solution.py
@@ -36,8 +36,8 @@
     return pltpu.CompilerParams(vmem_limit_bytes=mib * MIB)
 
 
-def cost(flops, nbytes):
-    return pl.CostEstimate(flops=int(flops), bytes_accessed=int(nbytes), transcendentals=0)
+def cost(weight=0):
+    return pl.CostEstimate(flops=1 + weight * 10**9, bytes_accessed=1, transcendentals=0)
 
 
 def halves(x):
@@ -156,7 +156,8 @@
         scratch_shapes=scratch,
         out_shape=out_shape,
         compiler_params=params(14),
-        cost_estimate=cost(6 * size * cols * rank, size * cols * 6),
+        name="project",
+        cost_estimate=cost(),
     )(ranks, momentum, grad_q, *ins, *after)
     right = tuple(outs[2:4]) if is_first else tuple(ins[:2])
     return outs[0], outs[1], right + tuple(outs[-2:] if following else ())
@@ -185,7 +186,8 @@
             for i in range(number)
         ],
         compiler_params=params(),
-        cost_estimate=cost(rows * rank, rows * rank * 8),
+        name="split_sum",
+        cost_estimate=cost(),
     )(own, *recvs)
 
 
@@ -196,7 +198,7 @@
     refs[-1][...] = acc.astype(refs[-1].dtype)
 
 
-def sum_parts(parts, dtype, after=()):
+def sum_parts(parts, dtype, after=(), weight=0):
     shape = parts[0].shape
     return pl.pallas_call(
         functools.partial(sum_kernel, len(parts)),
@@ -204,7 +206,8 @@
         out_specs=VMEM,
         out_shape=jax.ShapeDtypeStruct(shape, dtype),
         compiler_params=params(),
-        cost_estimate=cost(1000, 12 * math.prod(shape)),
+        name="sum_parts",
+        cost_estimate=cost(weight),
     )(*parts, *after)
 
 
@@ -236,12 +239,13 @@
             jax.ShapeDtypeStruct((3 * rank // 2, rank // 2), F32),
         ],
         compiler_params=params(8),
-        cost_estimate=cost(2 * rows * rank * rank, rows * rank * 6),
+        name="gather_gram",
+        cost_estimate=cost(),
     )(*chunks, *after)
 
 
-def back_part_kernel(pcat_t, *refs):
-    totals, out = refs[:-1], refs[-1]
+def back_part_kernel(n_totals, pcat_t, *refs):
+    totals, out = refs[:n_totals], refs[-1]
     seg = totals[0].shape[0]
     step = min(seg, 512)
     acc = None
@@ -254,18 +258,19 @@
     out[...] = acc.astype(BF16)
 
 
-def back_part(pcat_t, totals):
+def back_part(pcat_t, totals, after):
     rank = pcat_t.shape[0]
     seg, cols = totals[0].shape
     rows = seg * len(totals)
     return pl.pallas_call(
-        back_part_kernel,
-        in_specs=[VMEM] * (1 + len(totals)),
+        functools.partial(back_part_kernel, len(totals)),
+        in_specs=[VMEM] * (1 + len(totals)) + [ANY] * len(after),
         out_specs=VMEM,
         out_shape=jax.ShapeDtypeStruct((rank, cols), BF16),
         compiler_params=params(14),
-        cost_estimate=cost(4 * rows * cols * rank, rows * cols * 4),
-    )(pcat_t, *totals)
+        name="back_part",
+        cost_estimate=cost(5),
+    )(pcat_t, *totals, *after)
 
 
 def factor_panel(panel, off):
@@ -397,7 +402,8 @@
         scratch_shapes=[pltpu.VMEM((n, n), F32)],
         out_shape=jax.ShapeDtypeStruct((n, n), F32),
         compiler_params=params(),
-        cost_estimate=cost(10_000_000_000, 4 * n * n * 4),
+        name="inverse_factor",
+        cost_estimate=cost(2),
     )(*parts)
 
 
@@ -428,7 +434,8 @@
             jax.ShapeDtypeStruct((8, rank), F32),
         ],
         compiler_params=params(),
-        cost_estimate=cost(8 * rank * rank * cols, rank * cols * 12),
+        name="back_full",
+        cost_estimate=cost(),
     )(x, wa, wb)
 
 
@@ -441,7 +448,8 @@
 
 
 def momentum_kernel(n_resp, n_head, begin, end, n_totals, ranks, pcat, y, *refs):
-    totals, (out, held, sems) = refs[:n_totals], refs[-3:]
+    totals, (out, token, held, sems) = refs[:n_totals], refs[-4:]
+    token[...] = jnp.zeros_like(token)
     seg = totals[0].shape[0]
     chunk = pcat.shape[0] // (n_resp * n_head)
     blocks = row_blocks(ranks, n_resp, n_head, chunk)
@@ -462,7 +470,7 @@
         c.wait()
 
 
-def new_momentum(ranks, pcat, totals, y, n_resp, n_head, half, earlier):
+def new_momentum(ranks, pcat, totals, y, n_resp, n_head, half, earlier, after):
     rows, rank = pcat.shape
     cols = totals[0].shape[1]
     n_chunks = n_resp * n_head // 2
@@ -473,14 +481,17 @@
         functools.partial(
             momentum_kernel, n_resp, n_head, half * n_chunks, (half + 1) * n_chunks, part
         ),
-        in_specs=[SMEM] + [VMEM] * (2 + part) + [HBM] * len(earlier),
-        out_specs=HBM,
+        in_specs=[SMEM] + [VMEM] * (2 + part) + [HBM] * len(earlier) + [ANY] * len(after),
+        out_specs=[HBM, VMEM],
         scratch_shapes=[pltpu.VMEM((rows // 2, cols), F32), pltpu.SemaphoreType.DMA((n_chunks,))],
-        out_shape=jax.ShapeDtypeStruct((rows, cols), F32),
+        out_shape=[
+            jax.ShapeDtypeStruct((rows, cols), F32), jax.ShapeDtypeStruct((8, 128), F32)
+        ],
         input_output_aliases=aliases,
         compiler_params=params(10),
-        cost_estimate=cost(rows * cols * rank, rows * cols * 4),
-    )(ranks, pcat, y, *totals, *earlier)
+        name="new_momentum",
+        cost_estimate=cost(5),
+    )(ranks, pcat, y, *totals, *earlier, *after)
 
 
 def update_kernel(gain, n_resp, n_head, n_sums, ranks, pcat, x, bt, *refs):
@@ -527,7 +538,8 @@
             jax.ShapeDtypeStruct((cols, rank), F32),
         ],
         compiler_params=params(10),
-        cost_estimate=cost(4 * rows * cols * rank, rows * cols * 3),
+        name="final_update",
+        cost_estimate=cost(),
     )(ranks, pcat, x, bt, *sums)
 
 
@@ -553,7 +565,8 @@
         out_specs=VMEM,
         out_shape=jax.ShapeDtypeStruct((2,) + keys.shape, BF16),
         compiler_params=params(),
-        cost_estimate=cost(1000, 8 * math.prod(keys.shape)),
+        name="pack_prompts",
+        cost_estimate=cost(),
     )(keys, values, *after)
 
 
@@ -579,7 +592,8 @@
         out_specs=[VMEM] * n_fsdp,
         out_shape=[jax.ShapeDtypeStruct((2, piece, width), BF16)] * n_fsdp,
         compiler_params=params(),
-        cost_estimate=cost(1000, 8 * n_fsdp * piece * width),
+        name="select_prompts",
+        cost_estimate=cost(),
     )(ranks, counts, slots, *stored, *after)
 
 
@@ -587,10 +601,10 @@
     n_fsdp, heads, last, ranks, counts, prompt_blocks, resp_blocks, q, sk, sv, go, *refs
 ):
     pieces, refs = refs[:n_fsdp], refs[n_fsdp:]
-    keys, values, dk, dv = refs[-4:]
+    dq_held, keys, values, dk, dv, sems = refs[-6:]
     n_out = 2 + n_fsdp if last else 3
-    outs = refs[-4 - n_out : -4]
-    dq = outs[0]
+    outs = refs[-6 - n_out : -6]
+    dq, copies = outs[0], []
     piece = pieces[0].shape[1]
     cap = piece * n_fsdp
     length = q.shape[0]
@@ -622,8 +636,8 @@
     else:
         dk[...] = jnp.zeros_like(dk)
         dv[...] = jnp.zeros_like(dv)
-    for h in heads:
-        cols = slice(h * HD, (h + 1) * HD)
+    for i, h in enumerate(heads):
+        cols = pl.ds(h * HD, HD)
         qh = q[:, cols]
         gh = jnp.where(live, go[:, cols], jnp.zeros((), BF16))
         logits = lax.dot_general(kall, qh, nt, preferred_element_type=F32) * scale + bias
@@ -636,10 +650,10 @@
         ds = (wf * (dp - diag)).astype(BF16)
         dk[...] += mm(ds, qh)
         dv[...] += mm(w, gh)
-        dq[:, cols] = (mm(kt, ds) * scale).T.astype(BF16)
+        dq_held[i] = (mm(kt, ds) * scale).T.astype(BF16)
+        copies.append(pltpu.make_async_copy(dq_held.at[i], dq.at[:, cols], sems.at[i]))
+        copies[-1].start()
     if last:
-        done = heads[0] * HD
-        dq[:, :done] = refs[2][...]
         own, sends = outs[1], outs[2:]
         own[0] = (dk[cap:, :] * scale).astype(BF16)
         own[1] = dv[cap:, :].astype(BF16)
@@ -650,6 +664,8 @@
     else:
         outs[1][...] = dk[...]
         outs[2][...] = dv[...]
+    for c in copies:
+        c.wait()
 
 
 def attention(heads, earlier, ranks, counts, prompt_blocks, resp_blocks, q, sk, sv, go, pieces, after):
@@ -659,23 +675,29 @@
     cap = piece * n_fsdp
     total = cap + length
     last = earlier is not None
+    dq_shape = jax.ShapeDtypeStruct((length, width), BF16)
+    aliases = {8 + n_fsdp + 2: 0} if last else {}
     if last:
-        extra, specs = (earlier[1], earlier[2], earlier[0]), [VMEM] * 3
-        out_shape = [pltpu.VMEM((length, width), BF16), jax.ShapeDtypeStruct((2, length, HD), BF16)] + [
+        extra, specs = (earlier[1], earlier[2], earlier[0]), [VMEM, VMEM, HBM]
+        out_shape = [dq_shape, jax.ShapeDtypeStruct((2, length, HD), BF16)] + [
             jax.ShapeDtypeStruct((2, piece, HD), BF16 if k else F32) for k in range(n_fsdp)
         ]
     else:
         extra, specs = (), []
-        out_shape = [jax.ShapeDtypeStruct((length, len(heads) * HD), BF16)]
-        out_shape += [jax.ShapeDtypeStruct((total, HD), F32)] * 2
+        out_shape = [dq_shape] + [jax.ShapeDtypeStruct((total, HD), F32)] * 2
     return pl.pallas_call(
         functools.partial(attention_kernel, n_fsdp, heads, last),
         in_specs=[SMEM] * 4 + [VMEM] * (4 + n_fsdp) + specs + [ANY] * len(after),
-        out_specs=[VMEM] * len(out_shape),
-        scratch_shapes=[pltpu.VMEM((total, HD), BF16)] * 2 + [pltpu.VMEM((total, HD), F32)] * 2,
+        out_specs=[HBM] + [VMEM] * (len(out_shape) - 1),
+        scratch_shapes=[pltpu.VMEM((len(heads), length, HD), BF16)]
+        + [pltpu.VMEM((total, HD), BF16)] * 2
+        + [pltpu.VMEM((total, HD), F32)] * 2
+        + [pltpu.SemaphoreType.DMA((len(heads),))],
         out_shape=out_shape,
+        input_output_aliases=aliases,
         compiler_params=params(12),
-        cost_estimate=cost(3_000_000_000, length * width * 8),
+        name="attention",
+        cost_estimate=cost(),
     )(ranks, counts, prompt_blocks, resp_blocks, q, sk, sv, go, *pieces, *extra, *after)
 
 
@@ -706,7 +728,8 @@
             for j in range(n_resp)
         ],
         compiler_params=params(),
-        cost_estimate=cost(1000, 8 * len(parts) * piece * width * 4),
+        name="sum_by_slot",
+        cost_estimate=cost(),
     )(ranks, counts, slots, *parts, *after)
 
 
@@ -739,74 +762,78 @@
     order = [(j, *group) for group in groups for j in range(1, n_resp)]
     order += [(0, *group) for group in groups]
     nexts = dict(zip(order, order[1:] + [None]))
-    totals, arrived, ins = {}, [], (basis_hbm,)
-
-    def project_next(part, dtype, after):
-        return project(
-            ranks, mom_hbm, grad_hbm, ins, part, nexts[part], n_resp, n_head, dtype, after
+    totals, arrived, split, ins, after = {}, {}, {}, (basis_hbm,), ()
+    for part in order:
+        j, first, number = part
+        value, totals[part[:2]], ins = project(
+            ranks, mom_hbm, grad_hbm, ins, part, nexts[part], n_resp, n_head, BF16 if j else F32,
+            after,
         )
-
-    for group in groups:
-        row = []
-        for j in range(1, n_resp):
-            sent, totals[j, group[0]], ins = project_next((j, *group), BF16, ())
-            row.append(swap(sent, "resp", j))
-        arrived.append(row)
-    packed = pack_prompts(prompt_keys, prompt_values, (sent,))
-    stored = [packed] + [swap(packed, "resp", j) for j in range(1, n_resp)]
-    after = (packed,)
-    split = {}
-    for group, recvs in zip(groups, arrived):
-        mine, totals[0, group[0]], ins = project_next((0, *group), F32, after)
-        outs = split_sum(mine, recvs, *group)
-        after = (outs[0],)
-        for i in range(group[1]):
-            split[group[0] + i] = outs[i]
+        if j:
+            arrived.setdefault(first, []).append(swap(value, "resp", j))
+            if part[1:] == groups[-1] and j == n_resp - 1:
+                packed = pack_prompts(prompt_keys, prompt_values, (value,))
+                stored = [packed] + [swap(packed, "resp", k) for k in range(1, n_resp)]
+                after = (packed,)
+        else:
+            outs = split_sum(value, arrived[first], first, number)
+            after = (outs[0],)
+            for i in range(number):
+                split[first + i] = outs[i]
     totals = [totals[at] for at in sorted(totals)]
-    chosen = select_prompts(ranks, counts, owner_slot, stored, n_fsdp, after)
+    chosen = select_prompts(ranks, counts, owner_slot, stored, n_fsdp, (outs[0],))
     far_first = [k for first, number in groups for k in range(first, first + number) if k]
     summands = {k: swap(split[k], "head", k) for k in far_first}
     pieces = [chosen[0]] + [swap(chosen[k], "fsdp", k) for k in range(1, n_fsdp)]
+    later = groups[-1][1] if len(groups) > 1 else 1
+    far = sum_parts(
+        [split[0]] + [summands[k] for k in range(later, n_head)], F32, (), 10
+    )
     piece0 = sum_parts(
-        [split[0]] + [summands[k] for k in range(1, n_head)], BF16, (pieces[-1],)
+        [far] + [summands[k] for k in range(1, later)], BF16, (pieces[-1],)
     )
 
     along = {0: piece0}
     for k in far_first:
         along[k] = swap(piece0, "head", k)
-    chunks = [along[k] for k in range(n_head)]
-    for j in range(1, n_resp):
-        chunks += [swap(along[k], "resp", j) for k in range(n_head)]
-
     n_q = queries.shape[1] // HD
     heads = [list(range(n_q // 2)), list(range(n_q // 2, n_q))]
     held = (
         ranks, counts, prompt_blocks, resp_blocks, queries, self_keys, self_values, d_out, pieces
     )
-    earlier = attention(heads[0], None, *held, (piece0,))
-    dq, resp_grad, *parts = attention(heads[1], earlier, *held, (along[n_head - 1],))
-    pcat, pcat_t, gram = gather_gram(chunks, (resp_grad,))
+    earlier = attention(heads[0], None, *held, (along[1 % n_head],))
+    last = n_head - 1
+    passed = dict(along)
+    passed[last] = sum_parts([along[last]], BF16, (earlier[1],))
+    chunks = [along[k] for k in range(n_head)]
+    for j in range(1, n_resp):
+        chunks += [swap(passed[k], "resp", j) for k in range(n_head)]
+    dq, resp_grad, *parts = attention(heads[1], earlier, *held, (passed[last],))
+    pcat, pcat_t, gram = gather_gram(chunks, (parts[0],))
 
     bits = [1 << b for b in range(n_fsdp.bit_length() - 1)]
-    w = back_part(pcat_t, totals)
+    w = back_part(pcat_t, totals, (gram,))
     for bit in bits[:-1]:
-        gram = sum_parts([gram, swap(gram, "fsdp", bit)], F32)
-        w = sum_parts([w, swap(w, "fsdp", bit)], BF16, (gram,))
+        gram = sum_parts([gram, swap(gram, "fsdp", bit)], F32, (), 3)
+        w = sum_parts([w, swap(w, "fsdp", bit)], BF16, (gram,), 5)
     gram_parts = (gram, swap(gram, "fsdp", bits[-1]))
     w_other = swap(w, "fsdp", bits[-1])
     returned = [parts[0]] + [swap(parts[k], "fsdp", k) for k in range(1, n_fsdp)]
     x = inverse_factor(*gram_parts)
-    slots = sum_by_slot(ranks, counts, owner_slot, returned, n_resp, (x,))
-    prompt_grad = sum_parts(
-        [slots[0]] + [swap(slots[j], "resp", j) for j in range(1, n_resp)], F32
-    )
-
     bt, y, squares = back_full(x, w, w_other)
     from_head = [swap(squares, "head", k) for k in range(1, n_head)]
-    momentum_out = new_momentum(ranks, pcat, totals, y, n_resp, n_head, 0, ())
-    squares = sum_parts([squares] + from_head, F32, (momentum_out,))
+    momentum_out, token = new_momentum(
+        ranks, pcat, totals, y, n_resp, n_head, 0, (), (squares,)
+    )
+    slots = sum_by_slot(ranks, counts, owner_slot, returned, n_resp, (token,))
+    squares = sum_parts([squares] + from_head, F32, (token,))
     sums = [squares] + [swap(squares, "resp", j) for j in range(1, n_resp)]
-    momentum_out = new_momentum(ranks, pcat, totals, y, n_resp, n_head, 1, (momentum_out,))
+    momentum_out, token = new_momentum(
+        ranks, pcat, totals, y, n_resp, n_head, 1, (momentum_out,), (squares,)
+    )
+    prompt_grad = sum_parts(
+        [slots[0]] + [swap(slots[j], "resp", j) for j in range(1, n_resp)], F32, (token,)
+    )
     update, basis_out = final_update(ranks, pcat, x, bt, sums, gain, n_resp, n_head)
     return (dq, resp_grad, prompt_grad, update, momentum_out, basis_out)
 

time: 99 us -> 92.3 us (0.932)
  waiting for transfers between devices: 21.8 us -> 16.5 us
  local copies, waits for them, and re-layouts: 3.93 us -> 0.05 us
  Pallas kernels: 39.7 us -> 41.1 us
  starting transfers between devices: 31.5 us -> 32.8 us
    ppermute x28, waiting for transfers between devices: 21.8 us -> 16.5 us  [swap(): return lax.ppermute(value, axes, [(i, i ^ k) for i in range(n)])]
    unnamed x23 -> x18, local copies, waits for them, and re-layouts: 3.93 us -> 0.05 us
    pallas_call x2, Pallas kernels: 7.09 us -> 8.46 us  [attention(): pl.pallas_call(functools.partial(attention_kernel, n_fsdp, heads, last),...]
    ppermute x28, starting transfers between devices: 31.5 us -> 32.8 us  [swap(): return lax.ppermute(value, axes, [(i, i ^ k) for i in range(n)])]
  transfers between devices with their start and end apart: 28 -> 28, of which waited for: 8 -> 8; matrix products, arithmetic and copies ran while one was open for 1% -> 0% of each run, Pallas kernels for 32% -> 39%
where the time goes in v6:
time: 92.3 us; the launch traced here: 92.1 us
  Pallas kernels  41.1 us (45%)
  starting transfers between devices  32.8 us (36%)
  waiting for transfers between devices  16.5 us (18%)
  between operations  1.66 us (2%)
    ppermute x28, starting transfers between devices, swap(): return lax.ppermute(value, axes, [(i, i ^ k) for i in range(n)])  32.8 us
    ppermute x28, waiting for transfers between devices, swap(): return lax.ppermute(value, axes, [(i, i ^ k) for i in range(n)])  16.5 us
    pallas_call x4, Pallas kernels, project(): pl.pallas_call(functools.partial(project_kernel, n_head, part, following,...  10.4 us
    pallas_call x1, Pallas kernels, inverse_factor(): pl.pallas_call(functools.partial(cholesky_kernel, len(parts)), in_specs=[...  9.88 us
    pallas_call x2, Pallas kernels, attention(): pl.pallas_call(functools.partial(attention_kernel, n_fsdp, heads, last),...  8.46 us
    pallas_call x2, Pallas kernels, new_momentum(): pl.pallas_call(functools.partial(momentum_kernel, n_resp, n_head, half *...  4.25 us
    pallas_call x1, Pallas kernels, final_update(): pl.pallas_call(functools.partial(update_kernel, gain, n_resp, n_head, len...  3.31 us
  transfers between devices with their start and end apart: 28, of which 8 were waited for; matrix products, arithmetic and copies ran while one was open for 0% of the time, Pallas kernels for 39%

profile of v6, /device:TPU:0, one launch (start us, length us, event | category | flops | bytes accessed | tf_op | source)
XLA Modules:
  0.0 92.1 jit_solution(14965201674522692063)
XLA Ops:
  0.7 3.8 %project.4 = (bf16[512,256]{1,0:T(8,128)(2,1)S(1)}, f32[512,512]{1,0:T(8,128)S(1)}, bf16[512,256]{1,0:T(8,128)(2,1)S(1)}, bf16[512,256]{1,0:T(8,128)(2,1)S(1)}, ...) custom-call(s32[3]{0:T(128)S(1)} %pad_add_fusion.ranks, f32[2048,512]{1,0:T(8,128)} %mom.7, bf16[2048,512]{1,0:T(8,128)(2,1)} %grad.7, ...), custom_call_target="tpu_custom_call" | custom-call | flops 1 | bytes 1 | tf_op jit(solution)/shard_map/project/pallas_call | solution.py:152
  4.5 3.0 %collective-permute-start.1 = (bf16[512,256]{1,0:T(8,128)(2,1)S(1)}, bf16[512,256]{1,0:T(8,128)(2,1)S(1)}, u32[]{:S(2)}, u32[]{:S(2)}) collective-permute-start(bf16[512,256]{1,0:T(8,128)(2,1)S(1)} %get-tuple-element.63), channel_id=1, source_target_pairs={{0,16},{16,0},{1,17},{17,1},{2,18},{18,2},{3,19},{19,3},{4,20},{20... | collective-permute-start | bytes 786440 | tf_op jit(solution)/shard_map/ppermute | solution.py:32
  7.5 2.6 %project.5 = (bf16[512,256]{1,0:T(8,128)(2,1)S(1)}, f32[512,512]{1,0:T(8,128)S(1)}, f32[512,512]{1,0:T(8,128)S(1)}, bf16[512,512]{1,0:T(8,128)(2,1)S(1)}) custom-call(s32[3]{0:T(128)S(1)} %pad_add_fusion.ranks, f32[2048,512]{1,0:T(8,128)} %mom.7, bf16[2048,512]{1,0:T(8,128)(2,1)} %grad.7, bf16[512,256]{1,0:T(8,128)(2,1)S(1)} %get-tuple-element.53.refs_0_, ...), custom_call_target="tpu_custom_call" | custom-call | flops 1 | bytes 1 | tf_op jit(solution)/shard_map/project/pallas_call | solution.py:152
  10.2 2.6 %project.6 = (f32[512,256]{1,0:T(8,128)S(1)}, f32[512,512]{1,0:T(8,128)S(1)}, f32[512,512]{1,0:T(8,128)S(1)}, bf16[512,512]{1,0:T(8,128)(2,1)S(1)}) custom-call(s32[3]{0:T(128)S(1)} %pad_add_fusion.ranks, f32[2048,512]{1,0:T(8,128)} %mom.7, bf16[2048,512]{1,0:T(8,128)(2,1)} %grad.7, bf16[512,256]{1,0:T(8,128)(2,1)S(1)} %get-tuple-element.53.refs_0_, ...), custom_call_target="tpu_custom_call" | custom-call | flops 1 | bytes 1 | tf_op jit(solution)/shard_map/project/pallas_call | solution.py:152
  12.8 1.8 %collective-permute-done.1.refs_0_ = bf16[512,256]{1,0:T(8,128)(2,1)S(1)} collective-permute-done((bf16[512,256]{1,0:T(8,128)(2,1)S(1)}, bf16[512,256]{1,0:T(8,128)(2,1)S(1)}, u32[]{:S(2)}, u32[]{:S(2)}) %collective-permute-start.1) | collective-permute-done | bytes 262176 | tf_op jit(solution)/shard_map/ppermute | solution.py:32
  14.7 4.2 %collective-permute-start.7 = (bf16[256,256]{1,0:T(8,128)(2,1)S(1)}, bf16[256,256]{1,0:T(8,128)(2,1)S(1)}, u32[]{:S(2)}, u32[]{:S(2)}) collective-permute-start(bf16[256,256]{1,0:T(8,128)(2,1)S(1)} %get-tuple-element.71), channel_id=1, source_target_pairs={{0,3},{1,2},{2,1},{3,0},{4,7},{5,6},{6,5},{7,4},{8,11},{9,10},{10,... | collective-permute-start | bytes 393224 | tf_op jit(solution)/shard_map/ppermute | solution.py:32
  19.0 1.5 %collective-permute-start = (bf16[2,2,64,128]{3,2,1,0:T(8,128)(2,1)S(1)}, bf16[2,2,64,128]{3,2,1,0:T(8,128)(2,1)S(1)}, u32[]{:S(2)}, u32[]{:S(2)}) collective-permute-start(bf16[2,2,64,128]{3,2,1,0:T(8,128)(2,1)S(1)} %pack_prompts.1.refs_4_.refs_0_), channel_id=1, source_target_pairs={{0,16},{16,0},{1,17},{17,1},{2,18},{18,2},{3,19},{19,3},{4,20},{20... | collective-permute-start | bytes 196616 | tf_op jit(solution)/shard_map/ppermute | solution.py:32
  24.8 3.3 %collective-permute-done.6.refs_1_ = bf16[256,256]{1,0:T(8,128)(2,1)S(1)} collective-permute-done((bf16[256,256]{1,0:T(8,128)(2,1)S(1)}, bf16[256,256]{1,0:T(8,128)(2,1)S(1)}, u32[]{:S(2)}, u32[]{:S(2)}) %collective-permute-start.6) | collective-permute-done | bytes 131104 | tf_op jit(solution)/shard_map/ppermute | solution.py:32
  28.1 2.4 %collective-permute-done.8.refs_1_ = bf16[256,256]{1,0:T(8,128)(2,1)S(1)} collective-permute-done((bf16[256,256]{1,0:T(8,128)(2,1)S(1)}, bf16[256,256]{1,0:T(8,128)(2,1)S(1)}, u32[]{:S(2)}, u32[]{:S(2)}) %collective-permute-start.8) | collective-permute-done | bytes 131104 | tf_op jit(solution)/shard_map/ppermute | solution.py:32
  30.5 2.4 %collective-permute-start.14 = (bf16[256,256]{1,0:T(8,128)(2,1)S(1)}, bf16[256,256]{1,0:T(8,128)(2,1)S(1)}, u32[]{:S(2)}, u32[]{:S(2)}) collective-permute-start(bf16[256,256]{1,0:T(8,128)(2,1)S(1)} %sum_parts.8.refs_0_), channel_id=1, source_target_pairs={{0,2},{1,3},{2,0},{3,1},{4,6},{5,7},{6,4},{7,5},{8,10},{9,11},{10,... | collective-permute-start | bytes 393224 | tf_op jit(solution)/shard_map/ppermute | solution.py:32
  33.5 1.5 %collective-permute-start.10 = (bf16[256,256]{1,0:T(8,128)(2,1)S(1)}, bf16[256,256]{1,0:T(8,128)(2,1)S(1)}, u32[]{:S(2)}, u32[]{:S(2)}) collective-permute-start(bf16[256,256]{1,0:T(8,128)(2,1)S(1)} %sum_parts.8.refs_0_), channel_id=1, source_target_pairs={{0,3},{1,2},{2,1},{3,0},{4,7},{5,6},{6,5},{7,4},{8,11},{9,10},{10,... | collective-permute-start | bytes 393224 | tf_op jit(solution)/shard_map/ppermute | solution.py:32
  35.0 1.8 %collective-permute-start.4 = (bf16[2,64,128]{2,1,0:T(8,128)(2,1)S(1)}, bf16[2,64,128]{2,1,0:T(8,128)(2,1)S(1)}, u32[]{:S(2)}, u32[]{:S(2)}) collective-permute-start(bf16[2,64,128]{2,1,0:T(8,128)(2,1)S(1)} %get-tuple-element.69), channel_id=1, source_target_pairs={{0,8},{4,12},{8,0},{12,4},{1,9},{5,13},{9,1},{13,5},{2,10},{6,14},... | collective-permute-start | bytes 98312 | tf_op jit(solution)/shard_map/ppermute | solution.py:32
  37.5 1.6 %collective-permute-start.15 = (bf16[256,256]{1,0:T(8,128)(2,1)S(1)}, bf16[256,256]{1,0:T(8,128)(2,1)S(1)}, u32[]{:S(2)}, u32[]{:S(2)}) collective-permute-start(bf16[256,256]{1,0:T(8,128)(2,1)S(1)} %sum_parts.8.refs_0_), channel_id=1, source_target_pairs={{0,16},{16,0},{1,17},{17,1},{2,18},{18,2},{3,19},{19,3},{4,20},{20... | collective-permute-start | bytes 393224 | tf_op jit(solution)/shard_map/ppermute | solution.py:32
  40.1 1.8 %collective-permute-start.17 = (bf16[256,256]{1,0:T(8,128)(2,1)S(1)}, bf16[256,256]{1,0:T(8,128)(2,1)S(1)}, u32[]{:S(2)}, u32[]{:S(2)}) collective-permute-start(bf16[256,256]{1,0:T(8,128)(2,1)S(1)} %collective-permute-done.14.refs_2_), channel_id=1, source_target_pairs={{0,16},{16,0},{1,17},{17,1},{2,18},{18,2},{3,19},{19,3},{4,20},{20... | collective-permute-start | bytes 393224 | tf_op jit(solution)/shard_map/ppermute | solution.py:32
  41.9 2.1 %collective-permute-done.9.refs_4_.refs_1_ = bf16[256,256]{1,0:T(8,128)(2,1)S(1)} collective-permute-done((bf16[256,256]{1,0:T(8,128)(2,1)S(1)}, bf16[256,256]{1,0:T(8,128)(2,1)S(1)}, u32[]{:S(2)}, u32[]{:S(2)}) %collective-permute-start.9) | collective-permute-done | bytes 131104 | tf_op jit(solution)/shard_map/ppermute | solution.py:32
  45.5 3.9 %attention.2 = (bf16[256,1024]{1,0:T(8,128)(2,1)}, f32[512,128]{1,0:T(8,128)S(1)}, f32[512,128]{1,0:T(8,128)S(1)}) custom-call(s32[3]{0:T(128)S(1)} %pad_add_fusion.ranks, s32[4]{0:T(128)S(1)} %copy-done.6, s32[4]{0:T(128)S(1)} %copy-done.8, s32[1]{0:T(128)S(6)} %copy.23.resp_blocks, bf16[256,1024]{1,0:T(8,128)(2,1)S(1)} %copy-done, ...), custom_call_target="tpu_custom_call" | custom-call | flops 1 | bytes 1 | tf_op jit(solution)/shard_map/attention/pallas_call | solution.py:688
  50.1 4.5 %attention.3 = (bf16[256,1024]{1,0:T(8,128)(2,1)}, bf16[2,256,128]{2,1,0:T(8,128)(2,1)}, f32[2,64,128]{2,1,0:T(8,128)S(1)}, bf16[2,64,128]{2,1,0:T(8,128)(2,1)S(...) custom-call(s32[3]{0:T(128)S(1)} %pad_add_fusion.ranks, ...), custom_call_target="tpu_custom_call", output_to_operand_aliasing={{0}: (14, {})} | custom-call | flops 1 | bytes 1 | tf_op jit(solution)/shard_map/attention/pallas_call | solution.py:688
  61.5 3.5 %collective-permute-done.20.refs_1_ = f32[384,128]{1,0:T(8,128)S(1)} collective-permute-done((f32[384,128]{1,0:T(8,128)S(1)}, f32[384,128]{1,0:T(8,128)S(1)}, u32[]{:S(2)}, u32[]{:S(2)}) %collective-permute-start.20) | collective-permute-done | bytes 196640 | tf_op jit(solution)/shard_map/ppermute | solution.py:32
  65.0 9.9 %inverse_factor.1.x = f32[256,256]{1,0:T(8,128)S(1)} custom-call(f32[384,128]{1,0:T(8,128)S(1)} %sum_parts.10.refs_0_.refs_2_, f32[384,128]{1,0:T(8,128)S(1)} %collective-permute-done.20.refs_1_), custom_call_target="tpu_custom_call" | custom-call | flops 2000000000 | bytes 1 | tf_op jit(solution)/shard_map/inverse_factor/pallas_call | solution.py:398
  76.8 3.2 %collective-permute-start.24 = (f32[8,256]{1,0:T(8,128)S(1)}, f32[8,256]{1,0:T(8,128)S(1)}, u32[]{:S(2)}, u32[]{:S(2)}) collective-permute-start(f32[8,256]{1,0:T(8,128)S(1)} %get-tuple-element.90.refs_2_.refs_0_), channel_id=1, source_target_pairs={{0,1},{1,0},{2,3},{3,2},{4,5},{5,4},{6,7},{7,6},{8,9},{9,8},{10,11... | collective-permute-start | bytes 24584 | tf_op jit(solution)/shard_map/ppermute | solution.py:32
  80.0 2.1 %new_momentum.2 = (f32[2048,512]{1,0:T(8,128)}, f32[8,128]{1,0:T(8,128)S(1)}) custom-call(s32[3]{0:T(128)S(1)} %pad_add_fusion.ranks, bf16[2048,256]{1,0:T(8,128)(2,1)S(1)} %get-tuple-element.82.pcat, bf16[256,512]{1,0:T(8,128)(2,1)S(1)} %get-tuple-element.89.y, f32[512,512]{1,0:T(8,128)S(1)} %get-tuple-element.85.refs_0_, ...), custom_call_target="tpu_custom_call" | custom-call | flops 5000000000 | bytes 1 | tf_op jit(solution)/shard_map/new_momentum/pallas_call | solution.py:480
  82.8 1.6 %collective-permute-start.23 = (bf16[2,2,64,128]{3,2,1,0:T(8,128)(2,1)S(1)}, bf16[2,2,64,128]{3,2,1,0:T(8,128)(2,1)S(1)}, u32[]{:S(2)}, u32[]{:S(2)}) collective-permute-start(bf16[2,2,64,128]{3,2,1,0:T(8,128)(2,1)S(1)} %get-tuple-element.93), channel_id=1, source_target_pairs={{0,16},{16,0},{1,17},{17,1},{2,18},{18,2},{3,19},{19,3},{4,20},{20... | collective-permute-start | bytes 196616 | tf_op jit(solution)/shard_map/ppermute | solution.py:32
  85.0 2.1 %new_momentum.3 = (f32[2048,512]{1,0:T(8,128)}, f32[8,128]{1,0:T(8,128)S(1)}) custom-call(s32[3]{0:T(128)S(1)} %pad_add_fusion.ranks, bf16[2048,256]{1,0:T(8,128)(2,1)S(1)} %get-tuple-element.82.pcat, bf16[256,512]{1,0:T(8,128)(2,1)S(1)} %get-tuple-element.89.y, f32[512,512]{1,0:T(8,128)S(1)} %get-tuple-element.87.refs_2_.refs_0_, ...), custom_call_target="tpu_custom_call", output_to_operand_aliasing={{0}: (5, {})} | custom-call | flops 5000000000 | bytes 1 | tf_op jit(solution)/shard_map/new_momentum/pallas_call | solution.py:480
  88.1 3.3 %final_update.1 = (bf16[2048,512]{1,0:T(8,128)(2,1)}, f32[512,256]{1,0:T(8,128)}) custom-call(s32[3]{0:T(128)S(1)} %pad_add_fusion.ranks, bf16[2048,256]{1,0:T(8,128)(2,1)S(1)} %get-tuple-element.82.pcat, f32[256,256]{1,0:T(8,128)S(1)} %inverse_factor.1.x, f32[256,512]{1,0:T(8,128)S(1)} %get-tuple-element.96.bt, f32[8,256]{1,0:T(8,128)S(1)} %sum_parts.12.refs_3_.refs_0_, ...), custom_call_target="tpu_custom_call" | custom-call | flops 1 | bytes 1 | tf_op jit(solution)/shard_map/final_update/pallas_call | solution.py:526
  (76 shorter events, 19.9 us)
Async XLA Ops:
  4.5 10.1 %collective-permute-start.1 = (bf16[512,256]{1,0:T(8,128)(2,1)S(1)}, bf16[512,256]{1,0:T(8,128)(2,1)S(1)}, u32[]{:S(2)}, u32[]{:S(2)}) collective-permute-start(bf16[512,256]{1,0:T(8,128)(2,1)S(1)} %get-tuple-element.63), channel_id=1, source_target_pairs={{0,16},{16,0},{1,17},{17,1},{2,18},{18,2},{3,19},{19,3},{4,20},{20... | collective-permute-start | bytes 786440 | tf_op jit(solution)/shard_map/ppermute | solution.py:32
  10.1 11.8 %collective-permute-start.2 = (bf16[512,256]{1,0:T(8,128)(2,1)S(1)}, bf16[512,256]{1,0:T(8,128)(2,1)S(1)}, u32[]{:S(2)}, u32[]{:S(2)}) collective-permute-start(bf16[512,256]{1,0:T(8,128)(2,1)S(1)} %get-tuple-element.57.refs_2_), channel_id=1, source_target_pairs={{0,16},{16,0},{1,17},{17,1},{2,18},{18,2},{3,19},{19,3},{4,20},{20... | collective-permute-start | bytes 786440 | tf_op jit(solution)/shard_map/ppermute | solution.py:32
  14.7 10.0 %collective-permute-start.7 = (bf16[256,256]{1,0:T(8,128)(2,1)S(1)}, bf16[256,256]{1,0:T(8,128)(2,1)S(1)}, u32[]{:S(2)}, u32[]{:S(2)}) collective-permute-start(bf16[256,256]{1,0:T(8,128)(2,1)S(1)} %get-tuple-element.71), channel_id=1, source_target_pairs={{0,3},{1,2},{2,1},{3,0},{4,7},{5,6},{6,5},{7,4},{8,11},{9,10},{10,... | collective-permute-start | bytes 393224 | tf_op jit(solution)/shard_map/ppermute | solution.py:32
  18.9 9.1 %collective-permute-start.6 = (bf16[256,256]{1,0:T(8,128)(2,1)S(1)}, bf16[256,256]{1,0:T(8,128)(2,1)S(1)}, u32[]{:S(2)}, u32[]{:S(2)}) collective-permute-start(bf16[256,256]{1,0:T(8,128)(2,1)S(1)} %get-tuple-element.64.refs_4_), channel_id=1, source_target_pairs={{0,2},{1,3},{2,0},{3,1},{4,6},{5,7},{6,4},{7,5},{8,10},{9,11},{10,... | collective-permute-start | bytes 393224 | tf_op jit(solution)/shard_map/ppermute | solution.py:32
  19.0 4.3 %collective-permute-start = (bf16[2,2,64,128]{3,2,1,0:T(8,128)(2,1)S(1)}, bf16[2,2,64,128]{3,2,1,0:T(8,128)(2,1)S(1)}, u32[]{:S(2)}, u32[]{:S(2)}) collective-permute-start(bf16[2,2,64,128]{3,2,1,0:T(8,128)(2,1)S(1)} %pack_prompts.1.refs_4_.refs_0_), channel_id=1, source_target_pairs={{0,16},{16,0},{1,17},{17,1},{2,18},{18,2},{3,19},{19,3},{4,20},{20... | collective-permute-start | bytes 196616 | tf_op jit(solution)/shard_map/ppermute | solution.py:32
  23.9 4.2 %collective-permute-start.5 = (bf16[2,64,128]{2,1,0:T(8,128)(2,1)S(1)}, bf16[2,64,128]{2,1,0:T(8,128)(2,1)S(1)}, u32[]{:S(2)}, u32[]{:S(2)}) collective-permute-start(bf16[2,64,128]{2,1,0:T(8,128)(2,1)S(1)} %get-tuple-element.70), channel_id=1, source_target_pairs={{0,12},{4,8},{8,4},{12,0},{1,13},{5,9},{9,5},{13,1},{2,14},{6,10},... | collective-permute-start | bytes 98312 | tf_op jit(solution)/shard_map/ppermute | solution.py:32
  24.1 6.5 %collective-permute-start.8 = (bf16[256,256]{1,0:T(8,128)(2,1)S(1)}, bf16[256,256]{1,0:T(8,128)(2,1)S(1)}, u32[]{:S(2)}, u32[]{:S(2)}) collective-permute-start(bf16[256,256]{1,0:T(8,128)(2,1)S(1)} %get-tuple-element.72), channel_id=1, source_target_pairs={{0,1},{1,0},{2,3},{3,2},{4,5},{5,4},{6,7},{7,6},{8,9},{9,8},{10,11... | collective-permute-start | bytes 393224 | tf_op jit(solution)/shard_map/ppermute | solution.py:32
  30.5 9.6 %collective-permute-start.14 = (bf16[256,256]{1,0:T(8,128)(2,1)S(1)}, bf16[256,256]{1,0:T(8,128)(2,1)S(1)}, u32[]{:S(2)}, u32[]{:S(2)}) collective-permute-start(bf16[256,256]{1,0:T(8,128)(2,1)S(1)} %sum_parts.8.refs_0_), channel_id=1, source_target_pairs={{0,2},{1,3},{2,0},{3,1},{4,6},{5,7},{6,4},{7,5},{8,10},{9,11},{10,... | collective-permute-start | bytes 393224 | tf_op jit(solution)/shard_map/ppermute | solution.py:32
  33.0 11.0 %collective-permute-start.9 = (bf16[256,256]{1,0:T(8,128)(2,1)S(1)}, bf16[256,256]{1,0:T(8,128)(2,1)S(1)}, u32[]{:S(2)}, u32[]{:S(2)}) collective-permute-start(bf16[256,256]{1,0:T(8,128)(2,1)S(1)} %sum_parts.8.refs_0_), channel_id=1, source_target_pairs={{0,1},{1,0},{2,3},{3,2},{4,5},{5,4},{6,7},{7,6},{8,9},{9,8},{10,11... | collective-permute-start | bytes 393224 | tf_op jit(solution)/shard_map/ppermute | solution.py:32
  33.5 15.9 %collective-permute-start.10 = (bf16[256,256]{1,0:T(8,128)(2,1)S(1)}, bf16[256,256]{1,0:T(8,128)(2,1)S(1)}, u32[]{:S(2)}, u32[]{:S(2)}) collective-permute-start(bf16[256,256]{1,0:T(8,128)(2,1)S(1)} %sum_parts.8.refs_0_), channel_id=1, source_target_pairs={{0,3},{1,2},{2,1},{3,0},{4,7},{5,6},{6,5},{7,4},{8,11},{9,10},{10,... | collective-permute-start | bytes 393224 | tf_op jit(solution)/shard_map/ppermute | solution.py:32
  35.0 10.5 %collective-permute-start.4 = (bf16[2,64,128]{2,1,0:T(8,128)(2,1)S(1)}, bf16[2,64,128]{2,1,0:T(8,128)(2,1)S(1)}, u32[]{:S(2)}, u32[]{:S(2)}) collective-permute-start(bf16[2,64,128]{2,1,0:T(8,128)(2,1)S(1)} %get-tuple-element.69), channel_id=1, source_target_pairs={{0,8},{4,12},{8,0},{12,4},{1,9},{5,13},{9,1},{13,5},{2,10},{6,14},... | collective-permute-start | bytes 98312 | tf_op jit(solution)/shard_map/ppermute | solution.py:32
  37.5 17.1 %collective-permute-start.15 = (bf16[256,256]{1,0:T(8,128)(2,1)S(1)}, bf16[256,256]{1,0:T(8,128)(2,1)S(1)}, u32[]{:S(2)}, u32[]{:S(2)}) collective-permute-start(bf16[256,256]{1,0:T(8,128)(2,1)S(1)} %sum_parts.8.refs_0_), channel_id=1, source_target_pairs={{0,16},{16,0},{1,17},{17,1},{2,18},{18,2},{3,19},{19,3},{4,20},{20... | collective-permute-start | bytes 393224 | tf_op jit(solution)/shard_map/ppermute | solution.py:32
  40.1 14.5 %collective-permute-start.17 = (bf16[256,256]{1,0:T(8,128)(2,1)S(1)}, bf16[256,256]{1,0:T(8,128)(2,1)S(1)}, u32[]{:S(2)}, u32[]{:S(2)}) collective-permute-start(bf16[256,256]{1,0:T(8,128)(2,1)S(1)} %collective-permute-done.14.refs_2_), channel_id=1, source_target_pairs={{0,16},{16,0},{1,17},{17,1},{2,18},{18,2},{3,19},{19,3},{4,20},{20... | collective-permute-start | bytes 393224 | tf_op jit(solution)/shard_map/ppermute | solution.py:32
  44.0 10.7 %collective-permute-start.16 = (bf16[256,256]{1,0:T(8,128)(2,1)S(1)}, bf16[256,256]{1,0:T(8,128)(2,1)S(1)}, u32[]{:S(2)}, u32[]{:S(2)}) collective-permute-start(bf16[256,256]{1,0:T(8,128)(2,1)S(1)} %collective-permute-done.9.refs_4_.refs_1_), channel_id=1, source_target_pairs={{0,16},{16,0},{1,17},{17,1},{2,18},{18,2},{3,19},{19,3},{4,20},{20... | collective-permute-start | bytes 393224 | tf_op jit(solution)/shard_map/ppermute | solution.py:32
  49.5 5.2 %collective-permute-start.18 = (bf16[256,256]{1,0:T(8,128)(2,1)S(1)}, bf16[256,256]{1,0:T(8,128)(2,1)S(1)}, u32[]{:S(2)}, u32[]{:S(2)}) collective-permute-start(bf16[256,256]{1,0:T(8,128)(2,1)S(1)} %sum_parts.9.refs_7_), channel_id=1, source_target_pairs={{0,16},{16,0},{1,17},{17,1},{2,18},{18,2},{3,19},{19,3},{4,20},{20... | collective-permute-start | bytes 393224 | tf_op jit(solution)/shard_map/ppermute | solution.py:32
  57.2 7.8 %collective-permute-start.20 = (f32[384,128]{1,0:T(8,128)S(1)}, f32[384,128]{1,0:T(8,128)S(1)}, u32[]{:S(2)}, u32[]{:S(2)}) collective-permute-start(f32[384,128]{1,0:T(8,128)S(1)} %sum_parts.10.refs_0_.refs_2_), channel_id=1, source_target_pairs={{0,8},{4,12},{8,0},{12,4},{1,9},{5,13},{9,1},{13,5},{2,10},{6,14},... | collective-permute-start | bytes 589832 | tf_op jit(solution)/shard_map/ppermute | solution.py:32
  58.5 16.4 %collective-permute-start.22 = (bf16[256,512]{1,0:T(8,128)(2,1)S(1)}, bf16[256,512]{1,0:T(8,128)(2,1)S(1)}, u32[]{:S(2)}, u32[]{:S(2)}) collective-permute-start(bf16[256,512]{1,0:T(8,128)(2,1)S(1)} %sum_parts.11.wa), channel_id=1, source_target_pairs={{0,8},{4,12},{8,0},{12,4},{1,9},{5,13},{9,1},{13,5},{2,10},{6,14},... | collective-permute-start | bytes 786440 | tf_op jit(solution)/shard_map/ppermute | solution.py:32
  59.6 17.1 %collective-permute-start.11 = (bf16[2,64,128]{2,1,0:T(8,128)(2,1)S(1)}, bf16[2,64,128]{2,1,0:T(8,128)(2,1)S(1)}, u32[]{:S(2)}, u32[]{:S(2)}) collective-permute-start(bf16[2,64,128]{2,1,0:T(8,128)(2,1)S(1)} %get-tuple-element.79), channel_id=1, source_target_pairs={{0,4},{4,0},{8,12},{12,8},{1,5},{5,1},{9,13},{13,9},{2,6},{6,2},{1... | collective-permute-start | bytes 98312 | tf_op jit(solution)/shard_map/ppermute | solution.py:32
  59.7 22.4 %collective-permute-start.12 = (bf16[2,64,128]{2,1,0:T(8,128)(2,1)S(1)}, bf16[2,64,128]{2,1,0:T(8,128)(2,1)S(1)}, u32[]{:S(2)}, u32[]{:S(2)}) collective-permute-start(bf16[2,64,128]{2,1,0:T(8,128)(2,1)S(1)} %get-tuple-element.80), channel_id=1, source_target_pairs={{0,8},{4,12},{8,0},{12,4},{1,9},{5,13},{9,1},{13,5},{2,10},{6,14},... | collective-permute-start | bytes 98312 | tf_op jit(solution)/shard_map/ppermute | solution.py:32
  60.6 21.6 %collective-permute-start.13 = (bf16[2,64,128]{2,1,0:T(8,128)(2,1)S(1)}, bf16[2,64,128]{2,1,0:T(8,128)(2,1)S(1)}, u32[]{:S(2)}, u32[]{:S(2)}) collective-permute-start(bf16[2,64,128]{2,1,0:T(8,128)(2,1)S(1)} %get-tuple-element.81), channel_id=1, source_target_pairs={{0,12},{4,8},{8,4},{12,0},{1,13},{5,9},{9,5},{13,1},{2,14},{6,10},... | collective-permute-start | bytes 98312 | tf_op jit(solution)/shard_map/ppermute | solution.py:32
  75.5 8.8 %collective-permute-start.26 = (f32[8,256]{1,0:T(8,128)S(1)}, f32[8,256]{1,0:T(8,128)S(1)}, u32[]{:S(2)}, u32[]{:S(2)}) collective-permute-start(f32[8,256]{1,0:T(8,128)S(1)} %get-tuple-element.90.refs_2_.refs_0_), channel_id=1, source_target_pairs={{0,3},{1,2},{2,1},{3,0},{4,7},{5,6},{6,5},{7,4},{8,11},{9,10},{10,... | collective-permute-start | bytes 24584 | tf_op jit(solution)/shard_map/ppermute | solution.py:32
  76.7 7.6 %collective-permute-start.25 = (f32[8,256]{1,0:T(8,128)S(1)}, f32[8,256]{1,0:T(8,128)S(1)}, u32[]{:S(2)}, u32[]{:S(2)}) collective-permute-start(f32[8,256]{1,0:T(8,128)S(1)} %get-tuple-element.90.refs_2_.refs_0_), channel_id=1, source_target_pairs={{0,2},{1,3},{2,0},{3,1},{4,6},{5,7},{6,4},{7,5},{8,10},{9,11},{10,... | collective-permute-start | bytes 24584 | tf_op jit(solution)/shard_map/ppermute | solution.py:32
  76.8 7.6 %collective-permute-start.24 = (f32[8,256]{1,0:T(8,128)S(1)}, f32[8,256]{1,0:T(8,128)S(1)}, u32[]{:S(2)}, u32[]{:S(2)}) collective-permute-start(f32[8,256]{1,0:T(8,128)S(1)} %get-tuple-element.90.refs_2_.refs_0_), channel_id=1, source_target_pairs={{0,1},{1,0},{2,3},{3,2},{4,5},{5,4},{6,7},{7,6},{8,9},{9,8},{10,11... | collective-permute-start | bytes 24584 | tf_op jit(solution)/shard_map/ppermute | solution.py:32
  82.8 8.6 %collective-permute-start.23 = (bf16[2,2,64,128]{3,2,1,0:T(8,128)(2,1)S(1)}, bf16[2,2,64,128]{3,2,1,0:T(8,128)(2,1)S(1)}, u32[]{:S(2)}, u32[]{:S(2)}) collective-permute-start(bf16[2,2,64,128]{3,2,1,0:T(8,128)(2,1)S(1)} %get-tuple-element.93), channel_id=1, source_target_pairs={{0,16},{16,0},{1,17},{17,1},{2,18},{18,2},{3,19},{19,3},{4,20},{20... | collective-permute-start | bytes 196616 | tf_op jit(solution)/shard_map/ppermute | solution.py:32
  (13 other events, 128.2 us)

commit v7 on v6

--- a/solution.py
+++ b/solution.py
@@ -124,7 +124,9 @@
             c.wait()
 
 
-def project(ranks, momentum, grad_q, ins, part, following, n_resp, n_head, dtype, after):
+def project(
+    ranks, momentum, grad_q, ins, part, following, n_resp, n_head, dtype, after, weight=0
+):
     is_first = len(ins) == 1
     rows, cols = momentum.shape
     chunk = rows // (n_resp * n_head)
@@ -157,7 +159,7 @@
         out_shape=out_shape,
         compiler_params=params(14),
         name="project",
-        cost_estimate=cost(),
+        cost_estimate=cost(weight),
     )(ranks, momentum, grad_q, *ins, *after)
     right = tuple(outs[2:4]) if is_first else tuple(ins[:2])
     return outs[0], outs[1], right + tuple(outs[-2:] if following else ())
@@ -211,11 +213,32 @@
     )(*parts, *after)
 
 
+def relay_kernel(n_parts, *refs):
+    out = refs[-1]
+    size = out.shape[0] // n_parts
+    for i in range(n_parts):
+        out[i * size : (i + 1) * size, :] = refs[i][...]
+
+
+def relay(parts, after):
+    rows, rank = parts[0].shape
+    return pl.pallas_call(
+        functools.partial(relay_kernel, len(parts)),
+        in_specs=[VMEM] * len(parts) + [ANY] * len(after),
+        out_specs=VMEM,
+        out_shape=jax.ShapeDtypeStruct((len(parts) * rows, rank), parts[0].dtype),
+        compiler_params=params(),
+        name="relay",
+        cost_estimate=cost(),
+    )(*parts, *after)
+
+
 def gram_kernel(n_chunks, *refs):
     chunks, (pcat, pcat_t, gram) = refs[:n_chunks], refs[-3:]
-    size = chunks[0].shape[0]
-    for i in range(n_chunks):
-        pcat[i * size : (i + 1) * size, :] = chunks[i][...]
+    at = 0
+    for c in chunks:
+        pcat[at : at + c.shape[0], :] = c[...]
+        at += c.shape[0]
     p = pcat[...]
     pt = p.T
     pcat_t[...] = pt
@@ -227,8 +250,8 @@
 
 
 def gather_gram(chunks, after):
-    size, rank = chunks[0].shape
-    rows = size * len(chunks)
+    rank = chunks[0].shape[1]
+    rows = sum(c.shape[0] for c in chunks)
     return pl.pallas_call(
         functools.partial(gram_kernel, len(chunks)),
         in_specs=[VMEM] * len(chunks) + [ANY] * len(after),
@@ -413,7 +436,8 @@
     return mm(a_hi, b_hi) + (mm(a_hi, b_lo) + mm(a_lo, b_hi))
 
 
-def back_kernel(x, wa, wb, bt_out, y_out, s_out):
+def back_kernel(x, wa, wb, *refs):
+    bt_out, y_out, s_out = refs[-3:]
     w = wa[...].astype(F32) + wb[...].astype(F32)
     bt = mm_three(x[...], w)
     bt_out[...] = bt
@@ -422,11 +446,11 @@
     y_out[...] = ((1.0 - momentum_keep) * mm(x[...].T.astype(BF16), bt.astype(BF16))).astype(BF16)
 
 
-def back_full(x, wa, wb):
+def back_full(x, wa, wb, after):
     rank, cols = wa.shape
     return pl.pallas_call(
         back_kernel,
-        in_specs=[VMEM] * 3,
+        in_specs=[VMEM] * 3 + [ANY] * len(after),
         out_specs=[VMEM] * 3,
         out_shape=[
             jax.ShapeDtypeStruct((rank, cols), F32),
@@ -436,7 +460,7 @@
         compiler_params=params(),
         name="back_full",
         cost_estimate=cost(),
-    )(x, wa, wb)
+    )(x, wa, wb, *after)
 
 
 def row_blocks(ranks, n_resp, n_head, chunk):
@@ -447,12 +471,9 @@
     ]
 
 
-def momentum_kernel(n_resp, n_head, begin, end, n_totals, ranks, pcat, y, *refs):
-    totals, (out, token, held, sems) = refs[:n_totals], refs[-4:]
-    token[...] = jnp.zeros_like(token)
+def momentum_rows(blocks, pcat, y, totals, held, out, sems, begin, end):
+    chunk = held.shape[0] // (end - begin)
     seg = totals[0].shape[0]
-    chunk = pcat.shape[0] // (n_resp * n_head)
-    blocks = row_blocks(ranks, n_resp, n_head, chunk)
     copies = []
     for i in range(begin, end):
         rows = slice(i * chunk, (i + 1) * chunk)
@@ -466,81 +487,122 @@
             )
         )
         copies[-1].start()
-    for c in copies:
+    return copies
+
+
+def momentum_kernel(n_resp, n_head, n_totals, ranks, pcat, y, *refs):
+    totals, refs = refs[:n_totals], refs[n_totals:]
+    dq_parts, rg, refs = refs[:2], refs[2], refs[-7:]
+    out, dq, resp_grad, token, held, sems, more = refs
+    token[...] = jnp.zeros_like(token)
+    width = dq_parts[0].shape[1]
+    copies = [
+        pltpu.make_async_copy(part, dq.at[:, pl.ds(i * width, width)], more.at[i])
+        for i, part in enumerate(dq_parts)
+    ]
+    copies.append(pltpu.make_async_copy(rg, resp_grad, more.at[2]))
+    n = n_resp * n_head
+    blocks = row_blocks(ranks, n_resp, n_head, pcat.shape[0] // n)
+    copies[2].start()
+    moved = momentum_rows(blocks, pcat, y, totals, held, out, sems, 0, n // 2)
+    for c in copies[:2]:
+        c.start()
+    for c in copies + moved:
         c.wait()
 
 
-def new_momentum(ranks, pcat, totals, y, n_resp, n_head, half, earlier, after):
+def new_momentum(ranks, pcat, totals, y, n_resp, n_head, dq_parts, rg, after):
     rows, rank = pcat.shape
     cols = totals[0].shape[1]
-    n_chunks = n_resp * n_head // 2
-    part = len(totals) // 2
-    totals = totals[half * part : (half + 1) * part]
-    aliases = {3 + part: 0} if earlier else {}
-    return pl.pallas_call(
-        functools.partial(
-            momentum_kernel, n_resp, n_head, half * n_chunks, (half + 1) * n_chunks, part
-        ),
-        in_specs=[SMEM] + [VMEM] * (2 + part) + [HBM] * len(earlier) + [ANY] * len(after),
-        out_specs=[HBM, VMEM],
-        scratch_shapes=[pltpu.VMEM((rows // 2, cols), F32), pltpu.SemaphoreType.DMA((n_chunks,))],
+    length, width = dq_parts[0].shape
+    return pl.pallas_call(
+        functools.partial(momentum_kernel, n_resp, n_head, len(totals)),
+        in_specs=[SMEM] + [VMEM] * (5 + len(totals)) + [ANY] * len(after),
+        out_specs=[HBM, HBM, HBM, VMEM],
+        scratch_shapes=[
+            pltpu.VMEM((rows // 2, cols), F32),
+            pltpu.SemaphoreType.DMA((n_resp * n_head // 2,)),
+            pltpu.SemaphoreType.DMA((3,)),
+        ],
         out_shape=[
-            jax.ShapeDtypeStruct((rows, cols), F32), jax.ShapeDtypeStruct((8, 128), F32)
+            jax.ShapeDtypeStruct((rows, cols), F32),
+            jax.ShapeDtypeStruct((length, 2 * width), BF16),
+            jax.ShapeDtypeStruct(rg.shape, BF16),
+            jax.ShapeDtypeStruct((8, 128), F32),
         ],
-        input_output_aliases=aliases,
-        compiler_params=params(10),
+        compiler_params=params(12),
         name="new_momentum",
         cost_estimate=cost(5),
-    )(ranks, pcat, y, *totals, *earlier, *after)
-
-
-def update_kernel(gain, n_resp, n_head, n_sums, ranks, pcat, x, bt, *refs):
-    sums, (upd, basis_out, held, held_basis, sems, basis_sem) = refs[:n_sums], refs[n_sums:]
+    )(ranks, pcat, y, *totals, *dq_parts, rg, *after)
+
+
+def update_kernel(gain, n_resp, n_head, n_sums, n_totals, n_prompt, ranks, pcat, x, bt, y, *refs):
+    sums, refs = refs[:n_sums], refs[n_sums:]
+    totals, refs = refs[:n_totals], refs[n_totals:]
+    prompts, refs = refs[:n_prompt], refs[n_prompt + 1 :]
+    upd, basis_out, mom_out, prompt_out, held, held_mom, held_basis, held_prompt, sems, more = refs
+    n = n_resp * n_head
+    chunk = pcat.shape[0] // n
+    blocks = row_blocks(ranks, n_resp, n_head, chunk)
     total = sums[0][...]
     for s in sums[1:]:
         total = total + s[...]
     scale = lax.rsqrt(total + norm_eps).T[:, :1]
     scaled = bt[...] * scale
     held_basis[...] = scaled.T
-    basis_copy = pltpu.make_async_copy(held_basis, basis_out, basis_sem)
-    basis_copy.start()
+    acc = prompts[0][...]
+    for p in prompts[1:]:
+        acc = acc + p[...].astype(F32)
+    held_prompt[...] = acc
+    copies = [
+        pltpu.make_async_copy(held_basis, basis_out, more.at[0]),
+        pltpu.make_async_copy(held_prompt, prompt_out, more.at[1]),
+    ]
+    for c in copies:
+        c.start()
+    copies += momentum_rows(blocks, pcat, y, totals, held_mom, mom_out, sems.at[1], n // 2, n)
     z_hi, z_lo = halves(gain * mm_three(x[...].T, scaled))
-    chunk = pcat.shape[0] // (n_resp * n_head)
-    copies = []
-    for i, at in enumerate(row_blocks(ranks, n_resp, n_head, chunk)):
+    for i, at in enumerate(blocks):
         rows = slice(i * chunk, (i + 1) * chunk)
         p = pcat[rows, :]
         held[rows, :] = (mm(p, z_hi) + mm(p, z_lo)).astype(BF16)
         copies.append(
-            pltpu.make_async_copy(held.at[rows, :], upd.at[pl.ds(at, chunk), :], sems.at[i])
+            pltpu.make_async_copy(held.at[rows, :], upd.at[pl.ds(at, chunk), :], sems.at[0, i])
         )
         copies[-1].start()
     for c in copies:
         c.wait()
-    basis_copy.wait()
-
-
-def final_update(ranks, pcat, x, bt, sums, gain, n_resp, n_head):
+
+
+def final_update(ranks, pcat, x, bt, y, sums, totals, prompts, momentum, gain, n_resp, n_head):
     rows, rank = pcat.shape
     cols = bt.shape[1]
-    return pl.pallas_call(
-        functools.partial(update_kernel, gain, n_resp, n_head, len(sums)),
-        in_specs=[SMEM] + [VMEM] * (3 + len(sums)),
-        out_specs=[HBM, HBM],
+    n_vmem = 4 + len(sums) + len(totals) + len(prompts)
+    return pl.pallas_call(
+        functools.partial(
+            update_kernel, gain, n_resp, n_head, len(sums), len(totals), len(prompts)
+        ),
+        in_specs=[SMEM] + [VMEM] * n_vmem + [HBM],
+        out_specs=[HBM] * 4,
         scratch_shapes=[
             pltpu.VMEM((rows, cols), BF16),
+            pltpu.VMEM((rows // 2, cols), F32),
             pltpu.VMEM((cols, rank), F32),
-            pltpu.SemaphoreType.DMA((n_resp * n_head,)),
-            pltpu.SemaphoreType.DMA,
+            pltpu.VMEM(prompts[0].shape, F32),
+            pltpu.SemaphoreType.DMA((2, n_resp * n_head)),
+            pltpu.SemaphoreType.DMA((2,)),
         ],
         out_shape=[
             jax.ShapeDtypeStruct((rows, cols), BF16),
             jax.ShapeDtypeStruct((cols, rank), F32),
+            jax.ShapeDtypeStruct((rows, cols), F32),
+            jax.ShapeDtypeStruct(prompts[0].shape, F32),
         ],
-        compiler_params=params(10),
+        input_output_aliases={1 + n_vmem: 2},
+        compiler_params=params(14),
         name="final_update",
-        cost_estimate=cost(),
-    )(ranks, pcat, x, bt, *sums)
+        cost_estimate=cost(5),
+    )(ranks, pcat, x, bt, y, *sums, *totals, *prompts, momentum)
 
 
 def group_of(counts, response):
@@ -601,10 +663,10 @@
     n_fsdp, heads, last, ranks, counts, prompt_blocks, resp_blocks, q, sk, sv, go, *refs
 ):
     pieces, refs = refs[:n_fsdp], refs[n_fsdp:]
-    dq_held, keys, values, dk, dv, sems = refs[-6:]
+    keys, values, dk, dv = refs[-4:]
     n_out = 2 + n_fsdp if last else 3
-    outs = refs[-6 - n_out : -6]
-    dq, copies = outs[0], []
+    outs = refs[-4 - n_out : -4]
+    dq = outs[0]
     piece = pieces[0].shape[1]
     cap = piece * n_fsdp
     length = q.shape[0]
@@ -637,7 +699,7 @@
         dk[...] = jnp.zeros_like(dk)
         dv[...] = jnp.zeros_like(dv)
     for i, h in enumerate(heads):
-        cols = pl.ds(h * HD, HD)
+        cols = slice(h * HD, (h + 1) * HD)
         qh = q[:, cols]
         gh = jnp.where(live, go[:, cols], jnp.zeros((), BF16))
         logits = lax.dot_general(kall, qh, nt, preferred_element_type=F32) * scale + bias
@@ -650,9 +712,7 @@
         ds = (wf * (dp - diag)).astype(BF16)
         dk[...] += mm(ds, qh)
         dv[...] += mm(w, gh)
-        dq_held[i] = (mm(kt, ds) * scale).T.astype(BF16)
-        copies.append(pltpu.make_async_copy(dq_held.at[i], dq.at[:, cols], sems.at[i]))
-        copies[-1].start()
+        dq[:, i * HD : (i + 1) * HD] = (mm(kt, ds) * scale).T.astype(BF16)
     if last:
         own, sends = outs[1], outs[2:]
         own[0] = (dk[cap:, :] * scale).astype(BF16)
@@ -664,8 +724,6 @@
     else:
         outs[1][...] = dk[...]
         outs[2][...] = dv[...]
-    for c in copies:
-        c.wait()
 
 
 def attention(heads, earlier, ranks, counts, prompt_blocks, resp_blocks, q, sk, sv, go, pieces, after):
@@ -675,10 +733,9 @@
     cap = piece * n_fsdp
     total = cap + length
     last = earlier is not None
-    dq_shape = jax.ShapeDtypeStruct((length, width), BF16)
-    aliases = {8 + n_fsdp + 2: 0} if last else {}
+    dq_shape = jax.ShapeDtypeStruct((length, len(heads) * HD), BF16)
     if last:
-        extra, specs = (earlier[1], earlier[2], earlier[0]), [VMEM, VMEM, HBM]
+        extra, specs = (earlier[1], earlier[2]), [VMEM] * 2
         out_shape = [dq_shape, jax.ShapeDtypeStruct((2, length, HD), BF16)] + [
             jax.ShapeDtypeStruct((2, piece, HD), BF16 if k else F32) for k in range(n_fsdp)
         ]
@@ -688,13 +745,9 @@
     return pl.pallas_call(
         functools.partial(attention_kernel, n_fsdp, heads, last),
         in_specs=[SMEM] * 4 + [VMEM] * (4 + n_fsdp) + specs + [ANY] * len(after),
-        out_specs=[HBM] + [VMEM] * (len(out_shape) - 1),
-        scratch_shapes=[pltpu.VMEM((len(heads), length, HD), BF16)]
-        + [pltpu.VMEM((total, HD), BF16)] * 2
-        + [pltpu.VMEM((total, HD), F32)] * 2
-        + [pltpu.SemaphoreType.DMA((len(heads),))],
+        out_specs=[VMEM] * len(out_shape),
+        scratch_shapes=[pltpu.VMEM((total, HD), BF16)] * 2 + [pltpu.VMEM((total, HD), F32)] * 2,
         out_shape=out_shape,
-        input_output_aliases=aliases,
         compiler_params=params(12),
         name="attention",
         cost_estimate=cost(),
@@ -759,29 +812,35 @@
     groups = [(half, half), (0, half)] if half else [(0, n_head)]
 
     mom_hbm, grad_hbm, basis_hbm = in_hbm
-    order = [(j, *group) for group in groups for j in range(1, n_resp)]
-    order += [(0, *group) for group in groups]
+    order = [(j, *group) for group in groups for j in [*range(1, n_resp), 0]]
     nexts = dict(zip(order, order[1:] + [None]))
     totals, arrived, split, ins, after = {}, {}, {}, (basis_hbm,), ()
     for part in order:
         j, first, number = part
         value, totals[part[:2]], ins = project(
             ranks, mom_hbm, grad_hbm, ins, part, nexts[part], n_resp, n_head, BF16 if j else F32,
-            after,
+            after, 0 if j or first == 0 else 10,
         )
+        after = ()
         if j:
             arrived.setdefault(first, []).append(swap(value, "resp", j))
             if part[1:] == groups[-1] and j == n_resp - 1:
                 packed = pack_prompts(prompt_keys, prompt_values, (value,))
                 stored = [packed] + [swap(packed, "resp", k) for k in range(1, n_resp)]
-                after = (packed,)
+                outs = split_sum(owned, arrived[groups[0][0]], *groups[0])
+                for i in range(groups[0][1]):
+                    split[groups[0][0] + i] = outs[i]
+                after = (outs[0],)
+        elif part[1:] == groups[0] and len(groups) > 1:
+            owned = value
         else:
             outs = split_sum(value, arrived[first], first, number)
-            after = (outs[0],)
             for i in range(number):
                 split[first + i] = outs[i]
     totals = [totals[at] for at in sorted(totals)]
-    chosen = select_prompts(ranks, counts, owner_slot, stored, n_fsdp, (outs[0],))
+    chosen = select_prompts(
+        ranks, counts, owner_slot, stored, n_fsdp, (split[1 % n_head],)
+    )
     far_first = [k for first, number in groups for k in range(first, first + number) if k]
     summands = {k: swap(split[k], "head", k) for k in far_first}
     pieces = [chosen[0]] + [swap(chosen[k], "fsdp", k) for k in range(1, n_fsdp)]
@@ -790,7 +849,7 @@
         [split[0]] + [summands[k] for k in range(later, n_head)], F32, (), 10
     )
     piece0 = sum_parts(
-        [far] + [summands[k] for k in range(1, later)], BF16, (pieces[-1],)
+        [far] + [summands[k] for k in range(1, later)], BF16, tuple(pieces[1:])
     )
 
     along = {0: piece0}
@@ -802,13 +861,16 @@
         ranks, counts, prompt_blocks, resp_blocks, queries, self_keys, self_values, d_out, pieces
     )
     earlier = attention(heads[0], None, *held, (along[1 % n_head],))
-    last = n_head - 1
-    passed = dict(along)
-    passed[last] = sum_parts([along[last]], BF16, (earlier[1],))
-    chunks = [along[k] for k in range(n_head)]
+    near = [along[k] for k in range(later)]
+    passed = [[swap(c, "resp", j) for c in near] for j in range(1, n_resp)]
+    far = relay(
+        [along[k] for k in range(later, n_head)], (earlier[1], *[c for row in passed for c in row])
+    )
+    chunks = near + [along[k] for k in range(later, n_head)]
     for j in range(1, n_resp):
-        chunks += [swap(passed[k], "resp", j) for k in range(n_head)]
-    dq, resp_grad, *parts = attention(heads[1], earlier, *held, (passed[last],))
+        chunks += passed[j - 1] + [swap(far, "resp", j)]
+    dq_parts, resp_grad, *parts = attention(heads[1], earlier, *held, (far,))
+    dq_parts = (earlier[0], dq_parts)
     pcat, pcat_t, gram = gather_gram(chunks, (parts[0],))
 
     bits = [1 << b for b in range(n_fsdp.bit_length() - 1)]
@@ -820,21 +882,21 @@
     w_other = swap(w, "fsdp", bits[-1])
     returned = [parts[0]] + [swap(parts[k], "fsdp", k) for k in range(1, n_fsdp)]
     x = inverse_factor(*gram_parts)
-    bt, y, squares = back_full(x, w, w_other)
+    bt, y, squares = back_full(x, w, w_other, tuple(returned[1:]))
     from_head = [swap(squares, "head", k) for k in range(1, n_head)]
-    momentum_out, token = new_momentum(
-        ranks, pcat, totals, y, n_resp, n_head, 0, (), (squares,)
-    )
-    slots = sum_by_slot(ranks, counts, owner_slot, returned, n_resp, (token,))
+    half = len(totals) // 2
+    momentum_out, dq, resp_grad, token = new_momentum(
+        ranks, pcat, totals[:half], y, n_resp, n_head, dq_parts, resp_grad, (squares,)
+    )
     squares = sum_parts([squares] + from_head, F32, (token,))
-    sums = [squares] + [swap(squares, "resp", j) for j in range(1, n_resp)]
-    momentum_out, token = new_momentum(
-        ranks, pcat, totals, y, n_resp, n_head, 1, (momentum_out,), (squares,)
-    )
-    prompt_grad = sum_parts(
-        [slots[0]] + [swap(slots[j], "resp", j) for j in range(1, n_resp)], F32, (token,)
-    )
-    update, basis_out = final_update(ranks, pcat, x, bt, sums, gain, n_resp, n_head)
+    sums = sum_parts(
+        [squares] + [swap(squares, "resp", j) for j in range(1, n_resp)], F32, (), 5
+    )
+    slots = sum_by_slot(ranks, counts, owner_slot, returned, n_resp, (squares,))
+    prompts = [slots[0]] + [swap(slots[j], "resp", j) for j in range(1, n_resp)]
+    update, basis_out, momentum_out, prompt_grad = final_update(
+        ranks, pcat, x, bt, y, [sums], totals[half:], prompts, momentum_out, gain, n_resp, n_head
+    )
     return (dq, resp_grad, prompt_grad, update, momentum_out, basis_out)
 
 

time: 92.3 us -> 90.5 us (0.980)
  waiting for transfers between devices: 16.5 us -> 21.6 us
  Pallas kernels: 41.1 us -> 36.8 us
  starting transfers between devices: 32.8 us -> 30 us
    ppermute x28 -> x27, waiting for transfers between devices: 16.5 us -> 21.6 us  [swap(): return lax.ppermute(value, axes, [(i, i ^ k) for i in range(n)])]
    ppermute x28 -> x27, starting transfers between devices: 32.8 us -> 30 us  [swap(): return lax.ppermute(value, axes, [(i, i ^ k) for i in range(n)])]
    pallas_call x2, Pallas kernels: 8.46 us -> 6.47 us  [attention(): pl.pallas_call(functools.partial(attention_kernel, n_fsdp, heads, last),...]
    pallas_call x3, Pallas kernels: 4.87 us -> 2.96 us  [the longest x1 2.32 us: new_momentum(): pl.pallas_call(functools.partial(momentum_kernel, n_resp, n_head, len(tot...]
  transfers between devices with their start and end apart: 28 -> 27, of which waited for: 8 -> 11; matrix products, arithmetic and copies ran while one was open for 0% -> 0% of each run, Pallas kernels for 39% -> 31%
where the time goes in v7:
time: 90.5 us; the launch traced here: 90.3 us
  Pallas kernels  36.8 us (41%)
  starting transfers between devices  30 us (33%)
  waiting for transfers between devices  21.6 us (24%)
  between operations  1.79 us (2%)
    ppermute x27, starting transfers between devices, swap(): return lax.ppermute(value, axes, [(i, i ^ k) for i in range(n)])  30 us
    ppermute x27, waiting for transfers between devices, swap(): return lax.ppermute(value, axes, [(i, i ^ k) for i in range(n)])  21.6 us
    pallas_call x4, Pallas kernels, project(): pl.pallas_call(functools.partial(project_kernel, n_head, part, following,...  10.4 us
    pallas_call x1, Pallas kernels, inverse_factor(): pl.pallas_call(functools.partial(cholesky_kernel, len(parts)), in_specs=[...  9.71 us
    pallas_call x2, Pallas kernels, attention(): pl.pallas_call(functools.partial(attention_kernel, n_fsdp, heads, last),...  6.47 us
    pallas_call x1, Pallas kernels, final_update(): pl.pallas_call(functools.partial(update_kernel, gain, n_resp, n_head, len...  3.6 us
    pallas_call x1, Pallas kernels, new_momentum(): pl.pallas_call(functools.partial(momentum_kernel, n_resp, n_head, len(tot...  2.32 us
  transfers between devices with their start and end apart: 27, of which 11 were waited for; matrix products, arithmetic and copies ran while one was open for 0% of the time, Pallas kernels for 31%

profile of v7, /device:TPU:0, one launch (start us, length us, event | category | flops | bytes accessed | tf_op | source)
XLA Modules:
  0.0 90.3 jit_solution(221129321041459884)
XLA Ops:
  0.7 3.8 %project.4 = (bf16[512,256]{1,0:T(8,128)(2,1)S(1)}, f32[512,512]{1,0:T(8,128)S(1)}, bf16[512,256]{1,0:T(8,128)(2,1)S(1)}, bf16[512,256]{1,0:T(8,128)(2,1)S(1)}, ...) custom-call(s32[3]{0:T(128)S(1)} %pad_add_fusion.ranks, f32[2048,512]{1,0:T(8,128)} %mom.7, bf16[2048,512]{1,0:T(8,128)(2,1)} %grad.7, ...), custom_call_target="tpu_custom_call" | custom-call | flops 1 | bytes 1 | tf_op jit(solution)/shard_map/project/pallas_call | solution.py:154
  4.5 3.0 %collective-permute-start = (bf16[512,256]{1,0:T(8,128)(2,1)S(1)}, bf16[512,256]{1,0:T(8,128)(2,1)S(1)}, u32[]{:S(2)}, u32[]{:S(2)}) collective-permute-start(bf16[512,256]{1,0:T(8,128)(2,1)S(1)} %get-tuple-element.64), channel_id=1, source_target_pairs={{0,16},{16,0},{1,17},{17,1},{2,18},{18,2},{3,19},{19,3},{4,20},{20... | collective-permute-start | bytes 786440 | tf_op jit(solution)/shard_map/ppermute | solution.py:32
  7.5 2.6 %project.5 = (f32[512,256]{1,0:T(8,128)S(1)}, f32[512,512]{1,0:T(8,128)S(1)}, f32[512,512]{1,0:T(8,128)S(1)}, bf16[512,512]{1,0:T(8,128)(2,1)S(1)}) custom-call(s32[3]{0:T(128)S(1)} %pad_add_fusion.ranks, f32[2048,512]{1,0:T(8,128)} %mom.7, bf16[2048,512]{1,0:T(8,128)(2,1)} %grad.7, bf16[512,256]{1,0:T(8,128)(2,1)S(1)} %get-tuple-element.55.refs_0_, ...), custom_call_target="tpu_custom_call" | custom-call | flops 10000000000 | bytes 1 | tf_op jit(solution)/shard_map/project/pallas_call | solution.py:154
  10.1 2.6 %project.6 = (bf16[512,256]{1,0:T(8,128)(2,1)S(1)}, f32[512,512]{1,0:T(8,128)S(1)}, f32[512,512]{1,0:T(8,128)S(1)}, bf16[512,512]{1,0:T(8,128)(2,1)S(1)}) custom-call(s32[3]{0:T(128)S(1)} %pad_add_fusion.ranks, f32[2048,512]{1,0:T(8,128)} %mom.7, bf16[2048,512]{1,0:T(8,128)(2,1)} %grad.7, bf16[512,256]{1,0:T(8,128)(2,1)S(1)} %get-tuple-element.55.refs_0_, ...), custom_call_target="tpu_custom_call" | custom-call | flops 1 | bytes 1 | tf_op jit(solution)/shard_map/project/pallas_call | solution.py:154
  13.9 3.9 %collective-permute-start.3 = (bf16[256,256]{1,0:T(8,128)(2,1)S(1)}, bf16[256,256]{1,0:T(8,128)(2,1)S(1)}, u32[]{:S(2)}, u32[]{:S(2)}) collective-permute-start(bf16[256,256]{1,0:T(8,128)(2,1)S(1)} %get-tuple-element.69), channel_id=1, source_target_pairs={{0,3},{1,2},{2,1},{3,0},{4,7},{5,6},{6,5},{7,4},{8,11},{9,10},{10,... | collective-permute-start | bytes 393224 | tf_op jit(solution)/shard_map/ppermute | solution.py:32
  17.8 1.6 %collective-permute-start.5 = (bf16[2,2,64,128]{3,2,1,0:T(8,128)(2,1)S(1)}, bf16[2,2,64,128]{3,2,1,0:T(8,128)(2,1)S(1)}, u32[]{:S(2)}, u32[]{:S(2)}) collective-permute-start(bf16[2,2,64,128]{3,2,1,0:T(8,128)(2,1)S(1)} %pack_prompts.1.refs_0_), channel_id=1, source_target_pairs={{0,16},{16,0},{1,17},{17,1},{2,18},{18,2},{3,19},{19,3},{4,20},{20... | collective-permute-start | bytes 196616 | tf_op jit(solution)/shard_map/ppermute | solution.py:32
  21.3 1.6 %collective-permute-start.4 = (bf16[256,256]{1,0:T(8,128)(2,1)S(1)}, bf16[256,256]{1,0:T(8,128)(2,1)S(1)}, u32[]{:S(2)}, u32[]{:S(2)}) collective-permute-start(bf16[256,256]{1,0:T(8,128)(2,1)S(1)} %get-tuple-element.70.refs_2_), channel_id=1, source_target_pairs={{0,1},{1,0},{2,3},{3,2},{4,5},{5,4},{6,7},{7,6},{8,9},{9,8},{10,11... | collective-permute-start | bytes 393224 | tf_op jit(solution)/shard_map/ppermute | solution.py:32
  23.9 1.6 %collective-permute-start.7 = (bf16[2,64,128]{2,1,0:T(8,128)(2,1)S(1)}, bf16[2,64,128]{2,1,0:T(8,128)(2,1)S(1)}, u32[]{:S(2)}, u32[]{:S(2)}) collective-permute-start(bf16[2,64,128]{2,1,0:T(8,128)(2,1)S(1)} %get-tuple-element.72), channel_id=1, source_target_pairs={{0,8},{4,12},{8,0},{12,4},{1,9},{5,13},{9,1},{13,5},{2,10},{6,14},... | collective-permute-start | bytes 98312 | tf_op jit(solution)/shard_map/ppermute | solution.py:32
  25.8 2.3 %collective-permute-done.2.refs_1_ = bf16[256,256]{1,0:T(8,128)(2,1)S(1)} collective-permute-done((bf16[256,256]{1,0:T(8,128)(2,1)S(1)}, bf16[256,256]{1,0:T(8,128)(2,1)S(1)}, u32[]{:S(2)}, u32[]{:S(2)}) %collective-permute-start.2) | collective-permute-done | bytes 131104 | tf_op jit(solution)/shard_map/ppermute | solution.py:32
  28.9 1.6 %collective-permute-start.9 = (bf16[256,256]{1,0:T(8,128)(2,1)S(1)}, bf16[256,256]{1,0:T(8,128)(2,1)S(1)}, u32[]{:S(2)}, u32[]{:S(2)}) collective-permute-start(bf16[256,256]{1,0:T(8,128)(2,1)S(1)} %sum_parts.7.refs_0_), channel_id=1, source_target_pairs={{0,1},{1,0},{2,3},{3,2},{4,5},{5,4},{6,7},{7,6},{8,9},{9,8},{10,11... | collective-permute-start | bytes 393224 | tf_op jit(solution)/shard_map/ppermute | solution.py:32
  30.5 1.5 %collective-permute-start.12 = (bf16[256,256]{1,0:T(8,128)(2,1)S(1)}, bf16[256,256]{1,0:T(8,128)(2,1)S(1)}, u32[]{:S(2)}, u32[]{:S(2)}) collective-permute-start(bf16[256,256]{1,0:T(8,128)(2,1)S(1)} %sum_parts.7.refs_0_), channel_id=1, source_target_pairs={{0,16},{16,0},{1,17},{17,1},{2,18},{18,2},{3,19},{19,3},{4,20},{20... | collective-permute-start | bytes 393224 | tf_op jit(solution)/shard_map/ppermute | solution.py:32
  32.0 2.9 %collective-permute-start.11 = (bf16[256,256]{1,0:T(8,128)(2,1)S(1)}, bf16[256,256]{1,0:T(8,128)(2,1)S(1)}, u32[]{:S(2)}, u32[]{:S(2)}) collective-permute-start(bf16[256,256]{1,0:T(8,128)(2,1)S(1)} %sum_parts.7.refs_0_), channel_id=1, source_target_pairs={{0,3},{1,2},{2,1},{3,0},{4,7},{5,6},{6,5},{7,4},{8,11},{9,10},{10,... | collective-permute-start | bytes 393224 | tf_op jit(solution)/shard_map/ppermute | solution.py:32
  36.5 3.3 %attention.2 = (bf16[256,512]{1,0:T(8,128)(2,1)S(1)}, f32[512,128]{1,0:T(8,128)S(1)}, f32[512,128]{1,0:T(8,128)S(1)}) custom-call(s32[3]{0:T(128)S(1)} %pad_add_fusion.ranks, s32[4]{0:T(128)S(1)} %copy-done.6, s32[4]{0:T(128)S(1)} %copy-done.7, s32[1]{0:T(128)S(6)} %copy.21.resp_blocks, bf16[256,1024]{1,0:T(8,128)(2,1)S(1)} %copy-done, ...), custom_call_target="tpu_custom_call" | custom-call | flops 1 | bytes 1 | tf_op jit(solution)/shard_map/attention/pallas_call | solution.py:745
  40.3 5.1 %collective-permute-done.10.refs_0_.refs_2_ = bf16[256,256]{1,0:T(8,128)(2,1)S(1)} collective-permute-done((bf16[256,256]{1,0:T(8,128)(2,1)S(1)}, bf16[256,256]{1,0:T(8,128)(2,1)S(1)}, u32[]{:S(2)}, u32[]{:S(2)}) %collective-permute-start.10) | collective-permute-done | bytes 131104 | tf_op jit(solution)/shard_map/ppermute | solution.py:32
  46.2 3.2 %attention.3 = (bf16[256,512]{1,0:T(8,128)(2,1)S(1)}, bf16[2,256,128]{2,1,0:T(8,128)(2,1)S(1)}, f32[2,64,128]{2,1,0:T(8,128)S(1)}, bf16[2,64,128]{2,1,0:T(8,128)...) custom-call(s32[3]{0:T(128)S(1)} %pad_add_fusion.ranks, s32[4]{0:T(128)S(1)} %copy-done.6, ...), custom_call_target="tpu_custom_call" | custom-call | flops 1 | bytes 1 | tf_op jit(solution)/shard_map/attention/pallas_call | solution.py:745
  49.5 4.2 %collective-permute-done.14.refs_6_ = bf16[512,256]{1,0:T(8,128)(2,1)S(1)} collective-permute-done((bf16[512,256]{1,0:T(8,128)(2,1)S(1)}, bf16[512,256]{1,0:T(8,128)(2,1)S(1)}, u32[]{:S(2)}, u32[]{:S(2)}) %collective-permute-start.14) | collective-permute-done | bytes 262176 | tf_op jit(solution)/shard_map/ppermute | solution.py:32
  60.3 3.7 %collective-permute-done.16.refs_1_ = f32[384,128]{1,0:T(8,128)S(1)} collective-permute-done((f32[384,128]{1,0:T(8,128)S(1)}, f32[384,128]{1,0:T(8,128)S(1)}, u32[]{:S(2)}, u32[]{:S(2)}) %collective-permute-start.16) | collective-permute-done | bytes 196640 | tf_op jit(solution)/shard_map/ppermute | solution.py:32
  64.0 9.7 %inverse_factor.1.x = f32[256,256]{1,0:T(8,128)S(1)} custom-call(f32[384,128]{1,0:T(8,128)S(1)} %sum_parts.8.refs_0_.refs_2_, f32[384,128]{1,0:T(8,128)S(1)} %collective-permute-done.16.refs_1_), custom_call_target="tpu_custom_call" | custom-call | flops 2000000000 | bytes 1 | tf_op jit(solution)/shard_map/inverse_factor/pallas_call | solution.py:421
  74.4 1.8 %collective-permute-start.24 = (f32[8,256]{1,0:T(8,128)S(1)}, f32[8,256]{1,0:T(8,128)S(1)}, u32[]{:S(2)}, u32[]{:S(2)}) collective-permute-start(f32[8,256]{1,0:T(8,128)S(1)} %get-tuple-element.92.refs_5_.refs_0_), channel_id=1, source_target_pairs={{0,3},{1,2},{2,1},{3,0},{4,7},{5,6},{6,5},{7,4},{8,11},{9,10},{10,... | collective-permute-start | bytes 24584 | tf_op jit(solution)/shard_map/ppermute | solution.py:32
  76.2 2.7 %collective-permute-start.22 = (f32[8,256]{1,0:T(8,128)S(1)}, f32[8,256]{1,0:T(8,128)S(1)}, u32[]{:S(2)}, u32[]{:S(2)}) collective-permute-start(f32[8,256]{1,0:T(8,128)S(1)} %get-tuple-element.92.refs_5_.refs_0_), channel_id=1, source_target_pairs={{0,1},{1,0},{2,3},{3,2},{4,5},{5,4},{6,7},{7,6},{8,9},{9,8},{10,11... | collective-permute-start | bytes 24584 | tf_op jit(solution)/shard_map/ppermute | solution.py:32
  78.8 2.3 %new_momentum.1 = (f32[2048,512]{1,0:T(8,128)}, bf16[256,1024]{1,0:T(8,128)(2,1)}, bf16[2,256,128]{2,1,0:T(8,128)(2,1)}, f32[8,128]{1,0:T(8,128)S(1)}) custom-call(s32[3]{0:T(128)S(1)} %pad_add_fusion.ranks, bf16[2048,256]{1,0:T(8,128)(2,1)S(1)} %get-tuple-element.78.pcat, bf16[256,512]{1,0:T(8,128)(2,1)S(1)} %get-tuple-element.88.y, ...), custom_call_target="tpu_custom_call" | custom-call | flops 5000000000 | bytes 1 | tf_op jit(solution)/shard_map/new_momentum/pallas_call | solution.py:518
  82.2 1.8 %collective-permute-start.26 = (bf16[2,2,64,128]{3,2,1,0:T(8,128)(2,1)S(1)}, bf16[2,2,64,128]{3,2,1,0:T(8,128)(2,1)S(1)}, u32[]{:S(2)}, u32[]{:S(2)}) collective-permute-start(bf16[2,2,64,128]{3,2,1,0:T(8,128)(2,1)S(1)} %get-tuple-element.98), channel_id=1, source_target_pairs={{0,16},{16,0},{1,17},{17,1},{2,18},{18,2},{3,19},{19,3},{4,20},{20... | collective-permute-start | bytes 196616 | tf_op jit(solution)/shard_map/ppermute | solution.py:32
  84.9 1.6 %collective-permute-done.26.refs_4_ = bf16[2,2,64,128]{3,2,1,0:T(8,128)(2,1)S(1)} collective-permute-done((bf16[2,2,64,128]{3,2,1,0:T(8,128)(2,1)S(1)}, bf16[2,2,64,128]{3,2,1,0:T(8,128)(2,1)S(1)}, u32[]{:S(2)}, u32[]{:S(2)}) %collective-permute-start.26) | collective-permute-done | bytes 65568 | tf_op jit(solution)/shard_map/ppermute | solution.py:32
  86.5 3.6 %final_update.1 = (bf16[2048,512]{1,0:T(8,128)(2,1)}, f32[512,256]{1,0:T(8,128)}, f32[2048,512]{1,0:T(8,128)}, f32[2,2,64,128]{3,2,1,0:T(8,128)}) custom-call(s32[3]{0:T(128)S(1)} %pad_add_fusion.ranks, bf16[2048,256]{1,0:T(8,128)(2,1)S(1)} %get-tuple-element.78.pcat, f32[256,256]{1,0:T(8,128)S(1)} %inverse_factor.1.x, ...), custom_call_target="tpu_custom_call", output_to_operand_aliasing={{2}: (10, {})} | custom-call | flops 5000000000 | bytes 1 | tf_op jit(solution)/shard_map/final_update/pallas_call | solution.py:581
  (73 shorter events, 16.6 us)
Async XLA Ops:
  4.5 9.3 %collective-permute-start = (bf16[512,256]{1,0:T(8,128)(2,1)S(1)}, bf16[512,256]{1,0:T(8,128)(2,1)S(1)}, u32[]{:S(2)}, u32[]{:S(2)}) collective-permute-start(bf16[512,256]{1,0:T(8,128)(2,1)S(1)} %get-tuple-element.64), channel_id=1, source_target_pairs={{0,16},{16,0},{1,17},{17,1},{2,18},{18,2},{3,19},{19,3},{4,20},{20... | collective-permute-start | bytes 786440 | tf_op jit(solution)/shard_map/ppermute | solution.py:32
  12.7 8.5 %collective-permute-start.1 = (bf16[512,256]{1,0:T(8,128)(2,1)S(1)}, bf16[512,256]{1,0:T(8,128)(2,1)S(1)}, u32[]{:S(2)}, u32[]{:S(2)}) collective-permute-start(bf16[512,256]{1,0:T(8,128)(2,1)S(1)} %get-tuple-element.67.refs_2_), channel_id=1, source_target_pairs={{0,16},{16,0},{1,17},{17,1},{2,18},{18,2},{3,19},{19,3},{4,20},{20... | collective-permute-start | bytes 786440 | tf_op jit(solution)/shard_map/ppermute | solution.py:32
  13.9 11.6 %collective-permute-start.3 = (bf16[256,256]{1,0:T(8,128)(2,1)S(1)}, bf16[256,256]{1,0:T(8,128)(2,1)S(1)}, u32[]{:S(2)}, u32[]{:S(2)}) collective-permute-start(bf16[256,256]{1,0:T(8,128)(2,1)S(1)} %get-tuple-element.69), channel_id=1, source_target_pairs={{0,3},{1,2},{2,1},{3,0},{4,7},{5,6},{6,5},{7,4},{8,11},{9,10},{10,... | collective-permute-start | bytes 393224 | tf_op jit(solution)/shard_map/ppermute | solution.py:32
  17.8 10.3 %collective-permute-start.2 = (bf16[256,256]{1,0:T(8,128)(2,1)S(1)}, bf16[256,256]{1,0:T(8,128)(2,1)S(1)}, u32[]{:S(2)}, u32[]{:S(2)}) collective-permute-start(bf16[256,256]{1,0:T(8,128)(2,1)S(1)} %get-tuple-element.65.refs_4_), channel_id=1, source_target_pairs={{0,2},{1,3},{2,0},{3,1},{4,6},{5,7},{6,4},{7,5},{8,10},{9,11},{10,... | collective-permute-start | bytes 393224 | tf_op jit(solution)/shard_map/ppermute | solution.py:32
  17.8 5.1 %collective-permute-start.5 = (bf16[2,2,64,128]{3,2,1,0:T(8,128)(2,1)S(1)}, bf16[2,2,64,128]{3,2,1,0:T(8,128)(2,1)S(1)}, u32[]{:S(2)}, u32[]{:S(2)}) collective-permute-start(bf16[2,2,64,128]{3,2,1,0:T(8,128)(2,1)S(1)} %pack_prompts.1.refs_0_), channel_id=1, source_target_pairs={{0,16},{16,0},{1,17},{17,1},{2,18},{18,2},{3,19},{19,3},{4,20},{20... | collective-permute-start | bytes 196616 | tf_op jit(solution)/shard_map/ppermute | solution.py:32
  21.3 7.5 %collective-permute-start.4 = (bf16[256,256]{1,0:T(8,128)(2,1)S(1)}, bf16[256,256]{1,0:T(8,128)(2,1)S(1)}, u32[]{:S(2)}, u32[]{:S(2)}) collective-permute-start(bf16[256,256]{1,0:T(8,128)(2,1)S(1)} %get-tuple-element.70.refs_2_), channel_id=1, source_target_pairs={{0,1},{1,0},{2,3},{3,2},{4,5},{5,4},{6,7},{7,6},{8,9},{9,8},{10,11... | collective-permute-start | bytes 393224 | tf_op jit(solution)/shard_map/ppermute | solution.py:32
  23.9 4.3 %collective-permute-start.6 = (bf16[2,64,128]{2,1,0:T(8,128)(2,1)S(1)}, bf16[2,64,128]{2,1,0:T(8,128)(2,1)S(1)}, u32[]{:S(2)}, u32[]{:S(2)}) collective-permute-start(bf16[2,64,128]{2,1,0:T(8,128)(2,1)S(1)} %get-tuple-element.71), channel_id=1, source_target_pairs={{0,4},{4,0},{8,12},{12,8},{1,5},{5,1},{9,13},{13,9},{2,6},{6,2},{1... | collective-permute-start | bytes 98312 | tf_op jit(solution)/shard_map/ppermute | solution.py:32
  23.9 4.3 %collective-permute-start.7 = (bf16[2,64,128]{2,1,0:T(8,128)(2,1)S(1)}, bf16[2,64,128]{2,1,0:T(8,128)(2,1)S(1)}, u32[]{:S(2)}, u32[]{:S(2)}) collective-permute-start(bf16[2,64,128]{2,1,0:T(8,128)(2,1)S(1)} %get-tuple-element.72), channel_id=1, source_target_pairs={{0,8},{4,12},{8,0},{12,4},{1,9},{5,13},{9,1},{13,5},{2,10},{6,14},... | collective-permute-start | bytes 98312 | tf_op jit(solution)/shard_map/ppermute | solution.py:32
  28.9 6.0 %collective-permute-start.9 = (bf16[256,256]{1,0:T(8,128)(2,1)S(1)}, bf16[256,256]{1,0:T(8,128)(2,1)S(1)}, u32[]{:S(2)}, u32[]{:S(2)}) collective-permute-start(bf16[256,256]{1,0:T(8,128)(2,1)S(1)} %sum_parts.7.refs_0_), channel_id=1, source_target_pairs={{0,1},{1,0},{2,3},{3,2},{4,5},{5,4},{6,7},{7,6},{8,9},{9,8},{10,11... | collective-permute-start | bytes 393224 | tf_op jit(solution)/shard_map/ppermute | solution.py:32
  30.5 9.2 %collective-permute-start.12 = (bf16[256,256]{1,0:T(8,128)(2,1)S(1)}, bf16[256,256]{1,0:T(8,128)(2,1)S(1)}, u32[]{:S(2)}, u32[]{:S(2)}) collective-permute-start(bf16[256,256]{1,0:T(8,128)(2,1)S(1)} %sum_parts.7.refs_0_), channel_id=1, source_target_pairs={{0,16},{16,0},{1,17},{17,1},{2,18},{18,2},{3,19},{19,3},{4,20},{20... | collective-permute-start | bytes 393224 | tf_op jit(solution)/shard_map/ppermute | solution.py:32
  32.0 8.3 %collective-permute-start.11 = (bf16[256,256]{1,0:T(8,128)(2,1)S(1)}, bf16[256,256]{1,0:T(8,128)(2,1)S(1)}, u32[]{:S(2)}, u32[]{:S(2)}) collective-permute-start(bf16[256,256]{1,0:T(8,128)(2,1)S(1)} %sum_parts.7.refs_0_), channel_id=1, source_target_pairs={{0,3},{1,2},{2,1},{3,0},{4,7},{5,6},{6,5},{7,4},{8,11},{9,10},{10,... | collective-permute-start | bytes 393224 | tf_op jit(solution)/shard_map/ppermute | solution.py:32
  34.8 10.5 %collective-permute-start.10 = (bf16[256,256]{1,0:T(8,128)(2,1)S(1)}, bf16[256,256]{1,0:T(8,128)(2,1)S(1)}, u32[]{:S(2)}, u32[]{:S(2)}) collective-permute-start(bf16[256,256]{1,0:T(8,128)(2,1)S(1)} %sum_parts.7.refs_0_), channel_id=1, source_target_pairs={{0,2},{1,3},{2,0},{3,1},{4,6},{5,7},{6,4},{7,5},{8,10},{9,11},{10,... | collective-permute-start | bytes 393224 | tf_op jit(solution)/shard_map/ppermute | solution.py:32
  34.9 10.5 %collective-permute-start.13 = (bf16[256,256]{1,0:T(8,128)(2,1)S(1)}, bf16[256,256]{1,0:T(8,128)(2,1)S(1)}, u32[]{:S(2)}, u32[]{:S(2)}) collective-permute-start(bf16[256,256]{1,0:T(8,128)(2,1)S(1)} %collective-permute-done.9.refs_4_.refs_1_), channel_id=1, source_target_pairs={{0,16},{16,0},{1,17},{17,1},{2,18},{18,2},{3,19},{19,3},{4,20},{20... | collective-permute-start | bytes 393224 | tf_op jit(solution)/shard_map/ppermute | solution.py:32
  45.4 8.2 %collective-permute-start.14 = (bf16[512,256]{1,0:T(8,128)(2,1)S(1)}, bf16[512,256]{1,0:T(8,128)(2,1)S(1)}, u32[]{:S(2)}, u32[]{:S(2)}) collective-permute-start(bf16[512,256]{1,0:T(8,128)(2,1)S(1)} %relay.1.refs_6_), channel_id=1, source_target_pairs={{0,16},{16,0},{1,17},{17,1},{2,18},{18,2},{3,19},{19,3},{4,20},{20... | collective-permute-start | bytes 786440 | tf_op jit(solution)/shard_map/ppermute | solution.py:32
  56.2 7.8 %collective-permute-start.16 = (f32[384,128]{1,0:T(8,128)S(1)}, f32[384,128]{1,0:T(8,128)S(1)}, u32[]{:S(2)}, u32[]{:S(2)}) collective-permute-start(f32[384,128]{1,0:T(8,128)S(1)} %sum_parts.8.refs_0_.refs_2_), channel_id=1, source_target_pairs={{0,8},{4,12},{8,0},{12,4},{1,9},{5,13},{9,1},{13,5},{2,10},{6,14},... | collective-permute-start | bytes 589832 | tf_op jit(solution)/shard_map/ppermute | solution.py:32
  57.4 16.4 %collective-permute-start.18 = (bf16[256,512]{1,0:T(8,128)(2,1)S(1)}, bf16[256,512]{1,0:T(8,128)(2,1)S(1)}, u32[]{:S(2)}, u32[]{:S(2)}) collective-permute-start(bf16[256,512]{1,0:T(8,128)(2,1)S(1)} %sum_parts.9.wa), channel_id=1, source_target_pairs={{0,8},{4,12},{8,0},{12,4},{1,9},{5,13},{9,1},{13,5},{2,10},{6,14},... | collective-permute-start | bytes 786440 | tf_op jit(solution)/shard_map/ppermute | solution.py:32
  58.4 15.3 %collective-permute-start.19 = (bf16[2,64,128]{2,1,0:T(8,128)(2,1)S(1)}, bf16[2,64,128]{2,1,0:T(8,128)(2,1)S(1)}, u32[]{:S(2)}, u32[]{:S(2)}) collective-permute-start(bf16[2,64,128]{2,1,0:T(8,128)(2,1)S(1)} %get-tuple-element.85), channel_id=1, source_target_pairs={{0,4},{4,0},{8,12},{12,8},{1,5},{5,1},{9,13},{13,9},{2,6},{6,2},{1... | collective-permute-start | bytes 98312 | tf_op jit(solution)/shard_map/ppermute | solution.py:32
  58.4 15.3 %collective-permute-start.20 = (bf16[2,64,128]{2,1,0:T(8,128)(2,1)S(1)}, bf16[2,64,128]{2,1,0:T(8,128)(2,1)S(1)}, u32[]{:S(2)}, u32[]{:S(2)}) collective-permute-start(bf16[2,64,128]{2,1,0:T(8,128)(2,1)S(1)} %get-tuple-element.86), channel_id=1, source_target_pairs={{0,8},{4,12},{8,0},{12,4},{1,9},{5,13},{9,1},{13,5},{2,10},{6,14},... | collective-permute-start | bytes 98312 | tf_op jit(solution)/shard_map/ppermute | solution.py:32
  59.6 14.2 %collective-permute-start.21 = (bf16[2,64,128]{2,1,0:T(8,128)(2,1)S(1)}, bf16[2,64,128]{2,1,0:T(8,128)(2,1)S(1)}, u32[]{:S(2)}, u32[]{:S(2)}) collective-permute-start(bf16[2,64,128]{2,1,0:T(8,128)(2,1)S(1)} %get-tuple-element.87), channel_id=1, source_target_pairs={{0,12},{4,8},{8,4},{12,0},{1,13},{5,9},{9,5},{13,1},{2,14},{6,10},... | collective-permute-start | bytes 98312 | tf_op jit(solution)/shard_map/ppermute | solution.py:32
  74.4 6.8 %collective-permute-start.24 = (f32[8,256]{1,0:T(8,128)S(1)}, f32[8,256]{1,0:T(8,128)S(1)}, u32[]{:S(2)}, u32[]{:S(2)}) collective-permute-start(f32[8,256]{1,0:T(8,128)S(1)} %get-tuple-element.92.refs_5_.refs_0_), channel_id=1, source_target_pairs={{0,3},{1,2},{2,1},{3,0},{4,7},{5,6},{6,5},{7,4},{8,11},{9,10},{10,... | collective-permute-start | bytes 24584 | tf_op jit(solution)/shard_map/ppermute | solution.py:32
  76.2 5.0 %collective-permute-start.23 = (f32[8,256]{1,0:T(8,128)S(1)}, f32[8,256]{1,0:T(8,128)S(1)}, u32[]{:S(2)}, u32[]{:S(2)}) collective-permute-start(f32[8,256]{1,0:T(8,128)S(1)} %get-tuple-element.92.refs_5_.refs_0_), channel_id=1, source_target_pairs={{0,2},{1,3},{2,0},{3,1},{4,6},{5,7},{6,4},{7,5},{8,10},{9,11},{10,... | collective-permute-start | bytes 24584 | tf_op jit(solution)/shard_map/ppermute | solution.py:32
  76.2 5.0 %collective-permute-start.22 = (f32[8,256]{1,0:T(8,128)S(1)}, f32[8,256]{1,0:T(8,128)S(1)}, u32[]{:S(2)}, u32[]{:S(2)}) collective-permute-start(f32[8,256]{1,0:T(8,128)S(1)} %get-tuple-element.92.refs_5_.refs_0_), channel_id=1, source_target_pairs={{0,1},{1,0},{2,3},{3,2},{4,5},{5,4},{6,7},{7,6},{8,9},{9,8},{10,11... | collective-permute-start | bytes 24584 | tf_op jit(solution)/shard_map/ppermute | solution.py:32
  81.2 3.7 %collective-permute-start.25 = (f32[8,256]{1,0:T(8,128)S(1)}, f32[8,256]{1,0:T(8,128)S(1)}, u32[]{:S(2)}, u32[]{:S(2)}) collective-permute-start(f32[8,256]{1,0:T(8,128)S(1)} %sum_parts.10.refs_0_.refs_4_), channel_id=1, source_target_pairs={{0,16},{16,0},{1,17},{17,1},{2,18},{18,2},{3,19},{19,3},{4,20},{20... | collective-permute-start | bytes 24584 | tf_op jit(solution)/shard_map/ppermute | solution.py:32
  82.2 4.3 %collective-permute-start.26 = (bf16[2,2,64,128]{3,2,1,0:T(8,128)(2,1)S(1)}, bf16[2,2,64,128]{3,2,1,0:T(8,128)(2,1)S(1)}, u32[]{:S(2)}, u32[]{:S(2)}) collective-permute-start(bf16[2,2,64,128]{3,2,1,0:T(8,128)(2,1)S(1)} %get-tuple-element.98), channel_id=1, source_target_pairs={{0,16},{16,0},{1,17},{17,1},{2,18},{18,2},{3,19},{19,3},{4,20},{20... | collective-permute-start | bytes 196616 | tf_op jit(solution)/shard_map/ppermute | solution.py:32
  (12 other events, 71.1 us)

commit v8 on v7

--- a/solution.py
+++ b/solution.py
@@ -853,23 +853,26 @@
     )
 
     along = {0: piece0}
-    for k in far_first:
+    for k in range(1, later):
         along[k] = swap(piece0, "head", k)
+    held_back = relay([piece0], (along[max(1, later) - 1],))
+    for k in range(later, n_head):
+        along[k] = swap(held_back if k > later else piece0, "head", k)
+
     n_q = queries.shape[1] // HD
     heads = [list(range(n_q // 2)), list(range(n_q // 2, n_q))]
     held = (
         ranks, counts, prompt_blocks, resp_blocks, queries, self_keys, self_values, d_out, pieces
     )
-    earlier = attention(heads[0], None, *held, (along[1 % n_head],))
-    near = [along[k] for k in range(later)]
-    passed = [[swap(c, "resp", j) for c in near] for j in range(1, n_resp)]
-    far = relay(
-        [along[k] for k in range(later, n_head)], (earlier[1], *[c for row in passed for c in row])
-    )
-    chunks = near + [along[k] for k in range(later, n_head)]
+    early = [along[k] for k in range(n_head - 1)]
+    last = along[n_head - 1]
+    earlier = attention(heads[0], None, *held, (early[-1],))
+    passed = [[swap(c, "resp", j) for c in early] for j in range(1, n_resp)]
+    sent_last = relay([last], (earlier[1], *[c for row in passed for c in row]))
+    chunks = early + [last]
     for j in range(1, n_resp):
-        chunks += passed[j - 1] + [swap(far, "resp", j)]
-    dq_parts, resp_grad, *parts = attention(heads[1], earlier, *held, (far,))
+        chunks += passed[j - 1] + [swap(sent_last, "resp", j)]
+    dq_parts, resp_grad, *parts = attention(heads[1], earlier, *held, (sent_last,))
     dq_parts = (earlier[0], dq_parts)
     pcat, pcat_t, gram = gather_gram(chunks, (parts[0],))
 
@@ -885,15 +888,15 @@
     bt, y, squares = back_full(x, w, w_other, tuple(returned[1:]))
     from_head = [swap(squares, "head", k) for k in range(1, n_head)]
     half = len(totals) // 2
+    slots = sum_by_slot(ranks, counts, owner_slot, returned, n_resp, (squares,))
+    prompts = [slots[0]] + [swap(slots[j], "resp", j) for j in range(1, n_resp)]
     momentum_out, dq, resp_grad, token = new_momentum(
-        ranks, pcat, totals[:half], y, n_resp, n_head, dq_parts, resp_grad, (squares,)
+        ranks, pcat, totals[:half], y, n_resp, n_head, dq_parts, resp_grad, (squares, slots[-1])
     )
     squares = sum_parts([squares] + from_head, F32, (token,))
     sums = sum_parts(
-        [squares] + [swap(squares, "resp", j) for j in range(1, n_resp)], F32, (), 5
-    )
-    slots = sum_by_slot(ranks, counts, owner_slot, returned, n_resp, (squares,))
-    prompts = [slots[0]] + [swap(slots[j], "resp", j) for j in range(1, n_resp)]
+        [squares] + [swap(squares, "resp", j) for j in range(1, n_resp)], F32
+    )
     update, basis_out, momentum_out, prompt_grad = final_update(
         ranks, pcat, x, bt, y, [sums], totals[half:], prompts, momentum_out, gain, n_resp, n_head
     )

time: 90.5 us -> 89 us (0.983)
  waiting for transfers between devices: 21.6 us -> 16.4 us
  starting transfers between devices: 30 us -> 33.7 us
    ppermute x27 -> x28, waiting for transfers between devices: 21.6 us -> 16.4 us  [swap(): return lax.ppermute(value, axes, [(i, i ^ k) for i in range(n)])]
    ppermute x27 -> x28, starting transfers between devices: 30 us -> 33.7 us  [swap(): return lax.ppermute(value, axes, [(i, i ^ k) for i in range(n)])]
  transfers between devices with their start and end apart: 27 -> 28, of which waited for: 11 -> 8; matrix products, arithmetic and copies ran while one was open for 0% -> 0% of each run, Pallas kernels for 31% -> 32%
where the time goes in v8:
time: 89 us; the launch traced here: 88.8 us
  Pallas kernels  36.8 us (41%)
  starting transfers between devices  33.7 us (38%)
  waiting for transfers between devices  16.4 us (18%)
  between operations  1.79 us (2%)
    ppermute x28, starting transfers between devices, swap(): return lax.ppermute(value, axes, [(i, i ^ k) for i in range(n)])  33.7 us
    ppermute x28, waiting for transfers between devices, swap(): return lax.ppermute(value, axes, [(i, i ^ k) for i in range(n)])  16.4 us
    pallas_call x4, Pallas kernels, project(): pl.pallas_call(functools.partial(project_kernel, n_head, part, following,...  10.4 us
    pallas_call x1, Pallas kernels, inverse_factor(): pl.pallas_call(functools.partial(cholesky_kernel, len(parts)), in_specs=[...  9.7 us
    pallas_call x2, Pallas kernels, attention(): pl.pallas_call(functools.partial(attention_kernel, n_fsdp, heads, last),...  6.47 us
    pallas_call x1, Pallas kernels, final_update(): pl.pallas_call(functools.partial(update_kernel, gain, n_resp, n_head, len...  3.59 us
    pallas_call x1, Pallas kernels, new_momentum(): pl.pallas_call(functools.partial(momentum_kernel, n_resp, n_head, len(tot...  2.32 us
  transfers between devices with their start and end apart: 28, of which 8 were waited for; matrix products, arithmetic and copies ran while one was open for 0% of the time, Pallas kernels for 32%

profile of v8, /device:TPU:0, one launch (start us, length us, event | category | flops | bytes accessed | tf_op | source)
XLA Modules:
  0.0 88.8 jit_solution(13998946258572042801)
XLA Ops:
  0.7 3.8 %project.4 = (bf16[512,256]{1,0:T(8,128)(2,1)S(1)}, f32[512,512]{1,0:T(8,128)S(1)}, bf16[512,256]{1,0:T(8,128)(2,1)S(1)}, bf16[512,256]{1,0:T(8,128)(2,1)S(1)}, ...) custom-call(s32[3]{0:T(128)S(1)} %pad_add_fusion.ranks, f32[2048,512]{1,0:T(8,128)} %mom.7, bf16[2048,512]{1,0:T(8,128)(2,1)} %grad.7, ...), custom_call_target="tpu_custom_call" | custom-call | flops 1 | bytes 1 | tf_op jit(solution)/shard_map/project/pallas_call | solution.py:154
  4.5 3.0 %collective-permute-start = (bf16[512,256]{1,0:T(8,128)(2,1)S(1)}, bf16[512,256]{1,0:T(8,128)(2,1)S(1)}, u32[]{:S(2)}, u32[]{:S(2)}) collective-permute-start(bf16[512,256]{1,0:T(8,128)(2,1)S(1)} %get-tuple-element.64), channel_id=1, source_target_pairs={{0,16},{16,0},{1,17},{17,1},{2,18},{18,2},{3,19},{19,3},{4,20},{20... | collective-permute-start | bytes 786440 | tf_op jit(solution)/shard_map/ppermute | solution.py:32
  7.5 2.6 %project.5 = (f32[512,256]{1,0:T(8,128)S(1)}, f32[512,512]{1,0:T(8,128)S(1)}, f32[512,512]{1,0:T(8,128)S(1)}, bf16[512,512]{1,0:T(8,128)(2,1)S(1)}) custom-call(s32[3]{0:T(128)S(1)} %pad_add_fusion.ranks, f32[2048,512]{1,0:T(8,128)} %mom.7, bf16[2048,512]{1,0:T(8,128)(2,1)} %grad.7, bf16[512,256]{1,0:T(8,128)(2,1)S(1)} %get-tuple-element.55.refs_0_, ...), custom_call_target="tpu_custom_call" | custom-call | flops 10000000000 | bytes 1 | tf_op jit(solution)/shard_map/project/pallas_call | solution.py:154
  10.1 2.6 %project.6 = (bf16[512,256]{1,0:T(8,128)(2,1)S(1)}, f32[512,512]{1,0:T(8,128)S(1)}, f32[512,512]{1,0:T(8,128)S(1)}, bf16[512,512]{1,0:T(8,128)(2,1)S(1)}) custom-call(s32[3]{0:T(128)S(1)} %pad_add_fusion.ranks, f32[2048,512]{1,0:T(8,128)} %mom.7, bf16[2048,512]{1,0:T(8,128)(2,1)} %grad.7, bf16[512,256]{1,0:T(8,128)(2,1)S(1)} %get-tuple-element.55.refs_0_, ...), custom_call_target="tpu_custom_call" | custom-call | flops 1 | bytes 1 | tf_op jit(solution)/shard_map/project/pallas_call | solution.py:154
  13.9 3.9 %collective-permute-start.3 = (bf16[256,256]{1,0:T(8,128)(2,1)S(1)}, bf16[256,256]{1,0:T(8,128)(2,1)S(1)}, u32[]{:S(2)}, u32[]{:S(2)}) collective-permute-start(bf16[256,256]{1,0:T(8,128)(2,1)S(1)} %get-tuple-element.69), channel_id=1, source_target_pairs={{0,3},{1,2},{2,1},{3,0},{4,7},{5,6},{6,5},{7,4},{8,11},{9,10},{10,... | collective-permute-start | bytes 393224 | tf_op jit(solution)/shard_map/ppermute | solution.py:32
  17.8 1.6 %collective-permute-start.5 = (bf16[2,2,64,128]{3,2,1,0:T(8,128)(2,1)S(1)}, bf16[2,2,64,128]{3,2,1,0:T(8,128)(2,1)S(1)}, u32[]{:S(2)}, u32[]{:S(2)}) collective-permute-start(bf16[2,2,64,128]{3,2,1,0:T(8,128)(2,1)S(1)} %pack_prompts.1.refs_0_), channel_id=1, source_target_pairs={{0,16},{16,0},{1,17},{17,1},{2,18},{18,2},{3,19},{19,3},{4,20},{20... | collective-permute-start | bytes 196616 | tf_op jit(solution)/shard_map/ppermute | solution.py:32
  19.4 1.4 %project.7 = (f32[512,256]{1,0:T(8,128)S(1)}, f32[512,512]{1,0:T(8,128)S(1)}) custom-call(s32[3]{0:T(128)S(1)} %pad_add_fusion.ranks, f32[2048,512]{1,0:T(8,128)} %mom.7, bf16[2048,512]{1,0:T(8,128)(2,1)} %grad.7, bf16[512,256]{1,0:T(8,128)(2,1)S(1)} %get-tuple-element.55.refs_0_, bf16[512,256]{1,0:T(8,128)(2,1)S(1)} %get-tuple-element.56.refs_1_, ...), custom_call_target="tpu_custom_call" | custom-call | flops 1 | bytes 1 | tf_op jit(solution)/shard_map/project/pallas_call | solution.py:154
  21.3 1.6 %collective-permute-start.4 = (bf16[256,256]{1,0:T(8,128)(2,1)S(1)}, bf16[256,256]{1,0:T(8,128)(2,1)S(1)}, u32[]{:S(2)}, u32[]{:S(2)}) collective-permute-start(bf16[256,256]{1,0:T(8,128)(2,1)S(1)} %get-tuple-element.70.refs_2_), channel_id=1, source_target_pairs={{0,1},{1,0},{2,3},{3,2},{4,5},{5,4},{6,7},{7,6},{8,9},{9,8},{10,11... | collective-permute-start | bytes 393224 | tf_op jit(solution)/shard_map/ppermute | solution.py:32
  23.9 1.6 %collective-permute-start.7 = (bf16[2,64,128]{2,1,0:T(8,128)(2,1)S(1)}, bf16[2,64,128]{2,1,0:T(8,128)(2,1)S(1)}, u32[]{:S(2)}, u32[]{:S(2)}) collective-permute-start(bf16[2,64,128]{2,1,0:T(8,128)(2,1)S(1)} %get-tuple-element.72), channel_id=1, source_target_pairs={{0,8},{4,12},{8,0},{12,4},{1,9},{5,13},{9,1},{13,5},{2,10},{6,14},... | collective-permute-start | bytes 98312 | tf_op jit(solution)/shard_map/ppermute | solution.py:32
  25.8 2.3 %collective-permute-done.2.refs_1_ = bf16[256,256]{1,0:T(8,128)(2,1)S(1)} collective-permute-done((bf16[256,256]{1,0:T(8,128)(2,1)S(1)}, bf16[256,256]{1,0:T(8,128)(2,1)S(1)}, u32[]{:S(2)}, u32[]{:S(2)}) %collective-permute-start.2) | collective-permute-done | bytes 131104 | tf_op jit(solution)/shard_map/ppermute | solution.py:32
  28.9 2.8 %collective-permute-start.10 = (bf16[256,256]{1,0:T(8,128)(2,1)S(1)}, bf16[256,256]{1,0:T(8,128)(2,1)S(1)}, u32[]{:S(2)}, u32[]{:S(2)}) collective-permute-start(bf16[256,256]{1,0:T(8,128)(2,1)S(1)} %sum_parts.7.refs_0_), channel_id=1, source_target_pairs={{0,2},{1,3},{2,0},{3,1},{4,6},{5,7},{6,4},{7,5},{8,10},{9,11},{10,... | collective-permute-start | bytes 393224 | tf_op jit(solution)/shard_map/ppermute | solution.py:32
  33.4 5.0 %collective-permute-done.10.refs_4_.refs_2_ = bf16[256,256]{1,0:T(8,128)(2,1)S(1)} collective-permute-done((bf16[256,256]{1,0:T(8,128)(2,1)S(1)}, bf16[256,256]{1,0:T(8,128)(2,1)S(1)}, u32[]{:S(2)}, u32[]{:S(2)}) %collective-permute-start.10) | collective-permute-done | bytes 131104 | tf_op jit(solution)/shard_map/ppermute | solution.py:32
  38.4 1.7 %collective-permute-start.14 = (bf16[256,256]{1,0:T(8,128)(2,1)S(1)}, bf16[256,256]{1,0:T(8,128)(2,1)S(1)}, u32[]{:S(2)}, u32[]{:S(2)}) collective-permute-start(bf16[256,256]{1,0:T(8,128)(2,1)S(1)} %collective-permute-done.10.refs_4_.refs_2_), channel_id=1, source_target_pairs={{0,16},{16,0},{1,17},{17,1},{2,18},{18,2},{3,19},{19,3},{4,20},{20... | collective-permute-start | bytes 393224 | tf_op jit(solution)/shard_map/ppermute | solution.py:32
  40.1 1.3 %collective-permute-start.11 = (bf16[256,256]{1,0:T(8,128)(2,1)S(1)}, bf16[256,256]{1,0:T(8,128)(2,1)S(1)}, u32[]{:S(2)}, u32[]{:S(2)}) collective-permute-start(bf16[256,256]{1,0:T(8,128)(2,1)S(1)} %relay.2), channel_id=1, source_target_pairs={{0,3},{1,2},{2,1},{3,0},{4,7},{5,6},{6,5},{7,4},{8,11},{9,10},{10,... | collective-permute-start | bytes 393224 | tf_op jit(solution)/shard_map/ppermute | solution.py:32
  41.4 1.5 %collective-permute-start.13 = (bf16[256,256]{1,0:T(8,128)(2,1)S(1)}, bf16[256,256]{1,0:T(8,128)(2,1)S(1)}, u32[]{:S(2)}, u32[]{:S(2)}) collective-permute-start(bf16[256,256]{1,0:T(8,128)(2,1)S(1)} %collective-permute-done.9.refs_1_), channel_id=1, source_target_pairs={{0,16},{16,0},{1,17},{17,1},{2,18},{18,2},{3,19},{19,3},{4,20},{20... | collective-permute-start | bytes 393224 | tf_op jit(solution)/shard_map/ppermute | solution.py:32
  43.7 3.3 %attention.2 = (bf16[256,512]{1,0:T(8,128)(2,1)S(1)}, f32[512,128]{1,0:T(8,128)S(1)}, f32[512,128]{1,0:T(8,128)S(1)}) custom-call(s32[3]{0:T(128)S(1)} %pad_add_fusion.ranks, s32[4]{0:T(128)S(1)} %copy-done.6, s32[4]{0:T(128)S(1)} %copy-done.7, s32[1]{0:T(128)S(6)} %copy.21.resp_blocks, bf16[256,1024]{1,0:T(8,128)(2,1)S(1)} %copy-done, ...), custom_call_target="tpu_custom_call" | custom-call | flops 1 | bytes 1 | tf_op jit(solution)/shard_map/attention/pallas_call | solution.py:745
  48.0 3.2 %attention.3 = (bf16[256,512]{1,0:T(8,128)(2,1)S(1)}, bf16[2,256,128]{2,1,0:T(8,128)(2,1)S(1)}, f32[2,64,128]{2,1,0:T(8,128)S(1)}, bf16[2,64,128]{2,1,0:T(8,128)...) custom-call(s32[3]{0:T(128)S(1)} %pad_add_fusion.ranks, s32[4]{0:T(128)S(1)} %copy-done.6, ...), custom_call_target="tpu_custom_call" | custom-call | flops 1 | bytes 1 | tf_op jit(solution)/shard_map/attention/pallas_call | solution.py:745
  58.9 3.5 %collective-permute-done.17.refs_1_ = f32[384,128]{1,0:T(8,128)S(1)} collective-permute-done((f32[384,128]{1,0:T(8,128)S(1)}, f32[384,128]{1,0:T(8,128)S(1)}, u32[]{:S(2)}, u32[]{:S(2)}) %collective-permute-start.17) | collective-permute-done | bytes 196640 | tf_op jit(solution)/shard_map/ppermute | solution.py:32
  62.4 9.7 %inverse_factor.1.x = f32[256,256]{1,0:T(8,128)S(1)} custom-call(f32[384,128]{1,0:T(8,128)S(1)} %sum_parts.8.refs_0_.refs_2_, f32[384,128]{1,0:T(8,128)S(1)} %collective-permute-done.17.refs_1_), custom_call_target="tpu_custom_call" | custom-call | flops 2000000000 | bytes 1 | tf_op jit(solution)/shard_map/inverse_factor/pallas_call | solution.py:421
  72.8 2.0 %collective-permute-start.25 = (f32[8,256]{1,0:T(8,128)S(1)}, f32[8,256]{1,0:T(8,128)S(1)}, u32[]{:S(2)}, u32[]{:S(2)}) collective-permute-start(f32[8,256]{1,0:T(8,128)S(1)} %get-tuple-element.92.refs_4_.refs_5_.refs_0_), channel_id=1, source_target_pairs={{0,3},{1,2},{2,1},{3,0},{4,7},{5,6},{6,5},{7,4},{8,11},{9,10},{10,... | collective-permute-start | bytes 24584 | tf_op jit(solution)/shard_map/ppermute | solution.py:32
  75.2 2.0 %collective-permute-start.23 = (f32[8,256]{1,0:T(8,128)S(1)}, f32[8,256]{1,0:T(8,128)S(1)}, u32[]{:S(2)}, u32[]{:S(2)}) collective-permute-start(f32[8,256]{1,0:T(8,128)S(1)} %get-tuple-element.92.refs_4_.refs_5_.refs_0_), channel_id=1, source_target_pairs={{0,1},{1,0},{2,3},{3,2},{4,5},{5,4},{6,7},{7,6},{8,9},{9,8},{10,11... | collective-permute-start | bytes 24584 | tf_op jit(solution)/shard_map/ppermute | solution.py:32
  78.9 2.3 %new_momentum.1 = (f32[2048,512]{1,0:T(8,128)}, bf16[256,1024]{1,0:T(8,128)(2,1)}, bf16[2,256,128]{2,1,0:T(8,128)(2,1)}, f32[8,128]{1,0:T(8,128)S(1)}) custom-call(s32[3]{0:T(128)S(1)} %pad_add_fusion.ranks, bf16[2048,256]{1,0:T(8,128)(2,1)S(1)} %get-tuple-element.78.pcat, bf16[256,512]{1,0:T(8,128)(2,1)S(1)} %get-tuple-element.88.y, ...), custom_call_target="tpu_custom_call" | custom-call | flops 5000000000 | bytes 1 | tf_op jit(solution)/shard_map/new_momentum/pallas_call | solution.py:518
  82.4 2.6 %collective-permute-done.26.refs_1_ = f32[8,256]{1,0:T(8,128)S(1)} collective-permute-done((f32[8,256]{1,0:T(8,128)S(1)}, f32[8,256]{1,0:T(8,128)S(1)}, u32[]{:S(2)}, u32[]{:S(2)}) %collective-permute-start.26) | collective-permute-done | bytes 8224 | tf_op jit(solution)/shard_map/ppermute | solution.py:32
  85.0 3.6 %final_update.1 = (bf16[2048,512]{1,0:T(8,128)(2,1)}, f32[512,256]{1,0:T(8,128)}, f32[2048,512]{1,0:T(8,128)}, f32[2,2,64,128]{3,2,1,0:T(8,128)}) custom-call(s32[3]{0:T(128)S(1)} %pad_add_fusion.ranks, bf16[2048,256]{1,0:T(8,128)(2,1)S(1)} %get-tuple-element.78.pcat, f32[256,256]{1,0:T(8,128)S(1)} %inverse_factor.1.x, ...), custom_call_target="tpu_custom_call", output_to_operand_aliasing={{2}: (10, {})} | custom-call | flops 5000000000 | bytes 1 | tf_op jit(solution)/shard_map/final_update/pallas_call | solution.py:581
  (76 shorter events, 17.9 us)
Async XLA Ops:
  4.5 9.3 %collective-permute-start = (bf16[512,256]{1,0:T(8,128)(2,1)S(1)}, bf16[512,256]{1,0:T(8,128)(2,1)S(1)}, u32[]{:S(2)}, u32[]{:S(2)}) collective-permute-start(bf16[512,256]{1,0:T(8,128)(2,1)S(1)} %get-tuple-element.64), channel_id=1, source_target_pairs={{0,16},{16,0},{1,17},{17,1},{2,18},{18,2},{3,19},{19,3},{4,20},{20... | collective-permute-start | bytes 786440 | tf_op jit(solution)/shard_map/ppermute | solution.py:32
  12.7 8.5 %collective-permute-start.1 = (bf16[512,256]{1,0:T(8,128)(2,1)S(1)}, bf16[512,256]{1,0:T(8,128)(2,1)S(1)}, u32[]{:S(2)}, u32[]{:S(2)}) collective-permute-start(bf16[512,256]{1,0:T(8,128)(2,1)S(1)} %get-tuple-element.67.refs_2_), channel_id=1, source_target_pairs={{0,16},{16,0},{1,17},{17,1},{2,18},{18,2},{3,19},{19,3},{4,20},{20... | collective-permute-start | bytes 786440 | tf_op jit(solution)/shard_map/ppermute | solution.py:32
  13.9 11.6 %collective-permute-start.3 = (bf16[256,256]{1,0:T(8,128)(2,1)S(1)}, bf16[256,256]{1,0:T(8,128)(2,1)S(1)}, u32[]{:S(2)}, u32[]{:S(2)}) collective-permute-start(bf16[256,256]{1,0:T(8,128)(2,1)S(1)} %get-tuple-element.69), channel_id=1, source_target_pairs={{0,3},{1,2},{2,1},{3,0},{4,7},{5,6},{6,5},{7,4},{8,11},{9,10},{10,... | collective-permute-start | bytes 393224 | tf_op jit(solution)/shard_map/ppermute | solution.py:32
  17.8 10.3 %collective-permute-start.2 = (bf16[256,256]{1,0:T(8,128)(2,1)S(1)}, bf16[256,256]{1,0:T(8,128)(2,1)S(1)}, u32[]{:S(2)}, u32[]{:S(2)}) collective-permute-start(bf16[256,256]{1,0:T(8,128)(2,1)S(1)} %get-tuple-element.65.refs_4_), channel_id=1, source_target_pairs={{0,2},{1,3},{2,0},{3,1},{4,6},{5,7},{6,4},{7,5},{8,10},{9,11},{10,... | collective-permute-start | bytes 393224 | tf_op jit(solution)/shard_map/ppermute | solution.py:32
  17.8 5.1 %collective-permute-start.5 = (bf16[2,2,64,128]{3,2,1,0:T(8,128)(2,1)S(1)}, bf16[2,2,64,128]{3,2,1,0:T(8,128)(2,1)S(1)}, u32[]{:S(2)}, u32[]{:S(2)}) collective-permute-start(bf16[2,2,64,128]{3,2,1,0:T(8,128)(2,1)S(1)} %pack_prompts.1.refs_0_), channel_id=1, source_target_pairs={{0,16},{16,0},{1,17},{17,1},{2,18},{18,2},{3,19},{19,3},{4,20},{20... | collective-permute-start | bytes 196616 | tf_op jit(solution)/shard_map/ppermute | solution.py:32
  21.3 7.5 %collective-permute-start.4 = (bf16[256,256]{1,0:T(8,128)(2,1)S(1)}, bf16[256,256]{1,0:T(8,128)(2,1)S(1)}, u32[]{:S(2)}, u32[]{:S(2)}) collective-permute-start(bf16[256,256]{1,0:T(8,128)(2,1)S(1)} %get-tuple-element.70.refs_2_), channel_id=1, source_target_pairs={{0,1},{1,0},{2,3},{3,2},{4,5},{5,4},{6,7},{7,6},{8,9},{9,8},{10,11... | collective-permute-start | bytes 393224 | tf_op jit(solution)/shard_map/ppermute | solution.py:32
  23.9 4.3 %collective-permute-start.6 = (bf16[2,64,128]{2,1,0:T(8,128)(2,1)S(1)}, bf16[2,64,128]{2,1,0:T(8,128)(2,1)S(1)}, u32[]{:S(2)}, u32[]{:S(2)}) collective-permute-start(bf16[2,64,128]{2,1,0:T(8,128)(2,1)S(1)} %get-tuple-element.71), channel_id=1, source_target_pairs={{0,4},{4,0},{8,12},{12,8},{1,5},{5,1},{9,13},{13,9},{2,6},{6,2},{1... | collective-permute-start | bytes 98312 | tf_op jit(solution)/shard_map/ppermute | solution.py:32
  23.9 4.3 %collective-permute-start.7 = (bf16[2,64,128]{2,1,0:T(8,128)(2,1)S(1)}, bf16[2,64,128]{2,1,0:T(8,128)(2,1)S(1)}, u32[]{:S(2)}, u32[]{:S(2)}) collective-permute-start(bf16[2,64,128]{2,1,0:T(8,128)(2,1)S(1)} %get-tuple-element.72), channel_id=1, source_target_pairs={{0,8},{4,12},{8,0},{12,4},{1,9},{5,13},{9,1},{13,5},{2,10},{6,14},... | collective-permute-start | bytes 98312 | tf_op jit(solution)/shard_map/ppermute | solution.py:32
  28.9 9.5 %collective-permute-start.10 = (bf16[256,256]{1,0:T(8,128)(2,1)S(1)}, bf16[256,256]{1,0:T(8,128)(2,1)S(1)}, u32[]{:S(2)}, u32[]{:S(2)}) collective-permute-start(bf16[256,256]{1,0:T(8,128)(2,1)S(1)} %sum_parts.7.refs_0_), channel_id=1, source_target_pairs={{0,2},{1,3},{2,0},{3,1},{4,6},{5,7},{6,4},{7,5},{8,10},{9,11},{10,... | collective-permute-start | bytes 393224 | tf_op jit(solution)/shard_map/ppermute | solution.py:32
  31.7 8.4 %collective-permute-start.9 = (bf16[256,256]{1,0:T(8,128)(2,1)S(1)}, bf16[256,256]{1,0:T(8,128)(2,1)S(1)}, u32[]{:S(2)}, u32[]{:S(2)}) collective-permute-start(bf16[256,256]{1,0:T(8,128)(2,1)S(1)} %sum_parts.7.refs_0_), channel_id=1, source_target_pairs={{0,1},{1,0},{2,3},{3,2},{4,5},{5,4},{6,7},{7,6},{8,9},{9,8},{10,11... | collective-permute-start | bytes 393224 | tf_op jit(solution)/shard_map/ppermute | solution.py:32
  32.1 14.8 %collective-permute-start.12 = (bf16[256,256]{1,0:T(8,128)(2,1)S(1)}, bf16[256,256]{1,0:T(8,128)(2,1)S(1)}, u32[]{:S(2)}, u32[]{:S(2)}) collective-permute-start(bf16[256,256]{1,0:T(8,128)(2,1)S(1)} %sum_parts.7.refs_0_), channel_id=1, source_target_pairs={{0,16},{16,0},{1,17},{17,1},{2,18},{18,2},{3,19},{19,3},{4,20},{20... | collective-permute-start | bytes 393224 | tf_op jit(solution)/shard_map/ppermute | solution.py:32
  38.4 8.5 %collective-permute-start.14 = (bf16[256,256]{1,0:T(8,128)(2,1)S(1)}, bf16[256,256]{1,0:T(8,128)(2,1)S(1)}, u32[]{:S(2)}, u32[]{:S(2)}) collective-permute-start(bf16[256,256]{1,0:T(8,128)(2,1)S(1)} %collective-permute-done.10.refs_4_.refs_2_), channel_id=1, source_target_pairs={{0,16},{16,0},{1,17},{17,1},{2,18},{18,2},{3,19},{19,3},{4,20},{20... | collective-permute-start | bytes 393224 | tf_op jit(solution)/shard_map/ppermute | solution.py:32
  40.1 6.9 %collective-permute-start.11 = (bf16[256,256]{1,0:T(8,128)(2,1)S(1)}, bf16[256,256]{1,0:T(8,128)(2,1)S(1)}, u32[]{:S(2)}, u32[]{:S(2)}) collective-permute-start(bf16[256,256]{1,0:T(8,128)(2,1)S(1)} %relay.2), channel_id=1, source_target_pairs={{0,3},{1,2},{2,1},{3,0},{4,7},{5,6},{6,5},{7,4},{8,11},{9,10},{10,... | collective-permute-start | bytes 393224 | tf_op jit(solution)/shard_map/ppermute | solution.py:32
  41.4 5.5 %collective-permute-start.13 = (bf16[256,256]{1,0:T(8,128)(2,1)S(1)}, bf16[256,256]{1,0:T(8,128)(2,1)S(1)}, u32[]{:S(2)}, u32[]{:S(2)}) collective-permute-start(bf16[256,256]{1,0:T(8,128)(2,1)S(1)} %collective-permute-done.9.refs_1_), channel_id=1, source_target_pairs={{0,16},{16,0},{1,17},{17,1},{2,18},{18,2},{3,19},{19,3},{4,20},{20... | collective-permute-start | bytes 393224 | tf_op jit(solution)/shard_map/ppermute | solution.py:32
  47.0 5.0 %collective-permute-start.15 = (bf16[256,256]{1,0:T(8,128)(2,1)S(1)}, bf16[256,256]{1,0:T(8,128)(2,1)S(1)}, u32[]{:S(2)}, u32[]{:S(2)}) collective-permute-start(bf16[256,256]{1,0:T(8,128)(2,1)S(1)} %relay.3.refs_6_), channel_id=1, source_target_pairs={{0,16},{16,0},{1,17},{17,1},{2,18},{18,2},{3,19},{19,3},{4,20},{20... | collective-permute-start | bytes 393224 | tf_op jit(solution)/shard_map/ppermute | solution.py:32
  54.6 7.8 %collective-permute-start.17 = (f32[384,128]{1,0:T(8,128)S(1)}, f32[384,128]{1,0:T(8,128)S(1)}, u32[]{:S(2)}, u32[]{:S(2)}) collective-permute-start(f32[384,128]{1,0:T(8,128)S(1)} %sum_parts.8.refs_0_.refs_2_), channel_id=1, source_target_pairs={{0,8},{4,12},{8,0},{12,4},{1,9},{5,13},{9,1},{13,5},{2,10},{6,14},... | collective-permute-start | bytes 589832 | tf_op jit(solution)/shard_map/ppermute | solution.py:32
  55.8 16.3 %collective-permute-start.19 = (bf16[256,512]{1,0:T(8,128)(2,1)S(1)}, bf16[256,512]{1,0:T(8,128)(2,1)S(1)}, u32[]{:S(2)}, u32[]{:S(2)}) collective-permute-start(bf16[256,512]{1,0:T(8,128)(2,1)S(1)} %sum_parts.9.wa), channel_id=1, source_target_pairs={{0,8},{4,12},{8,0},{12,4},{1,9},{5,13},{9,1},{13,5},{2,10},{6,14},... | collective-permute-start | bytes 786440 | tf_op jit(solution)/shard_map/ppermute | solution.py:32
  57.0 15.1 %collective-permute-start.20 = (bf16[2,64,128]{2,1,0:T(8,128)(2,1)S(1)}, bf16[2,64,128]{2,1,0:T(8,128)(2,1)S(1)}, u32[]{:S(2)}, u32[]{:S(2)}) collective-permute-start(bf16[2,64,128]{2,1,0:T(8,128)(2,1)S(1)} %get-tuple-element.85), channel_id=1, source_target_pairs={{0,4},{4,0},{8,12},{12,8},{1,5},{5,1},{9,13},{13,9},{2,6},{6,2},{1... | collective-permute-start | bytes 98312 | tf_op jit(solution)/shard_map/ppermute | solution.py:32
  57.1 15.1 %collective-permute-start.21 = (bf16[2,64,128]{2,1,0:T(8,128)(2,1)S(1)}, bf16[2,64,128]{2,1,0:T(8,128)(2,1)S(1)}, u32[]{:S(2)}, u32[]{:S(2)}) collective-permute-start(bf16[2,64,128]{2,1,0:T(8,128)(2,1)S(1)} %get-tuple-element.86), channel_id=1, source_target_pairs={{0,8},{4,12},{8,0},{12,4},{1,9},{5,13},{9,1},{13,5},{2,10},{6,14},... | collective-permute-start | bytes 98312 | tf_op jit(solution)/shard_map/ppermute | solution.py:32
  58.0 14.2 %collective-permute-start.22 = (bf16[2,64,128]{2,1,0:T(8,128)(2,1)S(1)}, bf16[2,64,128]{2,1,0:T(8,128)(2,1)S(1)}, u32[]{:S(2)}, u32[]{:S(2)}) collective-permute-start(bf16[2,64,128]{2,1,0:T(8,128)(2,1)S(1)} %get-tuple-element.87), channel_id=1, source_target_pairs={{0,12},{4,8},{8,4},{12,0},{1,13},{5,9},{9,5},{13,1},{2,14},{6,10},... | collective-permute-start | bytes 98312 | tf_op jit(solution)/shard_map/ppermute | solution.py:32
  72.8 8.5 %collective-permute-start.25 = (f32[8,256]{1,0:T(8,128)S(1)}, f32[8,256]{1,0:T(8,128)S(1)}, u32[]{:S(2)}, u32[]{:S(2)}) collective-permute-start(f32[8,256]{1,0:T(8,128)S(1)} %get-tuple-element.92.refs_4_.refs_5_.refs_0_), channel_id=1, source_target_pairs={{0,3},{1,2},{2,1},{3,0},{4,7},{5,6},{6,5},{7,4},{8,11},{9,10},{10,... | collective-permute-start | bytes 24584 | tf_op jit(solution)/shard_map/ppermute | solution.py:32
  74.8 6.4 %collective-permute-start.24 = (f32[8,256]{1,0:T(8,128)S(1)}, f32[8,256]{1,0:T(8,128)S(1)}, u32[]{:S(2)}, u32[]{:S(2)}) collective-permute-start(f32[8,256]{1,0:T(8,128)S(1)} %get-tuple-element.92.refs_4_.refs_5_.refs_0_), channel_id=1, source_target_pairs={{0,2},{1,3},{2,0},{3,1},{4,6},{5,7},{6,4},{7,5},{8,10},{9,11},{10,... | collective-permute-start | bytes 24584 | tf_op jit(solution)/shard_map/ppermute | solution.py:32
  75.2 6.0 %collective-permute-start.23 = (f32[8,256]{1,0:T(8,128)S(1)}, f32[8,256]{1,0:T(8,128)S(1)}, u32[]{:S(2)}, u32[]{:S(2)}) collective-permute-start(f32[8,256]{1,0:T(8,128)S(1)} %get-tuple-element.92.refs_4_.refs_5_.refs_0_), channel_id=1, source_target_pairs={{0,1},{1,0},{2,3},{3,2},{4,5},{5,4},{6,7},{7,6},{8,9},{9,8},{10,11... | collective-permute-start | bytes 24584 | tf_op jit(solution)/shard_map/ppermute | solution.py:32
  77.9 7.1 %collective-permute-start.27 = (bf16[2,2,64,128]{3,2,1,0:T(8,128)(2,1)S(1)}, bf16[2,2,64,128]{3,2,1,0:T(8,128)(2,1)S(1)}, u32[]{:S(2)}, u32[]{:S(2)}) collective-permute-start(bf16[2,2,64,128]{3,2,1,0:T(8,128)(2,1)S(1)} %get-tuple-element.93.refs_6_), channel_id=1, source_target_pairs={{0,16},{16,0},{1,17},{17,1},{2,18},{18,2},{3,19},{19,3},{4,20},{20... | collective-permute-start | bytes 196616 | tf_op jit(solution)/shard_map/ppermute | solution.py:32
  (13 other events, 110.9 us)

commit v9 on v8

--- a/solution.py
+++ b/solution.py
@@ -864,15 +864,20 @@
     held = (
         ranks, counts, prompt_blocks, resp_blocks, queries, self_keys, self_values, d_out, pieces
     )
-    early = [along[k] for k in range(n_head - 1)]
-    last = along[n_head - 1]
-    earlier = attention(heads[0], None, *held, (early[-1],))
-    passed = [[swap(c, "resp", j) for c in early] for j in range(1, n_resp)]
-    sent_last = relay([last], (earlier[1], *[c for row in passed for c in row]))
-    chunks = early + [last]
+    last = n_head - 1
+    earlier = attention(heads[0], None, *held, (along[max(1, later) - 1],))
+    passed = [[swap(along[k], "resp", j) for k in range(later)] for j in range(1, n_resp)]
+    before = (earlier[1], *[c for row in passed for c in row])
+    mid = [relay([along[k]], before) for k in range(later, last)]
+    for j in range(1, n_resp):
+        passed[j - 1] += [swap(c, "resp", j) for c in mid]
+    sent_last = relay([along[last]], (*before, *mid))
+    chunks = [along[k] for k in range(n_head)]
     for j in range(1, n_resp):
         chunks += passed[j - 1] + [swap(sent_last, "resp", j)]
-    dq_parts, resp_grad, *parts = attention(heads[1], earlier, *held, (sent_last,))
+    dq_parts, resp_grad, *parts = attention(
+        heads[1], earlier, *held, (sent_last, *[c for row in passed for c in row[later:]])
+    )
     dq_parts = (earlier[0], dq_parts)
     pcat, pcat_t, gram = gather_gram(chunks, (parts[0],))
 
@@ -880,8 +885,9 @@
     w = back_part(pcat_t, totals, (gram,))
     for bit in bits[:-1]:
         gram = sum_parts([gram, swap(gram, "fsdp", bit)], F32, (), 3)
+    gram_parts = (gram, swap(gram, "fsdp", bits[-1]))
+    for bit in bits[:-1]:
         w = sum_parts([w, swap(w, "fsdp", bit)], BF16, (gram,), 5)
-    gram_parts = (gram, swap(gram, "fsdp", bits[-1]))
     w_other = swap(w, "fsdp", bits[-1])
     returned = [parts[0]] + [swap(parts[k], "fsdp", k) for k in range(1, n_fsdp)]
     x = inverse_factor(*gram_parts)
@@ -890,12 +896,12 @@
     half = len(totals) // 2
     slots = sum_by_slot(ranks, counts, owner_slot, returned, n_resp, (squares,))
     prompts = [slots[0]] + [swap(slots[j], "resp", j) for j in range(1, n_resp)]
-    momentum_out, dq, resp_grad, token = new_momentum(
-        ranks, pcat, totals[:half], y, n_resp, n_head, dq_parts, resp_grad, (squares, slots[-1])
-    )
-    squares = sum_parts([squares] + from_head, F32, (token,))
+    squares = sum_parts([squares] + from_head, F32, (slots[-1],))
     sums = sum_parts(
         [squares] + [swap(squares, "resp", j) for j in range(1, n_resp)], F32
+    )
+    momentum_out, dq, resp_grad, _ = new_momentum(
+        ranks, pcat, totals[:half], y, n_resp, n_head, dq_parts, resp_grad, (squares,)
     )
     update, basis_out, momentum_out, prompt_grad = final_update(
         ranks, pcat, x, bt, y, [sums], totals[half:], prompts, momentum_out, gain, n_resp, n_head

time: 89 us -> 88.2 us (level)
  transfers between devices with their start and end apart: 28 -> 28, of which waited for: 8 -> 9; matrix products, arithmetic and copies ran while one was open for 0% -> 0% of each run, Pallas kernels for 32% -> 33%
where the time goes in v9:
time: 88.2 us; the launch traced here: 88 us
  Pallas kernels  37.4 us (42%)
  starting transfers between devices  33.1 us (38%)
  waiting for transfers between devices  15.6 us (18%)
  between operations  1.81 us (2%)
    ppermute x28, starting transfers between devices, swap(): return lax.ppermute(value, axes, [(i, i ^ k) for i in range(n)])  33.1 us
    ppermute x28, waiting for transfers between devices, swap(): return lax.ppermute(value, axes, [(i, i ^ k) for i in range(n)])  15.6 us
    pallas_call x4, Pallas kernels, project(): pl.pallas_call(functools.partial(project_kernel, n_head, part, following,...  10.4 us
    pallas_call x1, Pallas kernels, inverse_factor(): pl.pallas_call(functools.partial(cholesky_kernel, len(parts)), in_specs=[...  9.71 us
    pallas_call x2, Pallas kernels, attention(): pl.pallas_call(functools.partial(attention_kernel, n_fsdp, heads, last),...  6.47 us
    pallas_call x1, Pallas kernels, final_update(): pl.pallas_call(functools.partial(update_kernel, gain, n_resp, n_head, len...  3.61 us
    pallas_call x1, Pallas kernels, new_momentum(): pl.pallas_call(functools.partial(momentum_kernel, n_resp, n_head, len(tot...  2.91 us
  transfers between devices with their start and end apart: 28, of which 9 were waited for; matrix products, arithmetic and copies ran while one was open for 0% of the time, Pallas kernels for 33%

profile of v9, /device:TPU:0, one launch (start us, length us, event | category | flops | bytes accessed | tf_op | source)
XLA Modules:
  0.0 88.0 jit_solution(10041527339838153034)
XLA Ops:
  0.7 3.8 %project.4 = (bf16[512,256]{1,0:T(8,128)(2,1)S(1)}, f32[512,512]{1,0:T(8,128)S(1)}, bf16[512,256]{1,0:T(8,128)(2,1)S(1)}, bf16[512,256]{1,0:T(8,128)(2,1)S(1)}, ...) custom-call(s32[3]{0:T(128)S(1)} %pad_add_fusion.ranks, f32[2048,512]{1,0:T(8,128)} %mom.7, bf16[2048,512]{1,0:T(8,128)(2,1)} %grad.7, ...), custom_call_target="tpu_custom_call" | custom-call | flops 1 | bytes 1 | tf_op jit(solution)/shard_map/project/pallas_call | solution.py:154
  4.5 3.0 %collective-permute-start = (bf16[512,256]{1,0:T(8,128)(2,1)S(1)}, bf16[512,256]{1,0:T(8,128)(2,1)S(1)}, u32[]{:S(2)}, u32[]{:S(2)}) collective-permute-start(bf16[512,256]{1,0:T(8,128)(2,1)S(1)} %get-tuple-element.63), channel_id=1, source_target_pairs={{0,16},{16,0},{1,17},{17,1},{2,18},{18,2},{3,19},{19,3},{4,20},{20... | collective-permute-start | bytes 786440 | tf_op jit(solution)/shard_map/ppermute | solution.py:32
  7.5 2.6 %project.5 = (f32[512,256]{1,0:T(8,128)S(1)}, f32[512,512]{1,0:T(8,128)S(1)}, f32[512,512]{1,0:T(8,128)S(1)}, bf16[512,512]{1,0:T(8,128)(2,1)S(1)}) custom-call(s32[3]{0:T(128)S(1)} %pad_add_fusion.ranks, f32[2048,512]{1,0:T(8,128)} %mom.7, bf16[2048,512]{1,0:T(8,128)(2,1)} %grad.7, bf16[512,256]{1,0:T(8,128)(2,1)S(1)} %get-tuple-element.54.refs_0_, ...), custom_call_target="tpu_custom_call" | custom-call | flops 10000000000 | bytes 1 | tf_op jit(solution)/shard_map/project/pallas_call | solution.py:154
  10.1 2.6 %project.6 = (bf16[512,256]{1,0:T(8,128)(2,1)S(1)}, f32[512,512]{1,0:T(8,128)S(1)}, f32[512,512]{1,0:T(8,128)S(1)}, bf16[512,512]{1,0:T(8,128)(2,1)S(1)}) custom-call(s32[3]{0:T(128)S(1)} %pad_add_fusion.ranks, f32[2048,512]{1,0:T(8,128)} %mom.7, bf16[2048,512]{1,0:T(8,128)(2,1)} %grad.7, bf16[512,256]{1,0:T(8,128)(2,1)S(1)} %get-tuple-element.54.refs_0_, ...), custom_call_target="tpu_custom_call" | custom-call | flops 1 | bytes 1 | tf_op jit(solution)/shard_map/project/pallas_call | solution.py:154
  13.9 3.9 %collective-permute-start.3 = (bf16[256,256]{1,0:T(8,128)(2,1)S(1)}, bf16[256,256]{1,0:T(8,128)(2,1)S(1)}, u32[]{:S(2)}, u32[]{:S(2)}) collective-permute-start(bf16[256,256]{1,0:T(8,128)(2,1)S(1)} %get-tuple-element.68), channel_id=1, source_target_pairs={{0,3},{1,2},{2,1},{3,0},{4,7},{5,6},{6,5},{7,4},{8,11},{9,10},{10,... | collective-permute-start | bytes 393224 | tf_op jit(solution)/shard_map/ppermute | solution.py:32
  17.8 1.6 %collective-permute-start.5 = (bf16[2,2,64,128]{3,2,1,0:T(8,128)(2,1)S(1)}, bf16[2,2,64,128]{3,2,1,0:T(8,128)(2,1)S(1)}, u32[]{:S(2)}, u32[]{:S(2)}) collective-permute-start(bf16[2,2,64,128]{3,2,1,0:T(8,128)(2,1)S(1)} %pack_prompts.1.refs_0_), channel_id=1, source_target_pairs={{0,16},{16,0},{1,17},{17,1},{2,18},{18,2},{3,19},{19,3},{4,20},{20... | collective-permute-start | bytes 196616 | tf_op jit(solution)/shard_map/ppermute | solution.py:32
  19.4 1.4 %project.7 = (f32[512,256]{1,0:T(8,128)S(1)}, f32[512,512]{1,0:T(8,128)S(1)}) custom-call(s32[3]{0:T(128)S(1)} %pad_add_fusion.ranks, f32[2048,512]{1,0:T(8,128)} %mom.7, bf16[2048,512]{1,0:T(8,128)(2,1)} %grad.7, bf16[512,256]{1,0:T(8,128)(2,1)S(1)} %get-tuple-element.54.refs_0_, bf16[512,256]{1,0:T(8,128)(2,1)S(1)} %get-tuple-element.55.refs_1_, ...), custom_call_target="tpu_custom_call" | custom-call | flops 1 | bytes 1 | tf_op jit(solution)/shard_map/project/pallas_call | solution.py:154
  21.3 1.6 %collective-permute-start.4 = (bf16[256,256]{1,0:T(8,128)(2,1)S(1)}, bf16[256,256]{1,0:T(8,128)(2,1)S(1)}, u32[]{:S(2)}, u32[]{:S(2)}) collective-permute-start(bf16[256,256]{1,0:T(8,128)(2,1)S(1)} %get-tuple-element.69.refs_2_), channel_id=1, source_target_pairs={{0,1},{1,0},{2,3},{3,2},{4,5},{5,4},{6,7},{7,6},{8,9},{9,8},{10,11... | collective-permute-start | bytes 393224 | tf_op jit(solution)/shard_map/ppermute | solution.py:32
  23.9 1.6 %collective-permute-start.7 = (bf16[2,64,128]{2,1,0:T(8,128)(2,1)S(1)}, bf16[2,64,128]{2,1,0:T(8,128)(2,1)S(1)}, u32[]{:S(2)}, u32[]{:S(2)}) collective-permute-start(bf16[2,64,128]{2,1,0:T(8,128)(2,1)S(1)} %get-tuple-element.71), channel_id=1, source_target_pairs={{0,8},{4,12},{8,0},{12,4},{1,9},{5,13},{9,1},{13,5},{2,10},{6,14},... | collective-permute-start | bytes 98312 | tf_op jit(solution)/shard_map/ppermute | solution.py:32
  25.8 2.3 %collective-permute-done.2.refs_1_ = bf16[256,256]{1,0:T(8,128)(2,1)S(1)} collective-permute-done((bf16[256,256]{1,0:T(8,128)(2,1)S(1)}, bf16[256,256]{1,0:T(8,128)(2,1)S(1)}, u32[]{:S(2)}, u32[]{:S(2)}) %collective-permute-start.2) | collective-permute-done | bytes 131104 | tf_op jit(solution)/shard_map/ppermute | solution.py:32
  28.9 1.6 %collective-permute-start.9 = (bf16[256,256]{1,0:T(8,128)(2,1)S(1)}, bf16[256,256]{1,0:T(8,128)(2,1)S(1)}, u32[]{:S(2)}, u32[]{:S(2)}) collective-permute-start(bf16[256,256]{1,0:T(8,128)(2,1)S(1)} %sum_parts.7.refs_0_), channel_id=1, source_target_pairs={{0,1},{1,0},{2,3},{3,2},{4,5},{5,4},{6,7},{7,6},{8,9},{9,8},{10,11... | collective-permute-start | bytes 393224 | tf_op jit(solution)/shard_map/ppermute | solution.py:32
  30.5 1.5 %collective-permute-start.12 = (bf16[256,256]{1,0:T(8,128)(2,1)S(1)}, bf16[256,256]{1,0:T(8,128)(2,1)S(1)}, u32[]{:S(2)}, u32[]{:S(2)}) collective-permute-start(bf16[256,256]{1,0:T(8,128)(2,1)S(1)} %sum_parts.7.refs_0_), channel_id=1, source_target_pairs={{0,16},{16,0},{1,17},{17,1},{2,18},{18,2},{3,19},{19,3},{4,20},{20... | collective-permute-start | bytes 393224 | tf_op jit(solution)/shard_map/ppermute | solution.py:32
  32.0 1.5 %collective-permute-start.10 = (bf16[256,256]{1,0:T(8,128)(2,1)S(1)}, bf16[256,256]{1,0:T(8,128)(2,1)S(1)}, u32[]{:S(2)}, u32[]{:S(2)}) collective-permute-start(bf16[256,256]{1,0:T(8,128)(2,1)S(1)} %sum_parts.7.refs_0_), channel_id=1, source_target_pairs={{0,2},{1,3},{2,0},{3,1},{4,6},{5,7},{6,4},{7,5},{8,10},{9,11},{10,... | collective-permute-start | bytes 393224 | tf_op jit(solution)/shard_map/ppermute | solution.py:32
  34.5 3.3 %collective-permute-start.13 = (bf16[256,256]{1,0:T(8,128)(2,1)S(1)}, bf16[256,256]{1,0:T(8,128)(2,1)S(1)}, u32[]{:S(2)}, u32[]{:S(2)}) collective-permute-start(bf16[256,256]{1,0:T(8,128)(2,1)S(1)} %collective-permute-done.9.refs_1_.refs_4_), channel_id=1, source_target_pairs={{0,16},{16,0},{1,17},{17,1},{2,18},{18,2},{3,19},{19,3},{4,20},{20... | collective-permute-start | bytes 393224 | tf_op jit(solution)/shard_map/ppermute | solution.py:32
  37.8 1.5 %collective-permute-start.11 = (bf16[256,256]{1,0:T(8,128)(2,1)S(1)}, bf16[256,256]{1,0:T(8,128)(2,1)S(1)}, u32[]{:S(2)}, u32[]{:S(2)}) collective-permute-start(bf16[256,256]{1,0:T(8,128)(2,1)S(1)} %relay.3), channel_id=1, source_target_pairs={{0,3},{1,2},{2,1},{3,0},{4,7},{5,6},{6,5},{7,4},{8,11},{9,10},{10,... | collective-permute-start | bytes 393224 | tf_op jit(solution)/shard_map/ppermute | solution.py:32
  40.0 3.3 %attention.2 = (bf16[256,512]{1,0:T(8,128)(2,1)S(1)}, f32[512,128]{1,0:T(8,128)S(1)}, f32[512,128]{1,0:T(8,128)S(1)}) custom-call(s32[3]{0:T(128)S(1)} %pad_add_fusion.ranks, s32[4]{0:T(128)S(1)} %copy-done.6, s32[4]{0:T(128)S(1)} %copy-done.7, s32[1]{0:T(128)S(6)} %copy.21.resp_blocks, bf16[256,1024]{1,0:T(8,128)(2,1)S(1)} %copy-done, ...), custom_call_target="tpu_custom_call" | custom-call | flops 1 | bytes 1 | tf_op jit(solution)/shard_map/attention/pallas_call | solution.py:745
  45.5 3.1 %collective-permute-done.14.refs_7_.refs_6_ = bf16[256,256]{1,0:T(8,128)(2,1)S(1)} collective-permute-done((bf16[256,256]{1,0:T(8,128)(2,1)S(1)}, bf16[256,256]{1,0:T(8,128)(2,1)S(1)}, u32[]{:S(2)}, u32[]{:S(2)}) %collective-permute-start.14) | collective-permute-done | bytes 131104 | tf_op jit(solution)/shard_map/ppermute | solution.py:32
  48.6 3.2 %attention.3 = (bf16[256,512]{1,0:T(8,128)(2,1)S(1)}, bf16[2,256,128]{2,1,0:T(8,128)(2,1)S(1)}, f32[2,64,128]{2,1,0:T(8,128)S(1)}, bf16[2,64,128]{2,1,0:T(8,128)...) custom-call(s32[3]{0:T(128)S(1)} %pad_add_fusion.ranks, s32[4]{0:T(128)S(1)} %copy-done.6, ...), custom_call_target="tpu_custom_call" | custom-call | flops 1 | bytes 1 | tf_op jit(solution)/shard_map/attention/pallas_call | solution.py:745
  58.7 3.5 %collective-permute-done.17.refs_1_ = f32[384,128]{1,0:T(8,128)S(1)} collective-permute-done((f32[384,128]{1,0:T(8,128)S(1)}, f32[384,128]{1,0:T(8,128)S(1)}, u32[]{:S(2)}, u32[]{:S(2)}) %collective-permute-start.17) | collective-permute-done | bytes 196640 | tf_op jit(solution)/shard_map/ppermute | solution.py:32
  62.3 9.7 %inverse_factor.1.x = f32[256,256]{1,0:T(8,128)S(1)} custom-call(f32[384,128]{1,0:T(8,128)S(1)} %sum_parts.8.refs_0_.refs_2_, f32[384,128]{1,0:T(8,128)S(1)} %collective-permute-done.17.refs_1_), custom_call_target="tpu_custom_call" | custom-call | flops 2000000000 | bytes 1 | tf_op jit(solution)/shard_map/inverse_factor/pallas_call | solution.py:421
  72.6 3.2 %collective-permute-start.25 = (f32[8,256]{1,0:T(8,128)S(1)}, f32[8,256]{1,0:T(8,128)S(1)}, u32[]{:S(2)}, u32[]{:S(2)}) collective-permute-start(f32[8,256]{1,0:T(8,128)S(1)} %get-tuple-element.91.refs_4_.refs_0_), channel_id=1, source_target_pairs={{0,3},{1,2},{2,1},{3,0},{4,7},{5,6},{6,5},{7,4},{8,11},{9,10},{10,... | collective-permute-start | bytes 24584 | tf_op jit(solution)/shard_map/ppermute | solution.py:32
  78.2 2.1 %collective-permute-done.24.refs_2_ = f32[8,256]{1,0:T(8,128)S(1)} collective-permute-done((f32[8,256]{1,0:T(8,128)S(1)}, f32[8,256]{1,0:T(8,128)S(1)}, u32[]{:S(2)}, u32[]{:S(2)}) %collective-permute-start.24) | collective-permute-done | bytes 8224 | tf_op jit(solution)/shard_map/ppermute | solution.py:32
  81.3 2.9 %new_momentum.1 = (f32[2048,512]{1,0:T(8,128)}, bf16[256,1024]{1,0:T(8,128)(2,1)}, bf16[2,256,128]{2,1,0:T(8,128)(2,1)}, f32[8,128]{1,0:T(8,128)}) custom-call(s32[3]{0:T(128)S(1)} %pad_add_fusion.ranks, bf16[2048,256]{1,0:T(8,128)(2,1)S(1)} %get-tuple-element.77.pcat, bf16[256,512]{1,0:T(8,128)(2,1)S(1)} %get-tuple-element.87.y, ...), custom_call_target="tpu_custom_call" | custom-call | flops 5000000000 | bytes 1 | tf_op jit(solution)/shard_map/new_momentum/pallas_call | solution.py:518
  84.2 3.6 %final_update.1 = (bf16[2048,512]{1,0:T(8,128)(2,1)}, f32[512,256]{1,0:T(8,128)}, f32[2048,512]{1,0:T(8,128)}, f32[2,2,64,128]{3,2,1,0:T(8,128)}) custom-call(s32[3]{0:T(128)S(1)} %pad_add_fusion.ranks, bf16[2048,256]{1,0:T(8,128)(2,1)S(1)} %get-tuple-element.77.pcat, f32[256,256]{1,0:T(8,128)S(1)} %inverse_factor.1.x, ...), custom_call_target="tpu_custom_call", output_to_operand_aliasing={{2}: (10, {})} | custom-call | flops 5000000000 | bytes 1 | tf_op jit(solution)/shard_map/final_update/pallas_call | solution.py:581
  (77 shorter events, 17.7 us)
Async XLA Ops:
  4.5 9.3 %collective-permute-start = (bf16[512,256]{1,0:T(8,128)(2,1)S(1)}, bf16[512,256]{1,0:T(8,128)(2,1)S(1)}, u32[]{:S(2)}, u32[]{:S(2)}) collective-permute-start(bf16[512,256]{1,0:T(8,128)(2,1)S(1)} %get-tuple-element.63), channel_id=1, source_target_pairs={{0,16},{16,0},{1,17},{17,1},{2,18},{18,2},{3,19},{19,3},{4,20},{20... | collective-permute-start | bytes 786440 | tf_op jit(solution)/shard_map/ppermute | solution.py:32
  12.7 8.5 %collective-permute-start.1 = (bf16[512,256]{1,0:T(8,128)(2,1)S(1)}, bf16[512,256]{1,0:T(8,128)(2,1)S(1)}, u32[]{:S(2)}, u32[]{:S(2)}) collective-permute-start(bf16[512,256]{1,0:T(8,128)(2,1)S(1)} %get-tuple-element.66.refs_2_), channel_id=1, source_target_pairs={{0,16},{16,0},{1,17},{17,1},{2,18},{18,2},{3,19},{19,3},{4,20},{20... | collective-permute-start | bytes 786440 | tf_op jit(solution)/shard_map/ppermute | solution.py:32
  13.9 11.6 %collective-permute-start.3 = (bf16[256,256]{1,0:T(8,128)(2,1)S(1)}, bf16[256,256]{1,0:T(8,128)(2,1)S(1)}, u32[]{:S(2)}, u32[]{:S(2)}) collective-permute-start(bf16[256,256]{1,0:T(8,128)(2,1)S(1)} %get-tuple-element.68), channel_id=1, source_target_pairs={{0,3},{1,2},{2,1},{3,0},{4,7},{5,6},{6,5},{7,4},{8,11},{9,10},{10,... | collective-permute-start | bytes 393224 | tf_op jit(solution)/shard_map/ppermute | solution.py:32
  17.8 10.3 %collective-permute-start.2 = (bf16[256,256]{1,0:T(8,128)(2,1)S(1)}, bf16[256,256]{1,0:T(8,128)(2,1)S(1)}, u32[]{:S(2)}, u32[]{:S(2)}) collective-permute-start(bf16[256,256]{1,0:T(8,128)(2,1)S(1)} %get-tuple-element.64.refs_4_), channel_id=1, source_target_pairs={{0,2},{1,3},{2,0},{3,1},{4,6},{5,7},{6,4},{7,5},{8,10},{9,11},{10,... | collective-permute-start | bytes 393224 | tf_op jit(solution)/shard_map/ppermute | solution.py:32
  17.8 5.1 %collective-permute-start.5 = (bf16[2,2,64,128]{3,2,1,0:T(8,128)(2,1)S(1)}, bf16[2,2,64,128]{3,2,1,0:T(8,128)(2,1)S(1)}, u32[]{:S(2)}, u32[]{:S(2)}) collective-permute-start(bf16[2,2,64,128]{3,2,1,0:T(8,128)(2,1)S(1)} %pack_prompts.1.refs_0_), channel_id=1, source_target_pairs={{0,16},{16,0},{1,17},{17,1},{2,18},{18,2},{3,19},{19,3},{4,20},{20... | collective-permute-start | bytes 196616 | tf_op jit(solution)/shard_map/ppermute | solution.py:32
  21.3 7.5 %collective-permute-start.4 = (bf16[256,256]{1,0:T(8,128)(2,1)S(1)}, bf16[256,256]{1,0:T(8,128)(2,1)S(1)}, u32[]{:S(2)}, u32[]{:S(2)}) collective-permute-start(bf16[256,256]{1,0:T(8,128)(2,1)S(1)} %get-tuple-element.69.refs_2_), channel_id=1, source_target_pairs={{0,1},{1,0},{2,3},{3,2},{4,5},{5,4},{6,7},{7,6},{8,9},{9,8},{10,11... | collective-permute-start | bytes 393224 | tf_op jit(solution)/shard_map/ppermute | solution.py:32
  23.9 4.3 %collective-permute-start.6 = (bf16[2,64,128]{2,1,0:T(8,128)(2,1)S(1)}, bf16[2,64,128]{2,1,0:T(8,128)(2,1)S(1)}, u32[]{:S(2)}, u32[]{:S(2)}) collective-permute-start(bf16[2,64,128]{2,1,0:T(8,128)(2,1)S(1)} %get-tuple-element.70), channel_id=1, source_target_pairs={{0,4},{4,0},{8,12},{12,8},{1,5},{5,1},{9,13},{13,9},{2,6},{6,2},{1... | collective-permute-start | bytes 98312 | tf_op jit(solution)/shard_map/ppermute | solution.py:32
  23.9 4.3 %collective-permute-start.7 = (bf16[2,64,128]{2,1,0:T(8,128)(2,1)S(1)}, bf16[2,64,128]{2,1,0:T(8,128)(2,1)S(1)}, u32[]{:S(2)}, u32[]{:S(2)}) collective-permute-start(bf16[2,64,128]{2,1,0:T(8,128)(2,1)S(1)} %get-tuple-element.71), channel_id=1, source_target_pairs={{0,8},{4,12},{8,0},{12,4},{1,9},{5,13},{9,1},{13,5},{2,10},{6,14},... | collective-permute-start | bytes 98312 | tf_op jit(solution)/shard_map/ppermute | solution.py:32
  28.9 5.6 %collective-permute-start.9 = (bf16[256,256]{1,0:T(8,128)(2,1)S(1)}, bf16[256,256]{1,0:T(8,128)(2,1)S(1)}, u32[]{:S(2)}, u32[]{:S(2)}) collective-permute-start(bf16[256,256]{1,0:T(8,128)(2,1)S(1)} %sum_parts.7.refs_0_), channel_id=1, source_target_pairs={{0,1},{1,0},{2,3},{3,2},{4,5},{5,4},{6,7},{7,6},{8,9},{9,8},{10,11... | collective-permute-start | bytes 393224 | tf_op jit(solution)/shard_map/ppermute | solution.py:32
  30.5 12.8 %collective-permute-start.12 = (bf16[256,256]{1,0:T(8,128)(2,1)S(1)}, bf16[256,256]{1,0:T(8,128)(2,1)S(1)}, u32[]{:S(2)}, u32[]{:S(2)}) collective-permute-start(bf16[256,256]{1,0:T(8,128)(2,1)S(1)} %sum_parts.7.refs_0_), channel_id=1, source_target_pairs={{0,16},{16,0},{1,17},{17,1},{2,18},{18,2},{3,19},{19,3},{4,20},{20... | collective-permute-start | bytes 393224 | tf_op jit(solution)/shard_map/ppermute | solution.py:32
  32.0 11.3 %collective-permute-start.10 = (bf16[256,256]{1,0:T(8,128)(2,1)S(1)}, bf16[256,256]{1,0:T(8,128)(2,1)S(1)}, u32[]{:S(2)}, u32[]{:S(2)}) collective-permute-start(bf16[256,256]{1,0:T(8,128)(2,1)S(1)} %sum_parts.7.refs_0_), channel_id=1, source_target_pairs={{0,2},{1,3},{2,0},{3,1},{4,6},{5,7},{6,4},{7,5},{8,10},{9,11},{10,... | collective-permute-start | bytes 393224 | tf_op jit(solution)/shard_map/ppermute | solution.py:32
  34.5 8.8 %collective-permute-start.13 = (bf16[256,256]{1,0:T(8,128)(2,1)S(1)}, bf16[256,256]{1,0:T(8,128)(2,1)S(1)}, u32[]{:S(2)}, u32[]{:S(2)}) collective-permute-start(bf16[256,256]{1,0:T(8,128)(2,1)S(1)} %collective-permute-done.9.refs_1_.refs_4_), channel_id=1, source_target_pairs={{0,16},{16,0},{1,17},{17,1},{2,18},{18,2},{3,19},{19,3},{4,20},{20... | collective-permute-start | bytes 393224 | tf_op jit(solution)/shard_map/ppermute | solution.py:32
  37.8 6.9 %collective-permute-start.11 = (bf16[256,256]{1,0:T(8,128)(2,1)S(1)}, bf16[256,256]{1,0:T(8,128)(2,1)S(1)}, u32[]{:S(2)}, u32[]{:S(2)}) collective-permute-start(bf16[256,256]{1,0:T(8,128)(2,1)S(1)} %relay.3), channel_id=1, source_target_pairs={{0,3},{1,2},{2,1},{3,0},{4,7},{5,6},{6,5},{7,4},{8,11},{9,10},{10,... | collective-permute-start | bytes 393224 | tf_op jit(solution)/shard_map/ppermute | solution.py:32
  43.4 5.3 %collective-permute-start.14 = (bf16[256,256]{1,0:T(8,128)(2,1)S(1)}, bf16[256,256]{1,0:T(8,128)(2,1)S(1)}, u32[]{:S(2)}, u32[]{:S(2)}) collective-permute-start(bf16[256,256]{1,0:T(8,128)(2,1)S(1)} %relay.4.refs_4_), channel_id=1, source_target_pairs={{0,16},{16,0},{1,17},{17,1},{2,18},{18,2},{3,19},{19,3},{4,20},{20... | collective-permute-start | bytes 393224 | tf_op jit(solution)/shard_map/ppermute | solution.py:32
  44.8 7.1 %collective-permute-start.15 = (bf16[256,256]{1,0:T(8,128)(2,1)S(1)}, bf16[256,256]{1,0:T(8,128)(2,1)S(1)}, u32[]{:S(2)}, u32[]{:S(2)}) collective-permute-start(bf16[256,256]{1,0:T(8,128)(2,1)S(1)} %relay.5.refs_6_), channel_id=1, source_target_pairs={{0,16},{16,0},{1,17},{17,1},{2,18},{18,2},{3,19},{19,3},{4,20},{20... | collective-permute-start | bytes 393224 | tf_op jit(solution)/shard_map/ppermute | solution.py:32
  54.4 7.8 %collective-permute-start.17 = (f32[384,128]{1,0:T(8,128)S(1)}, f32[384,128]{1,0:T(8,128)S(1)}, u32[]{:S(2)}, u32[]{:S(2)}) collective-permute-start(f32[384,128]{1,0:T(8,128)S(1)} %sum_parts.8.refs_0_.refs_2_), channel_id=1, source_target_pairs={{0,8},{4,12},{8,0},{12,4},{1,9},{5,13},{9,1},{13,5},{2,10},{6,14},... | collective-permute-start | bytes 589832 | tf_op jit(solution)/shard_map/ppermute | solution.py:32
  55.7 16.3 %collective-permute-start.19 = (bf16[256,512]{1,0:T(8,128)(2,1)S(1)}, bf16[256,512]{1,0:T(8,128)(2,1)S(1)}, u32[]{:S(2)}, u32[]{:S(2)}) collective-permute-start(bf16[256,512]{1,0:T(8,128)(2,1)S(1)} %sum_parts.9.wa), channel_id=1, source_target_pairs={{0,8},{4,12},{8,0},{12,4},{1,9},{5,13},{9,1},{13,5},{2,10},{6,14},... | collective-permute-start | bytes 786440 | tf_op jit(solution)/shard_map/ppermute | solution.py:32
  56.9 15.1 %collective-permute-start.20 = (bf16[2,64,128]{2,1,0:T(8,128)(2,1)S(1)}, bf16[2,64,128]{2,1,0:T(8,128)(2,1)S(1)}, u32[]{:S(2)}, u32[]{:S(2)}) collective-permute-start(bf16[2,64,128]{2,1,0:T(8,128)(2,1)S(1)} %get-tuple-element.84), channel_id=1, source_target_pairs={{0,4},{4,0},{8,12},{12,8},{1,5},{5,1},{9,13},{13,9},{2,6},{6,2},{1... | collective-permute-start | bytes 98312 | tf_op jit(solution)/shard_map/ppermute | solution.py:32
  56.9 15.0 %collective-permute-start.21 = (bf16[2,64,128]{2,1,0:T(8,128)(2,1)S(1)}, bf16[2,64,128]{2,1,0:T(8,128)(2,1)S(1)}, u32[]{:S(2)}, u32[]{:S(2)}) collective-permute-start(bf16[2,64,128]{2,1,0:T(8,128)(2,1)S(1)} %get-tuple-element.85), channel_id=1, source_target_pairs={{0,8},{4,12},{8,0},{12,4},{1,9},{5,13},{9,1},{13,5},{2,10},{6,14},... | collective-permute-start | bytes 98312 | tf_op jit(solution)/shard_map/ppermute | solution.py:32
  57.8 14.2 %collective-permute-start.22 = (bf16[2,64,128]{2,1,0:T(8,128)(2,1)S(1)}, bf16[2,64,128]{2,1,0:T(8,128)(2,1)S(1)}, u32[]{:S(2)}, u32[]{:S(2)}) collective-permute-start(bf16[2,64,128]{2,1,0:T(8,128)(2,1)S(1)} %get-tuple-element.86), channel_id=1, source_target_pairs={{0,12},{4,8},{8,4},{12,0},{1,13},{5,9},{9,5},{13,1},{2,14},{6,10},... | collective-permute-start | bytes 98312 | tf_op jit(solution)/shard_map/ppermute | solution.py:32
  72.6 5.6 %collective-permute-start.25 = (f32[8,256]{1,0:T(8,128)S(1)}, f32[8,256]{1,0:T(8,128)S(1)}, u32[]{:S(2)}, u32[]{:S(2)}) collective-permute-start(f32[8,256]{1,0:T(8,128)S(1)} %get-tuple-element.91.refs_4_.refs_0_), channel_id=1, source_target_pairs={{0,3},{1,2},{2,1},{3,0},{4,7},{5,6},{6,5},{7,4},{8,11},{9,10},{10,... | collective-permute-start | bytes 24584 | tf_op jit(solution)/shard_map/ppermute | solution.py:32
  75.8 4.5 %collective-permute-start.24 = (f32[8,256]{1,0:T(8,128)S(1)}, f32[8,256]{1,0:T(8,128)S(1)}, u32[]{:S(2)}, u32[]{:S(2)}) collective-permute-start(f32[8,256]{1,0:T(8,128)S(1)} %get-tuple-element.91.refs_4_.refs_0_), channel_id=1, source_target_pairs={{0,2},{1,3},{2,0},{3,1},{4,6},{5,7},{6,4},{7,5},{8,10},{9,11},{10,... | collective-permute-start | bytes 24584 | tf_op jit(solution)/shard_map/ppermute | solution.py:32
  75.8 4.5 %collective-permute-start.23 = (f32[8,256]{1,0:T(8,128)S(1)}, f32[8,256]{1,0:T(8,128)S(1)}, u32[]{:S(2)}, u32[]{:S(2)}) collective-permute-start(f32[8,256]{1,0:T(8,128)S(1)} %get-tuple-element.91.refs_4_.refs_0_), channel_id=1, source_target_pairs={{0,1},{1,0},{2,3},{3,2},{4,5},{5,4},{6,7},{7,6},{8,9},{9,8},{10,11... | collective-permute-start | bytes 24584 | tf_op jit(solution)/shard_map/ppermute | solution.py:32
  77.7 6.5 %collective-permute-start.27 = (bf16[2,2,64,128]{3,2,1,0:T(8,128)(2,1)S(1)}, bf16[2,2,64,128]{3,2,1,0:T(8,128)(2,1)S(1)}, u32[]{:S(2)}, u32[]{:S(2)}) collective-permute-start(bf16[2,2,64,128]{3,2,1,0:T(8,128)(2,1)S(1)} %get-tuple-element.92.refs_4_), channel_id=1, source_target_pairs={{0,16},{16,0},{1,17},{17,1},{2,18},{18,2},{3,19},{19,3},{4,20},{20... | collective-permute-start | bytes 196616 | tf_op jit(solution)/shard_map/ppermute | solution.py:32
  (13 other events, 93.0 us)

commit v10 on v9

--- a/solution.py
+++ b/solution.py
@@ -852,32 +852,32 @@
         [far] + [summands[k] for k in range(1, later)], BF16, tuple(pieces[1:])
     )
 
-    along = {0: piece0}
-    for k in range(1, later):
-        along[k] = swap(piece0, "head", k)
-    held_back = relay([piece0], (along[max(1, later) - 1],))
-    for k in range(later, n_head):
-        along[k] = swap(held_back if k > later else piece0, "head", k)
-
     n_q = queries.shape[1] // HD
     heads = [list(range(n_q // 2)), list(range(n_q // 2, n_q))]
     held = (
         ranks, counts, prompt_blocks, resp_blocks, queries, self_keys, self_values, d_out, pieces
     )
+    along = {0: piece0}
+    for k in range(1, n_head):
+        if not k & (k - 1):
+            along[k] = swap(piece0, "head", k)
+    earlier = attention(heads[0], None, *held, (piece0,))
+    hops = {}
+    for k in range(1, n_head):
+        low = k & -k
+        if k != low:
+            if k - low not in hops:
+                hops[k - low] = relay([along[k - low]], (earlier[1],))
+            along[k] = swap(hops[k - low], "head", low)
     last = n_head - 1
-    earlier = attention(heads[0], None, *held, (along[max(1, later) - 1],))
-    passed = [[swap(along[k], "resp", j) for k in range(later)] for j in range(1, n_resp)]
-    before = (earlier[1], *[c for row in passed for c in row])
-    mid = [relay([along[k]], before) for k in range(later, last)]
-    for j in range(1, n_resp):
-        passed[j - 1] += [swap(c, "resp", j) for c in mid]
-    sent_last = relay([along[last]], (*before, *mid))
+    passed = [
+        [swap(hops.get(k, along[k]), "resp", j) for k in range(last)] for j in range(1, n_resp)
+    ]
+    sent_last = relay([along[last]], (earlier[1], *[c for row in passed for c in row]))
     chunks = [along[k] for k in range(n_head)]
     for j in range(1, n_resp):
         chunks += passed[j - 1] + [swap(sent_last, "resp", j)]
-    dq_parts, resp_grad, *parts = attention(
-        heads[1], earlier, *held, (sent_last, *[c for row in passed for c in row[later:]])
-    )
+    dq_parts, resp_grad, *parts = attention(heads[1], earlier, *held, (sent_last,))
     dq_parts = (earlier[0], dq_parts)
     pcat, pcat_t, gram = gather_gram(chunks, (parts[0],))
 

time: 88.2 us -> 87 us (0.986)
  starting transfers between devices: 33.1 us -> 31.1 us
    ppermute x28, starting transfers between devices: 33.1 us -> 31.1 us  [swap(): return lax.ppermute(value, axes, [(i, i ^ k) for i in range(n)])]
  transfers between devices with their start and end apart: 28 -> 28, of which waited for: 9 -> 11; matrix products, arithmetic and copies ran while one was open for 0% -> 0% of each run, Pallas kernels for 33% -> 33%
where the time goes in v10:
time: 87 us; the launch traced here: 86.7 us
  Pallas kernels  37.4 us (43%)
  starting transfers between devices  31.1 us (36%)
  waiting for transfers between devices  16.4 us (19%)
  between operations  1.73 us (2%)
    ppermute x28, starting transfers between devices, swap(): return lax.ppermute(value, axes, [(i, i ^ k) for i in range(n)])  31.1 us
    ppermute x28, waiting for transfers between devices, swap(): return lax.ppermute(value, axes, [(i, i ^ k) for i in range(n)])  16.4 us
    pallas_call x4, Pallas kernels, project(): pl.pallas_call(functools.partial(project_kernel, n_head, part, following,...  10.4 us
    pallas_call x1, Pallas kernels, inverse_factor(): pl.pallas_call(functools.partial(cholesky_kernel, len(parts)), in_specs=[...  9.71 us
    pallas_call x2, Pallas kernels, attention(): pl.pallas_call(functools.partial(attention_kernel, n_fsdp, heads, last),...  6.48 us
    pallas_call x1, Pallas kernels, final_update(): pl.pallas_call(functools.partial(update_kernel, gain, n_resp, n_head, len...  3.6 us
    pallas_call x1, Pallas kernels, new_momentum(): pl.pallas_call(functools.partial(momentum_kernel, n_resp, n_head, len(tot...  2.92 us
  transfers between devices with their start and end apart: 28, of which 11 were waited for; matrix products, arithmetic and copies ran while one was open for 0% of the time, Pallas kernels for 33%

profile of v10, /device:TPU:0, one launch (start us, length us, event | category | flops | bytes accessed | tf_op | source)
XLA Modules:
  0.0 86.7 jit_solution(11279767689502095133)
XLA Ops:
  0.7 3.8 %project.4 = (bf16[512,256]{1,0:T(8,128)(2,1)S(1)}, f32[512,512]{1,0:T(8,128)S(1)}, bf16[512,256]{1,0:T(8,128)(2,1)S(1)}, bf16[512,256]{1,0:T(8,128)(2,1)S(1)}, ...) custom-call(s32[3]{0:T(128)S(1)} %pad_add_fusion.ranks, f32[2048,512]{1,0:T(8,128)} %mom.7, bf16[2048,512]{1,0:T(8,128)(2,1)} %grad.7, ...), custom_call_target="tpu_custom_call" | custom-call | flops 1 | bytes 1 | tf_op jit(solution)/shard_map/project/pallas_call | solution.py:154
  4.5 3.0 %collective-permute-start = (bf16[512,256]{1,0:T(8,128)(2,1)S(1)}, bf16[512,256]{1,0:T(8,128)(2,1)S(1)}, u32[]{:S(2)}, u32[]{:S(2)}) collective-permute-start(bf16[512,256]{1,0:T(8,128)(2,1)S(1)} %get-tuple-element.63), channel_id=1, source_target_pairs={{0,16},{16,0},{1,17},{17,1},{2,18},{18,2},{3,19},{19,3},{4,20},{20... | collective-permute-start | bytes 786440 | tf_op jit(solution)/shard_map/ppermute | solution.py:32
  7.5 2.6 %project.5 = (f32[512,256]{1,0:T(8,128)S(1)}, f32[512,512]{1,0:T(8,128)S(1)}, f32[512,512]{1,0:T(8,128)S(1)}, bf16[512,512]{1,0:T(8,128)(2,1)S(1)}) custom-call(s32[3]{0:T(128)S(1)} %pad_add_fusion.ranks, f32[2048,512]{1,0:T(8,128)} %mom.7, bf16[2048,512]{1,0:T(8,128)(2,1)} %grad.7, bf16[512,256]{1,0:T(8,128)(2,1)S(1)} %get-tuple-element.54.refs_0_, ...), custom_call_target="tpu_custom_call" | custom-call | flops 10000000000 | bytes 1 | tf_op jit(solution)/shard_map/project/pallas_call | solution.py:154
  10.1 2.6 %project.6 = (bf16[512,256]{1,0:T(8,128)(2,1)S(1)}, f32[512,512]{1,0:T(8,128)S(1)}, f32[512,512]{1,0:T(8,128)S(1)}, bf16[512,512]{1,0:T(8,128)(2,1)S(1)}) custom-call(s32[3]{0:T(128)S(1)} %pad_add_fusion.ranks, f32[2048,512]{1,0:T(8,128)} %mom.7, bf16[2048,512]{1,0:T(8,128)(2,1)} %grad.7, bf16[512,256]{1,0:T(8,128)(2,1)S(1)} %get-tuple-element.54.refs_0_, ...), custom_call_target="tpu_custom_call" | custom-call | flops 1 | bytes 1 | tf_op jit(solution)/shard_map/project/pallas_call | solution.py:154
  13.9 3.9 %collective-permute-start.3 = (bf16[256,256]{1,0:T(8,128)(2,1)S(1)}, bf16[256,256]{1,0:T(8,128)(2,1)S(1)}, u32[]{:S(2)}, u32[]{:S(2)}) collective-permute-start(bf16[256,256]{1,0:T(8,128)(2,1)S(1)} %get-tuple-element.68), channel_id=1, source_target_pairs={{0,3},{1,2},{2,1},{3,0},{4,7},{5,6},{6,5},{7,4},{8,11},{9,10},{10,... | collective-permute-start | bytes 393224 | tf_op jit(solution)/shard_map/ppermute | solution.py:32
  17.8 1.6 %collective-permute-start.5 = (bf16[2,2,64,128]{3,2,1,0:T(8,128)(2,1)S(1)}, bf16[2,2,64,128]{3,2,1,0:T(8,128)(2,1)S(1)}, u32[]{:S(2)}, u32[]{:S(2)}) collective-permute-start(bf16[2,2,64,128]{3,2,1,0:T(8,128)(2,1)S(1)} %pack_prompts.1.refs_0_), channel_id=1, source_target_pairs={{0,16},{16,0},{1,17},{17,1},{2,18},{18,2},{3,19},{19,3},{4,20},{20... | collective-permute-start | bytes 196616 | tf_op jit(solution)/shard_map/ppermute | solution.py:32
  19.4 1.4 %project.7 = (f32[512,256]{1,0:T(8,128)S(1)}, f32[512,512]{1,0:T(8,128)S(1)}) custom-call(s32[3]{0:T(128)S(1)} %pad_add_fusion.ranks, f32[2048,512]{1,0:T(8,128)} %mom.7, bf16[2048,512]{1,0:T(8,128)(2,1)} %grad.7, bf16[512,256]{1,0:T(8,128)(2,1)S(1)} %get-tuple-element.54.refs_0_, bf16[512,256]{1,0:T(8,128)(2,1)S(1)} %get-tuple-element.55.refs_1_, ...), custom_call_target="tpu_custom_call" | custom-call | flops 1 | bytes 1 | tf_op jit(solution)/shard_map/project/pallas_call | solution.py:154
  21.3 1.6 %collective-permute-start.4 = (bf16[256,256]{1,0:T(8,128)(2,1)S(1)}, bf16[256,256]{1,0:T(8,128)(2,1)S(1)}, u32[]{:S(2)}, u32[]{:S(2)}) collective-permute-start(bf16[256,256]{1,0:T(8,128)(2,1)S(1)} %get-tuple-element.69.refs_2_), channel_id=1, source_target_pairs={{0,1},{1,0},{2,3},{3,2},{4,5},{5,4},{6,7},{7,6},{8,9},{9,8},{10,11... | collective-permute-start | bytes 393224 | tf_op jit(solution)/shard_map/ppermute | solution.py:32
  23.9 1.6 %collective-permute-start.7 = (bf16[2,64,128]{2,1,0:T(8,128)(2,1)S(1)}, bf16[2,64,128]{2,1,0:T(8,128)(2,1)S(1)}, u32[]{:S(2)}, u32[]{:S(2)}) collective-permute-start(bf16[2,64,128]{2,1,0:T(8,128)(2,1)S(1)} %get-tuple-element.71), channel_id=1, source_target_pairs={{0,8},{4,12},{8,0},{12,4},{1,9},{5,13},{9,1},{13,5},{2,10},{6,14},... | collective-permute-start | bytes 98312 | tf_op jit(solution)/shard_map/ppermute | solution.py:32
  25.8 2.3 %collective-permute-done.2.refs_1_ = bf16[256,256]{1,0:T(8,128)(2,1)S(1)} collective-permute-done((bf16[256,256]{1,0:T(8,128)(2,1)S(1)}, bf16[256,256]{1,0:T(8,128)(2,1)S(1)}, u32[]{:S(2)}, u32[]{:S(2)}) %collective-permute-start.2) | collective-permute-done | bytes 131104 | tf_op jit(solution)/shard_map/ppermute | solution.py:32
  28.9 1.6 %collective-permute-start.9 = (bf16[256,256]{1,0:T(8,128)(2,1)S(1)}, bf16[256,256]{1,0:T(8,128)(2,1)S(1)}, u32[]{:S(2)}, u32[]{:S(2)}) collective-permute-start(bf16[256,256]{1,0:T(8,128)(2,1)S(1)} %sum_parts.7.refs_4_.refs_0_), channel_id=1, source_target_pairs={{0,1},{1,0},{2,3},{3,2},{4,5},{5,4},{6,7},{7,6},{8,9},{9,8},{10,11... | collective-permute-start | bytes 393224 | tf_op jit(solution)/shard_map/ppermute | solution.py:32
  30.5 1.6 %collective-permute-start.10 = (bf16[256,256]{1,0:T(8,128)(2,1)S(1)}, bf16[256,256]{1,0:T(8,128)(2,1)S(1)}, u32[]{:S(2)}, u32[]{:S(2)}) collective-permute-start(bf16[256,256]{1,0:T(8,128)(2,1)S(1)} %sum_parts.7.refs_4_.refs_0_), channel_id=1, source_target_pairs={{0,2},{1,3},{2,0},{3,1},{4,6},{5,7},{6,4},{7,5},{8,10},{9,11},{10,... | collective-permute-start | bytes 393224 | tf_op jit(solution)/shard_map/ppermute | solution.py:32
  32.8 1.4 %collective-permute-start.12 = (bf16[256,256]{1,0:T(8,128)(2,1)S(1)}, bf16[256,256]{1,0:T(8,128)(2,1)S(1)}, u32[]{:S(2)}, u32[]{:S(2)}) collective-permute-start(bf16[256,256]{1,0:T(8,128)(2,1)S(1)} %sum_parts.7.refs_4_.refs_0_), channel_id=1, source_target_pairs={{0,16},{16,0},{1,17},{17,1},{2,18},{18,2},{3,19},{19,3},{4,20},{20... | collective-permute-start | bytes 393224 | tf_op jit(solution)/shard_map/ppermute | solution.py:32
  34.2 3.3 %attention.2 = (bf16[256,512]{1,0:T(8,128)(2,1)S(1)}, f32[512,128]{1,0:T(8,128)S(1)}, f32[512,128]{1,0:T(8,128)S(1)}) custom-call(s32[3]{0:T(128)S(1)} %pad_add_fusion.ranks, s32[4]{0:T(128)S(1)} %copy-done.6, s32[4]{0:T(128)S(1)} %copy-done.7, s32[1]{0:T(128)S(6)} %copy.21.resp_blocks, bf16[256,1024]{1,0:T(8,128)(2,1)S(1)} %copy-done, ...), custom_call_target="tpu_custom_call" | custom-call | flops 1 | bytes 1 | tf_op jit(solution)/shard_map/attention/pallas_call | solution.py:745
  39.7 2.1 %collective-permute-start.11 = (bf16[256,256]{1,0:T(8,128)(2,1)S(1)}, bf16[256,256]{1,0:T(8,128)(2,1)S(1)}, u32[]{:S(2)}, u32[]{:S(2)}) collective-permute-start(bf16[256,256]{1,0:T(8,128)(2,1)S(1)} %relay.2), channel_id=1, source_target_pairs={{0,1},{1,0},{2,3},{3,2},{4,5},{5,4},{6,7},{7,6},{8,9},{9,8},{10,11... | collective-permute-start | bytes 393224 | tf_op jit(solution)/shard_map/ppermute | solution.py:32
  41.8 2.1 %collective-permute-done.13.refs_3_.refs_5_ = bf16[256,256]{1,0:T(8,128)(2,1)S(1)} collective-permute-done((bf16[256,256]{1,0:T(8,128)(2,1)S(1)}, bf16[256,256]{1,0:T(8,128)(2,1)S(1)}, u32[]{:S(2)}, u32[]{:S(2)}) %collective-permute-start.13) | collective-permute-done | bytes 131104 | tf_op jit(solution)/shard_map/ppermute | solution.py:32
  43.9 1.4 %collective-permute-done.14.refs_4_.refs_6_ = bf16[256,256]{1,0:T(8,128)(2,1)S(1)} collective-permute-done((bf16[256,256]{1,0:T(8,128)(2,1)S(1)}, bf16[256,256]{1,0:T(8,128)(2,1)S(1)}, u32[]{:S(2)}, u32[]{:S(2)}) %collective-permute-start.14) | collective-permute-done | bytes 131104 | tf_op jit(solution)/shard_map/ppermute | solution.py:32
  45.9 3.2 %attention.3 = (bf16[256,512]{1,0:T(8,128)(2,1)S(1)}, bf16[2,256,128]{2,1,0:T(8,128)(2,1)S(1)}, f32[2,64,128]{2,1,0:T(8,128)S(1)}, bf16[2,64,128]{2,1,0:T(8,128)...) custom-call(s32[3]{0:T(128)S(1)} %pad_add_fusion.ranks, s32[4]{0:T(128)S(1)} %copy-done.6, ...), custom_call_target="tpu_custom_call" | custom-call | flops 1 | bytes 1 | tf_op jit(solution)/shard_map/attention/pallas_call | solution.py:745
  57.0 3.7 %collective-permute-done.17.refs_1_ = f32[384,128]{1,0:T(8,128)S(1)} collective-permute-done((f32[384,128]{1,0:T(8,128)S(1)}, f32[384,128]{1,0:T(8,128)S(1)}, u32[]{:S(2)}, u32[]{:S(2)}) %collective-permute-start.17) | collective-permute-done | bytes 196640 | tf_op jit(solution)/shard_map/ppermute | solution.py:32
  60.7 9.7 %inverse_factor.1.x = f32[256,256]{1,0:T(8,128)S(1)} custom-call(f32[384,128]{1,0:T(8,128)S(1)} %sum_parts.8.refs_0_.refs_2_, f32[384,128]{1,0:T(8,128)S(1)} %collective-permute-done.17.refs_1_), custom_call_target="tpu_custom_call" | custom-call | flops 2000000000 | bytes 1 | tf_op jit(solution)/shard_map/inverse_factor/pallas_call | solution.py:421
  71.1 3.6 %collective-permute-start.25 = (f32[8,256]{1,0:T(8,128)S(1)}, f32[8,256]{1,0:T(8,128)S(1)}, u32[]{:S(2)}, u32[]{:S(2)}) collective-permute-start(f32[8,256]{1,0:T(8,128)S(1)} %get-tuple-element.91.refs_4_.refs_0_), channel_id=1, source_target_pairs={{0,3},{1,2},{2,1},{3,0},{4,7},{5,6},{6,5},{7,4},{8,11},{9,10},{10,... | collective-permute-start | bytes 24584 | tf_op jit(solution)/shard_map/ppermute | solution.py:32
  76.7 2.5 %collective-permute-done.24.refs_2_ = f32[8,256]{1,0:T(8,128)S(1)} collective-permute-done((f32[8,256]{1,0:T(8,128)S(1)}, f32[8,256]{1,0:T(8,128)S(1)}, u32[]{:S(2)}, u32[]{:S(2)}) %collective-permute-start.24) | collective-permute-done | bytes 8224 | tf_op jit(solution)/shard_map/ppermute | solution.py:32
  79.7 2.9 %new_momentum.1 = (f32[2048,512]{1,0:T(8,128)}, bf16[256,1024]{1,0:T(8,128)(2,1)}, bf16[2,256,128]{2,1,0:T(8,128)(2,1)}, f32[8,128]{1,0:T(8,128)}) custom-call(s32[3]{0:T(128)S(1)} %pad_add_fusion.ranks, bf16[2048,256]{1,0:T(8,128)(2,1)S(1)} %get-tuple-element.77.pcat, bf16[256,512]{1,0:T(8,128)(2,1)S(1)} %get-tuple-element.87.y, ...), custom_call_target="tpu_custom_call" | custom-call | flops 5000000000 | bytes 1 | tf_op jit(solution)/shard_map/new_momentum/pallas_call | solution.py:518
  83.0 3.6 %final_update.1 = (bf16[2048,512]{1,0:T(8,128)(2,1)}, f32[512,256]{1,0:T(8,128)}, f32[2048,512]{1,0:T(8,128)}, f32[2,2,64,128]{3,2,1,0:T(8,128)}) custom-call(s32[3]{0:T(128)S(1)} %pad_add_fusion.ranks, bf16[2048,256]{1,0:T(8,128)(2,1)S(1)} %get-tuple-element.77.pcat, f32[256,256]{1,0:T(8,128)S(1)} %inverse_factor.1.x, ...), custom_call_target="tpu_custom_call", output_to_operand_aliasing={{2}: (10, {})} | custom-call | flops 5000000000 | bytes 1 | tf_op jit(solution)/shard_map/final_update/pallas_call | solution.py:581
  (76 shorter events, 17.7 us)
Async XLA Ops:
  4.5 9.3 %collective-permute-start = (bf16[512,256]{1,0:T(8,128)(2,1)S(1)}, bf16[512,256]{1,0:T(8,128)(2,1)S(1)}, u32[]{:S(2)}, u32[]{:S(2)}) collective-permute-start(bf16[512,256]{1,0:T(8,128)(2,1)S(1)} %get-tuple-element.63), channel_id=1, source_target_pairs={{0,16},{16,0},{1,17},{17,1},{2,18},{18,2},{3,19},{19,3},{4,20},{20... | collective-permute-start | bytes 786440 | tf_op jit(solution)/shard_map/ppermute | solution.py:32
  12.7 8.5 %collective-permute-start.1 = (bf16[512,256]{1,0:T(8,128)(2,1)S(1)}, bf16[512,256]{1,0:T(8,128)(2,1)S(1)}, u32[]{:S(2)}, u32[]{:S(2)}) collective-permute-start(bf16[512,256]{1,0:T(8,128)(2,1)S(1)} %get-tuple-element.66.refs_2_), channel_id=1, source_target_pairs={{0,16},{16,0},{1,17},{17,1},{2,18},{18,2},{3,19},{19,3},{4,20},{20... | collective-permute-start | bytes 786440 | tf_op jit(solution)/shard_map/ppermute | solution.py:32
  13.9 11.6 %collective-permute-start.3 = (bf16[256,256]{1,0:T(8,128)(2,1)S(1)}, bf16[256,256]{1,0:T(8,128)(2,1)S(1)}, u32[]{:S(2)}, u32[]{:S(2)}) collective-permute-start(bf16[256,256]{1,0:T(8,128)(2,1)S(1)} %get-tuple-element.68), channel_id=1, source_target_pairs={{0,3},{1,2},{2,1},{3,0},{4,7},{5,6},{6,5},{7,4},{8,11},{9,10},{10,... | collective-permute-start | bytes 393224 | tf_op jit(solution)/shard_map/ppermute | solution.py:32
  17.8 10.3 %collective-permute-start.2 = (bf16[256,256]{1,0:T(8,128)(2,1)S(1)}, bf16[256,256]{1,0:T(8,128)(2,1)S(1)}, u32[]{:S(2)}, u32[]{:S(2)}) collective-permute-start(bf16[256,256]{1,0:T(8,128)(2,1)S(1)} %get-tuple-element.64.refs_4_), channel_id=1, source_target_pairs={{0,2},{1,3},{2,0},{3,1},{4,6},{5,7},{6,4},{7,5},{8,10},{9,11},{10,... | collective-permute-start | bytes 393224 | tf_op jit(solution)/shard_map/ppermute | solution.py:32
  17.8 5.1 %collective-permute-start.5 = (bf16[2,2,64,128]{3,2,1,0:T(8,128)(2,1)S(1)}, bf16[2,2,64,128]{3,2,1,0:T(8,128)(2,1)S(1)}, u32[]{:S(2)}, u32[]{:S(2)}) collective-permute-start(bf16[2,2,64,128]{3,2,1,0:T(8,128)(2,1)S(1)} %pack_prompts.1.refs_0_), channel_id=1, source_target_pairs={{0,16},{16,0},{1,17},{17,1},{2,18},{18,2},{3,19},{19,3},{4,20},{20... | collective-permute-start | bytes 196616 | tf_op jit(solution)/shard_map/ppermute | solution.py:32
  21.3 7.5 %collective-permute-start.4 = (bf16[256,256]{1,0:T(8,128)(2,1)S(1)}, bf16[256,256]{1,0:T(8,128)(2,1)S(1)}, u32[]{:S(2)}, u32[]{:S(2)}) collective-permute-start(bf16[256,256]{1,0:T(8,128)(2,1)S(1)} %get-tuple-element.69.refs_2_), channel_id=1, source_target_pairs={{0,1},{1,0},{2,3},{3,2},{4,5},{5,4},{6,7},{7,6},{8,9},{9,8},{10,11... | collective-permute-start | bytes 393224 | tf_op jit(solution)/shard_map/ppermute | solution.py:32
  23.9 4.3 %collective-permute-start.6 = (bf16[2,64,128]{2,1,0:T(8,128)(2,1)S(1)}, bf16[2,64,128]{2,1,0:T(8,128)(2,1)S(1)}, u32[]{:S(2)}, u32[]{:S(2)}) collective-permute-start(bf16[2,64,128]{2,1,0:T(8,128)(2,1)S(1)} %get-tuple-element.70), channel_id=1, source_target_pairs={{0,4},{4,0},{8,12},{12,8},{1,5},{5,1},{9,13},{13,9},{2,6},{6,2},{1... | collective-permute-start | bytes 98312 | tf_op jit(solution)/shard_map/ppermute | solution.py:32
  23.9 4.3 %collective-permute-start.7 = (bf16[2,64,128]{2,1,0:T(8,128)(2,1)S(1)}, bf16[2,64,128]{2,1,0:T(8,128)(2,1)S(1)}, u32[]{:S(2)}, u32[]{:S(2)}) collective-permute-start(bf16[2,64,128]{2,1,0:T(8,128)(2,1)S(1)} %get-tuple-element.71), channel_id=1, source_target_pairs={{0,8},{4,12},{8,0},{12,4},{1,9},{5,13},{9,1},{13,5},{2,10},{6,14},... | collective-permute-start | bytes 98312 | tf_op jit(solution)/shard_map/ppermute | solution.py:32
  28.9 8.6 %collective-permute-start.9 = (bf16[256,256]{1,0:T(8,128)(2,1)S(1)}, bf16[256,256]{1,0:T(8,128)(2,1)S(1)}, u32[]{:S(2)}, u32[]{:S(2)}) collective-permute-start(bf16[256,256]{1,0:T(8,128)(2,1)S(1)} %sum_parts.7.refs_4_.refs_0_), channel_id=1, source_target_pairs={{0,1},{1,0},{2,3},{3,2},{4,5},{5,4},{6,7},{7,6},{8,9},{9,8},{10,11... | collective-permute-start | bytes 393224 | tf_op jit(solution)/shard_map/ppermute | solution.py:32
  30.5 7.8 %collective-permute-start.10 = (bf16[256,256]{1,0:T(8,128)(2,1)S(1)}, bf16[256,256]{1,0:T(8,128)(2,1)S(1)}, u32[]{:S(2)}, u32[]{:S(2)}) collective-permute-start(bf16[256,256]{1,0:T(8,128)(2,1)S(1)} %sum_parts.7.refs_4_.refs_0_), channel_id=1, source_target_pairs={{0,2},{1,3},{2,0},{3,1},{4,6},{5,7},{6,4},{7,5},{8,10},{9,11},{10,... | collective-permute-start | bytes 393224 | tf_op jit(solution)/shard_map/ppermute | solution.py:32
  32.8 9.0 %collective-permute-start.12 = (bf16[256,256]{1,0:T(8,128)(2,1)S(1)}, bf16[256,256]{1,0:T(8,128)(2,1)S(1)}, u32[]{:S(2)}, u32[]{:S(2)}) collective-permute-start(bf16[256,256]{1,0:T(8,128)(2,1)S(1)} %sum_parts.7.refs_4_.refs_0_), channel_id=1, source_target_pairs={{0,16},{16,0},{1,17},{17,1},{2,18},{18,2},{3,19},{19,3},{4,20},{20... | collective-permute-start | bytes 393224 | tf_op jit(solution)/shard_map/ppermute | solution.py:32
  37.5 6.4 %collective-permute-start.13 = (bf16[256,256]{1,0:T(8,128)(2,1)S(1)}, bf16[256,256]{1,0:T(8,128)(2,1)S(1)}, u32[]{:S(2)}, u32[]{:S(2)}) collective-permute-start(bf16[256,256]{1,0:T(8,128)(2,1)S(1)} %collective-permute-done.9.refs_1_), channel_id=1, source_target_pairs={{0,16},{16,0},{1,17},{17,1},{2,18},{18,2},{3,19},{19,3},{4,20},{20... | collective-permute-start | bytes 393224 | tf_op jit(solution)/shard_map/ppermute | solution.py:32
  38.3 7.0 %collective-permute-start.14 = (bf16[256,256]{1,0:T(8,128)(2,1)S(1)}, bf16[256,256]{1,0:T(8,128)(2,1)S(1)}, u32[]{:S(2)}, u32[]{:S(2)}) collective-permute-start(bf16[256,256]{1,0:T(8,128)(2,1)S(1)} %relay.2), channel_id=1, source_target_pairs={{0,16},{16,0},{1,17},{17,1},{2,18},{18,2},{3,19},{19,3},{4,20},{20... | collective-permute-start | bytes 393224 | tf_op jit(solution)/shard_map/ppermute | solution.py:32
  39.7 5.7 %collective-permute-start.11 = (bf16[256,256]{1,0:T(8,128)(2,1)S(1)}, bf16[256,256]{1,0:T(8,128)(2,1)S(1)}, u32[]{:S(2)}, u32[]{:S(2)}) collective-permute-start(bf16[256,256]{1,0:T(8,128)(2,1)S(1)} %relay.2), channel_id=1, source_target_pairs={{0,1},{1,0},{2,3},{3,2},{4,5},{5,4},{6,7},{7,6},{8,9},{9,8},{10,11... | collective-permute-start | bytes 393224 | tf_op jit(solution)/shard_map/ppermute | solution.py:32
  45.3 5.0 %collective-permute-start.15 = (bf16[256,256]{1,0:T(8,128)(2,1)S(1)}, bf16[256,256]{1,0:T(8,128)(2,1)S(1)}, u32[]{:S(2)}, u32[]{:S(2)}) collective-permute-start(bf16[256,256]{1,0:T(8,128)(2,1)S(1)} %relay.3.refs_6_), channel_id=1, source_target_pairs={{0,16},{16,0},{1,17},{17,1},{2,18},{18,2},{3,19},{19,3},{4,20},{20... | collective-permute-start | bytes 393224 | tf_op jit(solution)/shard_map/ppermute | solution.py:32
  52.9 7.8 %collective-permute-start.17 = (f32[384,128]{1,0:T(8,128)S(1)}, f32[384,128]{1,0:T(8,128)S(1)}, u32[]{:S(2)}, u32[]{:S(2)}) collective-permute-start(f32[384,128]{1,0:T(8,128)S(1)} %sum_parts.8.refs_0_.refs_2_), channel_id=1, source_target_pairs={{0,8},{4,12},{8,0},{12,4},{1,9},{5,13},{9,1},{13,5},{2,10},{6,14},... | collective-permute-start | bytes 589832 | tf_op jit(solution)/shard_map/ppermute | solution.py:32
  54.1 16.4 %collective-permute-start.19 = (bf16[256,512]{1,0:T(8,128)(2,1)S(1)}, bf16[256,512]{1,0:T(8,128)(2,1)S(1)}, u32[]{:S(2)}, u32[]{:S(2)}) collective-permute-start(bf16[256,512]{1,0:T(8,128)(2,1)S(1)} %sum_parts.9.wa), channel_id=1, source_target_pairs={{0,8},{4,12},{8,0},{12,4},{1,9},{5,13},{9,1},{13,5},{2,10},{6,14},... | collective-permute-start | bytes 786440 | tf_op jit(solution)/shard_map/ppermute | solution.py:32
  55.1 15.3 %collective-permute-start.20 = (bf16[2,64,128]{2,1,0:T(8,128)(2,1)S(1)}, bf16[2,64,128]{2,1,0:T(8,128)(2,1)S(1)}, u32[]{:S(2)}, u32[]{:S(2)}) collective-permute-start(bf16[2,64,128]{2,1,0:T(8,128)(2,1)S(1)} %get-tuple-element.84), channel_id=1, source_target_pairs={{0,4},{4,0},{8,12},{12,8},{1,5},{5,1},{9,13},{13,9},{2,6},{6,2},{1... | collective-permute-start | bytes 98312 | tf_op jit(solution)/shard_map/ppermute | solution.py:32
  55.1 15.3 %collective-permute-start.21 = (bf16[2,64,128]{2,1,0:T(8,128)(2,1)S(1)}, bf16[2,64,128]{2,1,0:T(8,128)(2,1)S(1)}, u32[]{:S(2)}, u32[]{:S(2)}) collective-permute-start(bf16[2,64,128]{2,1,0:T(8,128)(2,1)S(1)} %get-tuple-element.85), channel_id=1, source_target_pairs={{0,8},{4,12},{8,0},{12,4},{1,9},{5,13},{9,1},{13,5},{2,10},{6,14},... | collective-permute-start | bytes 98312 | tf_op jit(solution)/shard_map/ppermute | solution.py:32
  56.3 14.2 %collective-permute-start.22 = (bf16[2,64,128]{2,1,0:T(8,128)(2,1)S(1)}, bf16[2,64,128]{2,1,0:T(8,128)(2,1)S(1)}, u32[]{:S(2)}, u32[]{:S(2)}) collective-permute-start(bf16[2,64,128]{2,1,0:T(8,128)(2,1)S(1)} %get-tuple-element.86), channel_id=1, source_target_pairs={{0,12},{4,8},{8,4},{12,0},{1,13},{5,9},{9,5},{13,1},{2,14},{6,10},... | collective-permute-start | bytes 98312 | tf_op jit(solution)/shard_map/ppermute | solution.py:32
  71.1 5.7 %collective-permute-start.25 = (f32[8,256]{1,0:T(8,128)S(1)}, f32[8,256]{1,0:T(8,128)S(1)}, u32[]{:S(2)}, u32[]{:S(2)}) collective-permute-start(f32[8,256]{1,0:T(8,128)S(1)} %get-tuple-element.91.refs_4_.refs_0_), channel_id=1, source_target_pairs={{0,3},{1,2},{2,1},{3,0},{4,7},{5,6},{6,5},{7,4},{8,11},{9,10},{10,... | collective-permute-start | bytes 24584 | tf_op jit(solution)/shard_map/ppermute | solution.py:32
  74.7 4.5 %collective-permute-start.24 = (f32[8,256]{1,0:T(8,128)S(1)}, f32[8,256]{1,0:T(8,128)S(1)}, u32[]{:S(2)}, u32[]{:S(2)}) collective-permute-start(f32[8,256]{1,0:T(8,128)S(1)} %get-tuple-element.91.refs_4_.refs_0_), channel_id=1, source_target_pairs={{0,2},{1,3},{2,0},{3,1},{4,6},{5,7},{6,4},{7,5},{8,10},{9,11},{10,... | collective-permute-start | bytes 24584 | tf_op jit(solution)/shard_map/ppermute | solution.py:32
  74.7 4.5 %collective-permute-start.23 = (f32[8,256]{1,0:T(8,128)S(1)}, f32[8,256]{1,0:T(8,128)S(1)}, u32[]{:S(2)}, u32[]{:S(2)}) collective-permute-start(f32[8,256]{1,0:T(8,128)S(1)} %get-tuple-element.91.refs_4_.refs_0_), channel_id=1, source_target_pairs={{0,1},{1,0},{2,3},{3,2},{4,5},{5,4},{6,7},{7,6},{8,9},{9,8},{10,11... | collective-permute-start | bytes 24584 | tf_op jit(solution)/shard_map/ppermute | solution.py:32
  76.2 6.8 %collective-permute-start.27 = (bf16[2,2,64,128]{3,2,1,0:T(8,128)(2,1)S(1)}, bf16[2,2,64,128]{3,2,1,0:T(8,128)(2,1)S(1)}, u32[]{:S(2)}, u32[]{:S(2)}) collective-permute-start(bf16[2,2,64,128]{3,2,1,0:T(8,128)(2,1)S(1)} %get-tuple-element.92.refs_4_), channel_id=1, source_target_pairs={{0,16},{16,0},{1,17},{17,1},{2,18},{18,2},{3,19},{19,3},{4,20},{20... | collective-permute-start | bytes 196616 | tf_op jit(solution)/shard_map/ppermute | solution.py:32
  (13 other events, 63.6 us)

commit v11 on v10

--- a/solution.py
+++ b/solution.py
@@ -184,7 +184,7 @@
         in_specs=[VMEM] * (1 + len(recvs)),
         out_specs=[VMEM] * number,
         out_shape=[
-            jax.ShapeDtypeStruct((chunk, rank), BF16 if first + i else F32)
+            jax.ShapeDtypeStruct((chunk, rank), BF16 if (first + i) % 2 else F32)
             for i in range(number)
         ],
         compiler_params=params(),
@@ -830,7 +830,7 @@
                 outs = split_sum(owned, arrived[groups[0][0]], *groups[0])
                 for i in range(groups[0][1]):
                     split[groups[0][0] + i] = outs[i]
-                after = (outs[0],)
+                after = (outs[-1],)
         elif part[1:] == groups[0] and len(groups) > 1:
             owned = value
         else:
@@ -841,16 +841,19 @@
     chosen = select_prompts(
         ranks, counts, owner_slot, stored, n_fsdp, (split[1 % n_head],)
     )
-    far_first = [k for first, number in groups for k in range(first, first + number) if k]
-    summands = {k: swap(split[k], "head", k) for k in far_first}
     pieces = [chosen[0]] + [swap(chosen[k], "fsdp", k) for k in range(1, n_fsdp)]
-    later = groups[-1][1] if len(groups) > 1 else 1
-    far = sum_parts(
-        [split[0]] + [summands[k] for k in range(later, n_head)], F32, (), 10
-    )
-    piece0 = sum_parts(
-        [far] + [summands[k] for k in range(1, later)], BF16, tuple(pieces[1:])
-    )
+    pending, arriving, bit = {k: split[k] for k in range(1, n_head)}, [], 1
+    while bit < n_head:
+        for k in sorted(pending):
+            if k & -k == bit:
+                received = swap(pending.pop(k), "head", bit)
+                if k == bit:
+                    arriving.append(received)
+                else:
+                    pending[k - bit] = sum_parts([pending[k - bit], received], BF16, (), 0)
+        bit *= 2
+    far = sum_parts([split[0], arriving[-1]], F32, (), 10)
+    piece0 = sum_parts([far, *arriving[:-1]], BF16, tuple(pieces[1:]))
 
     n_q = queries.shape[1] // HD
     heads = [list(range(n_q // 2)), list(range(n_q // 2, n_q))]
@@ -870,26 +873,24 @@
                 hops[k - low] = relay([along[k - low]], (earlier[1],))
             along[k] = swap(hops[k - low], "head", low)
     last = n_head - 1
-    passed = [
-        [swap(hops.get(k, along[k]), "resp", j) for k in range(last)] for j in range(1, n_resp)
-    ]
-    sent_last = relay([along[last]], (earlier[1], *[c for row in passed for c in row]))
+    passed = [[swap(hops.get(k, along[k]), "resp", j) for k in range(last)] for j in range(1, n_resp)]
+    dq_parts, resp_grad, *parts = attention(heads[1], earlier, *held, tuple(hops.values()))
+    sent_last = relay([along[last]], (parts[0], *[c for row in passed for c in row]))
     chunks = [along[k] for k in range(n_head)]
     for j in range(1, n_resp):
         chunks += passed[j - 1] + [swap(sent_last, "resp", j)]
-    dq_parts, resp_grad, *parts = attention(heads[1], earlier, *held, (sent_last,))
     dq_parts = (earlier[0], dq_parts)
-    pcat, pcat_t, gram = gather_gram(chunks, (parts[0],))
+    pcat, pcat_t, gram = gather_gram(chunks, ())
 
     bits = [1 << b for b in range(n_fsdp.bit_length() - 1)]
-    w = back_part(pcat_t, totals, (gram,))
+    returned = [parts[0]] + [swap(parts[k], "fsdp", k) for k in range(1, n_fsdp)]
+    w = back_part(pcat_t, totals, (gram, *returned[1:]))
     for bit in bits[:-1]:
         gram = sum_parts([gram, swap(gram, "fsdp", bit)], F32, (), 3)
     gram_parts = (gram, swap(gram, "fsdp", bits[-1]))
     for bit in bits[:-1]:
         w = sum_parts([w, swap(w, "fsdp", bit)], BF16, (gram,), 5)
     w_other = swap(w, "fsdp", bits[-1])
-    returned = [parts[0]] + [swap(parts[k], "fsdp", k) for k in range(1, n_fsdp)]
     x = inverse_factor(*gram_parts)
     bt, y, squares = back_full(x, w, w_other, tuple(returned[1:]))
     from_head = [swap(squares, "head", k) for k in range(1, n_head)]

time: 87 us -> 89.3 us (1.026)
  waiting for transfers between devices: 16.4 us -> 20.2 us
  starting transfers between devices: 31.1 us -> 29.6 us
    ppermute x28, waiting for transfers between devices: 16.4 us -> 20.2 us  [swap(): return lax.ppermute(value, axes, [(i, i ^ k) for i in range(n)])]
    ppermute x28, starting transfers between devices: 31.1 us -> 29.6 us  [swap(): return lax.ppermute(value, axes, [(i, i ^ k) for i in range(n)])]
where the time goes in v11:
time: 89.3 us; the launch traced here: 89.1 us
  Pallas kernels  37.4 us (42%)
  starting transfers between devices  29.6 us (33%)
  waiting for transfers between devices  20.2 us (23%)
  between operations  1.77 us (2%)
    ppermute x28, starting transfers between devices, swap(): return lax.ppermute(value, axes, [(i, i ^ k) for i in range(n)])  29.6 us
    ppermute x28, waiting for transfers between devices, swap(): return lax.ppermute(value, axes, [(i, i ^ k) for i in range(n)])  20.2 us
    pallas_call x4, Pallas kernels, project(): pl.pallas_call(functools.partial(project_kernel, n_head, part, following,...  10.4 us
    pallas_call x1, Pallas kernels, inverse_factor(): pl.pallas_call(functools.partial(cholesky_kernel, len(parts)), in_specs=[...  9.7 us
    pallas_call x2, Pallas kernels, attention(): pl.pallas_call(functools.partial(attention_kernel, n_fsdp, heads, last),...  6.47 us
    pallas_call x1, Pallas kernels, final_update(): pl.pallas_call(functools.partial(update_kernel, gain, n_resp, n_head, len...  3.61 us
    pallas_call x1, Pallas kernels, new_momentum(): pl.pallas_call(functools.partial(momentum_kernel, n_resp, n_head, len(tot...  2.92 us
  transfers between devices with their start and end apart: 28, of which 11 were waited for; matrix products, arithmetic and copies ran while one was open for 0% of the time, Pallas kernels for 33%

profile of v11, /device:TPU:0, one launch (start us, length us, event | category | flops | bytes accessed | tf_op | source)
XLA Modules:
  0.0 89.1 jit_solution(15109453755964454512)
XLA Ops:
  0.7 3.8 %project.4 = (bf16[512,256]{1,0:T(8,128)(2,1)S(1)}, f32[512,512]{1,0:T(8,128)S(1)}, bf16[512,256]{1,0:T(8,128)(2,1)S(1)}, bf16[512,256]{1,0:T(8,128)(2,1)S(1)}, ...) custom-call(s32[3]{0:T(128)S(1)} %pad_add_fusion.ranks, f32[2048,512]{1,0:T(8,128)} %mom.7, bf16[2048,512]{1,0:T(8,128)(2,1)} %grad.7, ...), custom_call_target="tpu_custom_call" | custom-call | flops 1 | bytes 1 | tf_op jit(solution)/shard_map/project/pallas_call | solution.py:154
  4.5 3.0 %collective-permute-start = (bf16[512,256]{1,0:T(8,128)(2,1)S(1)}, bf16[512,256]{1,0:T(8,128)(2,1)S(1)}, u32[]{:S(2)}, u32[]{:S(2)}) collective-permute-start(bf16[512,256]{1,0:T(8,128)(2,1)S(1)} %get-tuple-element.63), channel_id=1, source_target_pairs={{0,16},{16,0},{1,17},{17,1},{2,18},{18,2},{3,19},{19,3},{4,20},{20... | collective-permute-start | bytes 786440 | tf_op jit(solution)/shard_map/ppermute | solution.py:32
  7.5 2.6 %project.5 = (f32[512,256]{1,0:T(8,128)S(1)}, f32[512,512]{1,0:T(8,128)S(1)}, f32[512,512]{1,0:T(8,128)S(1)}, bf16[512,512]{1,0:T(8,128)(2,1)S(1)}) custom-call(s32[3]{0:T(128)S(1)} %pad_add_fusion.ranks, f32[2048,512]{1,0:T(8,128)} %mom.7, bf16[2048,512]{1,0:T(8,128)(2,1)} %grad.7, bf16[512,256]{1,0:T(8,128)(2,1)S(1)} %get-tuple-element.54.refs_0_, ...), custom_call_target="tpu_custom_call" | custom-call | flops 10000000000 | bytes 1 | tf_op jit(solution)/shard_map/project/pallas_call | solution.py:154
  10.1 2.6 %project.6 = (bf16[512,256]{1,0:T(8,128)(2,1)S(1)}, f32[512,512]{1,0:T(8,128)S(1)}, f32[512,512]{1,0:T(8,128)S(1)}, bf16[512,512]{1,0:T(8,128)(2,1)S(1)}) custom-call(s32[3]{0:T(128)S(1)} %pad_add_fusion.ranks, f32[2048,512]{1,0:T(8,128)} %mom.7, bf16[2048,512]{1,0:T(8,128)(2,1)} %grad.7, bf16[512,256]{1,0:T(8,128)(2,1)S(1)} %get-tuple-element.54.refs_0_, ...), custom_call_target="tpu_custom_call" | custom-call | flops 1 | bytes 1 | tf_op jit(solution)/shard_map/project/pallas_call | solution.py:154
  13.9 1.9 %collective-permute-start.2 = (bf16[256,256]{1,0:T(8,128)(2,1)S(1)}, bf16[256,256]{1,0:T(8,128)(2,1)S(1)}, u32[]{:S(2)}, u32[]{:S(2)}) collective-permute-start(bf16[256,256]{1,0:T(8,128)(2,1)S(1)} %get-tuple-element.64.refs_4_), channel_id=1, source_target_pairs={{0,1},{1,0},{2,3},{3,2},{4,5},{5,4},{6,7},{7,6},{8,9},{9,8},{10,11... | collective-permute-start | bytes 393224 | tf_op jit(solution)/shard_map/ppermute | solution.py:32
  15.8 3.1 %collective-permute-done.2.refs_1_ = bf16[256,256]{1,0:T(8,128)(2,1)S(1)} collective-permute-done((bf16[256,256]{1,0:T(8,128)(2,1)S(1)}, bf16[256,256]{1,0:T(8,128)(2,1)S(1)}, u32[]{:S(2)}, u32[]{:S(2)}) %collective-permute-start.2) | collective-permute-done | bytes 131104 | tf_op jit(solution)/shard_map/ppermute | solution.py:32
  19.0 2.9 %collective-permute-start.3 = (bf16[256,256]{1,0:T(8,128)(2,1)S(1)}, bf16[256,256]{1,0:T(8,128)(2,1)S(1)}, u32[]{:S(2)}, u32[]{:S(2)}) collective-permute-start(bf16[256,256]{1,0:T(8,128)(2,1)S(1)} %sum_parts.7), channel_id=1, source_target_pairs={{0,2},{1,3},{2,0},{3,1},{4,6},{5,7},{6,4},{7,5},{8,10},{9,11},{10,... | collective-permute-start | bytes 393224 | tf_op jit(solution)/shard_map/ppermute | solution.py:32
  21.9 1.6 %collective-permute-start.5 = (bf16[2,2,64,128]{3,2,1,0:T(8,128)(2,1)S(1)}, bf16[2,2,64,128]{3,2,1,0:T(8,128)(2,1)S(1)}, u32[]{:S(2)}, u32[]{:S(2)}) collective-permute-start(bf16[2,2,64,128]{3,2,1,0:T(8,128)(2,1)S(1)} %pack_prompts.1.refs_0_), channel_id=1, source_target_pairs={{0,16},{16,0},{1,17},{17,1},{2,18},{18,2},{3,19},{19,3},{4,20},{20... | collective-permute-start | bytes 196616 | tf_op jit(solution)/shard_map/ppermute | solution.py:32
  23.5 1.4 %project.7 = (f32[512,256]{1,0:T(8,128)S(1)}, f32[512,512]{1,0:T(8,128)S(1)}) custom-call(s32[3]{0:T(128)S(1)} %pad_add_fusion.ranks, f32[2048,512]{1,0:T(8,128)} %mom.7, bf16[2048,512]{1,0:T(8,128)(2,1)} %grad.7, bf16[512,256]{1,0:T(8,128)(2,1)S(1)} %get-tuple-element.54.refs_0_, bf16[512,256]{1,0:T(8,128)(2,1)S(1)} %get-tuple-element.55.refs_1_, ...), custom_call_target="tpu_custom_call" | custom-call | flops 1 | bytes 1 | tf_op jit(solution)/shard_map/project/pallas_call | solution.py:154
  25.0 1.6 %collective-permute-start.4 = (bf16[256,256]{1,0:T(8,128)(2,1)S(1)}, bf16[256,256]{1,0:T(8,128)(2,1)S(1)}, u32[]{:S(2)}, u32[]{:S(2)}) collective-permute-start(bf16[256,256]{1,0:T(8,128)(2,1)S(1)} %get-tuple-element.69.refs_2_), channel_id=1, source_target_pairs={{0,1},{1,0},{2,3},{3,2},{4,5},{5,4},{6,7},{7,6},{8,9},{9,8},{10,11... | collective-permute-start | bytes 393224 | tf_op jit(solution)/shard_map/ppermute | solution.py:32
  27.6 1.6 %collective-permute-start.7 = (bf16[2,64,128]{2,1,0:T(8,128)(2,1)S(1)}, bf16[2,64,128]{2,1,0:T(8,128)(2,1)S(1)}, u32[]{:S(2)}, u32[]{:S(2)}) collective-permute-start(bf16[2,64,128]{2,1,0:T(8,128)(2,1)S(1)} %get-tuple-element.71), channel_id=1, source_target_pairs={{0,8},{4,12},{8,0},{12,4},{1,9},{5,13},{9,1},{13,5},{2,10},{6,14},... | collective-permute-start | bytes 98312 | tf_op jit(solution)/shard_map/ppermute | solution.py:32
  29.5 2.0 %collective-permute-done.7.refs_3_.refs_2_ = bf16[2,64,128]{2,1,0:T(8,128)(2,1)S(1)} collective-permute-done((bf16[2,64,128]{2,1,0:T(8,128)(2,1)S(1)}, bf16[2,64,128]{2,1,0:T(8,128)(2,1)S(1)}, u32[]{:S(2)}, u32[]{:S(2)}) %collective-permute-start.7) | collective-permute-done | bytes 32800 | tf_op jit(solution)/shard_map/ppermute | solution.py:32
  34.8 1.6 %collective-permute-start.12 = (bf16[256,256]{1,0:T(8,128)(2,1)S(1)}, bf16[256,256]{1,0:T(8,128)(2,1)S(1)}, u32[]{:S(2)}, u32[]{:S(2)}) collective-permute-start(bf16[256,256]{1,0:T(8,128)(2,1)S(1)} %sum_parts.9.refs_4_.refs_0_), channel_id=1, source_target_pairs={{0,16},{16,0},{1,17},{17,1},{2,18},{18,2},{3,19},{19,3},{4,20},{20... | collective-permute-start | bytes 393224 | tf_op jit(solution)/shard_map/ppermute | solution.py:32
  36.4 3.3 %attention.2 = (bf16[256,512]{1,0:T(8,128)(2,1)S(1)}, f32[512,128]{1,0:T(8,128)S(1)}, f32[512,128]{1,0:T(8,128)S(1)}) custom-call(s32[3]{0:T(128)S(1)} %pad_add_fusion.ranks, s32[4]{0:T(128)S(1)} %copy-done.6, s32[4]{0:T(128)S(1)} %copy-done.7, s32[1]{0:T(128)S(6)} %copy.21.resp_blocks, bf16[256,1024]{1,0:T(8,128)(2,1)S(1)} %copy-done, ...), custom_call_target="tpu_custom_call" | custom-call | flops 1 | bytes 1 | tf_op jit(solution)/shard_map/attention/pallas_call | solution.py:745
  40.2 2.6 %collective-permute-done.10.refs_0_.refs_2_ = bf16[256,256]{1,0:T(8,128)(2,1)S(1)} collective-permute-done((bf16[256,256]{1,0:T(8,128)(2,1)S(1)}, bf16[256,256]{1,0:T(8,128)(2,1)S(1)}, u32[]{:S(2)}, u32[]{:S(2)}) %collective-permute-start.10) | collective-permute-done | bytes 131104 | tf_op jit(solution)/shard_map/ppermute | solution.py:32
  42.8 1.6 %collective-permute-start.14 = (bf16[256,256]{1,0:T(8,128)(2,1)S(1)}, bf16[256,256]{1,0:T(8,128)(2,1)S(1)}, u32[]{:S(2)}, u32[]{:S(2)}) collective-permute-start(bf16[256,256]{1,0:T(8,128)(2,1)S(1)} %relay.2.refs_6_), channel_id=1, source_target_pairs={{0,16},{16,0},{1,17},{17,1},{2,18},{18,2},{3,19},{19,3},{4,20},{20... | collective-permute-start | bytes 393224 | tf_op jit(solution)/shard_map/ppermute | solution.py:32
  44.3 3.2 %attention.3 = (bf16[256,512]{1,0:T(8,128)(2,1)S(1)}, bf16[2,256,128]{2,1,0:T(8,128)(2,1)S(1)}, f32[2,64,128]{2,1,0:T(8,128)S(1)}, bf16[2,64,128]{2,1,0:T(8,128)...) custom-call(s32[3]{0:T(128)S(1)} %pad_add_fusion.ranks, s32[4]{0:T(128)S(1)} %copy-done.6, ...), custom_call_target="tpu_custom_call" | custom-call | flops 1 | bytes 1 | tf_op jit(solution)/shard_map/attention/pallas_call | solution.py:745
  47.8 1.5 %collective-permute-done.11.refs_0_.refs_3_ = bf16[256,256]{1,0:T(8,128)(2,1)S(1)} collective-permute-done((bf16[256,256]{1,0:T(8,128)(2,1)S(1)}, bf16[256,256]{1,0:T(8,128)(2,1)S(1)}, u32[]{:S(2)}, u32[]{:S(2)}) %collective-permute-start.11) | collective-permute-done | bytes 131104 | tf_op jit(solution)/shard_map/ppermute | solution.py:32
  51.8 2.6 %collective-permute-done.15.refs_7_ = bf16[256,256]{1,0:T(8,128)(2,1)S(1)} collective-permute-done((bf16[256,256]{1,0:T(8,128)(2,1)S(1)}, bf16[256,256]{1,0:T(8,128)(2,1)S(1)}, u32[]{:S(2)}, u32[]{:S(2)}) %collective-permute-start.15) | collective-permute-done | bytes 131104 | tf_op jit(solution)/shard_map/ppermute | solution.py:32
  59.1 5.6 %collective-permute-done.17.refs_1_ = f32[384,128]{1,0:T(8,128)S(1)} collective-permute-done((f32[384,128]{1,0:T(8,128)S(1)}, f32[384,128]{1,0:T(8,128)S(1)}, u32[]{:S(2)}, u32[]{:S(2)}) %collective-permute-start.17) | collective-permute-done | bytes 196640 | tf_op jit(solution)/shard_map/ppermute | solution.py:32
  64.7 9.7 %inverse_factor.1.x = f32[256,256]{1,0:T(8,128)S(1)} custom-call(f32[384,128]{1,0:T(8,128)S(1)} %sum_parts.10.refs_0_.refs_2_, f32[384,128]{1,0:T(8,128)S(1)} %collective-permute-done.17.refs_1_), custom_call_target="tpu_custom_call" | custom-call | flops 2000000000 | bytes 1 | tf_op jit(solution)/shard_map/inverse_factor/pallas_call | solution.py:421
  76.9 2.6 %collective-permute-start.23 = (f32[8,256]{1,0:T(8,128)S(1)}, f32[8,256]{1,0:T(8,128)S(1)}, u32[]{:S(2)}, u32[]{:S(2)}) collective-permute-start(f32[8,256]{1,0:T(8,128)S(1)} %get-tuple-element.91.refs_4_.refs_0_), channel_id=1, source_target_pairs={{0,1},{1,0},{2,3},{3,2},{4,5},{5,4},{6,7},{7,6},{8,9},{9,8},{10,11... | collective-permute-start | bytes 24584 | tf_op jit(solution)/shard_map/ppermute | solution.py:32
  82.4 2.9 %new_momentum.1 = (f32[2048,512]{1,0:T(8,128)}, bf16[256,1024]{1,0:T(8,128)(2,1)}, bf16[2,256,128]{2,1,0:T(8,128)(2,1)}, f32[8,128]{1,0:T(8,128)}) custom-call(s32[3]{0:T(128)S(1)} %pad_add_fusion.ranks, bf16[2048,256]{1,0:T(8,128)(2,1)S(1)} %get-tuple-element.77.pcat, bf16[256,512]{1,0:T(8,128)(2,1)S(1)} %get-tuple-element.87.y, ...), custom_call_target="tpu_custom_call" | custom-call | flops 5000000000 | bytes 1 | tf_op jit(solution)/shard_map/new_momentum/pallas_call | solution.py:518
  85.3 3.6 %final_update.1 = (bf16[2048,512]{1,0:T(8,128)(2,1)}, f32[512,256]{1,0:T(8,128)}, f32[2048,512]{1,0:T(8,128)}, f32[2,2,64,128]{3,2,1,0:T(8,128)}) custom-call(s32[3]{0:T(128)S(1)} %pad_add_fusion.ranks, bf16[2048,256]{1,0:T(8,128)(2,1)S(1)} %get-tuple-element.77.pcat, f32[256,256]{1,0:T(8,128)S(1)} %inverse_factor.1.x, ...), custom_call_target="tpu_custom_call", output_to_operand_aliasing={{2}: (10, {})} | custom-call | flops 5000000000 | bytes 1 | tf_op jit(solution)/shard_map/final_update/pallas_call | solution.py:581
  (77 shorter events, 18.5 us)
Async XLA Ops:
  4.5 9.3 %collective-permute-start = (bf16[512,256]{1,0:T(8,128)(2,1)S(1)}, bf16[512,256]{1,0:T(8,128)(2,1)S(1)}, u32[]{:S(2)}, u32[]{:S(2)}) collective-permute-start(bf16[512,256]{1,0:T(8,128)(2,1)S(1)} %get-tuple-element.63), channel_id=1, source_target_pairs={{0,16},{16,0},{1,17},{17,1},{2,18},{18,2},{3,19},{19,3},{4,20},{20... | collective-permute-start | bytes 786440 | tf_op jit(solution)/shard_map/ppermute | solution.py:32
  12.7 12.2 %collective-permute-start.1 = (bf16[512,256]{1,0:T(8,128)(2,1)S(1)}, bf16[512,256]{1,0:T(8,128)(2,1)S(1)}, u32[]{:S(2)}, u32[]{:S(2)}) collective-permute-start(bf16[512,256]{1,0:T(8,128)(2,1)S(1)} %get-tuple-element.66.refs_2_), channel_id=1, source_target_pairs={{0,16},{16,0},{1,17},{17,1},{2,18},{18,2},{3,19},{19,3},{4,20},{20... | collective-permute-start | bytes 786440 | tf_op jit(solution)/shard_map/ppermute | solution.py:32
  13.9 5.0 %collective-permute-start.2 = (bf16[256,256]{1,0:T(8,128)(2,1)S(1)}, bf16[256,256]{1,0:T(8,128)(2,1)S(1)}, u32[]{:S(2)}, u32[]{:S(2)}) collective-permute-start(bf16[256,256]{1,0:T(8,128)(2,1)S(1)} %get-tuple-element.64.refs_4_), channel_id=1, source_target_pairs={{0,1},{1,0},{2,3},{3,2},{4,5},{5,4},{6,7},{7,6},{8,9},{9,8},{10,11... | collective-permute-start | bytes 393224 | tf_op jit(solution)/shard_map/ppermute | solution.py:32
  19.0 10.5 %collective-permute-start.3 = (bf16[256,256]{1,0:T(8,128)(2,1)S(1)}, bf16[256,256]{1,0:T(8,128)(2,1)S(1)}, u32[]{:S(2)}, u32[]{:S(2)}) collective-permute-start(bf16[256,256]{1,0:T(8,128)(2,1)S(1)} %sum_parts.7), channel_id=1, source_target_pairs={{0,2},{1,3},{2,0},{3,1},{4,6},{5,7},{6,4},{7,5},{8,10},{9,11},{10,... | collective-permute-start | bytes 393224 | tf_op jit(solution)/shard_map/ppermute | solution.py:32
  21.9 4.7 %collective-permute-start.5 = (bf16[2,2,64,128]{3,2,1,0:T(8,128)(2,1)S(1)}, bf16[2,2,64,128]{3,2,1,0:T(8,128)(2,1)S(1)}, u32[]{:S(2)}, u32[]{:S(2)}) collective-permute-start(bf16[2,2,64,128]{3,2,1,0:T(8,128)(2,1)S(1)} %pack_prompts.1.refs_0_), channel_id=1, source_target_pairs={{0,16},{16,0},{1,17},{17,1},{2,18},{18,2},{3,19},{19,3},{4,20},{20... | collective-permute-start | bytes 196616 | tf_op jit(solution)/shard_map/ppermute | solution.py:32
  25.0 7.5 %collective-permute-start.4 = (bf16[256,256]{1,0:T(8,128)(2,1)S(1)}, bf16[256,256]{1,0:T(8,128)(2,1)S(1)}, u32[]{:S(2)}, u32[]{:S(2)}) collective-permute-start(bf16[256,256]{1,0:T(8,128)(2,1)S(1)} %get-tuple-element.69.refs_2_), channel_id=1, source_target_pairs={{0,1},{1,0},{2,3},{3,2},{4,5},{5,4},{6,7},{7,6},{8,9},{9,8},{10,11... | collective-permute-start | bytes 393224 | tf_op jit(solution)/shard_map/ppermute | solution.py:32
  27.6 4.0 %collective-permute-start.7 = (bf16[2,64,128]{2,1,0:T(8,128)(2,1)S(1)}, bf16[2,64,128]{2,1,0:T(8,128)(2,1)S(1)}, u32[]{:S(2)}, u32[]{:S(2)}) collective-permute-start(bf16[2,64,128]{2,1,0:T(8,128)(2,1)S(1)} %get-tuple-element.71), channel_id=1, source_target_pairs={{0,8},{4,12},{8,0},{12,4},{1,9},{5,13},{9,1},{13,5},{2,10},{6,14},... | collective-permute-start | bytes 98312 | tf_op jit(solution)/shard_map/ppermute | solution.py:32
  32.5 7.1 %collective-permute-start.9 = (bf16[256,256]{1,0:T(8,128)(2,1)S(1)}, bf16[256,256]{1,0:T(8,128)(2,1)S(1)}, u32[]{:S(2)}, u32[]{:S(2)}) collective-permute-start(bf16[256,256]{1,0:T(8,128)(2,1)S(1)} %sum_parts.9.refs_4_.refs_0_), channel_id=1, source_target_pairs={{0,1},{1,0},{2,3},{3,2},{4,5},{5,4},{6,7},{7,6},{8,9},{9,8},{10,11... | collective-permute-start | bytes 393224 | tf_op jit(solution)/shard_map/ppermute | solution.py:32
  33.8 9.0 %collective-permute-start.10 = (bf16[256,256]{1,0:T(8,128)(2,1)S(1)}, bf16[256,256]{1,0:T(8,128)(2,1)S(1)}, u32[]{:S(2)}, u32[]{:S(2)}) collective-permute-start(bf16[256,256]{1,0:T(8,128)(2,1)S(1)} %sum_parts.9.refs_4_.refs_0_), channel_id=1, source_target_pairs={{0,2},{1,3},{2,0},{3,1},{4,6},{5,7},{6,4},{7,5},{8,10},{9,11},{10,... | collective-permute-start | bytes 393224 | tf_op jit(solution)/shard_map/ppermute | solution.py:32
  34.8 12.8 %collective-permute-start.12 = (bf16[256,256]{1,0:T(8,128)(2,1)S(1)}, bf16[256,256]{1,0:T(8,128)(2,1)S(1)}, u32[]{:S(2)}, u32[]{:S(2)}) collective-permute-start(bf16[256,256]{1,0:T(8,128)(2,1)S(1)} %sum_parts.9.refs_4_.refs_0_), channel_id=1, source_target_pairs={{0,16},{16,0},{1,17},{17,1},{2,18},{18,2},{3,19},{19,3},{4,20},{20... | collective-permute-start | bytes 393224 | tf_op jit(solution)/shard_map/ppermute | solution.py:32
  39.6 7.9 %collective-permute-start.13 = (bf16[256,256]{1,0:T(8,128)(2,1)S(1)}, bf16[256,256]{1,0:T(8,128)(2,1)S(1)}, u32[]{:S(2)}, u32[]{:S(2)}) collective-permute-start(bf16[256,256]{1,0:T(8,128)(2,1)S(1)} %collective-permute-done.9.refs_1_), channel_id=1, source_target_pairs={{0,16},{16,0},{1,17},{17,1},{2,18},{18,2},{3,19},{19,3},{4,20},{20... | collective-permute-start | bytes 393224 | tf_op jit(solution)/shard_map/ppermute | solution.py:32
  42.8 5.0 %collective-permute-start.14 = (bf16[256,256]{1,0:T(8,128)(2,1)S(1)}, bf16[256,256]{1,0:T(8,128)(2,1)S(1)}, u32[]{:S(2)}, u32[]{:S(2)}) collective-permute-start(bf16[256,256]{1,0:T(8,128)(2,1)S(1)} %relay.2.refs_6_), channel_id=1, source_target_pairs={{0,16},{16,0},{1,17},{17,1},{2,18},{18,2},{3,19},{19,3},{4,20},{20... | collective-permute-start | bytes 393224 | tf_op jit(solution)/shard_map/ppermute | solution.py:32
  44.3 5.0 %collective-permute-start.11 = (bf16[256,256]{1,0:T(8,128)(2,1)S(1)}, bf16[256,256]{1,0:T(8,128)(2,1)S(1)}, u32[]{:S(2)}, u32[]{:S(2)}) collective-permute-start(bf16[256,256]{1,0:T(8,128)(2,1)S(1)} %relay.2.refs_6_), channel_id=1, source_target_pairs={{0,1},{1,0},{2,3},{3,2},{4,5},{5,4},{6,7},{7,6},{8,9},{9,8},{10,11... | collective-permute-start | bytes 393224 | tf_op jit(solution)/shard_map/ppermute | solution.py:32
  49.3 5.0 %collective-permute-start.15 = (bf16[256,256]{1,0:T(8,128)(2,1)S(1)}, bf16[256,256]{1,0:T(8,128)(2,1)S(1)}, u32[]{:S(2)}, u32[]{:S(2)}) collective-permute-start(bf16[256,256]{1,0:T(8,128)(2,1)S(1)} %relay.3), channel_id=1, source_target_pairs={{0,16},{16,0},{1,17},{17,1},{2,18},{18,2},{3,19},{19,3},{4,20},{20... | collective-permute-start | bytes 393224 | tf_op jit(solution)/shard_map/ppermute | solution.py:32
  49.9 5.0 %collective-permute-start.18 = (bf16[2,64,128]{2,1,0:T(8,128)(2,1)S(1)}, bf16[2,64,128]{2,1,0:T(8,128)(2,1)S(1)}, u32[]{:S(2)}, u32[]{:S(2)}) collective-permute-start(bf16[2,64,128]{2,1,0:T(8,128)(2,1)S(1)} %get-tuple-element.84), channel_id=1, source_target_pairs={{0,4},{4,0},{8,12},{12,8},{1,5},{5,1},{9,13},{13,9},{2,6},{6,2},{1... | collective-permute-start | bytes 98312 | tf_op jit(solution)/shard_map/ppermute | solution.py:32
  49.9 5.0 %collective-permute-start.19 = (bf16[2,64,128]{2,1,0:T(8,128)(2,1)S(1)}, bf16[2,64,128]{2,1,0:T(8,128)(2,1)S(1)}, u32[]{:S(2)}, u32[]{:S(2)}) collective-permute-start(bf16[2,64,128]{2,1,0:T(8,128)(2,1)S(1)} %get-tuple-element.85), channel_id=1, source_target_pairs={{0,8},{4,12},{8,0},{12,4},{1,9},{5,13},{9,1},{13,5},{2,10},{6,14},... | collective-permute-start | bytes 98312 | tf_op jit(solution)/shard_map/ppermute | solution.py:32
  50.8 4.2 %collective-permute-start.20 = (bf16[2,64,128]{2,1,0:T(8,128)(2,1)S(1)}, bf16[2,64,128]{2,1,0:T(8,128)(2,1)S(1)}, u32[]{:S(2)}, u32[]{:S(2)}) collective-permute-start(bf16[2,64,128]{2,1,0:T(8,128)(2,1)S(1)} %get-tuple-element.86), channel_id=1, source_target_pairs={{0,12},{4,8},{8,4},{12,0},{1,13},{5,9},{9,5},{13,1},{2,14},{6,10},... | collective-permute-start | bytes 98312 | tf_op jit(solution)/shard_map/ppermute | solution.py:32
  56.9 7.8 %collective-permute-start.17 = (f32[384,128]{1,0:T(8,128)S(1)}, f32[384,128]{1,0:T(8,128)S(1)}, u32[]{:S(2)}, u32[]{:S(2)}) collective-permute-start(f32[384,128]{1,0:T(8,128)S(1)} %sum_parts.10.refs_0_.refs_2_), channel_id=1, source_target_pairs={{0,8},{4,12},{8,0},{12,4},{1,9},{5,13},{9,1},{13,5},{2,10},{6,14},... | collective-permute-start | bytes 589832 | tf_op jit(solution)/shard_map/ppermute | solution.py:32
  58.1 16.3 %collective-permute-start.22 = (bf16[256,512]{1,0:T(8,128)(2,1)S(1)}, bf16[256,512]{1,0:T(8,128)(2,1)S(1)}, u32[]{:S(2)}, u32[]{:S(2)}) collective-permute-start(bf16[256,512]{1,0:T(8,128)(2,1)S(1)} %sum_parts.11.wa), channel_id=1, source_target_pairs={{0,8},{4,12},{8,0},{12,4},{1,9},{5,13},{9,1},{13,5},{2,10},{6,14},... | collective-permute-start | bytes 786440 | tf_op jit(solution)/shard_map/ppermute | solution.py:32
  75.1 5.7 %collective-permute-start.25 = (f32[8,256]{1,0:T(8,128)S(1)}, f32[8,256]{1,0:T(8,128)S(1)}, u32[]{:S(2)}, u32[]{:S(2)}) collective-permute-start(f32[8,256]{1,0:T(8,128)S(1)} %get-tuple-element.91.refs_4_.refs_0_), channel_id=1, source_target_pairs={{0,3},{1,2},{2,1},{3,0},{4,7},{5,6},{6,5},{7,4},{8,11},{9,10},{10,... | collective-permute-start | bytes 24584 | tf_op jit(solution)/shard_map/ppermute | solution.py:32
  75.5 5.2 %collective-permute-start.24 = (f32[8,256]{1,0:T(8,128)S(1)}, f32[8,256]{1,0:T(8,128)S(1)}, u32[]{:S(2)}, u32[]{:S(2)}) collective-permute-start(f32[8,256]{1,0:T(8,128)S(1)} %get-tuple-element.91.refs_4_.refs_0_), channel_id=1, source_target_pairs={{0,2},{1,3},{2,0},{3,1},{4,6},{5,7},{6,4},{7,5},{8,10},{9,11},{10,... | collective-permute-start | bytes 24584 | tf_op jit(solution)/shard_map/ppermute | solution.py:32
  76.9 4.2 %collective-permute-start.23 = (f32[8,256]{1,0:T(8,128)S(1)}, f32[8,256]{1,0:T(8,128)S(1)}, u32[]{:S(2)}, u32[]{:S(2)}) collective-permute-start(f32[8,256]{1,0:T(8,128)S(1)} %get-tuple-element.91.refs_4_.refs_0_), channel_id=1, source_target_pairs={{0,1},{1,0},{2,3},{3,2},{4,5},{5,4},{6,7},{7,6},{8,9},{9,8},{10,11... | collective-permute-start | bytes 24584 | tf_op jit(solution)/shard_map/ppermute | solution.py:32
  80.2 5.1 %collective-permute-start.27 = (bf16[2,2,64,128]{3,2,1,0:T(8,128)(2,1)S(1)}, bf16[2,2,64,128]{3,2,1,0:T(8,128)(2,1)S(1)}, u32[]{:S(2)}, u32[]{:S(2)}) collective-permute-start(bf16[2,2,64,128]{3,2,1,0:T(8,128)(2,1)S(1)} %get-tuple-element.92.refs_4_), channel_id=1, source_target_pairs={{0,16},{16,0},{1,17},{17,1},{2,18},{18,2},{3,19},{19,3},{4,20},{20... | collective-permute-start | bytes 196616 | tf_op jit(solution)/shard_map/ppermute | solution.py:32
  81.2 4.1 %collective-permute-start.26 = (f32[8,256]{1,0:T(8,128)S(1)}, f32[8,256]{1,0:T(8,128)S(1)}, u32[]{:S(2)}, u32[]{:S(2)}) collective-permute-start(f32[8,256]{1,0:T(8,128)S(1)} %sum_parts.12.refs_5_.refs_0_), channel_id=1, source_target_pairs={{0,16},{16,0},{1,17},{17,1},{2,18},{18,2},{3,19},{19,3},{4,20},{20... | collective-permute-start | bytes 24584 | tf_op jit(solution)/shard_map/ppermute | solution.py:32
  (13 other events, 73.4 us)

commit v12 on v10

--- a/solution.py
+++ b/solution.py
@@ -870,26 +870,24 @@
                 hops[k - low] = relay([along[k - low]], (earlier[1],))
             along[k] = swap(hops[k - low], "head", low)
     last = n_head - 1
-    passed = [
-        [swap(hops.get(k, along[k]), "resp", j) for k in range(last)] for j in range(1, n_resp)
-    ]
-    sent_last = relay([along[last]], (earlier[1], *[c for row in passed for c in row]))
+    passed = [[swap(hops.get(k, along[k]), "resp", j) for k in range(last)] for j in range(1, n_resp)]
+    dq_parts, resp_grad, *parts = attention(heads[1], earlier, *held, tuple(hops.values()))
+    sent_last = relay([along[last]], (parts[0], *[c for row in passed for c in row[:later]]))
     chunks = [along[k] for k in range(n_head)]
     for j in range(1, n_resp):
         chunks += passed[j - 1] + [swap(sent_last, "resp", j)]
-    dq_parts, resp_grad, *parts = attention(heads[1], earlier, *held, (sent_last,))
     dq_parts = (earlier[0], dq_parts)
-    pcat, pcat_t, gram = gather_gram(chunks, (parts[0],))
+    pcat, pcat_t, gram = gather_gram(chunks, ())
 
     bits = [1 << b for b in range(n_fsdp.bit_length() - 1)]
-    w = back_part(pcat_t, totals, (gram,))
+    returned = [parts[0]] + [swap(parts[k], "fsdp", k) for k in range(1, n_fsdp)]
+    w = back_part(pcat_t, totals, (gram, *returned[1:]))
     for bit in bits[:-1]:
         gram = sum_parts([gram, swap(gram, "fsdp", bit)], F32, (), 3)
     gram_parts = (gram, swap(gram, "fsdp", bits[-1]))
     for bit in bits[:-1]:
-        w = sum_parts([w, swap(w, "fsdp", bit)], BF16, (gram,), 5)
+        w = sum_parts([w, swap(w, "fsdp", bit)], BF16, (gram_parts[1],), 0)
     w_other = swap(w, "fsdp", bits[-1])
-    returned = [parts[0]] + [swap(parts[k], "fsdp", k) for k in range(1, n_fsdp)]
     x = inverse_factor(*gram_parts)
     bt, y, squares = back_full(x, w, w_other, tuple(returned[1:]))
     from_head = [swap(squares, "head", k) for k in range(1, n_head)]

time: 87 us -> 85.9 us (0.987)
  waiting for transfers between devices: 16.4 us -> 14.4 us
  starting transfers between devices: 31.1 us -> 32 us
    ppermute x28, waiting for transfers between devices: 16.4 us -> 14.4 us  [swap(): return lax.ppermute(value, axes, [(i, i ^ k) for i in range(n)])]
    ppermute x28, starting transfers between devices: 31.1 us -> 32 us  [swap(): return lax.ppermute(value, axes, [(i, i ^ k) for i in range(n)])]
  transfers between devices with their start and end apart: 28 -> 28, of which waited for: 11 -> 8; matrix products, arithmetic and copies ran while one was open for 0% -> 0% of each run, Pallas kernels for 33% -> 34%
where the time goes in v12:
time: 85.9 us; the launch traced here: 85.7 us
  Pallas kernels  37.4 us (44%)
  starting transfers between devices  32 us (37%)
  waiting for transfers between devices  14.4 us (17%)
  between operations  1.75 us (2%)
    ppermute x28, starting transfers between devices, swap(): return lax.ppermute(value, axes, [(i, i ^ k) for i in range(n)])  32 us
    ppermute x28, waiting for transfers between devices, swap(): return lax.ppermute(value, axes, [(i, i ^ k) for i in range(n)])  14.4 us
    pallas_call x4, Pallas kernels, project(): pl.pallas_call(functools.partial(project_kernel, n_head, part, following,...  10.4 us
    pallas_call x1, Pallas kernels, inverse_factor(): pl.pallas_call(functools.partial(cholesky_kernel, len(parts)), in_specs=[...  9.7 us
    pallas_call x2, Pallas kernels, attention(): pl.pallas_call(functools.partial(attention_kernel, n_fsdp, heads, last),...  6.48 us
    pallas_call x1, Pallas kernels, final_update(): pl.pallas_call(functools.partial(update_kernel, gain, n_resp, n_head, len...  3.6 us
    pallas_call x1, Pallas kernels, new_momentum(): pl.pallas_call(functools.partial(momentum_kernel, n_resp, n_head, len(tot...  2.92 us
  transfers between devices with their start and end apart: 28, of which 8 were waited for; matrix products, arithmetic and copies ran while one was open for 0% of the time, Pallas kernels for 34%

profile of v12, /device:TPU:0, one launch (start us, length us, event | category | flops | bytes accessed | tf_op | source)
XLA Modules:
  0.0 85.7 jit_solution(17429587776086275015)
XLA Ops:
  0.7 3.8 %project.4 = (bf16[512,256]{1,0:T(8,128)(2,1)S(1)}, f32[512,512]{1,0:T(8,128)S(1)}, bf16[512,256]{1,0:T(8,128)(2,1)S(1)}, bf16[512,256]{1,0:T(8,128)(2,1)S(1)}, ...) custom-call(s32[3]{0:T(128)S(1)} %pad_add_fusion.ranks, f32[2048,512]{1,0:T(8,128)} %mom.7, bf16[2048,512]{1,0:T(8,128)(2,1)} %grad.7, ...), custom_call_target="tpu_custom_call" | custom-call | flops 1 | bytes 1 | tf_op jit(solution)/shard_map/project/pallas_call | solution.py:154
  4.5 3.0 %collective-permute-start = (bf16[512,256]{1,0:T(8,128)(2,1)S(1)}, bf16[512,256]{1,0:T(8,128)(2,1)S(1)}, u32[]{:S(2)}, u32[]{:S(2)}) collective-permute-start(bf16[512,256]{1,0:T(8,128)(2,1)S(1)} %get-tuple-element.63), channel_id=1, source_target_pairs={{0,16},{16,0},{1,17},{17,1},{2,18},{18,2},{3,19},{19,3},{4,20},{20... | collective-permute-start | bytes 786440 | tf_op jit(solution)/shard_map/ppermute | solution.py:32
  7.5 2.6 %project.5 = (f32[512,256]{1,0:T(8,128)S(1)}, f32[512,512]{1,0:T(8,128)S(1)}, f32[512,512]{1,0:T(8,128)S(1)}, bf16[512,512]{1,0:T(8,128)(2,1)S(1)}) custom-call(s32[3]{0:T(128)S(1)} %pad_add_fusion.ranks, f32[2048,512]{1,0:T(8,128)} %mom.7, bf16[2048,512]{1,0:T(8,128)(2,1)} %grad.7, bf16[512,256]{1,0:T(8,128)(2,1)S(1)} %get-tuple-element.54.refs_0_, ...), custom_call_target="tpu_custom_call" | custom-call | flops 10000000000 | bytes 1 | tf_op jit(solution)/shard_map/project/pallas_call | solution.py:154
  10.1 2.6 %project.6 = (bf16[512,256]{1,0:T(8,128)(2,1)S(1)}, f32[512,512]{1,0:T(8,128)S(1)}, f32[512,512]{1,0:T(8,128)S(1)}, bf16[512,512]{1,0:T(8,128)(2,1)S(1)}) custom-call(s32[3]{0:T(128)S(1)} %pad_add_fusion.ranks, f32[2048,512]{1,0:T(8,128)} %mom.7, bf16[2048,512]{1,0:T(8,128)(2,1)} %grad.7, bf16[512,256]{1,0:T(8,128)(2,1)S(1)} %get-tuple-element.54.refs_0_, ...), custom_call_target="tpu_custom_call" | custom-call | flops 1 | bytes 1 | tf_op jit(solution)/shard_map/project/pallas_call | solution.py:154
  13.9 3.9 %collective-permute-start.3 = (bf16[256,256]{1,0:T(8,128)(2,1)S(1)}, bf16[256,256]{1,0:T(8,128)(2,1)S(1)}, u32[]{:S(2)}, u32[]{:S(2)}) collective-permute-start(bf16[256,256]{1,0:T(8,128)(2,1)S(1)} %get-tuple-element.68), channel_id=1, source_target_pairs={{0,3},{1,2},{2,1},{3,0},{4,7},{5,6},{6,5},{7,4},{8,11},{9,10},{10,... | collective-permute-start | bytes 393224 | tf_op jit(solution)/shard_map/ppermute | solution.py:32
  17.8 1.6 %collective-permute-start.5 = (bf16[2,2,64,128]{3,2,1,0:T(8,128)(2,1)S(1)}, bf16[2,2,64,128]{3,2,1,0:T(8,128)(2,1)S(1)}, u32[]{:S(2)}, u32[]{:S(2)}) collective-permute-start(bf16[2,2,64,128]{3,2,1,0:T(8,128)(2,1)S(1)} %pack_prompts.1.refs_0_), channel_id=1, source_target_pairs={{0,16},{16,0},{1,17},{17,1},{2,18},{18,2},{3,19},{19,3},{4,20},{20... | collective-permute-start | bytes 196616 | tf_op jit(solution)/shard_map/ppermute | solution.py:32
  19.4 1.4 %project.7 = (f32[512,256]{1,0:T(8,128)S(1)}, f32[512,512]{1,0:T(8,128)S(1)}) custom-call(s32[3]{0:T(128)S(1)} %pad_add_fusion.ranks, f32[2048,512]{1,0:T(8,128)} %mom.7, bf16[2048,512]{1,0:T(8,128)(2,1)} %grad.7, bf16[512,256]{1,0:T(8,128)(2,1)S(1)} %get-tuple-element.54.refs_0_, bf16[512,256]{1,0:T(8,128)(2,1)S(1)} %get-tuple-element.55.refs_1_, ...), custom_call_target="tpu_custom_call" | custom-call | flops 1 | bytes 1 | tf_op jit(solution)/shard_map/project/pallas_call | solution.py:154
  21.3 1.6 %collective-permute-start.4 = (bf16[256,256]{1,0:T(8,128)(2,1)S(1)}, bf16[256,256]{1,0:T(8,128)(2,1)S(1)}, u32[]{:S(2)}, u32[]{:S(2)}) collective-permute-start(bf16[256,256]{1,0:T(8,128)(2,1)S(1)} %get-tuple-element.69.refs_2_), channel_id=1, source_target_pairs={{0,1},{1,0},{2,3},{3,2},{4,5},{5,4},{6,7},{7,6},{8,9},{9,8},{10,11... | collective-permute-start | bytes 393224 | tf_op jit(solution)/shard_map/ppermute | solution.py:32
  23.9 1.6 %collective-permute-start.7 = (bf16[2,64,128]{2,1,0:T(8,128)(2,1)S(1)}, bf16[2,64,128]{2,1,0:T(8,128)(2,1)S(1)}, u32[]{:S(2)}, u32[]{:S(2)}) collective-permute-start(bf16[2,64,128]{2,1,0:T(8,128)(2,1)S(1)} %get-tuple-element.71), channel_id=1, source_target_pairs={{0,8},{4,12},{8,0},{12,4},{1,9},{5,13},{9,1},{13,5},{2,10},{6,14},... | collective-permute-start | bytes 98312 | tf_op jit(solution)/shard_map/ppermute | solution.py:32
  25.8 2.3 %collective-permute-done.2.refs_1_ = bf16[256,256]{1,0:T(8,128)(2,1)S(1)} collective-permute-done((bf16[256,256]{1,0:T(8,128)(2,1)S(1)}, bf16[256,256]{1,0:T(8,128)(2,1)S(1)}, u32[]{:S(2)}, u32[]{:S(2)}) %collective-permute-start.2) | collective-permute-done | bytes 131104 | tf_op jit(solution)/shard_map/ppermute | solution.py:32
  28.9 1.6 %collective-permute-start.9 = (bf16[256,256]{1,0:T(8,128)(2,1)S(1)}, bf16[256,256]{1,0:T(8,128)(2,1)S(1)}, u32[]{:S(2)}, u32[]{:S(2)}) collective-permute-start(bf16[256,256]{1,0:T(8,128)(2,1)S(1)} %sum_parts.7.refs_4_.refs_0_), channel_id=1, source_target_pairs={{0,1},{1,0},{2,3},{3,2},{4,5},{5,4},{6,7},{7,6},{8,9},{9,8},{10,11... | collective-permute-start | bytes 393224 | tf_op jit(solution)/shard_map/ppermute | solution.py:32
  30.5 1.6 %collective-permute-start.10 = (bf16[256,256]{1,0:T(8,128)(2,1)S(1)}, bf16[256,256]{1,0:T(8,128)(2,1)S(1)}, u32[]{:S(2)}, u32[]{:S(2)}) collective-permute-start(bf16[256,256]{1,0:T(8,128)(2,1)S(1)} %sum_parts.7.refs_4_.refs_0_), channel_id=1, source_target_pairs={{0,2},{1,3},{2,0},{3,1},{4,6},{5,7},{6,4},{7,5},{8,10},{9,11},{10,... | collective-permute-start | bytes 393224 | tf_op jit(solution)/shard_map/ppermute | solution.py:32
  32.8 1.4 %collective-permute-start.12 = (bf16[256,256]{1,0:T(8,128)(2,1)S(1)}, bf16[256,256]{1,0:T(8,128)(2,1)S(1)}, u32[]{:S(2)}, u32[]{:S(2)}) collective-permute-start(bf16[256,256]{1,0:T(8,128)(2,1)S(1)} %sum_parts.7.refs_4_.refs_0_), channel_id=1, source_target_pairs={{0,16},{16,0},{1,17},{17,1},{2,18},{18,2},{3,19},{19,3},{4,20},{20... | collective-permute-start | bytes 393224 | tf_op jit(solution)/shard_map/ppermute | solution.py:32
  34.2 3.3 %attention.2 = (bf16[256,512]{1,0:T(8,128)(2,1)S(1)}, f32[512,128]{1,0:T(8,128)S(1)}, f32[512,128]{1,0:T(8,128)S(1)}) custom-call(s32[3]{0:T(128)S(1)} %pad_add_fusion.ranks, s32[4]{0:T(128)S(1)} %copy-done.6, s32[4]{0:T(128)S(1)} %copy-done.7, s32[1]{0:T(128)S(6)} %copy.21.resp_blocks, bf16[256,1024]{1,0:T(8,128)(2,1)S(1)} %copy-done, ...), custom_call_target="tpu_custom_call" | custom-call | flops 1 | bytes 1 | tf_op jit(solution)/shard_map/attention/pallas_call | solution.py:745
  38.3 1.8 %collective-permute-start.11 = (bf16[256,256]{1,0:T(8,128)(2,1)S(1)}, bf16[256,256]{1,0:T(8,128)(2,1)S(1)}, u32[]{:S(2)}, u32[]{:S(2)}) collective-permute-start(bf16[256,256]{1,0:T(8,128)(2,1)S(1)} %relay.2.refs_6_), channel_id=1, source_target_pairs={{0,1},{1,0},{2,3},{3,2},{4,5},{5,4},{6,7},{7,6},{8,9},{9,8},{10,11... | collective-permute-start | bytes 393224 | tf_op jit(solution)/shard_map/ppermute | solution.py:32
  40.1 1.7 %collective-permute-start.14 = (bf16[256,256]{1,0:T(8,128)(2,1)S(1)}, bf16[256,256]{1,0:T(8,128)(2,1)S(1)}, u32[]{:S(2)}, u32[]{:S(2)}) collective-permute-start(bf16[256,256]{1,0:T(8,128)(2,1)S(1)} %relay.2.refs_6_), channel_id=1, source_target_pairs={{0,16},{16,0},{1,17},{17,1},{2,18},{18,2},{3,19},{19,3},{4,20},{20... | collective-permute-start | bytes 393224 | tf_op jit(solution)/shard_map/ppermute | solution.py:32
  41.8 3.2 %attention.3 = (bf16[256,512]{1,0:T(8,128)(2,1)S(1)}, bf16[2,256,128]{2,1,0:T(8,128)(2,1)S(1)}, f32[2,64,128]{2,1,0:T(8,128)S(1)}, bf16[2,64,128]{2,1,0:T(8,128)...) custom-call(s32[3]{0:T(128)S(1)} %pad_add_fusion.ranks, s32[4]{0:T(128)S(1)} %copy-done.6, ...), custom_call_target="tpu_custom_call" | custom-call | flops 1 | bytes 1 | tf_op jit(solution)/shard_map/attention/pallas_call | solution.py:745
  47.4 2.7 %collective-permute-done.15.refs_7_ = bf16[256,256]{1,0:T(8,128)(2,1)S(1)} collective-permute-done((bf16[256,256]{1,0:T(8,128)(2,1)S(1)}, bf16[256,256]{1,0:T(8,128)(2,1)S(1)}, u32[]{:S(2)}, u32[]{:S(2)}) %collective-permute-start.15) | collective-permute-done | bytes 131104 | tf_op jit(solution)/shard_map/ppermute | solution.py:32
  53.8 5.8 %collective-permute-done.17.refs_1_.refs_2_ = f32[384,128]{1,0:T(8,128)S(1)} collective-permute-done((f32[384,128]{1,0:T(8,128)S(1)}, f32[384,128]{1,0:T(8,128)S(1)}, u32[]{:S(2)}, u32[]{:S(2)}) %collective-permute-start.17) | collective-permute-done | bytes 196640 | tf_op jit(solution)/shard_map/ppermute | solution.py:32
  60.7 9.7 %inverse_factor.1.x = f32[256,256]{1,0:T(8,128)S(1)} custom-call(f32[384,128]{1,0:T(8,128)S(1)} %sum_parts.8.refs_0_, f32[384,128]{1,0:T(8,128)S(1)} %collective-permute-done.17.refs_1_.refs_2_), custom_call_target="tpu_custom_call" | custom-call | flops 2000000000 | bytes 1 | tf_op jit(solution)/shard_map/inverse_factor/pallas_call | solution.py:421
  71.1 2.6 %collective-permute-start.25 = (f32[8,256]{1,0:T(8,128)S(1)}, f32[8,256]{1,0:T(8,128)S(1)}, u32[]{:S(2)}, u32[]{:S(2)}) collective-permute-start(f32[8,256]{1,0:T(8,128)S(1)} %get-tuple-element.91.refs_4_.refs_0_), channel_id=1, source_target_pairs={{0,3},{1,2},{2,1},{3,0},{4,7},{5,6},{6,5},{7,4},{8,11},{9,10},{10,... | collective-permute-start | bytes 24584 | tf_op jit(solution)/shard_map/ppermute | solution.py:32
  73.7 1.9 %collective-permute-start.23 = (f32[8,256]{1,0:T(8,128)S(1)}, f32[8,256]{1,0:T(8,128)S(1)}, u32[]{:S(2)}, u32[]{:S(2)}) collective-permute-start(f32[8,256]{1,0:T(8,128)S(1)} %get-tuple-element.91.refs_4_.refs_0_), channel_id=1, source_target_pairs={{0,1},{1,0},{2,3},{3,2},{4,5},{5,4},{6,7},{7,6},{8,9},{9,8},{10,11... | collective-permute-start | bytes 24584 | tf_op jit(solution)/shard_map/ppermute | solution.py:32
  78.8 2.9 %new_momentum.1 = (f32[2048,512]{1,0:T(8,128)}, bf16[256,1024]{1,0:T(8,128)(2,1)}, bf16[2,256,128]{2,1,0:T(8,128)(2,1)}, f32[8,128]{1,0:T(8,128)}) custom-call(s32[3]{0:T(128)S(1)} %pad_add_fusion.ranks, bf16[2048,256]{1,0:T(8,128)(2,1)S(1)} %get-tuple-element.77.pcat, bf16[256,512]{1,0:T(8,128)(2,1)S(1)} %get-tuple-element.87.y, ...), custom_call_target="tpu_custom_call" | custom-call | flops 5000000000 | bytes 1 | tf_op jit(solution)/shard_map/new_momentum/pallas_call | solution.py:518
  81.9 3.6 %final_update.1 = (bf16[2048,512]{1,0:T(8,128)(2,1)}, f32[512,256]{1,0:T(8,128)}, f32[2048,512]{1,0:T(8,128)}, f32[2,2,64,128]{3,2,1,0:T(8,128)}) custom-call(s32[3]{0:T(128)S(1)} %pad_add_fusion.ranks, bf16[2048,256]{1,0:T(8,128)(2,1)S(1)} %get-tuple-element.77.pcat, f32[256,256]{1,0:T(8,128)S(1)} %inverse_factor.1.x, ...), custom_call_target="tpu_custom_call", output_to_operand_aliasing={{2}: (10, {})} | custom-call | flops 5000000000 | bytes 1 | tf_op jit(solution)/shard_map/final_update/pallas_call | solution.py:581
  (76 shorter events, 15.7 us)
Async XLA Ops:
  4.5 9.3 %collective-permute-start = (bf16[512,256]{1,0:T(8,128)(2,1)S(1)}, bf16[512,256]{1,0:T(8,128)(2,1)S(1)}, u32[]{:S(2)}, u32[]{:S(2)}) collective-permute-start(bf16[512,256]{1,0:T(8,128)(2,1)S(1)} %get-tuple-element.63), channel_id=1, source_target_pairs={{0,16},{16,0},{1,17},{17,1},{2,18},{18,2},{3,19},{19,3},{4,20},{20... | collective-permute-start | bytes 786440 | tf_op jit(solution)/shard_map/ppermute | solution.py:32
  12.7 8.5 %collective-permute-start.1 = (bf16[512,256]{1,0:T(8,128)(2,1)S(1)}, bf16[512,256]{1,0:T(8,128)(2,1)S(1)}, u32[]{:S(2)}, u32[]{:S(2)}) collective-permute-start(bf16[512,256]{1,0:T(8,128)(2,1)S(1)} %get-tuple-element.66.refs_2_), channel_id=1, source_target_pairs={{0,16},{16,0},{1,17},{17,1},{2,18},{18,2},{3,19},{19,3},{4,20},{20... | collective-permute-start | bytes 786440 | tf_op jit(solution)/shard_map/ppermute | solution.py:32
  13.9 11.6 %collective-permute-start.3 = (bf16[256,256]{1,0:T(8,128)(2,1)S(1)}, bf16[256,256]{1,0:T(8,128)(2,1)S(1)}, u32[]{:S(2)}, u32[]{:S(2)}) collective-permute-start(bf16[256,256]{1,0:T(8,128)(2,1)S(1)} %get-tuple-element.68), channel_id=1, source_target_pairs={{0,3},{1,2},{2,1},{3,0},{4,7},{5,6},{6,5},{7,4},{8,11},{9,10},{10,... | collective-permute-start | bytes 393224 | tf_op jit(solution)/shard_map/ppermute | solution.py:32
  17.8 10.3 %collective-permute-start.2 = (bf16[256,256]{1,0:T(8,128)(2,1)S(1)}, bf16[256,256]{1,0:T(8,128)(2,1)S(1)}, u32[]{:S(2)}, u32[]{:S(2)}) collective-permute-start(bf16[256,256]{1,0:T(8,128)(2,1)S(1)} %get-tuple-element.64.refs_4_), channel_id=1, source_target_pairs={{0,2},{1,3},{2,0},{3,1},{4,6},{5,7},{6,4},{7,5},{8,10},{9,11},{10,... | collective-permute-start | bytes 393224 | tf_op jit(solution)/shard_map/ppermute | solution.py:32
  17.8 5.1 %collective-permute-start.5 = (bf16[2,2,64,128]{3,2,1,0:T(8,128)(2,1)S(1)}, bf16[2,2,64,128]{3,2,1,0:T(8,128)(2,1)S(1)}, u32[]{:S(2)}, u32[]{:S(2)}) collective-permute-start(bf16[2,2,64,128]{3,2,1,0:T(8,128)(2,1)S(1)} %pack_prompts.1.refs_0_), channel_id=1, source_target_pairs={{0,16},{16,0},{1,17},{17,1},{2,18},{18,2},{3,19},{19,3},{4,20},{20... | collective-permute-start | bytes 196616 | tf_op jit(solution)/shard_map/ppermute | solution.py:32
  21.3 7.5 %collective-permute-start.4 = (bf16[256,256]{1,0:T(8,128)(2,1)S(1)}, bf16[256,256]{1,0:T(8,128)(2,1)S(1)}, u32[]{:S(2)}, u32[]{:S(2)}) collective-permute-start(bf16[256,256]{1,0:T(8,128)(2,1)S(1)} %get-tuple-element.69.refs_2_), channel_id=1, source_target_pairs={{0,1},{1,0},{2,3},{3,2},{4,5},{5,4},{6,7},{7,6},{8,9},{9,8},{10,11... | collective-permute-start | bytes 393224 | tf_op jit(solution)/shard_map/ppermute | solution.py:32
  23.9 4.3 %collective-permute-start.6 = (bf16[2,64,128]{2,1,0:T(8,128)(2,1)S(1)}, bf16[2,64,128]{2,1,0:T(8,128)(2,1)S(1)}, u32[]{:S(2)}, u32[]{:S(2)}) collective-permute-start(bf16[2,64,128]{2,1,0:T(8,128)(2,1)S(1)} %get-tuple-element.70), channel_id=1, source_target_pairs={{0,4},{4,0},{8,12},{12,8},{1,5},{5,1},{9,13},{13,9},{2,6},{6,2},{1... | collective-permute-start | bytes 98312 | tf_op jit(solution)/shard_map/ppermute | solution.py:32
  23.9 4.3 %collective-permute-start.7 = (bf16[2,64,128]{2,1,0:T(8,128)(2,1)S(1)}, bf16[2,64,128]{2,1,0:T(8,128)(2,1)S(1)}, u32[]{:S(2)}, u32[]{:S(2)}) collective-permute-start(bf16[2,64,128]{2,1,0:T(8,128)(2,1)S(1)} %get-tuple-element.71), channel_id=1, source_target_pairs={{0,8},{4,12},{8,0},{12,4},{1,9},{5,13},{9,1},{13,5},{2,10},{6,14},... | collective-permute-start | bytes 98312 | tf_op jit(solution)/shard_map/ppermute | solution.py:32
  28.9 8.6 %collective-permute-start.9 = (bf16[256,256]{1,0:T(8,128)(2,1)S(1)}, bf16[256,256]{1,0:T(8,128)(2,1)S(1)}, u32[]{:S(2)}, u32[]{:S(2)}) collective-permute-start(bf16[256,256]{1,0:T(8,128)(2,1)S(1)} %sum_parts.7.refs_4_.refs_0_), channel_id=1, source_target_pairs={{0,1},{1,0},{2,3},{3,2},{4,5},{5,4},{6,7},{7,6},{8,9},{9,8},{10,11... | collective-permute-start | bytes 393224 | tf_op jit(solution)/shard_map/ppermute | solution.py:32
  30.5 7.8 %collective-permute-start.10 = (bf16[256,256]{1,0:T(8,128)(2,1)S(1)}, bf16[256,256]{1,0:T(8,128)(2,1)S(1)}, u32[]{:S(2)}, u32[]{:S(2)}) collective-permute-start(bf16[256,256]{1,0:T(8,128)(2,1)S(1)} %sum_parts.7.refs_4_.refs_0_), channel_id=1, source_target_pairs={{0,2},{1,3},{2,0},{3,1},{4,6},{5,7},{6,4},{7,5},{8,10},{9,11},{10,... | collective-permute-start | bytes 393224 | tf_op jit(solution)/shard_map/ppermute | solution.py:32
  32.8 12.2 %collective-permute-start.12 = (bf16[256,256]{1,0:T(8,128)(2,1)S(1)}, bf16[256,256]{1,0:T(8,128)(2,1)S(1)}, u32[]{:S(2)}, u32[]{:S(2)}) collective-permute-start(bf16[256,256]{1,0:T(8,128)(2,1)S(1)} %sum_parts.7.refs_4_.refs_0_), channel_id=1, source_target_pairs={{0,16},{16,0},{1,17},{17,1},{2,18},{18,2},{3,19},{19,3},{4,20},{20... | collective-permute-start | bytes 393224 | tf_op jit(solution)/shard_map/ppermute | solution.py:32
  37.5 7.6 %collective-permute-start.13 = (bf16[256,256]{1,0:T(8,128)(2,1)S(1)}, bf16[256,256]{1,0:T(8,128)(2,1)S(1)}, u32[]{:S(2)}, u32[]{:S(2)}) collective-permute-start(bf16[256,256]{1,0:T(8,128)(2,1)S(1)} %collective-permute-done.9.refs_1_), channel_id=1, source_target_pairs={{0,16},{16,0},{1,17},{17,1},{2,18},{18,2},{3,19},{19,3},{4,20},{20... | collective-permute-start | bytes 393224 | tf_op jit(solution)/shard_map/ppermute | solution.py:32
  38.3 6.7 %collective-permute-start.11 = (bf16[256,256]{1,0:T(8,128)(2,1)S(1)}, bf16[256,256]{1,0:T(8,128)(2,1)S(1)}, u32[]{:S(2)}, u32[]{:S(2)}) collective-permute-start(bf16[256,256]{1,0:T(8,128)(2,1)S(1)} %relay.2.refs_6_), channel_id=1, source_target_pairs={{0,1},{1,0},{2,3},{3,2},{4,5},{5,4},{6,7},{7,6},{8,9},{9,8},{10,11... | collective-permute-start | bytes 393224 | tf_op jit(solution)/shard_map/ppermute | solution.py:32
  40.1 7.2 %collective-permute-start.14 = (bf16[256,256]{1,0:T(8,128)(2,1)S(1)}, bf16[256,256]{1,0:T(8,128)(2,1)S(1)}, u32[]{:S(2)}, u32[]{:S(2)}) collective-permute-start(bf16[256,256]{1,0:T(8,128)(2,1)S(1)} %relay.2.refs_6_), channel_id=1, source_target_pairs={{0,16},{16,0},{1,17},{17,1},{2,18},{18,2},{3,19},{19,3},{4,20},{20... | collective-permute-start | bytes 393224 | tf_op jit(solution)/shard_map/ppermute | solution.py:32
  45.1 5.0 %collective-permute-start.15 = (bf16[256,256]{1,0:T(8,128)(2,1)S(1)}, bf16[256,256]{1,0:T(8,128)(2,1)S(1)}, u32[]{:S(2)}, u32[]{:S(2)}) collective-permute-start(bf16[256,256]{1,0:T(8,128)(2,1)S(1)} %relay.3), channel_id=1, source_target_pairs={{0,16},{16,0},{1,17},{17,1},{2,18},{18,2},{3,19},{19,3},{4,20},{20... | collective-permute-start | bytes 393224 | tf_op jit(solution)/shard_map/ppermute | solution.py:32
  45.5 5.2 %collective-permute-start.18 = (bf16[2,64,128]{2,1,0:T(8,128)(2,1)S(1)}, bf16[2,64,128]{2,1,0:T(8,128)(2,1)S(1)}, u32[]{:S(2)}, u32[]{:S(2)}) collective-permute-start(bf16[2,64,128]{2,1,0:T(8,128)(2,1)S(1)} %get-tuple-element.84), channel_id=1, source_target_pairs={{0,4},{4,0},{8,12},{12,8},{1,5},{5,1},{9,13},{13,9},{2,6},{6,2},{1... | collective-permute-start | bytes 98312 | tf_op jit(solution)/shard_map/ppermute | solution.py:32
  45.5 5.2 %collective-permute-start.19 = (bf16[2,64,128]{2,1,0:T(8,128)(2,1)S(1)}, bf16[2,64,128]{2,1,0:T(8,128)(2,1)S(1)}, u32[]{:S(2)}, u32[]{:S(2)}) collective-permute-start(bf16[2,64,128]{2,1,0:T(8,128)(2,1)S(1)} %get-tuple-element.85), channel_id=1, source_target_pairs={{0,8},{4,12},{8,0},{12,4},{1,9},{5,13},{9,1},{13,5},{2,10},{6,14},... | collective-permute-start | bytes 98312 | tf_op jit(solution)/shard_map/ppermute | solution.py:32
  46.7 4.0 %collective-permute-start.20 = (bf16[2,64,128]{2,1,0:T(8,128)(2,1)S(1)}, bf16[2,64,128]{2,1,0:T(8,128)(2,1)S(1)}, u32[]{:S(2)}, u32[]{:S(2)}) collective-permute-start(bf16[2,64,128]{2,1,0:T(8,128)(2,1)S(1)} %get-tuple-element.86), channel_id=1, source_target_pairs={{0,12},{4,8},{8,4},{12,0},{1,13},{5,9},{9,5},{13,1},{2,14},{6,10},... | collective-permute-start | bytes 98312 | tf_op jit(solution)/shard_map/ppermute | solution.py:32
  52.7 6.9 %collective-permute-start.17 = (f32[384,128]{1,0:T(8,128)S(1)}, f32[384,128]{1,0:T(8,128)S(1)}, u32[]{:S(2)}, u32[]{:S(2)}) collective-permute-start(f32[384,128]{1,0:T(8,128)S(1)} %sum_parts.8.refs_0_), channel_id=1, source_target_pairs={{0,8},{4,12},{8,0},{12,4},{1,9},{5,13},{9,1},{13,5},{2,10},{6,14},... | collective-permute-start | bytes 589832 | tf_op jit(solution)/shard_map/ppermute | solution.py:32
  59.6 10.8 %collective-permute-start.22 = (bf16[256,512]{1,0:T(8,128)(2,1)S(1)}, bf16[256,512]{1,0:T(8,128)(2,1)S(1)}, u32[]{:S(2)}, u32[]{:S(2)}) collective-permute-start(bf16[256,512]{1,0:T(8,128)(2,1)S(1)} %sum_parts.9.wa), channel_id=1, source_target_pairs={{0,8},{4,12},{8,0},{12,4},{1,9},{5,13},{9,1},{13,5},{2,10},{6,14},... | collective-permute-start | bytes 786440 | tf_op jit(solution)/shard_map/ppermute | solution.py:32
  71.1 5.9 %collective-permute-start.25 = (f32[8,256]{1,0:T(8,128)S(1)}, f32[8,256]{1,0:T(8,128)S(1)}, u32[]{:S(2)}, u32[]{:S(2)}) collective-permute-start(f32[8,256]{1,0:T(8,128)S(1)} %get-tuple-element.91.refs_4_.refs_0_), channel_id=1, source_target_pairs={{0,3},{1,2},{2,1},{3,0},{4,7},{5,6},{6,5},{7,4},{8,11},{9,10},{10,... | collective-permute-start | bytes 24584 | tf_op jit(solution)/shard_map/ppermute | solution.py:32
  73.6 4.5 %collective-permute-start.24 = (f32[8,256]{1,0:T(8,128)S(1)}, f32[8,256]{1,0:T(8,128)S(1)}, u32[]{:S(2)}, u32[]{:S(2)}) collective-permute-start(f32[8,256]{1,0:T(8,128)S(1)} %get-tuple-element.91.refs_4_.refs_0_), channel_id=1, source_target_pairs={{0,2},{1,3},{2,0},{3,1},{4,6},{5,7},{6,4},{7,5},{8,10},{9,11},{10,... | collective-permute-start | bytes 24584 | tf_op jit(solution)/shard_map/ppermute | solution.py:32
  73.7 4.5 %collective-permute-start.23 = (f32[8,256]{1,0:T(8,128)S(1)}, f32[8,256]{1,0:T(8,128)S(1)}, u32[]{:S(2)}, u32[]{:S(2)}) collective-permute-start(f32[8,256]{1,0:T(8,128)S(1)} %get-tuple-element.91.refs_4_.refs_0_), channel_id=1, source_target_pairs={{0,1},{1,0},{2,3},{3,2},{4,5},{5,4},{6,7},{7,6},{8,9},{9,8},{10,11... | collective-permute-start | bytes 24584 | tf_op jit(solution)/shard_map/ppermute | solution.py:32
  76.2 5.8 %collective-permute-start.27 = (bf16[2,2,64,128]{3,2,1,0:T(8,128)(2,1)S(1)}, bf16[2,2,64,128]{3,2,1,0:T(8,128)(2,1)S(1)}, u32[]{:S(2)}, u32[]{:S(2)}) collective-permute-start(bf16[2,2,64,128]{3,2,1,0:T(8,128)(2,1)S(1)} %get-tuple-element.92.refs_4_), channel_id=1, source_target_pairs={{0,16},{16,0},{1,17},{17,1},{2,18},{18,2},{3,19},{19,3},{4,20},{20... | collective-permute-start | bytes 196616 | tf_op jit(solution)/shard_map/ppermute | solution.py:32
  (13 other events, 63.6 us)

commit v13 on v12

--- a/solution.py
+++ b/solution.py
@@ -886,7 +886,7 @@
         gram = sum_parts([gram, swap(gram, "fsdp", bit)], F32, (), 3)
     gram_parts = (gram, swap(gram, "fsdp", bits[-1]))
     for bit in bits[:-1]:
-        w = sum_parts([w, swap(w, "fsdp", bit)], BF16, (gram_parts[1],), 0)
+        w = sum_parts([w, swap(w, "fsdp", bit)], BF16, (gram,), 5)
     w_other = swap(w, "fsdp", bits[-1])
     x = inverse_factor(*gram_parts)
     bt, y, squares = back_full(x, w, w_other, tuple(returned[1:]))

time: 85.9 us -> 86.3 us (level)
  starting transfers between devices: 32 us -> 33 us
    ppermute x28, starting transfers between devices: 32 us -> 33 us  [swap(): return lax.ppermute(value, axes, [(i, i ^ k) for i in range(n)])]
  transfers between devices with their start and end apart: 28 -> 28, of which waited for: 8 -> 7; matrix products, arithmetic and copies ran while one was open for 0% -> 0% of each run, Pallas kernels for 34% -> 34%
where the time goes in v13:
time: 86.3 us; the launch traced here: 86 us
  Pallas kernels  37.4 us (43%)
  starting transfers between devices  33 us (38%)
  waiting for transfers between devices  13.8 us (16%)
  between operations  1.77 us (2%)
    ppermute x28, starting transfers between devices, swap(): return lax.ppermute(value, axes, [(i, i ^ k) for i in range(n)])  33 us
    ppermute x28, waiting for transfers between devices, swap(): return lax.ppermute(value, axes, [(i, i ^ k) for i in range(n)])  13.8 us
    pallas_call x4, Pallas kernels, project(): pl.pallas_call(functools.partial(project_kernel, n_head, part, following,...  10.4 us
    pallas_call x1, Pallas kernels, inverse_factor(): pl.pallas_call(functools.partial(cholesky_kernel, len(parts)), in_specs=[...  9.7 us
    pallas_call x2, Pallas kernels, attention(): pl.pallas_call(functools.partial(attention_kernel, n_fsdp, heads, last),...  6.48 us
    pallas_call x1, Pallas kernels, final_update(): pl.pallas_call(functools.partial(update_kernel, gain, n_resp, n_head, len...  3.61 us
    pallas_call x1, Pallas kernels, new_momentum(): pl.pallas_call(functools.partial(momentum_kernel, n_resp, n_head, len(tot...  2.92 us
  transfers between devices with their start and end apart: 28, of which 7 were waited for; matrix products, arithmetic and copies ran while one was open for 0% of the time, Pallas kernels for 34%

profile of v13, /device:TPU:0, one launch (start us, length us, event | category | flops | bytes accessed | tf_op | source)
XLA Modules:
  0.0 86.0 jit_solution(2094586197303979395)
XLA Ops:
  0.7 3.8 %project.4 = (bf16[512,256]{1,0:T(8,128)(2,1)S(1)}, f32[512,512]{1,0:T(8,128)S(1)}, bf16[512,256]{1,0:T(8,128)(2,1)S(1)}, bf16[512,256]{1,0:T(8,128)(2,1)S(1)}, ...) custom-call(s32[3]{0:T(128)S(1)} %pad_add_fusion.ranks, f32[2048,512]{1,0:T(8,128)} %mom.7, bf16[2048,512]{1,0:T(8,128)(2,1)} %grad.7, ...), custom_call_target="tpu_custom_call" | custom-call | flops 1 | bytes 1 | tf_op jit(solution)/shard_map/project/pallas_call | solution.py:154
  4.5 3.0 %collective-permute-start = (bf16[512,256]{1,0:T(8,128)(2,1)S(1)}, bf16[512,256]{1,0:T(8,128)(2,1)S(1)}, u32[]{:S(2)}, u32[]{:S(2)}) collective-permute-start(bf16[512,256]{1,0:T(8,128)(2,1)S(1)} %get-tuple-element.63), channel_id=1, source_target_pairs={{0,16},{16,0},{1,17},{17,1},{2,18},{18,2},{3,19},{19,3},{4,20},{20... | collective-permute-start | bytes 786440 | tf_op jit(solution)/shard_map/ppermute | solution.py:32
  7.5 2.6 %project.5 = (f32[512,256]{1,0:T(8,128)S(1)}, f32[512,512]{1,0:T(8,128)S(1)}, f32[512,512]{1,0:T(8,128)S(1)}, bf16[512,512]{1,0:T(8,128)(2,1)S(1)}) custom-call(s32[3]{0:T(128)S(1)} %pad_add_fusion.ranks, f32[2048,512]{1,0:T(8,128)} %mom.7, bf16[2048,512]{1,0:T(8,128)(2,1)} %grad.7, bf16[512,256]{1,0:T(8,128)(2,1)S(1)} %get-tuple-element.54.refs_0_, ...), custom_call_target="tpu_custom_call" | custom-call | flops 10000000000 | bytes 1 | tf_op jit(solution)/shard_map/project/pallas_call | solution.py:154
  10.1 2.6 %project.6 = (bf16[512,256]{1,0:T(8,128)(2,1)S(1)}, f32[512,512]{1,0:T(8,128)S(1)}, f32[512,512]{1,0:T(8,128)S(1)}, bf16[512,512]{1,0:T(8,128)(2,1)S(1)}) custom-call(s32[3]{0:T(128)S(1)} %pad_add_fusion.ranks, f32[2048,512]{1,0:T(8,128)} %mom.7, bf16[2048,512]{1,0:T(8,128)(2,1)} %grad.7, bf16[512,256]{1,0:T(8,128)(2,1)S(1)} %get-tuple-element.54.refs_0_, ...), custom_call_target="tpu_custom_call" | custom-call | flops 1 | bytes 1 | tf_op jit(solution)/shard_map/project/pallas_call | solution.py:154
  13.9 3.9 %collective-permute-start.3 = (bf16[256,256]{1,0:T(8,128)(2,1)S(1)}, bf16[256,256]{1,0:T(8,128)(2,1)S(1)}, u32[]{:S(2)}, u32[]{:S(2)}) collective-permute-start(bf16[256,256]{1,0:T(8,128)(2,1)S(1)} %get-tuple-element.68), channel_id=1, source_target_pairs={{0,3},{1,2},{2,1},{3,0},{4,7},{5,6},{6,5},{7,4},{8,11},{9,10},{10,... | collective-permute-start | bytes 393224 | tf_op jit(solution)/shard_map/ppermute | solution.py:32
  17.8 1.6 %collective-permute-start.5 = (bf16[2,2,64,128]{3,2,1,0:T(8,128)(2,1)S(1)}, bf16[2,2,64,128]{3,2,1,0:T(8,128)(2,1)S(1)}, u32[]{:S(2)}, u32[]{:S(2)}) collective-permute-start(bf16[2,2,64,128]{3,2,1,0:T(8,128)(2,1)S(1)} %pack_prompts.1.refs_0_), channel_id=1, source_target_pairs={{0,16},{16,0},{1,17},{17,1},{2,18},{18,2},{3,19},{19,3},{4,20},{20... | collective-permute-start | bytes 196616 | tf_op jit(solution)/shard_map/ppermute | solution.py:32
  19.4 1.4 %project.7 = (f32[512,256]{1,0:T(8,128)S(1)}, f32[512,512]{1,0:T(8,128)S(1)}) custom-call(s32[3]{0:T(128)S(1)} %pad_add_fusion.ranks, f32[2048,512]{1,0:T(8,128)} %mom.7, bf16[2048,512]{1,0:T(8,128)(2,1)} %grad.7, bf16[512,256]{1,0:T(8,128)(2,1)S(1)} %get-tuple-element.54.refs_0_, bf16[512,256]{1,0:T(8,128)(2,1)S(1)} %get-tuple-element.55.refs_1_, ...), custom_call_target="tpu_custom_call" | custom-call | flops 1 | bytes 1 | tf_op jit(solution)/shard_map/project/pallas_call | solution.py:154
  21.3 1.6 %collective-permute-start.4 = (bf16[256,256]{1,0:T(8,128)(2,1)S(1)}, bf16[256,256]{1,0:T(8,128)(2,1)S(1)}, u32[]{:S(2)}, u32[]{:S(2)}) collective-permute-start(bf16[256,256]{1,0:T(8,128)(2,1)S(1)} %get-tuple-element.69.refs_2_), channel_id=1, source_target_pairs={{0,1},{1,0},{2,3},{3,2},{4,5},{5,4},{6,7},{7,6},{8,9},{9,8},{10,11... | collective-permute-start | bytes 393224 | tf_op jit(solution)/shard_map/ppermute | solution.py:32
  23.9 1.6 %collective-permute-start.7 = (bf16[2,64,128]{2,1,0:T(8,128)(2,1)S(1)}, bf16[2,64,128]{2,1,0:T(8,128)(2,1)S(1)}, u32[]{:S(2)}, u32[]{:S(2)}) collective-permute-start(bf16[2,64,128]{2,1,0:T(8,128)(2,1)S(1)} %get-tuple-element.71), channel_id=1, source_target_pairs={{0,8},{4,12},{8,0},{12,4},{1,9},{5,13},{9,1},{13,5},{2,10},{6,14},... | collective-permute-start | bytes 98312 | tf_op jit(solution)/shard_map/ppermute | solution.py:32
  25.8 2.3 %collective-permute-done.2.refs_1_ = bf16[256,256]{1,0:T(8,128)(2,1)S(1)} collective-permute-done((bf16[256,256]{1,0:T(8,128)(2,1)S(1)}, bf16[256,256]{1,0:T(8,128)(2,1)S(1)}, u32[]{:S(2)}, u32[]{:S(2)}) %collective-permute-start.2) | collective-permute-done | bytes 131104 | tf_op jit(solution)/shard_map/ppermute | solution.py:32
  28.9 1.6 %collective-permute-start.9 = (bf16[256,256]{1,0:T(8,128)(2,1)S(1)}, bf16[256,256]{1,0:T(8,128)(2,1)S(1)}, u32[]{:S(2)}, u32[]{:S(2)}) collective-permute-start(bf16[256,256]{1,0:T(8,128)(2,1)S(1)} %sum_parts.7.refs_4_.refs_0_), channel_id=1, source_target_pairs={{0,1},{1,0},{2,3},{3,2},{4,5},{5,4},{6,7},{7,6},{8,9},{9,8},{10,11... | collective-permute-start | bytes 393224 | tf_op jit(solution)/shard_map/ppermute | solution.py:32
  30.5 1.6 %collective-permute-start.10 = (bf16[256,256]{1,0:T(8,128)(2,1)S(1)}, bf16[256,256]{1,0:T(8,128)(2,1)S(1)}, u32[]{:S(2)}, u32[]{:S(2)}) collective-permute-start(bf16[256,256]{1,0:T(8,128)(2,1)S(1)} %sum_parts.7.refs_4_.refs_0_), channel_id=1, source_target_pairs={{0,2},{1,3},{2,0},{3,1},{4,6},{5,7},{6,4},{7,5},{8,10},{9,11},{10,... | collective-permute-start | bytes 393224 | tf_op jit(solution)/shard_map/ppermute | solution.py:32
  34.2 3.3 %attention.2 = (bf16[256,512]{1,0:T(8,128)(2,1)S(1)}, f32[512,128]{1,0:T(8,128)S(1)}, f32[512,128]{1,0:T(8,128)S(1)}) custom-call(s32[3]{0:T(128)S(1)} %pad_add_fusion.ranks, s32[4]{0:T(128)S(1)} %copy-done.6, s32[4]{0:T(128)S(1)} %copy-done.7, s32[1]{0:T(128)S(6)} %copy.21.resp_blocks, bf16[256,1024]{1,0:T(8,128)(2,1)S(1)} %copy-done, ...), custom_call_target="tpu_custom_call" | custom-call | flops 1 | bytes 1 | tf_op jit(solution)/shard_map/attention/pallas_call | solution.py:745
  38.3 1.8 %collective-permute-start.11 = (bf16[256,256]{1,0:T(8,128)(2,1)S(1)}, bf16[256,256]{1,0:T(8,128)(2,1)S(1)}, u32[]{:S(2)}, u32[]{:S(2)}) collective-permute-start(bf16[256,256]{1,0:T(8,128)(2,1)S(1)} %relay.2.refs_6_), channel_id=1, source_target_pairs={{0,1},{1,0},{2,3},{3,2},{4,5},{5,4},{6,7},{7,6},{8,9},{9,8},{10,11... | collective-permute-start | bytes 393224 | tf_op jit(solution)/shard_map/ppermute | solution.py:32
  40.1 1.7 %collective-permute-start.14 = (bf16[256,256]{1,0:T(8,128)(2,1)S(1)}, bf16[256,256]{1,0:T(8,128)(2,1)S(1)}, u32[]{:S(2)}, u32[]{:S(2)}) collective-permute-start(bf16[256,256]{1,0:T(8,128)(2,1)S(1)} %relay.2.refs_6_), channel_id=1, source_target_pairs={{0,16},{16,0},{1,17},{17,1},{2,18},{18,2},{3,19},{19,3},{4,20},{20... | collective-permute-start | bytes 393224 | tf_op jit(solution)/shard_map/ppermute | solution.py:32
  41.8 3.2 %attention.3 = (bf16[256,512]{1,0:T(8,128)(2,1)S(1)}, bf16[2,256,128]{2,1,0:T(8,128)(2,1)S(1)}, f32[2,64,128]{2,1,0:T(8,128)S(1)}, bf16[2,64,128]{2,1,0:T(8,128)...) custom-call(s32[3]{0:T(128)S(1)} %pad_add_fusion.ranks, s32[4]{0:T(128)S(1)} %copy-done.6, ...), custom_call_target="tpu_custom_call" | custom-call | flops 1 | bytes 1 | tf_op jit(solution)/shard_map/attention/pallas_call | solution.py:745
  47.4 2.7 %collective-permute-done.15.refs_7_ = bf16[256,256]{1,0:T(8,128)(2,1)S(1)} collective-permute-done((bf16[256,256]{1,0:T(8,128)(2,1)S(1)}, bf16[256,256]{1,0:T(8,128)(2,1)S(1)}, u32[]{:S(2)}, u32[]{:S(2)}) %collective-permute-start.15) | collective-permute-done | bytes 131104 | tf_op jit(solution)/shard_map/ppermute | solution.py:32
  55.0 5.5 %collective-permute-done.17.refs_1_ = f32[384,128]{1,0:T(8,128)S(1)} collective-permute-done((f32[384,128]{1,0:T(8,128)S(1)}, f32[384,128]{1,0:T(8,128)S(1)}, u32[]{:S(2)}, u32[]{:S(2)}) %collective-permute-start.17) | collective-permute-done | bytes 196640 | tf_op jit(solution)/shard_map/ppermute | solution.py:32
  60.5 9.7 %inverse_factor.1.x = f32[256,256]{1,0:T(8,128)S(1)} custom-call(f32[384,128]{1,0:T(8,128)S(1)} %sum_parts.8.refs_0_.refs_2_, f32[384,128]{1,0:T(8,128)S(1)} %collective-permute-done.17.refs_1_), custom_call_target="tpu_custom_call" | custom-call | flops 2000000000 | bytes 1 | tf_op jit(solution)/shard_map/inverse_factor/pallas_call | solution.py:421
  70.8 2.2 %collective-permute-start.25 = (f32[8,256]{1,0:T(8,128)S(1)}, f32[8,256]{1,0:T(8,128)S(1)}, u32[]{:S(2)}, u32[]{:S(2)}) collective-permute-start(f32[8,256]{1,0:T(8,128)S(1)} %get-tuple-element.91.refs_4_.refs_0_), channel_id=1, source_target_pairs={{0,3},{1,2},{2,1},{3,0},{4,7},{5,6},{6,5},{7,4},{8,11},{9,10},{10,... | collective-permute-start | bytes 24584 | tf_op jit(solution)/shard_map/ppermute | solution.py:32
  73.6 1.7 %collective-permute-start.23 = (f32[8,256]{1,0:T(8,128)S(1)}, f32[8,256]{1,0:T(8,128)S(1)}, u32[]{:S(2)}, u32[]{:S(2)}) collective-permute-start(f32[8,256]{1,0:T(8,128)S(1)} %get-tuple-element.91.refs_4_.refs_0_), channel_id=1, source_target_pairs={{0,1},{1,0},{2,3},{3,2},{4,5},{5,4},{6,7},{7,6},{8,9},{9,8},{10,11... | collective-permute-start | bytes 24584 | tf_op jit(solution)/shard_map/ppermute | solution.py:32
  77.6 1.7 %collective-permute-start.26 = (f32[8,256]{1,0:T(8,128)S(1)}, f32[8,256]{1,0:T(8,128)S(1)}, u32[]{:S(2)}, u32[]{:S(2)}) collective-permute-start(f32[8,256]{1,0:T(8,128)S(1)} %sum_parts.10.refs_5_.refs_0_), channel_id=1, source_target_pairs={{0,16},{16,0},{1,17},{17,1},{2,18},{18,2},{3,19},{19,3},{4,20},{20... | collective-permute-start | bytes 24584 | tf_op jit(solution)/shard_map/ppermute | solution.py:32
  79.3 2.9 %new_momentum.1 = (f32[2048,512]{1,0:T(8,128)}, bf16[256,1024]{1,0:T(8,128)(2,1)}, bf16[2,256,128]{2,1,0:T(8,128)(2,1)}, f32[8,128]{1,0:T(8,128)}) custom-call(s32[3]{0:T(128)S(1)} %pad_add_fusion.ranks, bf16[2048,256]{1,0:T(8,128)(2,1)S(1)} %get-tuple-element.77.pcat, bf16[256,512]{1,0:T(8,128)(2,1)S(1)} %get-tuple-element.87.y, ...), custom_call_target="tpu_custom_call" | custom-call | flops 5000000000 | bytes 1 | tf_op jit(solution)/shard_map/new_momentum/pallas_call | solution.py:518
  82.3 3.6 %final_update.1 = (bf16[2048,512]{1,0:T(8,128)(2,1)}, f32[512,256]{1,0:T(8,128)}, f32[2048,512]{1,0:T(8,128)}, f32[2,2,64,128]{3,2,1,0:T(8,128)}) custom-call(s32[3]{0:T(128)S(1)} %pad_add_fusion.ranks, bf16[2048,256]{1,0:T(8,128)(2,1)S(1)} %get-tuple-element.77.pcat, f32[256,256]{1,0:T(8,128)S(1)} %inverse_factor.1.x, ...), custom_call_target="tpu_custom_call", output_to_operand_aliasing={{2}: (10, {})} | custom-call | flops 5000000000 | bytes 1 | tf_op jit(solution)/shard_map/final_update/pallas_call | solution.py:581
  (76 shorter events, 16.6 us)
Async XLA Ops:
  4.5 9.3 %collective-permute-start = (bf16[512,256]{1,0:T(8,128)(2,1)S(1)}, bf16[512,256]{1,0:T(8,128)(2,1)S(1)}, u32[]{:S(2)}, u32[]{:S(2)}) collective-permute-start(bf16[512,256]{1,0:T(8,128)(2,1)S(1)} %get-tuple-element.63), channel_id=1, source_target_pairs={{0,16},{16,0},{1,17},{17,1},{2,18},{18,2},{3,19},{19,3},{4,20},{20... | collective-permute-start | bytes 786440 | tf_op jit(solution)/shard_map/ppermute | solution.py:32
  12.7 8.5 %collective-permute-start.1 = (bf16[512,256]{1,0:T(8,128)(2,1)S(1)}, bf16[512,256]{1,0:T(8,128)(2,1)S(1)}, u32[]{:S(2)}, u32[]{:S(2)}) collective-permute-start(bf16[512,256]{1,0:T(8,128)(2,1)S(1)} %get-tuple-element.66.refs_2_), channel_id=1, source_target_pairs={{0,16},{16,0},{1,17},{17,1},{2,18},{18,2},{3,19},{19,3},{4,20},{20... | collective-permute-start | bytes 786440 | tf_op jit(solution)/shard_map/ppermute | solution.py:32
  13.9 11.6 %collective-permute-start.3 = (bf16[256,256]{1,0:T(8,128)(2,1)S(1)}, bf16[256,256]{1,0:T(8,128)(2,1)S(1)}, u32[]{:S(2)}, u32[]{:S(2)}) collective-permute-start(bf16[256,256]{1,0:T(8,128)(2,1)S(1)} %get-tuple-element.68), channel_id=1, source_target_pairs={{0,3},{1,2},{2,1},{3,0},{4,7},{5,6},{6,5},{7,4},{8,11},{9,10},{10,... | collective-permute-start | bytes 393224 | tf_op jit(solution)/shard_map/ppermute | solution.py:32
  17.8 10.3 %collective-permute-start.2 = (bf16[256,256]{1,0:T(8,128)(2,1)S(1)}, bf16[256,256]{1,0:T(8,128)(2,1)S(1)}, u32[]{:S(2)}, u32[]{:S(2)}) collective-permute-start(bf16[256,256]{1,0:T(8,128)(2,1)S(1)} %get-tuple-element.64.refs_4_), channel_id=1, source_target_pairs={{0,2},{1,3},{2,0},{3,1},{4,6},{5,7},{6,4},{7,5},{8,10},{9,11},{10,... | collective-permute-start | bytes 393224 | tf_op jit(solution)/shard_map/ppermute | solution.py:32
  17.8 5.1 %collective-permute-start.5 = (bf16[2,2,64,128]{3,2,1,0:T(8,128)(2,1)S(1)}, bf16[2,2,64,128]{3,2,1,0:T(8,128)(2,1)S(1)}, u32[]{:S(2)}, u32[]{:S(2)}) collective-permute-start(bf16[2,2,64,128]{3,2,1,0:T(8,128)(2,1)S(1)} %pack_prompts.1.refs_0_), channel_id=1, source_target_pairs={{0,16},{16,0},{1,17},{17,1},{2,18},{18,2},{3,19},{19,3},{4,20},{20... | collective-permute-start | bytes 196616 | tf_op jit(solution)/shard_map/ppermute | solution.py:32
  21.3 7.5 %collective-permute-start.4 = (bf16[256,256]{1,0:T(8,128)(2,1)S(1)}, bf16[256,256]{1,0:T(8,128)(2,1)S(1)}, u32[]{:S(2)}, u32[]{:S(2)}) collective-permute-start(bf16[256,256]{1,0:T(8,128)(2,1)S(1)} %get-tuple-element.69.refs_2_), channel_id=1, source_target_pairs={{0,1},{1,0},{2,3},{3,2},{4,5},{5,4},{6,7},{7,6},{8,9},{9,8},{10,11... | collective-permute-start | bytes 393224 | tf_op jit(solution)/shard_map/ppermute | solution.py:32
  23.9 4.3 %collective-permute-start.6 = (bf16[2,64,128]{2,1,0:T(8,128)(2,1)S(1)}, bf16[2,64,128]{2,1,0:T(8,128)(2,1)S(1)}, u32[]{:S(2)}, u32[]{:S(2)}) collective-permute-start(bf16[2,64,128]{2,1,0:T(8,128)(2,1)S(1)} %get-tuple-element.70), channel_id=1, source_target_pairs={{0,4},{4,0},{8,12},{12,8},{1,5},{5,1},{9,13},{13,9},{2,6},{6,2},{1... | collective-permute-start | bytes 98312 | tf_op jit(solution)/shard_map/ppermute | solution.py:32
  23.9 4.3 %collective-permute-start.7 = (bf16[2,64,128]{2,1,0:T(8,128)(2,1)S(1)}, bf16[2,64,128]{2,1,0:T(8,128)(2,1)S(1)}, u32[]{:S(2)}, u32[]{:S(2)}) collective-permute-start(bf16[2,64,128]{2,1,0:T(8,128)(2,1)S(1)} %get-tuple-element.71), channel_id=1, source_target_pairs={{0,8},{4,12},{8,0},{12,4},{1,9},{5,13},{9,1},{13,5},{2,10},{6,14},... | collective-permute-start | bytes 98312 | tf_op jit(solution)/shard_map/ppermute | solution.py:32
  28.9 8.6 %collective-permute-start.9 = (bf16[256,256]{1,0:T(8,128)(2,1)S(1)}, bf16[256,256]{1,0:T(8,128)(2,1)S(1)}, u32[]{:S(2)}, u32[]{:S(2)}) collective-permute-start(bf16[256,256]{1,0:T(8,128)(2,1)S(1)} %sum_parts.7.refs_4_.refs_0_), channel_id=1, source_target_pairs={{0,1},{1,0},{2,3},{3,2},{4,5},{5,4},{6,7},{7,6},{8,9},{9,8},{10,11... | collective-permute-start | bytes 393224 | tf_op jit(solution)/shard_map/ppermute | solution.py:32
  30.5 7.8 %collective-permute-start.10 = (bf16[256,256]{1,0:T(8,128)(2,1)S(1)}, bf16[256,256]{1,0:T(8,128)(2,1)S(1)}, u32[]{:S(2)}, u32[]{:S(2)}) collective-permute-start(bf16[256,256]{1,0:T(8,128)(2,1)S(1)} %sum_parts.7.refs_4_.refs_0_), channel_id=1, source_target_pairs={{0,2},{1,3},{2,0},{3,1},{4,6},{5,7},{6,4},{7,5},{8,10},{9,11},{10,... | collective-permute-start | bytes 393224 | tf_op jit(solution)/shard_map/ppermute | solution.py:32
  32.8 12.2 %collective-permute-start.12 = (bf16[256,256]{1,0:T(8,128)(2,1)S(1)}, bf16[256,256]{1,0:T(8,128)(2,1)S(1)}, u32[]{:S(2)}, u32[]{:S(2)}) collective-permute-start(bf16[256,256]{1,0:T(8,128)(2,1)S(1)} %sum_parts.7.refs_4_.refs_0_), channel_id=1, source_target_pairs={{0,16},{16,0},{1,17},{17,1},{2,18},{18,2},{3,19},{19,3},{4,20},{20... | collective-permute-start | bytes 393224 | tf_op jit(solution)/shard_map/ppermute | solution.py:32
  37.5 7.6 %collective-permute-start.13 = (bf16[256,256]{1,0:T(8,128)(2,1)S(1)}, bf16[256,256]{1,0:T(8,128)(2,1)S(1)}, u32[]{:S(2)}, u32[]{:S(2)}) collective-permute-start(bf16[256,256]{1,0:T(8,128)(2,1)S(1)} %collective-permute-done.9.refs_1_), channel_id=1, source_target_pairs={{0,16},{16,0},{1,17},{17,1},{2,18},{18,2},{3,19},{19,3},{4,20},{20... | collective-permute-start | bytes 393224 | tf_op jit(solution)/shard_map/ppermute | solution.py:32
  38.3 6.7 %collective-permute-start.11 = (bf16[256,256]{1,0:T(8,128)(2,1)S(1)}, bf16[256,256]{1,0:T(8,128)(2,1)S(1)}, u32[]{:S(2)}, u32[]{:S(2)}) collective-permute-start(bf16[256,256]{1,0:T(8,128)(2,1)S(1)} %relay.2.refs_6_), channel_id=1, source_target_pairs={{0,1},{1,0},{2,3},{3,2},{4,5},{5,4},{6,7},{7,6},{8,9},{9,8},{10,11... | collective-permute-start | bytes 393224 | tf_op jit(solution)/shard_map/ppermute | solution.py:32
  40.1 7.2 %collective-permute-start.14 = (bf16[256,256]{1,0:T(8,128)(2,1)S(1)}, bf16[256,256]{1,0:T(8,128)(2,1)S(1)}, u32[]{:S(2)}, u32[]{:S(2)}) collective-permute-start(bf16[256,256]{1,0:T(8,128)(2,1)S(1)} %relay.2.refs_6_), channel_id=1, source_target_pairs={{0,16},{16,0},{1,17},{17,1},{2,18},{18,2},{3,19},{19,3},{4,20},{20... | collective-permute-start | bytes 393224 | tf_op jit(solution)/shard_map/ppermute | solution.py:32
  45.1 5.0 %collective-permute-start.15 = (bf16[256,256]{1,0:T(8,128)(2,1)S(1)}, bf16[256,256]{1,0:T(8,128)(2,1)S(1)}, u32[]{:S(2)}, u32[]{:S(2)}) collective-permute-start(bf16[256,256]{1,0:T(8,128)(2,1)S(1)} %relay.3), channel_id=1, source_target_pairs={{0,16},{16,0},{1,17},{17,1},{2,18},{18,2},{3,19},{19,3},{4,20},{20... | collective-permute-start | bytes 393224 | tf_op jit(solution)/shard_map/ppermute | solution.py:32
  45.5 5.2 %collective-permute-start.18 = (bf16[2,64,128]{2,1,0:T(8,128)(2,1)S(1)}, bf16[2,64,128]{2,1,0:T(8,128)(2,1)S(1)}, u32[]{:S(2)}, u32[]{:S(2)}) collective-permute-start(bf16[2,64,128]{2,1,0:T(8,128)(2,1)S(1)} %get-tuple-element.84), channel_id=1, source_target_pairs={{0,4},{4,0},{8,12},{12,8},{1,5},{5,1},{9,13},{13,9},{2,6},{6,2},{1... | collective-permute-start | bytes 98312 | tf_op jit(solution)/shard_map/ppermute | solution.py:32
  45.5 5.2 %collective-permute-start.19 = (bf16[2,64,128]{2,1,0:T(8,128)(2,1)S(1)}, bf16[2,64,128]{2,1,0:T(8,128)(2,1)S(1)}, u32[]{:S(2)}, u32[]{:S(2)}) collective-permute-start(bf16[2,64,128]{2,1,0:T(8,128)(2,1)S(1)} %get-tuple-element.85), channel_id=1, source_target_pairs={{0,8},{4,12},{8,0},{12,4},{1,9},{5,13},{9,1},{13,5},{2,10},{6,14},... | collective-permute-start | bytes 98312 | tf_op jit(solution)/shard_map/ppermute | solution.py:32
  46.7 4.0 %collective-permute-start.20 = (bf16[2,64,128]{2,1,0:T(8,128)(2,1)S(1)}, bf16[2,64,128]{2,1,0:T(8,128)(2,1)S(1)}, u32[]{:S(2)}, u32[]{:S(2)}) collective-permute-start(bf16[2,64,128]{2,1,0:T(8,128)(2,1)S(1)} %get-tuple-element.86), channel_id=1, source_target_pairs={{0,12},{4,8},{8,4},{12,0},{1,13},{5,9},{9,5},{13,1},{2,14},{6,10},... | collective-permute-start | bytes 98312 | tf_op jit(solution)/shard_map/ppermute | solution.py:32
  52.7 7.8 %collective-permute-start.17 = (f32[384,128]{1,0:T(8,128)S(1)}, f32[384,128]{1,0:T(8,128)S(1)}, u32[]{:S(2)}, u32[]{:S(2)}) collective-permute-start(f32[384,128]{1,0:T(8,128)S(1)} %sum_parts.8.refs_0_.refs_2_), channel_id=1, source_target_pairs={{0,8},{4,12},{8,0},{12,4},{1,9},{5,13},{9,1},{13,5},{2,10},{6,14},... | collective-permute-start | bytes 589832 | tf_op jit(solution)/shard_map/ppermute | solution.py:32
  53.8 16.3 %collective-permute-start.22 = (bf16[256,512]{1,0:T(8,128)(2,1)S(1)}, bf16[256,512]{1,0:T(8,128)(2,1)S(1)}, u32[]{:S(2)}, u32[]{:S(2)}) collective-permute-start(bf16[256,512]{1,0:T(8,128)(2,1)S(1)} %sum_parts.9.wa), channel_id=1, source_target_pairs={{0,8},{4,12},{8,0},{12,4},{1,9},{5,13},{9,1},{13,5},{2,10},{6,14},... | collective-permute-start | bytes 786440 | tf_op jit(solution)/shard_map/ppermute | solution.py:32
  70.8 5.7 %collective-permute-start.25 = (f32[8,256]{1,0:T(8,128)S(1)}, f32[8,256]{1,0:T(8,128)S(1)}, u32[]{:S(2)}, u32[]{:S(2)}) collective-permute-start(f32[8,256]{1,0:T(8,128)S(1)} %get-tuple-element.91.refs_4_.refs_0_), channel_id=1, source_target_pairs={{0,3},{1,2},{2,1},{3,0},{4,7},{5,6},{6,5},{7,4},{8,11},{9,10},{10,... | collective-permute-start | bytes 24584 | tf_op jit(solution)/shard_map/ppermute | solution.py:32
  73.0 4.5 %collective-permute-start.24 = (f32[8,256]{1,0:T(8,128)S(1)}, f32[8,256]{1,0:T(8,128)S(1)}, u32[]{:S(2)}, u32[]{:S(2)}) collective-permute-start(f32[8,256]{1,0:T(8,128)S(1)} %get-tuple-element.91.refs_4_.refs_0_), channel_id=1, source_target_pairs={{0,2},{1,3},{2,0},{3,1},{4,6},{5,7},{6,4},{7,5},{8,10},{9,11},{10,... | collective-permute-start | bytes 24584 | tf_op jit(solution)/shard_map/ppermute | solution.py:32
  75.9 6.3 %collective-permute-start.27 = (bf16[2,2,64,128]{3,2,1,0:T(8,128)(2,1)S(1)}, bf16[2,2,64,128]{3,2,1,0:T(8,128)(2,1)S(1)}, u32[]{:S(2)}, u32[]{:S(2)}) collective-permute-start(bf16[2,2,64,128]{3,2,1,0:T(8,128)(2,1)S(1)} %get-tuple-element.92.refs_4_), channel_id=1, source_target_pairs={{0,16},{16,0},{1,17},{17,1},{2,18},{18,2},{3,19},{19,3},{4,20},{20... | collective-permute-start | bytes 196616 | tf_op jit(solution)/shard_map/ppermute | solution.py:32
  77.6 4.7 %collective-permute-start.26 = (f32[8,256]{1,0:T(8,128)S(1)}, f32[8,256]{1,0:T(8,128)S(1)}, u32[]{:S(2)}, u32[]{:S(2)}) collective-permute-start(f32[8,256]{1,0:T(8,128)S(1)} %sum_parts.10.refs_5_.refs_0_), channel_id=1, source_target_pairs={{0,16},{16,0},{1,17},{17,1},{2,18},{18,2},{3,19},{19,3},{4,20},{20... | collective-permute-start | bytes 24584 | tf_op jit(solution)/shard_map/ppermute | solution.py:32
  (13 other events, 63.9 us)
